TPU v7x, 32 devices: a whole 2x2x4 slice. The times are simulated.
32 devices in a mesh: dp: 8 (over z, y), rep: 4 (over x, core).
Axes of the slice: x: 2, y: 2, z: 4, core: 2. Of those that a mesh axis runs over, the one named last changes fastest.
Arguments:
- hot_ids: int32 [4096, 13], P(('dp', 'rep')), may hold values from 0 to 1023
- cold_rows: int32 [4096, 13], P(('dp', 'rep')), may hold values from 0 to 2047
- cold_owner: int32 [53248, 1], P(('dp', 'rep')), may hold values from 0 to 7; in each aligned block of 1664 rows (0 to 1663, 1664 to 3327, ...) at most 416 rows name the same one
- labels: int32 [4096], P(('dp', 'rep')), may hold values 0 or 1
- hot_table: float32 [1024, 128], replicated, may hold values from -6 to 6
- hot_backup: bfloat16 [1024, 128], replicated, may hold values from -6 to 6
- cold_table: float32 [16384, 128], P('dp'), may hold values from -6 to 6
- cold_backup: bfloat16 [16384, 128], P('dp'), may hold values from -6 to 6
- cross_down: bfloat16 [3328, 512], P(None, ('dp', 'rep')), may hold values from -0.109375 to 0.109375
- cross_up: bfloat16 [512, 3328], P(('dp', 'rep')), may hold values from -0.25 to 0.25
- cross_bias: float32 [3328], replicated, may hold values from -3 to 3
- out_weight: float32 [3328], replicated, may hold values from -0.109375 to 0.109375
Outputs:
- new_hot: float32 [1024, 128], replicated
- new_cold: float32 [16384, 128], P('dp')
Inputs may be any that keep to these rules, and one draw needn't show every extreme that they name: `cold_owner`: among the 1664 lookups of one device no owner is named more than 416 times, and in some device one owner is named exactly 416 times.
All inputs are finite; a program needn't handle non-finite values. No bound on the sum of `labels` on one device may be relied on, other than what follows from the above.
Results may differ from a plain program's by a relative error of at most 0.0028.
Values may be sent and summed in bfloat16 or wider, within the bound.
No kernel may reach another device: no remote copies, remote signals or barrier semaphores. Data moves between devices by JAX's collectives and lax.ppermute only.
A program may use at most 64 MiB of HBM per device.

v0:
```python
import math

import jax
import jax.numpy as jnp
from jax import lax
from jax.sharding import PartitionSpec as P

E = 128
NH = 13
NC = 13
HOT = 1024
F = 3328


def compensate(table, backup, grad, rate):
    step_size = rate * grad
    return table - step_size - 0.5 * step_size * step_size * (table - backup.astype(jnp.float32))


def shards(
    hot_ids,
    cold_rows,
    cold_owner,
    labels,
    hot_table,
    hot_backup,
    cold_table,
    cold_backup,
    cross_down,
    cross_up,
    cross_bias,
    out_weight,
):
    rows = hot_ids.shape[0]
    n_data = lax.axis_size("dp")
    n_reps = lax.axis_size("rep")
    lookups = rows * NC
    capacity = 2 * ((lookups + n_data - 1) // n_data)
    owned = cold_table.shape[0]
    owner = cold_owner.reshape(lookups)
    local_row = cold_rows.reshape(lookups)
    onehot = (owner[:, None] == jnp.arange(n_data, dtype=jnp.int32)[None, :]).astype(jnp.int32)
    running = jnp.cumsum(onehot, axis=0)
    slot = jnp.sum(onehot * running, axis=1) - 1
    place = owner * capacity + slot
    requests = (
        jnp.full((n_data * capacity,), -1, jnp.int32)
        .at[place]
        .set(local_row)
        .reshape(n_data, capacity)
    )
    asked = lax.all_to_all(requests, "dp", split_axis=0, concat_axis=0, tiled=True)
    safe = jnp.maximum(asked, 0)
    found = jnp.take(cold_table, safe, axis=0).astype(jnp.bfloat16)
    found = jnp.where((asked >= 0)[:, :, None], found, jnp.zeros_like(found))
    returned = lax.all_to_all(found, "dp", split_axis=0, concat_axis=0, tiled=True)
    cold_emb = returned.reshape(n_data * capacity, E)[place].reshape(rows, NC, E)
    hot_emb = hot_table[hot_ids].astype(jnp.bfloat16)
    first = jnp.concatenate([hot_emb, cold_emb], axis=1).reshape(rows, F)
    down_full, up_full = (
        lax.all_gather(cross_down, ("dp", "rep"), axis=1, tiled=True),
        lax.all_gather(cross_up, ("dp", "rep"), axis=0, tiled=True),
    )
    hidden = jnp.dot(first, down_full, preferred_element_type=jnp.float32).astype(jnp.bfloat16)
    upper = jnp.dot(hidden, up_full, preferred_element_type=jnp.float32) + cross_bias[None, :]
    first_f = first.astype(jnp.float32)
    second = first_f * upper + first_f
    logit = jnp.sum(second * out_weight[None, :], axis=1)
    delta = jax.nn.sigmoid(logit) - labels.astype(jnp.float32)
    d_second = delta[:, None] * out_weight[None, :]
    d_upper = (d_second * first_f).astype(jnp.bfloat16)
    d_hidden = jnp.dot(d_upper, up_full.T, preferred_element_type=jnp.float32).astype(jnp.bfloat16)
    d_first = d_second * (upper + 1.0) + jnp.dot(
        d_hidden, down_full.T, preferred_element_type=jnp.float32
    )
    grads = d_first.reshape(rows, NH + NC, E)
    hot_partial = jax.ops.segment_sum(grads[:, :NH].reshape(rows * NH, E), hot_ids.reshape(-1), HOT)
    cold_low = grads[:, NH:].astype(jnp.bfloat16).reshape(lookups, E)
    outgoing = (
        jnp.zeros((n_data * capacity, E), jnp.bfloat16)
        .at[place]
        .set(cold_low)
        .reshape(n_data, capacity, E)
    )
    incoming = lax.all_to_all(outgoing, "dp", split_axis=0, concat_axis=0, tiled=True)
    flat_ids = asked.reshape(-1)
    segment = jnp.where(flat_ids >= 0, flat_ids, owned)
    cold_partial = jax.ops.segment_sum(
        incoming.reshape(n_data * capacity, E).astype(jnp.float32), segment, owned
    )
    batch_all = rows * n_data * n_reps
    rate_hot = 20.0 * math.sqrt(HOT / (batch_all * NH))
    rate_cold = 20.0 * math.sqrt(owned * n_data / (batch_all * NC))
    hot_grad = lax.psum(hot_partial, ("dp", "rep"))
    new_hot = compensate(hot_table, hot_backup, hot_grad, rate_hot)
    cold_grad = lax.psum(cold_partial, "rep")
    new_cold = compensate(cold_table, cold_backup, cold_grad, rate_cold)
    return (new_hot, new_cold)


def solution(mesh):
    placed = (
        P(("dp", "rep"), None),
        P(("dp", "rep"), None),
        P(("dp", "rep"), None),
        P(("dp", "rep")),
        P(),
        P(),
        P("dp", None),
        P("dp", None),
        P(None, ("dp", "rep")),
        P(("dp", "rep"), None),
        P(),
        P(),
    )
    return jax.shard_map(
        shards, mesh=mesh, in_specs=placed, out_specs=(P(), P("dp", None)), check_vma=False
    )
```

profile of v0, /device:TPU:0, one launch (start us, length us, event | category | flops | bytes accessed | tf_op | source)
XLA Modules:
  0.0 365.6 jit_solution(12886167079261448742)
XLA Ops:
  7.2 0.0 copy-start
  7.2 0.0 all-gather.3.cloned.1.call-start
  7.2 0.7 all-gather.3.cloned.1.call-update
  7.9 0.0 all-gather.5.cloned.1.call-start
  8.0 0.7 all-gather.5.cloned.1.call-update
  8.7 0.7 reduce
  9.4 2.3 reduce-window.6
  11.7 0.3 slice_reduce_fusion
  12.0 0.2 reduce-window.9
  12.1 0.8 copy.32
  12.9 0.2 reshape.155
  13.1 0.1 add_bitcast_fusion
  13.3 0.7 fusion.23
  14.0 8.8 %scatter_custom_fusion = s32[3328]{0:T(1024)S(1)} fusion(s32[1664]{0:T(1024)S(1)} %fusion.23, s32[1664]{0:T(1024)S(1)} %reshape.155, s32[]{:T(128)} %constant.19.clone.1), kind=kCustom, calls=%fused_computation.50 | custom fusion | bytes 13316 | tf_op jit(solution)/shard_map/scatter | solution.py:49
  22.8 0.1 all_to_all.12
  22.9 13.7 %all_to_all.19 = s32[8,1,416]{2,1,0:T(1,128)S(1)} all-to-all(s32[8,1,416]{2,1,0:T(1,128)S(1)} %all_to_all.12), channel_id=1, replica_groups=mesh['dp'=8,'rep'=4] {'dp'}, dimensions={0} | all-to-all | bytes 26624 | tf_op jit(solution)/shard_map/all_to_all | solution.py:52
  36.6 0.1 reshape.137
  36.7 5.5 %gather_fusion.1 = bf16[3328,128]{1,0:T(8,128)(2,1)S(1)} fusion(f32[2048,128]{1,0:T(8,128)S(1)} %copy-done, s32[4096]{0:T(1024)S(1)} %pad_clamp_fusion), kind=kCustom, calls=%fused_computation.1 | custom fusion | bytes 1717248 | tf_op jit(solution)/shard_map/jit(_take)/gather | solution.py:54
  42.3 0.0 copy-start.5
  42.3 0.0 copy-start.1
  42.3 2.3 fusion.5
  44.5 3.6 all-to-all-start.1
  48.1 0.0 copy-done.5
  48.1 0.1 copy.31
  48.2 0.2 reshape.129
  48.5 0.0 copy-done.1
  48.5 3.3 gather_fusion
  51.8 0.1 reshape.188
  52.0 26.0 %all-to-all-done.1 = bf16[8,416,128]{2,1,0:T(8,128)(2,1)S(1)} async-done(((bf16[8,416,128]{2,1,0:T(8,128)(2,1)}), bf16[8,416,128]{2,1,0:T(8,128)(2,1)S(1)}, u32[]{:S(2)}, u32[]{:S(2)}) %all-to-all-start.1) | async-done | bytes 852000 | tf_op jit(solution)/shard_map/all_to_all | solution.py:56
  78.0 3.9 %gather_fusion.2 = bf16[1664,128]{1,0:T(8,128)(2,1)S(1)} fusion(bf16[3328,128]{1,0:T(8,128)(2,1)S(1)} %bitcast.34, s32[2048]{0:T(1024)S(1)} %pad_clamp_fusion.1), kind=kCustom, calls=%fused_computation.2 | custom fusion | bytes 858624 | tf_op jit(solution)/shard_map/gather | solution.py:57
  81.9 0.1 reshape.119
  82.1 1.3 pad_maximum_fusion
  83.4 2.2 copy.35
  85.6 0.6 copy.36
  86.2 0.0 copy-start.7
  86.2 0.0 all-gather.3.cloned.1.call-done
  86.3 54.9 %all-gather.5.cloned.1.call-done = bf16[512,3328]{1,0:T(8,128)(2,1)} async-done(((bf16[16,3328]{1,0:T(8,128)(2,1)}), bf16[512,3328]{1,0:T(8,128)(2,1)}) %all-gather.5.cloned.1.call-update) | async-done | bytes 3407888 | tf_op jit(solution)/shard_map/all_gather | solution.py:62
  141.2 6.1 %fusion.2 = (f32[128]{0:T(128)S(1)}, f32[128,3328]{1,0:T(8,128)}) fusion(bf16[128,3328]{1,0:T(8,128)(2,1)S(1)} %copy.36, f32[3328]{0:T(1024)S(1)} %copy-done.4, f32[3328]{0:T(1024)S(1)} %copy-done.6, bf16[512,3328]{1,0:T(8,128)(2,1)} %all-gather.5.cloned.1.call-done, bf16[128,3328]{0,1:T(8,128)(2,1)S(1)} %bitcast.36, ...), kind=kOutput, calls=%fused_computation.14 | convolution fusion | flops 875036544 | bytes 10250752 | tf_op jit(solution)/shard_map/dot_general | solution.py:65
  147.3 0.0 copy-done.7
  147.3 6.5 %convolution_add_fusion = f32[128,3328]{1,0:T(8,128)} fusion(bf16[3328,512]{0,1:T(8,128)(2,1)} %all-gather.3.cloned.1.call-done, f32[128,3328]{1,0:T(8,128)} %get-tuple-element.5, bf16[512,3328]{1,0:T(8,128)(2,1)} %all-gather.5.cloned.1.call-done, bf16[128,3328]{1,0:T(8,128)(2,1)S(1)} %copy.36, f32[128]{0:T(128)S(1)} %divide_subtract_fusion, ...), kind=kOutput, calls=%fused_computation.7 | convolution fusion | flops 875888640 | bytes 11089408 | tf_op jit(solution)/shard_map/dot_general | solution.py:73
  153.8 1.8 copy.37
  155.6 0.8 slice.28
  156.4 2.2 copy.39
  158.6 2.0 reshape.171
  160.5 9.2 %scatter_custom_fusion.2 = bf16[3328,128]{1,0:T(8,128)(2,1)} fusion(s32[1664]{0:T(1024)S(1)} %fusion.23, bf16[1664,128]{1,0:T(8,128)(2,1)} %reshape.171, bf16[]{:T(256)} %constant.24.clone.1), kind=kCustom, calls=%fused_computation.28 | custom fusion | bytes 852480 | tf_op jit(solution)/shard_map/scatter | solution.py:82
  169.8 4.3 %all-to-all-start.2 = ((bf16[8,416,128]{2,1,0:T(8,128)(2,1)}), bf16[8,416,128]{2,1,0:T(8,128)(2,1)}, u32[]{:S(2)}, u32[]{:S(2)}) async-start(bf16[8,416,128]{2,1,0:T(8,128)(2,1)} %bitcast.39), calls=%async_computation.2 | async-start | bytes 1703936 | tf_op jit(solution)/shard_map/all_to_all | solution.py:85
  174.1 0.2 all-reduce.3.cloned.1.call-start
  174.3 0.1 copy.30
  174.4 0.2 reshape.161
  174.6 1.0 slice.24
  175.6 1.7 copy.38
  177.2 0.1 reshape.163
  177.3 12.4 %scatter_custom_fusion.1 = f32[1024,128]{1,0:T(8,128)} fusion(s32[1664]{0:T(1024)S(1)} %reshape.161, f32[1664,128]{1,0:T(8,128)S(1)} %reshape.163, f32[]{:T(128)} %constant.15.clone.1), kind=kCustom, calls=%fused_computation.30 | custom fusion | flops 212992 | bytes 524292 | tf_op jit(solution)/shard_map/scatter-add | solution.py:77
  189.7 0.0 all-reduce.3.cloned.1.call-update
  189.7 0.0 all-reduce.5.cloned.1.call-start
  189.8 0.1 reshape.123
  189.9 6.3 %all-to-all-done.2 = bf16[8,416,128]{2,1,0:T(8,128)(2,1)} async-done(((bf16[8,416,128]{2,1,0:T(8,128)(2,1)}), bf16[8,416,128]{2,1,0:T(8,128)(2,1)}, u32[]{:S(2)}, u32[]{:S(2)}) %all-to-all-start.2) | async-done | bytes 852000 | tf_op jit(solution)/shard_map/all_to_all | solution.py:85
  196.3 21.1 %scatter_custom_fusion.3 = f32[2048,128]{1,0:T(8,128)} fusion(s32[3328]{0:T(1024)S(1)} %fusion.20, bf16[3328,128]{1,0:T(8,128)(2,1)} %bitcast.9, f32[]{:T(128)} %constant.15.clone.1), kind=kCustom, calls=%fused_computation.15 | custom fusion | flops 851968 | bytes 1900548 | tf_op jit(solution)/shard_map/scatter-add | solution.py:88
  217.3 0.0 all-reduce.5.cloned.1.call-update
  217.4 101.1 %all-reduce.3.cloned.1.call-done = f32[1024,128]{1,0:T(8,128)} async-done(((f32[1024,128]{1,0:T(8,128)}), f32[1024,128]{1,0:T(8,128)}) %all-reduce.3.cloned.1.call-update) | async-done | bytes 524304 | tf_op jit(solution)/shard_map/psum | solution.py:94
  318.5 0.0 copy-done.3
  318.5 2.0 multiply_subtract_fusion.1
  320.5 36.1 %all-reduce.5.cloned.1.call-done = f32[2048,128]{1,0:T(8,128)} async-done(((f32[2048,128]{1,0:T(8,128)}), f32[2048,128]{1,0:T(8,128)}) %all-reduce.5.cloned.1.call-update) | async-done | bytes 1048592 | tf_op jit(solution)/shard_map/psum | solution.py:96
  356.6 2.5 multiply_subtract_fusion
  (20 shorter events, 0.2 us)
Async XLA Ops:
  7.2 29.5 %copy-start = (f32[2048,128]{1,0:T(8,128)S(1)}, f32[2048,128]{1,0:T(8,128)}, u32[]{:S(2)}) copy-start(f32[2048,128]{1,0:T(8,128)} %param.18) | copy-start | bytes 3145732
  7.2 79.1 %all-gather.3.cloned.1.call-start = ((), (), s32[]{:S(2)}) async-start(), calls=%async_computation.3 | async-start | bytes 3514368 | tf_op jit(solution)/shard_map/all_gather | solution.py:61
  7.9 133.3 %all-gather.5.cloned.1.call-start = ((), (), s32[]{:S(2)}) async-start(), calls=%async_computation.4 | async-start | bytes 3514368 | tf_op jit(solution)/shard_map/all_gather | solution.py:62
  42.3 5.9 %copy-start.5 = (s32[128,13]{0,1:T(8,128)S(1)}, s32[128,13]{0,1:T(8,128)}, u32[]{:S(2)}) copy-start(s32[128,13]{0,1:T(8,128)} %param.12) | copy-start | bytes 19972
  42.3 6.2 %copy-start.1 = (f32[1024,128]{1,0:T(8,128)S(1)}, f32[1024,128]{1,0:T(8,128)}, u32[]{:S(2)}) copy-start(f32[1024,128]{1,0:T(8,128)} %param.16) | copy-start | bytes 1572868
  44.5 33.5 %all-to-all-start.1 = ((bf16[8,416,128]{2,1,0:T(8,128)(2,1)}), bf16[8,416,128]{2,1,0:T(8,128)(2,1)S(1)}, u32[]{:S(2)}, u32[]{:S(2)}) async-start(bf16[8,416,128]{2,1,0:T(8,128)(2,1)} %fusion.5), calls=%async_computation.1 | async-start | bytes 1703936 | tf_op jit(solution)/shard_map/all_to_all | solution.py:56
  83.4 57.8 %copy-start.4 = (f32[3328]{0:T(1024)S(1)}, f32[3328]{0:T(1024)}, u32[]{:S(2)}) copy-start(f32[3328]{0:T(1024)} %param.23) | copy-start | bytes 39940
  83.4 57.8 %copy-start.6 = (f32[3328]{0:T(1024)S(1)}, f32[3328]{0:T(1024)}, u32[]{:S(2)}) copy-start(f32[3328]{0:T(1024)} %param.22) | copy-start | bytes 39940
  86.2 61.1 %copy-start.7 = (s32[128]{0:T(128)S(1)}, s32[128]{0:T(128)}, u32[]{:S(2)}) copy-start(s32[128]{0:T(128)} %param.15) | copy-start | bytes 1540
  169.8 26.5 %all-to-all-start.2 = ((bf16[8,416,128]{2,1,0:T(8,128)(2,1)}), bf16[8,416,128]{2,1,0:T(8,128)(2,1)}, u32[]{:S(2)}, u32[]{:S(2)}) async-start(bf16[8,416,128]{2,1,0:T(8,128)(2,1)} %bitcast.39), calls=%async_computation.2 | async-start | bytes 1703936 | tf_op jit(solution)/shard_map/all_to_all | solution.py:85
  174.1 144.4 %all-reduce.3.cloned.1.call-start = ((), (), s32[]{:S(2)}) async-start(), calls=%async_computation.5 | async-start | bytes 1048576 | tf_op jit(solution)/shard_map/psum | solution.py:94
  189.6 128.8 %copy-start.3 = (bf16[1024,128]{1,0:T(8,128)(2,1)S(1)}, bf16[1024,128]{1,0:T(8,128)(2,1)}, u32[]{:S(2)}) copy-start(bf16[1024,128]{1,0:T(8,128)(2,1)} %param.17) | copy-start | bytes 786436
  189.7 166.9 %all-reduce.5.cloned.1.call-start = ((), (), s32[]{:S(2)}) async-start(), calls=%async_computation.6 | async-start | bytes 2097152 | tf_op jit(solution)/shard_map/psum | solution.py:96
  217.3 139.2 %copy-start.2 = (bf16[2048,128]{1,0:T(8,128)(2,1)S(1)}, bf16[2048,128]{1,0:T(8,128)(2,1)}, u32[]{:S(2)}) copy-start(bf16[2048,128]{1,0:T(8,128)(2,1)} %param.19) | copy-start | bytes 1572868
Sparse Core Ops, SparseCore 0:
  10.8 68.7 all-gather.2
  82.5 58.6 all-gather.4
  189.8 128.6 all-reduce.2
  321.4 35.1 all-reduce.4
where the time goes:
time: 366 us
  waiting for transfers between devices  226 us (62%)
  other arithmetic  45.6 us (12%)
  local copies, waits for them, and re-layouts  45.5 us (12%)
  between operations  14 us (4%)
  blocking collectives  13.7 us (4%)
  matrix products  12.6 us (3%)
  starting transfers between devices  8.18 us (2%)
    psum x1, waiting for transfers between devices, shards(): hot_grad = lax.psum(hot_partial, ('dp', 'rep'))  101 us
    all_gather x1, waiting for transfers between devices, shards(): lax.all_gather(cross_up, ('dp', 'rep'), axis=0, tiled=True)  54.9 us
    psum x1, waiting for transfers between devices, shards(): cold_grad = lax.psum(cold_partial, 'rep')  36.1 us
    all_to_all x1, waiting for transfers between devices, shards(): lax.all_to_all(found, 'dp', split_axis=0, concat_axis=0, tiled=True)  26 us
    scatter-add x1, other arithmetic, shards(): jax.ops.segment_sum(incoming.reshape(n_data * capacity, E).astype(jnp.flo...  21.1 us
    all_to_all x1, blocking collectives, shards(): lax.all_to_all(requests, 'dp', split_axis=0, concat_axis=0, tiled=True)  13.7 us
    scatter-add x1, other arithmetic, shards(): jax.ops.segment_sum(grads[:, :NH].reshape(rows * NH, E), hot_ids.reshape(...  12.4 us
    scatter x1, local copies, waits for them, and re-layouts, shards(): outgoing = jnp.zeros((n_data * capacity, E), jnp.bfloat16).at[place].set(...  9.22 us
  transfers between devices with their start and end apart: 6, of which 5 were waited for; matrix products, arithmetic and copies ran while one was open for 20% of the time, Pallas kernels for 0%

commit v1 on v0

--- a/solution.py
+++ b/solution.py
@@ -15,6 +15,86 @@
 def compensate(table, backup, grad, rate):
     step_size = rate * grad
     return table - step_size - 0.5 * step_size * step_size * (table - backup.astype(jnp.float32))
+
+
+def is_small(n_data, n_reps):
+    return n_reps == 4 and n_data % 2 == 0 and n_data <= 16
+
+
+def swap(value, axis, distance):
+    size = lax.axis_size(axis)
+    return lax.ppermute(value, axis, [(i, i ^ distance) for i in range(size)])
+
+
+def shift(value, axis, distance):
+    size = lax.axis_size(axis)
+    return lax.ppermute(value, axis, [(i, (i + distance) % size) for i in range(size)])
+
+
+def gather_weights(down_t, up):
+    n_data = lax.axis_size("dp")
+    own = jnp.concatenate([down_t, up], axis=0)
+    rank = down_t.shape[0]
+    column = [own] + [shift(own, "dp", 2 * k) for k in range(1, n_data // 2)]
+    half = len(column) * rank
+    column = jnp.concatenate([c[:rank] for c in column] + [c[rank:] for c in column], axis=0)
+    over_x = swap(column, "rep", 2)
+    over_y = swap(column, "dp", 1)
+    across = jnp.concatenate(
+        [swap(over_y[:half], "rep", 2), swap(over_x[half:], "dp", 1)], axis=0
+    )
+    pieces = []
+    for piece in (column, over_x, over_y, across):
+        pieces += [piece, swap(piece, "rep", 1)]
+    return (
+        jnp.concatenate([p[:half] for p in pieces], axis=0),
+        jnp.concatenate([p[half:] for p in pieces], axis=0),
+    )
+
+
+def half_of(value, index, count):
+    rows = value.shape[0] // count
+    return lax.dynamic_slice_in_dim(value, index * rows, rows, axis=0)
+
+
+def paired(mine, other, index):
+    return jnp.where(
+        index == 0,
+        jnp.concatenate([mine, other], axis=0),
+        jnp.concatenate([other, mine], axis=0),
+    )
+
+
+def sum_hot(partial):
+    n_data = lax.axis_size("dp")
+    nz = n_data // 2
+    rep, data = lax.axis_index("rep"), lax.axis_index("dp")
+    core, x, y, z = rep % 2, rep // 2, data % 2, data // 2
+    total = partial
+    for axis, distance, index in (("rep", 1, core), ("rep", 2, x), ("dp", 1, y)):
+        total = half_of(total, index, 2) + swap(half_of(total, 1 - index, 2), axis, distance)
+    rows = total.shape[0] // nz
+    parts = [half_of(total, z, nz)]
+    for k in range(1, nz):
+        parts.append(shift(half_of(total, (z + k) % nz, nz), "dp", 2 * k))
+    total = sum(parts[1:], parts[0])
+    back = [total] + [shift(total, "dp", 2 * k) for k in range(1, nz)]
+    whole = jnp.zeros((rows * nz, E), total.dtype)
+    for k, piece in enumerate(back):
+        whole = lax.dynamic_update_slice_in_dim(whole, piece, ((z - k) % nz) * rows, axis=0)
+    total = whole
+    for axis, distance, index in (("dp", 1, y), ("rep", 2, x), ("rep", 1, core)):
+        total = paired(total, swap(total, axis, distance), index)
+    return total
+
+
+def sum_cold(partial):
+    rep = lax.axis_index("rep")
+    core = rep % 2
+    chip = partial + swap(partial, "rep", 1)
+    mine = half_of(chip, core, 2).astype(jnp.bfloat16)
+    mine = mine.astype(jnp.float32) + swap(mine, "rep", 2).astype(jnp.float32)
+    return paired(mine, swap(mine, "rep", 1), core)
 
 
 def shards(
@@ -37,6 +117,11 @@
     lookups = rows * NC
     capacity = 2 * ((lookups + n_data - 1) // n_data)
     owned = cold_table.shape[0]
+    if is_small(n_data, n_reps):
+        down_t, up_full = gather_weights(cross_down.T, cross_up)
+    else:
+        down_t = lax.all_gather(cross_down.T, ("dp", "rep"), axis=0, tiled=True)
+        up_full = lax.all_gather(cross_up, ("dp", "rep"), axis=0, tiled=True)
     owner = cold_owner.reshape(lookups)
     local_row = cold_rows.reshape(lookups)
     onehot = (owner[:, None] == jnp.arange(n_data, dtype=jnp.int32)[None, :]).astype(jnp.int32)
@@ -52,16 +137,11 @@
     asked = lax.all_to_all(requests, "dp", split_axis=0, concat_axis=0, tiled=True)
     safe = jnp.maximum(asked, 0)
     found = jnp.take(cold_table, safe, axis=0).astype(jnp.bfloat16)
-    found = jnp.where((asked >= 0)[:, :, None], found, jnp.zeros_like(found))
     returned = lax.all_to_all(found, "dp", split_axis=0, concat_axis=0, tiled=True)
     cold_emb = returned.reshape(n_data * capacity, E)[place].reshape(rows, NC, E)
     hot_emb = hot_table[hot_ids].astype(jnp.bfloat16)
     first = jnp.concatenate([hot_emb, cold_emb], axis=1).reshape(rows, F)
-    down_full, up_full = (
-        lax.all_gather(cross_down, ("dp", "rep"), axis=1, tiled=True),
-        lax.all_gather(cross_up, ("dp", "rep"), axis=0, tiled=True),
-    )
-    hidden = jnp.dot(first, down_full, preferred_element_type=jnp.float32).astype(jnp.bfloat16)
+    hidden = jnp.dot(first, down_t.T, preferred_element_type=jnp.float32).astype(jnp.bfloat16)
     upper = jnp.dot(hidden, up_full, preferred_element_type=jnp.float32) + cross_bias[None, :]
     first_f = first.astype(jnp.float32)
     second = first_f * upper + first_f
@@ -71,7 +151,7 @@
     d_upper = (d_second * first_f).astype(jnp.bfloat16)
     d_hidden = jnp.dot(d_upper, up_full.T, preferred_element_type=jnp.float32).astype(jnp.bfloat16)
     d_first = d_second * (upper + 1.0) + jnp.dot(
-        d_hidden, down_full.T, preferred_element_type=jnp.float32
+        d_hidden, down_t, preferred_element_type=jnp.float32
     )
     grads = d_first.reshape(rows, NH + NC, E)
     hot_partial = jax.ops.segment_sum(grads[:, :NH].reshape(rows * NH, E), hot_ids.reshape(-1), HOT)
@@ -91,9 +171,13 @@
     batch_all = rows * n_data * n_reps
     rate_hot = 20.0 * math.sqrt(HOT / (batch_all * NH))
     rate_cold = 20.0 * math.sqrt(owned * n_data / (batch_all * NC))
-    hot_grad = lax.psum(hot_partial, ("dp", "rep"))
+    if is_small(n_data, n_reps):
+        hot_grad = sum_hot(hot_partial)
+        cold_grad = sum_cold(cold_partial)
+    else:
+        hot_grad = lax.psum(hot_partial, ("dp", "rep"))
+        cold_grad = lax.psum(cold_partial, "rep")
     new_hot = compensate(hot_table, hot_backup, hot_grad, rate_hot)
-    cold_grad = lax.psum(cold_partial, "rep")
     new_cold = compensate(cold_table, cold_backup, cold_grad, rate_cold)
     return (new_hot, new_cold)
 

time: 366 us -> 225 us (0.61)
  waiting for transfers between devices: 226 us -> 53.9 us
  starting transfers between devices: 8.18 us -> 41.5 us
  local copies, waits for them, and re-layouts: 45.5 us -> 67.9 us
  blocking collectives: 13.7 us -> 0 us
  between operations: 14 us -> 1.08 us
    psum x2 -> x0, waiting for transfers between devices: 137 us -> none  [the longest x1 101 us: shards(): hot_grad = lax.psum(hot_partial, ('dp', 'rep'))]
    all_gather x2 -> x0, waiting for transfers between devices: 54.9 us -> none  [the longest x1 54.9 us: shards(): lax.all_gather(cross_up, ('dp', 'rep'), axis=0, tiled=True)]
    ppermute x0 -> x26, waiting for transfers between devices: none -> 49 us  [the longest x17 44.6 us: swap(): return lax.ppermute(value, axis, [(i, i ^ distance) for i in range(size)])]
    ppermute x0 -> x26, starting transfers between devices: none -> 27.8 us  [the longest x9 15.5 us: shift(): lax.ppermute(value, axis, [(i, (i + distance) % size) for i in range(size)])]
    all_to_all x1, waiting for transfers between devices: 26 us -> 0.01 us  [shards(): lax.all_to_all(found, 'dp', split_axis=0, concat_axis=0, tiled=True)]
    unnamed x18 -> x31, local copies, waits for them, and re-layouts: 0.96 us -> 21.6 us
    all_to_all x1 -> x0, blocking collectives: 13.7 us -> none  [shards(): lax.all_to_all(requests, 'dp', split_axis=0, concat_axis=0, tiled=True)]
  transfers between devices with their start and end apart: 6 -> 29, of which waited for: 5 -> 14; matrix products, arithmetic and copies ran while one was open for 20% -> 42% of each run, Pallas kernels for 0% -> 0%
where the time goes in v1:
time: 225 us; the launch traced here: 224 us
  local copies, waits for them, and re-layouts  67.9 us (30%)
  waiting for transfers between devices  53.9 us (24%)
  other arithmetic  47.5 us (21%)
  starting transfers between devices  41.5 us (18%)
  matrix products  12.6 us (6%)
    ppermute x17, waiting for transfers between devices, swap(): return lax.ppermute(value, axis, [(i, i ^ distance) for i in range(size)])  44.6 us
    unnamed x31, local copies, waits for them, and re-layouts  21.6 us
    scatter-add x1, other arithmetic, shards(): jax.ops.segment_sum(incoming.reshape(n_data * capacity, E).astype(jnp.flo...  20.4 us
    ppermute x9, starting transfers between devices, shift(): lax.ppermute(value, axis, [(i, (i + distance) % size) for i in range(size)])  15.5 us
    ppermute x17, starting transfers between devices, swap(): return lax.ppermute(value, axis, [(i, i ^ distance) for i in range(size)])  12.3 us
    scatter-add x1, other arithmetic, shards(): jax.ops.segment_sum(grads[:, :NH].reshape(rows * NH, E), hot_ids.reshape(...  11.9 us
    scatter x1, local copies, waits for them, and re-layouts, shards(): outgoing = jnp.zeros((n_data * capacity, E), jnp.bfloat16).at[place].set(...  9.24 us
    scatter x1, local copies, waits for them, and re-layouts, shards(): requests = jnp.full((n_data * capacity,), -1, jnp.int32).at[place].set(lo...  8.81 us
  transfers between devices with their start and end apart: 29, of which 14 were waited for; matrix products, arithmetic and copies ran while one was open for 42% of the time, Pallas kernels for 0%

profile of v1, /device:TPU:0, one launch (start us, length us, event | category | flops | bytes accessed | tf_op | source)
XLA Modules:
  0.0 224.4 jit_solution(969469423881838647)
XLA Ops:
  0.6 1.0 pad_maximum_fusion.2
  1.7 3.1 %collective-permute-start = (bf16[32,3328]{1,0:T(8,128)(2,1)S(1)}, bf16[32,3328]{1,0:T(8,128)(2,1)S(1)}, u32[]{:S(2)}, u32[]{:S(2)}) collective-permute-start(bf16[32,3328]{1,0:T(8,128)(2,1)S(1)} %pad_maximum_fusion.2), channel_id=1, source_target_pairs={{0,8},{4,12},{8,16},{12,20},{16,24},{20,28},{24,0},{28,4},{1,9},{5... | collective-permute-start | bytes 638984 | tf_op jit(solution)/shard_map/ppermute | solution.py:31
  4.7 2.6 %collective-permute-start.1 = (bf16[32,3328]{1,0:T(8,128)(2,1)S(1)}, bf16[32,3328]{1,0:T(8,128)(2,1)S(1)}, u32[]{:S(2)}, u32[]{:S(2)}) collective-permute-start(bf16[32,3328]{1,0:T(8,128)(2,1)S(1)} %pad_maximum_fusion.2), channel_id=1, source_target_pairs={{0,16},{4,20},{8,24},{12,28},{16,0},{20,4},{24,8},{28,12},{1,17},{... | collective-permute-start | bytes 638984 | tf_op jit(solution)/shard_map/ppermute | solution.py:31
  7.3 1.3 collective-permute-start.2
  9.4 2.3 %reduce-window.6 = s32[8,13,128]{2,1,0:T(8,128)S(1)} reduce-window(s32[8,13,128]{2,1,0:T(8,128)S(1)} %fusion.17, s32[]{:T(128)} %constant.125.clone.1), window={size=1x1x128 pad=0_0x0_0x127_0}, to_apply=%region_0.0 | reduce-window | flops 1690624 | bytes 106500 | tf_op jit(solution)/shard_map/reduce-window
  13.0 0.8 copy.32
  14.0 8.8 %scatter_custom_fusion = s32[3328]{0:T(1024)S(1)} fusion(s32[1664]{0:T(1024)S(1)} %fusion.23, s32[1664]{0:T(1024)S(1)} %reshape.148, s32[]{:T(128)} %constant.128.clone.1), kind=kCustom, calls=%fused_computation.91 | custom fusion | bytes 13316 | tf_op jit(solution)/shard_map/scatter | solution.py:134
  23.5 3.3 %all-to-all-start = ((s32[8,1,416]{2,1,0:T(1,128)}), s32[8,1,416]{2,1,0:T(1,128)S(1)}, u32[]{:S(2)}, u32[]{:S(2)}) async-start(s32[8,1,416]{2,1,0:T(1,128)} %all_to_all.12), calls=%async_computation | async-start | bytes 32768 | tf_op jit(solution)/shard_map/all_to_all | solution.py:137
  26.9 1.6 constant_dynamic-update-slice_fusion.1
  31.5 1.6 constant_dynamic-update-slice_fusion.7
  35.3 1.5 collective-permute-start.4
  36.8 3.3 %gather_fusion = bf16[1664,128]{1,0:T(8,128)(2,1)S(1)} fusion(f32[1024,128]{1,0:T(8,128)S(1)} %copy-done.1, s32[2048]{0:T(1024)S(1)} %pad_clamp_fusion.2), kind=kCustom, calls=%fused_computation | custom fusion | bytes 858624 | tf_op jit(solution)/shard_map/gather | solution.py:142
  40.4 5.5 %gather_fusion.1 = bf16[3328,128]{1,0:T(8,128)(2,1)S(1)} fusion(f32[2048,128]{1,0:T(8,128)S(1)} %copy-done, s32[4096]{0:T(1024)S(1)} %pad_clamp_fusion), kind=kCustom, calls=%fused_computation.1 | custom fusion | bytes 1717248 | tf_op jit(solution)/shard_map/jit(_take)/gather | solution.py:139
  45.9 1.4 select_convert_fusion
  47.3 5.9 %all-to-all-start.1 = ((bf16[8,416,128]{2,1,0:T(8,128)(2,1)}), bf16[8,416,128]{2,1,0:T(8,128)(2,1)S(1)}, u32[]{:S(2)}, u32[]{:S(2)}) async-start(bf16[8,416,128]{2,1,0:T(8,128)(2,1)} %select_convert_fusion), calls=%async_computation.1 | async-start | bytes 1703936 | tf_op jit(solution)/shard_map/all_to_all | solution.py:140
  53.3 2.0 collective-permute-start.6
  55.3 1.6 collective-permute-done.4
  56.9 2.1 slice_dynamic-update-slice_fusion.4
  59.0 2.2 constant_dynamic-update-slice_fusion.6
  61.3 1.9 collective-permute-start.9
  63.2 21.3 %collective-permute-done.6 = bf16[128,3328]{1,0:T(8,128)(2,1)} collective-permute-done((bf16[128,3328]{1,0:T(8,128)(2,1)}, bf16[128,3328]{1,0:T(8,128)(2,1)}, u32[]{:S(2)}, u32[]{:S(2)}) %collective-permute-start.6) | collective-permute-done | bytes 852000 | tf_op jit(solution)/shard_map/ppermute | solution.py:26
  84.5 3.9 %gather_fusion.2 = bf16[1664,128]{1,0:T(8,128)(2,1)S(1)} fusion(bf16[3328,128]{1,0:T(8,128)(2,1)S(1)} %bitcast.35, s32[2048]{0:T(1024)S(1)} %pad_clamp_fusion.1), kind=kCustom, calls=%fused_computation.2 | custom fusion | bytes 858624 | tf_op jit(solution)/shard_map/gather | solution.py:141
  88.6 1.3 pad_maximum_fusion
  89.9 2.2 copy.34
  92.7 2.1 slice_dynamic-update-slice_fusion.3
  94.8 2.1 slice_dynamic-update-slice_fusion.2
  97.5 2.1 slice_dynamic-update-slice_fusion.1
  99.6 9.5 %collective-permute-done.8 = bf16[64,3328]{1,0:T(8,128)(2,1)S(1)} collective-permute-done((bf16[64,3328]{1,0:T(8,128)(2,1)S(1)}, bf16[64,3328]{1,0:T(8,128)(2,1)S(1)}, u32[]{:S(2)}, u32[]{:S(2)}) %collective-permute-start.8) | collective-permute-done | bytes 426016 | tf_op jit(solution)/shard_map/ppermute | solution.py:26
  109.2 1.1 pad_maximum_fusion.1
  110.3 1.8 constant_dynamic-update-slice_fusion.5
  112.1 0.8 constant_dynamic-update-slice_fusion.2
  113.0 1.0 slice_dynamic-update-slice_fusion
  113.9 6.1 %fusion.2 = (f32[128]{0:T(128)S(1)}, f32[128,3328]{1,0:T(8,128)}) fusion(bf16[128,3328]{1,0:T(8,128)(2,1)S(1)} %copy.35, f32[3328]{0:T(1024)S(1)} %copy-done.3, f32[3328]{0:T(1024)S(1)} %copy-done.5, bf16[512,3328]{1,0:T(8,128)(2,1)} %get-tuple-element.4, bf16[128,3328]{0,1:T(8,128)(2,1)S(1)} %bitcast.37, bf16[512,3328]{1,0:T(8,128)(2,1)} %get-tuple-element.5), kind=kOutput, calls=%fused_computation.14 | convolution fusion | flops 875036544 | bytes 10250752 | tf_op jit(solution)/shard_map/dot_general | solution.py:145
  120.1 6.5 %convolution_add_fusion = f32[128,3328]{1,0:T(8,128)} fusion(bf16[512,3328]{1,0:T(8,128)(2,1)} %get-tuple-element.5, f32[128,3328]{1,0:T(8,128)} %get-tuple-element.35, bf16[512,3328]{1,0:T(8,128)(2,1)} %get-tuple-element.4, bf16[128,3328]{1,0:T(8,128)(2,1)S(1)} %copy.35, f32[128]{0:T(128)S(1)} %divide_subtract_fusion, f32[3328]{0:T(1024)S(1)} %copy-done.3), kind=kOutput, calls=%fused_computation.7 | convolution fusion | flops 875888640 | bytes 11089408 | tf_op jit(solution)/shard_map/dot_general | solution.py:153
  126.6 1.8 copy.36
  128.4 0.8 slice.148
  129.2 2.2 copy.38
  131.4 2.0 reshape.164
  133.4 9.2 %scatter_custom_fusion.2 = bf16[3328,128]{1,0:T(8,128)(2,1)} fusion(s32[1664]{0:T(1024)S(1)} %fusion.23, bf16[1664,128]{1,0:T(8,128)(2,1)} %reshape.164, bf16[]{:T(256)} %constant.149.clone.1), kind=kCustom, calls=%fused_computation.43 | custom fusion | bytes 852480 | tf_op jit(solution)/shard_map/scatter | solution.py:162
  142.6 4.4 %all-to-all-start.2 = ((bf16[8,416,128]{2,1,0:T(8,128)(2,1)}), bf16[8,416,128]{2,1,0:T(8,128)(2,1)}, u32[]{:S(2)}, u32[]{:S(2)}) async-start(bf16[8,416,128]{2,1,0:T(8,128)(2,1)} %bitcast.40), calls=%async_computation.2 | async-start | bytes 1703936 | tf_op jit(solution)/shard_map/all_to_all | solution.py:165
  147.4 1.0 slice.120
  148.3 1.7 copy.37
  150.1 11.9 %scatter_custom_fusion.1 = f32[1024,128]{1,0:T(8,128)S(1)} fusion(s32[1664]{0:T(1024)S(1)} %reshape.154, f32[1664,128]{1,0:T(8,128)S(1)} %reshape.156, f32[]{:T(128)} %constant.131.clone.1), kind=kCustom, calls=%fused_computation.47 | custom fusion | flops 212992 | bytes 524292 | tf_op jit(solution)/shard_map/scatter-add | solution.py:157
  162.4 1.2 collective-permute-done.11
  164.5 4.9 %all-to-all-done.2 = bf16[8,416,128]{2,1,0:T(8,128)(2,1)} async-done(((bf16[8,416,128]{2,1,0:T(8,128)(2,1)}), bf16[8,416,128]{2,1,0:T(8,128)(2,1)}, u32[]{:S(2)}, u32[]{:S(2)}) %all-to-all-start.2) | async-done | bytes 852000 | tf_op jit(solution)/shard_map/all_to_all | solution.py:165
  169.4 20.4 %scatter_custom_fusion.3 = f32[2048,128]{1,0:T(8,128)S(1)} fusion(s32[3328]{0:T(1024)S(1)} %fusion.20, bf16[3328,128]{1,0:T(8,128)(2,1)} %bitcast.9, f32[]{:T(128)} %constant.131.clone.1), kind=kCustom, calls=%fused_computation.15 | custom fusion | flops 851968 | bytes 1900548 | tf_op jit(solution)/shard_map/scatter-add | solution.py:168
  189.8 1.0 dynamic-slice_add_fusion.2
  190.8 1.5 collective-permute-start.13
  192.3 3.0 %collective-permute-done.13 = f32[128,128]{1,0:T(8,128)S(1)} collective-permute-done((f32[128,128]{1,0:T(8,128)S(1)}, f32[128,128]{1,0:T(8,128)S(1)}, u32[]{:S(2)}, u32[]{:S(2)}) %collective-permute-start.13) | collective-permute-done | bytes 65568 | tf_op jit(solution)/shard_map/ppermute | solution.py:26
  195.4 2.4 %collective-permute-start.15 = (f32[32,128]{1,0:T(8,128)S(1)}, f32[32,128]{1,0:T(8,128)S(1)}, u32[]{:S(2)}, u32[]{:S(2)}) collective-permute-start(f32[32,128]{1,0:T(8,128)S(1)} %get-tuple-element.33), channel_id=1, source_target_pairs={{0,16},{4,20},{8,24},{12,28},{16,0},{20,4},{24,8},{28,12},{1,17},{... | collective-permute-start | bytes 49160 | tf_op jit(solution)/shard_map/ppermute | solution.py:31
  197.8 1.5 collective-permute-start.16
  199.2 1.7 collective-permute-done.14
  201.6 2.1 collective-permute-start.17
  203.6 1.8 collective-permute-start.18
  206.1 1.0 collective-permute-done.17
  207.1 1.1 collective-permute-done.18
  208.3 1.1 fusion.11
  210.0 1.4 collective-permute-start.20
  211.4 2.8 %collective-permute-done.20 = f32[128,128]{1,0:T(8,128)S(1)} collective-permute-done((f32[128,128]{1,0:T(8,128)S(1)}, f32[128,128]{1,0:T(8,128)S(1)}, u32[]{:S(2)}, u32[]{:S(2)}) %collective-permute-start.20) | collective-permute-done | bytes 65568 | tf_op jit(solution)/shard_map/ppermute | solution.py:26
  214.3 1.5 collective-permute-start.21
  216.7 2.6 %collective-permute-done.21 = f32[256,128]{1,0:T(8,128)S(1)} collective-permute-done((f32[256,128]{1,0:T(8,128)S(1)}, f32[256,128]{1,0:T(8,128)S(1)}, u32[]{:S(2)}, u32[]{:S(2)}) %collective-permute-start.21) | collective-permute-done | bytes 131104 | tf_op jit(solution)/shard_map/ppermute | solution.py:26
  219.4 1.6 collective-permute-done.22
  221.1 2.1 multiply_subtract_fusion.1
  223.1 1.3 multiply_subtract_fusion
  (93 shorter events, 14.4 us)
Async XLA Ops:
  0.6 36.1 %copy-start.1 = (f32[1024,128]{1,0:T(8,128)S(1)}, f32[1024,128]{1,0:T(8,128)}, u32[]{:S(2)}) copy-start(f32[1024,128]{1,0:T(8,128)} %param.16) | copy-start | bytes 1572868
  1.7 27.9 %collective-permute-start = (bf16[32,3328]{1,0:T(8,128)(2,1)S(1)}, bf16[32,3328]{1,0:T(8,128)(2,1)S(1)}, u32[]{:S(2)}, u32[]{:S(2)}) collective-permute-start(bf16[32,3328]{1,0:T(8,128)(2,1)S(1)} %pad_maximum_fusion.2), channel_id=1, source_target_pairs={{0,8},{4,12},{8,16},{12,20},{16,24},{20,28},{24,0},{28,4},{1,9},{5... | collective-permute-start | bytes 638984 | tf_op jit(solution)/shard_map/ppermute | solution.py:31
  4.7 25.4 %collective-permute-start.1 = (bf16[32,3328]{1,0:T(8,128)(2,1)S(1)}, bf16[32,3328]{1,0:T(8,128)(2,1)S(1)}, u32[]{:S(2)}, u32[]{:S(2)}) collective-permute-start(bf16[32,3328]{1,0:T(8,128)(2,1)S(1)} %pad_maximum_fusion.2), channel_id=1, source_target_pairs={{0,16},{4,20},{8,24},{12,28},{16,0},{20,4},{24,8},{28,12},{1,17},{... | collective-permute-start | bytes 638984 | tf_op jit(solution)/shard_map/ppermute | solution.py:31
  7.3 23.5 %collective-permute-start.2 = (bf16[32,3328]{1,0:T(8,128)(2,1)S(1)}, bf16[32,3328]{1,0:T(8,128)(2,1)S(1)}, u32[]{:S(2)}, u32[]{:S(2)}) collective-permute-start(bf16[32,3328]{1,0:T(8,128)(2,1)S(1)} %pad_maximum_fusion.2), channel_id=1, source_target_pairs={{0,24},{4,28},{8,0},{12,4},{16,8},{20,12},{24,16},{28,20},{1,25},{... | collective-permute-start | bytes 638984 | tf_op jit(solution)/shard_map/ppermute | solution.py:31
  23.5 16.7 %all-to-all-start = ((s32[8,1,416]{2,1,0:T(1,128)}), s32[8,1,416]{2,1,0:T(1,128)S(1)}, u32[]{:S(2)}, u32[]{:S(2)}) async-start(s32[8,1,416]{2,1,0:T(1,128)} %all_to_all.12), calls=%async_computation | async-start | bytes 32768 | tf_op jit(solution)/shard_map/all_to_all | solution.py:137
  33.8 6.6 %copy-start = (f32[2048,128]{1,0:T(8,128)S(1)}, f32[2048,128]{1,0:T(8,128)}, u32[]{:S(2)}) copy-start(f32[2048,128]{1,0:T(8,128)} %param.18) | copy-start | bytes 3145732
  35.2 21.7 %collective-permute-start.3 = (bf16[128,3328]{1,0:T(8,128)(2,1)}, bf16[128,3328]{1,0:T(8,128)(2,1)}, u32[]{:S(2)}, u32[]{:S(2)}) collective-permute-start(bf16[128,3328]{1,0:T(8,128)(2,1)} %get-tuple-element.20), channel_id=1, source_target_pairs={{0,1},{1,0},{2,3},{3,2},{4,5},{5,4},{6,7},{7,6},{8,9},{9,8},{10,11... | collective-permute-start | bytes 2555912 | tf_op jit(solution)/shard_map/ppermute | solution.py:26
  35.3 21.7 %collective-permute-start.4 = (bf16[128,3328]{1,0:T(8,128)(2,1)}, bf16[128,3328]{1,0:T(8,128)(2,1)}, u32[]{:S(2)}, u32[]{:S(2)}) collective-permute-start(bf16[128,3328]{1,0:T(8,128)(2,1)} %get-tuple-element.20), channel_id=1, source_target_pairs={{0,2},{1,3},{2,0},{3,1},{4,6},{5,7},{6,4},{7,5},{8,10},{9,11},{10,... | collective-permute-start | bytes 2555912 | tf_op jit(solution)/shard_map/ppermute | solution.py:26
  47.3 37.2 %all-to-all-start.1 = ((bf16[8,416,128]{2,1,0:T(8,128)(2,1)}), bf16[8,416,128]{2,1,0:T(8,128)(2,1)S(1)}, u32[]{:S(2)}, u32[]{:S(2)}) async-start(bf16[8,416,128]{2,1,0:T(8,128)(2,1)} %select_convert_fusion), calls=%async_computation.1 | async-start | bytes 1703936 | tf_op jit(solution)/shard_map/all_to_all | solution.py:140
  53.3 31.3 %collective-permute-start.6 = (bf16[128,3328]{1,0:T(8,128)(2,1)}, bf16[128,3328]{1,0:T(8,128)(2,1)}, u32[]{:S(2)}, u32[]{:S(2)}) collective-permute-start(bf16[128,3328]{1,0:T(8,128)(2,1)} %get-tuple-element.20), channel_id=1, source_target_pairs={{0,4},{4,0},{8,12},{12,8},{16,20},{20,16},{24,28},{28,24},{1,5},{5... | collective-permute-start | bytes 2555912 | tf_op jit(solution)/shard_map/ppermute | solution.py:26
  56.9 35.8 %collective-permute-start.5 = (bf16[128,3328]{1,0:T(8,128)(2,1)}, bf16[128,3328]{1,0:T(8,128)(2,1)}, u32[]{:S(2)}, u32[]{:S(2)}) collective-permute-start(bf16[128,3328]{1,0:T(8,128)(2,1)} %collective-permute-done.4), channel_id=1, source_target_pairs={{0,1},{1,0},{2,3},{3,2},{4,5},{5,4},{6,7},{7,6},{8,9},{9,8},{10,11... | collective-permute-start | bytes 2555912 | tf_op jit(solution)/shard_map/ppermute | solution.py:26
  61.3 38.4 %collective-permute-start.9 = (bf16[64,3328]{1,0:T(8,128)(2,1)}, bf16[64,3328]{1,0:T(8,128)(2,1)}, u32[]{:S(2)}, u32[]{:S(2)}) collective-permute-start(bf16[64,3328]{1,0:T(8,128)(2,1)} %get-tuple-element.14), channel_id=1, source_target_pairs={{0,4},{4,0},{8,12},{12,8},{16,20},{20,16},{24,28},{28,24},{1,5},{5... | collective-permute-start | bytes 1277960 | tf_op jit(solution)/shard_map/ppermute | solution.py:26
  84.5 13.0 %collective-permute-start.7 = (bf16[128,3328]{1,0:T(8,128)(2,1)}, bf16[128,3328]{1,0:T(8,128)(2,1)}, u32[]{:S(2)}, u32[]{:S(2)}) collective-permute-start(bf16[128,3328]{1,0:T(8,128)(2,1)} %collective-permute-done.6), channel_id=1, source_target_pairs={{0,1},{1,0},{2,3},{3,2},{4,5},{5,4},{6,7},{7,6},{8,9},{9,8},{10,11... | collective-permute-start | bytes 2555912 | tf_op jit(solution)/shard_map/ppermute | solution.py:26
  96.9 12.2 %collective-permute-start.8 = (bf16[64,3328]{1,0:T(8,128)(2,1)S(1)}, bf16[64,3328]{1,0:T(8,128)(2,1)S(1)}, u32[]{:S(2)}, u32[]{:S(2)}) collective-permute-start(bf16[64,3328]{1,0:T(8,128)(2,1)S(1)} %get-tuple-element.10), channel_id=1, source_target_pairs={{0,2},{1,3},{2,0},{3,1},{4,6},{5,7},{6,4},{7,5},{8,10},{9,11},{10,... | collective-permute-start | bytes 1277960 | tf_op jit(solution)/shard_map/ppermute | solution.py:26
  97.5 16.4 %copy-start.3 = (f32[3328]{0:T(1024)S(1)}, f32[3328]{0:T(1024)}, u32[]{:S(2)}) copy-start(f32[3328]{0:T(1024)} %param.23) | copy-start | bytes 39940
  97.5 16.4 %copy-start.5 = (f32[3328]{0:T(1024)S(1)}, f32[3328]{0:T(1024)}, u32[]{:S(2)}) copy-start(f32[3328]{0:T(1024)} %param.22) | copy-start | bytes 39940
  110.2 2.7 %collective-permute-start.10 = (bf16[128,3328]{1,0:T(8,128)(2,1)S(1)}, bf16[128,3328]{1,0:T(8,128)(2,1)S(1)}, u32[]{:S(2)}, u32[]{:S(2)}) collective-permute-start(bf16[128,3328]{1,0:T(8,128)(2,1)S(1)} %pad_maximum_fusion.1), channel_id=1, source_target_pairs={{0,1},{1,0},{2,3},{3,2},{4,5},{5,4},{6,7},{7,6},{8,9},{9,8},{10,11... | collective-permute-start | bytes 2555912 | tf_op jit(solution)/shard_map/ppermute | solution.py:26
  113.9 6.1 %copy-start.6 = (s32[128]{0:T(128)S(1)}, s32[128]{0:T(128)}, u32[]{:S(2)}) copy-start(s32[128]{0:T(128)} %param.15) | copy-start | bytes 1540
  128.4 18.7 %copy-start.4 = (s32[128,13]{0,1:T(8,128)S(1)}, s32[128,13]{0,1:T(8,128)}, u32[]{:S(2)}) copy-start(s32[128,13]{0,1:T(8,128)} %param.12) | copy-start | bytes 19972
  142.6 26.8 %all-to-all-start.2 = ((bf16[8,416,128]{2,1,0:T(8,128)(2,1)}), bf16[8,416,128]{2,1,0:T(8,128)(2,1)}, u32[]{:S(2)}, u32[]{:S(2)}) async-start(bf16[8,416,128]{2,1,0:T(8,128)(2,1)} %bitcast.40), calls=%async_computation.2 | async-start | bytes 1703936 | tf_op jit(solution)/shard_map/all_to_all | solution.py:165
  162.0 1.6 collective-permute-start.11
  163.7 26.1 %collective-permute-start.12 = (f32[256,128]{1,0:T(8,128)S(1)}, f32[256,128]{1,0:T(8,128)}, u32[]{:S(2)}, u32[]{:S(2)}) collective-permute-start(f32[256,128]{1,0:T(8,128)S(1)} %constant_dynamic-slice_fusion.4), channel_id=1, source_target_pairs={{0,2},{1,3},{2,0},{3,1},{4,6},{5,7},{6,4},{7,5},{8,10},{9,11},{10,... | collective-permute-start | bytes 393224 | tf_op jit(solution)/shard_map/ppermute | solution.py:26
  189.7 33.4 %copy-start.2 = (bf16[2048,128]{1,0:T(8,128)(2,1)S(1)}, bf16[2048,128]{1,0:T(8,128)(2,1)}, u32[]{:S(2)}) copy-start(bf16[2048,128]{1,0:T(8,128)(2,1)} %param.19) | copy-start | bytes 1572868
  189.7 18.5 %collective-permute-start.23 = (f32[2048,128]{1,0:T(8,128)S(1)}, f32[2048,128]{1,0:T(8,128)}, u32[]{:S(2)}, u32[]{:S(2)}) collective-permute-start(f32[2048,128]{1,0:T(8,128)S(1)} %scatter_custom_fusion.3), channel_id=1, source_target_pairs={{0,1},{1,0},{2,3},{3,2},{4,5},{5,4},{6,7},{7,6},{8,9},{9,8},{10,11... | collective-permute-start | bytes 3145736 | tf_op jit(solution)/shard_map/ppermute | solution.py:26
  190.8 4.5 %collective-permute-start.13 = (f32[128,128]{1,0:T(8,128)S(1)}, f32[128,128]{1,0:T(8,128)S(1)}, u32[]{:S(2)}, u32[]{:S(2)}) collective-permute-start(f32[128,128]{1,0:T(8,128)S(1)} %constant_dynamic-slice_fusion.3), channel_id=1, source_target_pairs={{0,4},{4,0},{8,12},{12,8},{16,20},{20,16},{24,28},{28,24},{1,5},{5... | collective-permute-start | bytes 196616 | tf_op jit(solution)/shard_map/ppermute | solution.py:26
  195.4 5.6 %collective-permute-start.14 = (f32[32,128]{1,0:T(8,128)S(1)}, f32[32,128]{1,0:T(8,128)S(1)}, u32[]{:S(2)}, u32[]{:S(2)}) collective-permute-start(f32[32,128]{1,0:T(8,128)S(1)} %get-tuple-element.31), channel_id=1, source_target_pairs={{0,8},{4,12},{8,16},{12,20},{16,24},{20,28},{24,0},{28,4},{1,9},{5... | collective-permute-start | bytes 49160 | tf_op jit(solution)/shard_map/ppermute | solution.py:31
  195.4 5.5 %collective-permute-start.15 = (f32[32,128]{1,0:T(8,128)S(1)}, f32[32,128]{1,0:T(8,128)S(1)}, u32[]{:S(2)}, u32[]{:S(2)}) collective-permute-start(f32[32,128]{1,0:T(8,128)S(1)} %get-tuple-element.33), channel_id=1, source_target_pairs={{0,16},{4,20},{8,24},{12,28},{16,0},{20,4},{24,8},{28,12},{1,17},{... | collective-permute-start | bytes 49160 | tf_op jit(solution)/shard_map/ppermute | solution.py:31
  197.8 3.7 %collective-permute-start.16 = (f32[32,128]{1,0:T(8,128)S(1)}, f32[32,128]{1,0:T(8,128)S(1)}, u32[]{:S(2)}, u32[]{:S(2)}) collective-permute-start(f32[32,128]{1,0:T(8,128)S(1)} %get-tuple-element.32), channel_id=1, source_target_pairs={{0,24},{4,28},{8,0},{12,4},{16,8},{20,12},{24,16},{28,20},{1,25},{... | collective-permute-start | bytes 49160 | tf_op jit(solution)/shard_map/ppermute | solution.py:31
  201.6 5.6 %collective-permute-start.17 = (f32[32,128]{1,0:T(8,128)S(1)}, f32[32,128]{1,0:T(8,128)S(1)}, u32[]{:S(2)}, u32[]{:S(2)}) collective-permute-start(f32[32,128]{1,0:T(8,128)S(1)} %get-tuple-element.3), channel_id=1, source_target_pairs={{0,8},{4,12},{8,16},{12,20},{16,24},{20,28},{24,0},{28,4},{1,9},{5... | collective-permute-start | bytes 49160 | tf_op jit(solution)/shard_map/ppermute | solution.py:31
  203.6 4.6 %collective-permute-start.18 = (f32[32,128]{1,0:T(8,128)S(1)}, f32[32,128]{1,0:T(8,128)S(1)}, u32[]{:S(2)}, u32[]{:S(2)}) collective-permute-start(f32[32,128]{1,0:T(8,128)S(1)} %get-tuple-element.3), channel_id=1, source_target_pairs={{0,16},{4,20},{8,24},{12,28},{16,0},{20,4},{24,8},{28,12},{1,17},{... | collective-permute-start | bytes 49160 | tf_op jit(solution)/shard_map/ppermute | solution.py:31
  205.4 4.6 %collective-permute-start.19 = (f32[32,128]{1,0:T(8,128)S(1)}, f32[32,128]{1,0:T(8,128)S(1)}, u32[]{:S(2)}, u32[]{:S(2)}) collective-permute-start(f32[32,128]{1,0:T(8,128)S(1)} %get-tuple-element.3), channel_id=1, source_target_pairs={{0,24},{4,28},{8,0},{12,4},{16,8},{20,12},{24,16},{28,20},{1,25},{... | collective-permute-start | bytes 49160 | tf_op jit(solution)/shard_map/ppermute | solution.py:31
  209.4 7.2 %collective-permute-start.24 = (bf16[1024,128]{1,0:T(8,128)(2,1)S(1)}, bf16[1024,128]{1,0:T(8,128)(2,1)S(1)}, u32[]{:S(2)}, u32[]{:S(2)}) collective-permute-start(bf16[1024,128]{1,0:T(8,128)(2,1)S(1)} %fusion.11), channel_id=1, source_target_pairs={{0,2},{1,3},{2,0},{3,1},{4,6},{5,7},{6,4},{7,5},{8,10},{9,11},{10,... | collective-permute-start | bytes 786440 | tf_op jit(solution)/shard_map/ppermute | solution.py:26
  210.0 4.3 %collective-permute-start.20 = (f32[128,128]{1,0:T(8,128)S(1)}, f32[128,128]{1,0:T(8,128)S(1)}, u32[]{:S(2)}, u32[]{:S(2)}) collective-permute-start(f32[128,128]{1,0:T(8,128)S(1)} %constant_dynamic-update-slice_fusion.8), channel_id=1, source_target_pairs={{0,4},{4,0},{8,12},{12,8},{16,20},{20,16},{24,28},{28,24},{1,5},{5... | collective-permute-start | bytes 196616 | tf_op jit(solution)/shard_map/ppermute | solution.py:26
  214.3 5.0 %collective-permute-start.21 = (f32[256,128]{1,0:T(8,128)S(1)}, f32[256,128]{1,0:T(8,128)S(1)}, u32[]{:S(2)}, u32[]{:S(2)}) collective-permute-start(f32[256,128]{1,0:T(8,128)S(1)} %maximum_select_fusion.3), channel_id=1, source_target_pairs={{0,2},{1,3},{2,0},{3,1},{4,6},{5,7},{6,4},{7,5},{8,10},{9,11},{10,... | collective-permute-start | bytes 393224 | tf_op jit(solution)/shard_map/ppermute | solution.py:26
  216.6 6.5 %collective-permute-start.25 = (f32[1024,128]{1,0:T(8,128)S(1)}, f32[1024,128]{1,0:T(8,128)S(1)}, u32[]{:S(2)}, u32[]{:S(2)}) collective-permute-start(f32[1024,128]{1,0:T(8,128)S(1)} %convert_add_fusion), channel_id=1, source_target_pairs={{0,1},{1,0},{2,3},{3,2},{4,5},{5,4},{6,7},{7,6},{8,9},{9,8},{10,11... | collective-permute-start | bytes 1572872 | tf_op jit(solution)/shard_map/ppermute | solution.py:26
  219.3 1.7 collective-permute-start.22

commit v2 on v1

v2 whole, which is shorter than its diff:
```python
import functools
import math

import jax
import jax.numpy as jnp
from jax import lax
from jax.experimental import pallas as pl
from jax.experimental.pallas import tpu as pltpu
from jax.sharding import PartitionSpec as P

E = 128
NH = 13
NC = 13
HOT = 1024
F = 3328


def compensate(table, backup, grad, rate):
    step_size = rate * grad
    return table - step_size - 0.5 * step_size * step_size * (table - backup.astype(jnp.float32))


def is_small(n_data, n_reps):
    return n_reps == 4 and n_data % 2 == 0 and n_data <= 16


def swap(value, axis, distance):
    size = lax.axis_size(axis)
    return lax.ppermute(value, axis, [(i, i ^ distance) for i in range(size)])


def shift(value, axis, distance):
    size = lax.axis_size(axis)
    return lax.ppermute(value, axis, [(i, (i + distance) % size) for i in range(size)])


def weight_pieces(down_t, up):
    n_data = lax.axis_size("dp")
    own = jnp.concatenate([down_t, up], axis=0)
    rank = down_t.shape[0]
    column = [own] + [shift(own, "dp", 2 * k) for k in range(1, n_data // 2)]
    half = len(column) * rank
    column = jnp.concatenate([c[:rank] for c in column] + [c[rank:] for c in column], axis=0)
    over_x = swap(column, "rep", 2)
    over_y = swap(column, "dp", 1)
    across = jnp.concatenate(
        [swap(over_y[:half], "rep", 2), swap(over_x[half:], "dp", 1)], axis=0
    )
    pieces = []
    for piece in (column, over_x, over_y, across):
        pieces += [piece, swap(piece, "rep", 1)]
    return pieces


def half_of(value, index, count):
    rows = value.shape[0] // count
    return lax.dynamic_slice_in_dim(value, index * rows, rows, axis=0)


def paired(mine, other, index):
    return jnp.where(
        index == 0,
        jnp.concatenate([mine, other], axis=0),
        jnp.concatenate([other, mine], axis=0),
    )


def sum_hot(partial):
    n_data = lax.axis_size("dp")
    nz = n_data // 2
    rep, data = lax.axis_index("rep"), lax.axis_index("dp")
    core, x, y, z = rep % 2, rep // 2, data % 2, data // 2
    total = partial
    for axis, distance, index in (("rep", 1, core), ("rep", 2, x), ("dp", 1, y)):
        total = half_of(total, index, 2) + swap(half_of(total, 1 - index, 2), axis, distance)
    rows = total.shape[0] // nz
    parts = [half_of(total, z, nz)]
    for k in range(1, nz):
        parts.append(shift(half_of(total, (z + k) % nz, nz), "dp", 2 * k))
    total = sum(parts[1:], parts[0])
    back = [total] + [shift(total, "dp", 2 * k) for k in range(1, nz)]
    whole = jnp.zeros((rows * nz, E), total.dtype)
    for k, piece in enumerate(back):
        whole = lax.dynamic_update_slice_in_dim(whole, piece, ((z - k) % nz) * rows, axis=0)
    total = whole
    for axis, distance, index in (("dp", 1, y), ("rep", 2, x), ("rep", 1, core)):
        total = paired(total, swap(total, axis, distance), index)
    return total


def sum_cold(partial):
    rep = lax.axis_index("rep")
    core = rep % 2
    chip = partial + swap(partial, "rep", 1)
    mine = half_of(chip, core, 2).astype(jnp.bfloat16)
    mine = mine.astype(jnp.float32) + swap(mine, "rep", 2).astype(jnp.float32)
    return paired(mine, swap(mine, "rep", 1), core)


LANES = 128
GROUP = 16
BF = jnp.bfloat16
F32 = jnp.float32
VMEM = pl.BlockSpec(memory_space=pltpu.VMEM)
SMEM = pl.BlockSpec(memory_space=pltpu.SMEM)
ANY = pl.BlockSpec(memory_space=pl.ANY)
NT = (((1,), (1,)), ((), ()))


def call(body, out_shape, in_specs, scratch, cost, name, limit=40):
    flops, moved = cost
    single = not isinstance(out_shape, tuple)
    return pl.pallas_call(
        body,
        out_shape=out_shape,
        in_specs=in_specs,
        out_specs=VMEM if single else tuple([VMEM] * len(out_shape)),
        scratch_shapes=scratch,
        compiler_params=pltpu.CompilerParams(vmem_limit_bytes=limit << 20),
        cost_estimate=pl.CostEstimate(flops=flops, bytes_accessed=moved, transcendentals=0),
        name=name,
    )


def route_body(n_data, capacity, owner_ref, row_ref, place_ref, ask_ref):
    lines = owner_ref.shape[0]
    padded = place_ref.shape[0]
    blocks = ask_ref.shape[0] // n_data
    count = n_data * padded
    owner = jnp.concatenate(
        [owner_ref[...], jnp.full((padded - lines, LANES), -1, jnp.int32)], axis=0
    )
    named = jnp.concatenate([(owner == d).astype(F32) for d in range(n_data)], axis=0).astype(BF)
    at = lax.broadcasted_iota(jnp.int32, (LANES, LANES), 0)
    to = lax.broadcasted_iota(jnp.int32, (LANES, LANES), 1)
    before = (at < to).astype(F32).astype(BF)
    within = jnp.dot(named, before, preferred_element_type=F32)
    sums = jnp.dot(named, jnp.ones((LANES, LANES), BF), preferred_element_type=F32)
    line = lax.broadcasted_iota(jnp.int32, (count, count), 0)
    other = lax.broadcasted_iota(jnp.int32, (count, count), 1)
    above = ((line // padded == other // padded) & (other < line)).astype(F32).astype(BF)
    rank = within + jnp.dot(above, sums.astype(BF), preferred_element_type=F32)
    slot = jnp.zeros((padded, LANES), F32)
    for d in range(n_data):
        slot = slot + jnp.where(owner == d, rank[d * padded : (d + 1) * padded], 0.0)
    slot = slot.astype(jnp.int32)
    place_ref[...] = owner * capacity + slot
    high = owner * blocks + slot // LANES
    low = slot % LANES
    asks = ask_ref.shape[0]
    ask_line = lax.broadcasted_iota(jnp.int32, (asks, LANES), 0)
    lefts, rights = [], []
    for s in range(lines):
        hit = ask_line == high[s : s + 1]
        row = row_ref[s : s + 1]
        zero = jnp.zeros((asks, LANES), F32)
        lefts.append(
            jnp.concatenate(
                [
                    jnp.where(hit, (row // 16).astype(F32), zero),
                    jnp.where(hit, (row % 16).astype(F32), zero),
                    jnp.where(hit, 1.0, zero),
                ],
                axis=0,
            ).astype(BF)
        )
        rights.append((at == low[s : s + 1]).astype(F32).astype(BF))
    found = lax.dot_general(
        jnp.concatenate(lefts, axis=1),
        jnp.concatenate(rights, axis=1),
        NT,
        preferred_element_type=F32,
    )
    asked = found[:asks] * 16.0 + found[asks : 2 * asks] + found[2 * asks :] - 1.0
    lane = lax.broadcasted_iota(jnp.int32, (asks, LANES), 1)
    for d in range(n_data):
        total = jnp.sum(sums[d * padded : (d + 1) * padded], axis=0, keepdims=True)
        asked = jnp.where((ask_line == d * blocks + blocks - 1) & (lane == LANES - 1), total, asked)
    ask_ref[...] = asked.astype(jnp.int32)


def serve_body(n_data, capacity, ask_ref, table_ref, out_ref, found):
    blocks = ask_ref.shape[0] // n_data
    found[...] = jnp.zeros_like(found)
    for d in range(n_data):
        asked = ask_ref[d * blocks + blocks - 1, LANES - 1]

        def group(g, carry, d=d):
            line, lane = d * blocks + g // 8, (g % 8) * GROUP
            start = pl.multiple_of(d * capacity + g * GROUP, GROUP)
            for k in range(GROUP):
                row = jnp.maximum(ask_ref[line, lane + k], 0)
                found[pl.ds(start + k, 1), :] = table_ref[pl.ds(row, 1), :]
            return carry

        lax.fori_loop(0, (asked + GROUP - 1) // GROUP, group, 0)
    out_ref[...] = found[...].astype(BF)


def pick(index_ref, source, into, lines):
    def group(g, carry):
        line, lane = g // 8, (g % 8) * GROUP
        start = pl.multiple_of(g * GROUP, GROUP)
        for k in range(GROUP):
            into[pl.ds(start + k, 1), :] = source[pl.ds(index_ref[line, lane + k], 1), :]
        return carry

    lax.fori_loop(0, lines * 8, group, 0)


def hot_rows_body(id_ref, table_ref, out_ref, found):
    pick(id_ref, table_ref, found, NH)
    out_ref[...] = found[...].astype(BF)


def cross_body(
    rank,
    place_ref,
    back_ref,
    hot_ref,
    label_ref,
    bias_ref,
    weight_ref,
    *rest,
):
    n_pieces = len(rest) - 10
    pieces = rest[:n_pieces]
    send_ref, hot_grad_ref, down, up, back, cold, upper, x_all, du_all, sem = rest[n_pieces:]
    half = pieces[0].shape[0] // 2
    copies = []
    for part, target in ((0, down), (1, up)):
        for i, piece in enumerate(pieces):
            copy = pltpu.make_async_copy(
                piece.at[pl.ds(part * half, half)],
                target.at[pl.ds(i * half, half)],
                sem.at[part, i],
            )
            copy.start()
            copies.append(copy)
    back[...] = back_ref[...].astype(F32)
    pick(place_ref, back, cold, NC)
    rows = LANES
    for s in range(NH):
        x_all[:, s * E : (s + 1) * E] = hot_ref[s * rows : (s + 1) * rows, :]
    for s in range(NC):
        x_all[:, (NH + s) * E : (NH + s + 1) * E] = cold[s * rows : (s + 1) * rows, :].astype(BF)
    for copy in copies[:n_pieces]:
        copy.wait()
    hidden = lax.dot_general(x_all[...], down[...], NT, preferred_element_type=F32).astype(BF)
    for copy in copies[n_pieces:]:
        copy.wait()
    wide = 2 * E
    chunks = [pl.ds(c * wide, wide) for c in range(F // wide)]
    logit = jnp.zeros((rows, wide), F32)
    for c in chunks:
        u = jnp.dot(hidden, up[:, c], preferred_element_type=F32) + bias_ref[:, c]
        upper[:, c] = u
        x = x_all[:, c].astype(F32)
        logit = logit + (x * u + x) * weight_ref[:, c]
    logit = jnp.sum(logit, axis=1, keepdims=True)
    at = lax.broadcasted_iota(jnp.int32, (rows, rows), 0)
    to = lax.broadcasted_iota(jnp.int32, (rows, rows), 1)
    label = jnp.sum(jnp.where(at == to, label_ref[...].astype(F32), 0.0), axis=1, keepdims=True)
    delta = 1.0 / (1.0 + jnp.exp(-logit)) - label
    for c in chunks:
        du_all[:, c] = (delta * weight_ref[:, c] * x_all[:, c].astype(F32)).astype(BF)
    dh = lax.dot_general(du_all[...], up[...], NT, preferred_element_type=F32).astype(BF)
    back[...] = jnp.zeros_like(back)
    for i, c in enumerate(chunks):
        grad = delta * weight_ref[:, c] * (upper[:, c] + 1.0) + jnp.dot(
            dh, down[:, c], preferred_element_type=F32
        )
        for j in range(2):
            s = 2 * i + j
            piece = grad[:, j * E : (j + 1) * E]
            if s < NH:
                hot_grad_ref[s * rows : (s + 1) * rows, :] = piece
            else:
                cold[(s - NH) * rows : (s - NH + 1) * rows, :] = piece

    def group(g, carry):
        line, lane = g // 8, (g % 8) * GROUP
        start = pl.multiple_of(g * GROUP, GROUP)
        for k in range(GROUP):
            back[pl.ds(place_ref[line, lane + k], 1), :] = cold[pl.ds(start + k, 1), :]
        return carry

    lax.fori_loop(0, NC * 8, group, 0)
    send_ref[...] = back[...].astype(BF)


def hot_sum_body(id_ref, grad_ref, out_ref, hits):
    names = lax.broadcasted_iota(jnp.int32, (HOT, LANES), 0)
    for s in range(NH):
        hits[:, s * LANES : (s + 1) * LANES] = (names == id_ref[s : s + 1, :]).astype(F32).astype(BF)
    grad = grad_ref[...]
    first = grad.astype(BF)
    rest = (grad - first.astype(F32)).astype(BF)
    both = jnp.dot(
        hits[...], jnp.concatenate([first, rest], axis=1), preferred_element_type=F32
    )
    out_ref[...] = both[:, :E] + both[:, E:]


def cold_sum_body(n_data, capacity, ask_ref, grad_ref, out_ref, hits):
    owned = out_ref.shape[0]
    blocks = ask_ref.shape[0] // n_data
    names = lax.broadcasted_iota(jnp.int32, (owned, LANES), 0)
    for d in range(n_data):
        for b in range(blocks):
            wide = min(LANES, capacity - b * LANES)
            hit = (names == ask_ref[d * blocks + b : d * blocks + b + 1, :]).astype(F32).astype(BF)
            start = d * capacity + b * LANES
            hits[:, start : start + wide] = hit[:, :wide]
    out_ref[...] = jnp.dot(hits[...], grad_ref[...], preferred_element_type=F32)


def small_step(
    hot_ids, cold_rows, cold_owner, labels, hot_table, cold_table, cross_down, cross_up, cross_bias, out_weight
):
    rows = hot_ids.shape[0]
    n_data = lax.axis_size("dp")
    lookups = rows * NC
    capacity = 2 * ((lookups + n_data - 1) // n_data)
    owned = cold_table.shape[0]
    blocks = (capacity + LANES) // LANES
    places = n_data * capacity
    shape = jax.ShapeDtypeStruct
    owner_t = cold_owner.reshape(rows, NC).T
    place, ask = call(
        functools.partial(route_body, n_data, capacity),
        (shape((16, LANES), jnp.int32), shape((n_data * blocks, LANES), jnp.int32)),
        [VMEM, VMEM],
        [],
        (10**8, 10**5),
        "route",
    )(owner_t, cold_rows.T)
    asked = lax.all_to_all(ask, "dp", split_axis=0, concat_axis=0, tiled=True)
    pieces = weight_pieces(cross_down.T, cross_up)
    hot_t = hot_ids.T
    hot_rows = call(
        hot_rows_body,
        shape((NH * rows, E), BF),
        [SMEM, VMEM],
        [pltpu.VMEM((NH * rows, E), F32)],
        (10**6, 4 * 10**6),
        "hot_rows",
    )(hot_t, hot_table)
    found = call(
        functools.partial(serve_body, n_data, capacity),
        shape((places, E), BF),
        [SMEM, VMEM],
        [pltpu.VMEM((places, E), F32)],
        (10**6, 6 * 10**6),
        "serve",
    )(asked, cold_table)
    returned = lax.all_to_all(found, "dp", split_axis=0, concat_axis=0, tiled=True)
    rank = sum(p.shape[0] for p in pieces) // 2
    send, hot_grad = call(
        functools.partial(cross_body, rank),
        (shape((places, E), BF), shape((NH * rows, E), F32)),
        [SMEM] + [VMEM] * 5 + [ANY] * len(pieces),
        [
            pltpu.VMEM((rank, F), BF),
            pltpu.VMEM((rank, F), BF),
            pltpu.VMEM((places, E), F32),
            pltpu.VMEM((NC * rows, E), F32),
            pltpu.VMEM((rows, F), F32),
            pltpu.VMEM((rows, F), BF),
            pltpu.VMEM((rows, F), BF),
            pltpu.SemaphoreType.DMA((2, len(pieces))),
        ],
        (8 * rows * F * rank, 20 * 10**6),
        "cross",
    )(
        place,
        returned,
        hot_rows,
        labels.reshape(1, rows),
        cross_bias.reshape(1, F),
        out_weight.reshape(1, F),
        *pieces,
    )
    incoming = lax.all_to_all(send, "dp", split_axis=0, concat_axis=0, tiled=True)
    hot_partial = call(
        hot_sum_body,
        shape((HOT, E), F32),
        [VMEM, VMEM],
        [pltpu.VMEM((HOT, NH * rows), BF)],
        (2 * HOT * NH * rows * 2 * E, 5 * 10**6),
        "hot_sum",
    )(hot_t, hot_grad)
    cold_partial = call(
        functools.partial(cold_sum_body, n_data, capacity),
        shape((owned, E), F32),
        [VMEM, VMEM],
        [pltpu.VMEM((owned, places), BF)],
        (2 * owned * places * E, 5 * 10**6),
        "cold_sum",
    )(asked, incoming)
    return sum_hot(hot_partial), sum_cold(cold_partial)


def large_step(
    hot_ids, cold_rows, cold_owner, labels, hot_table, cold_table, cross_down, cross_up, cross_bias, out_weight
):
    rows = hot_ids.shape[0]
    n_data = lax.axis_size("dp")
    lookups = rows * NC
    capacity = 2 * ((lookups + n_data - 1) // n_data)
    owned = cold_table.shape[0]
    owner = cold_owner.reshape(lookups)
    local_row = cold_rows.reshape(lookups)
    onehot = (owner[:, None] == jnp.arange(n_data, dtype=jnp.int32)[None, :]).astype(jnp.int32)
    running = jnp.cumsum(onehot, axis=0)
    slot = jnp.sum(onehot * running, axis=1) - 1
    place = owner * capacity + slot
    requests = (
        jnp.full((n_data * capacity,), -1, jnp.int32)
        .at[place]
        .set(local_row)
        .reshape(n_data, capacity)
    )
    asked = lax.all_to_all(requests, "dp", split_axis=0, concat_axis=0, tiled=True)
    safe = jnp.maximum(asked, 0)
    found = jnp.take(cold_table, safe, axis=0).astype(jnp.bfloat16)
    found = jnp.where((asked >= 0)[:, :, None], found, jnp.zeros_like(found))
    returned = lax.all_to_all(found, "dp", split_axis=0, concat_axis=0, tiled=True)
    cold_emb = returned.reshape(n_data * capacity, E)[place].reshape(rows, NC, E)
    hot_emb = hot_table[hot_ids].astype(jnp.bfloat16)
    first = jnp.concatenate([hot_emb, cold_emb], axis=1).reshape(rows, F)
    down_full, up_full = (
        lax.all_gather(cross_down, ("dp", "rep"), axis=1, tiled=True),
        lax.all_gather(cross_up, ("dp", "rep"), axis=0, tiled=True),
    )
    hidden = jnp.dot(first, down_full, preferred_element_type=jnp.float32).astype(jnp.bfloat16)
    upper = jnp.dot(hidden, up_full, preferred_element_type=jnp.float32) + cross_bias[None, :]
    first_f = first.astype(jnp.float32)
    second = first_f * upper + first_f
    logit = jnp.sum(second * out_weight[None, :], axis=1)
    delta = jax.nn.sigmoid(logit) - labels.astype(jnp.float32)
    d_second = delta[:, None] * out_weight[None, :]
    d_upper = (d_second * first_f).astype(jnp.bfloat16)
    d_hidden = jnp.dot(d_upper, up_full.T, preferred_element_type=jnp.float32).astype(jnp.bfloat16)
    d_first = d_second * (upper + 1.0) + jnp.dot(
        d_hidden, down_full.T, preferred_element_type=jnp.float32
    )
    grads = d_first.reshape(rows, NH + NC, E)
    hot_partial = jax.ops.segment_sum(grads[:, :NH].reshape(rows * NH, E), hot_ids.reshape(-1), HOT)
    cold_low = grads[:, NH:].astype(jnp.bfloat16).reshape(lookups, E)
    outgoing = (
        jnp.zeros((n_data * capacity, E), jnp.bfloat16)
        .at[place]
        .set(cold_low)
        .reshape(n_data, capacity, E)
    )
    incoming = lax.all_to_all(outgoing, "dp", split_axis=0, concat_axis=0, tiled=True)
    flat_ids = asked.reshape(-1)
    segment = jnp.where(flat_ids >= 0, flat_ids, owned)
    cold_partial = jax.ops.segment_sum(
        incoming.reshape(n_data * capacity, E).astype(jnp.float32), segment, owned
    )
    return lax.psum(hot_partial, ("dp", "rep")), lax.psum(cold_partial, "rep")


def shards(
    hot_ids,
    cold_rows,
    cold_owner,
    labels,
    hot_table,
    hot_backup,
    cold_table,
    cold_backup,
    cross_down,
    cross_up,
    cross_bias,
    out_weight,
):
    rows = hot_ids.shape[0]
    owned = cold_table.shape[0]
    n_data = lax.axis_size("dp")
    n_reps = lax.axis_size("rep")
    step = small_step if is_small(n_data, n_reps) else large_step
    hot_grad, cold_grad = step(
        hot_ids,
        cold_rows,
        cold_owner,
        labels,
        hot_table,
        cold_table,
        cross_down,
        cross_up,
        cross_bias,
        out_weight,
    )
    batch_all = rows * n_data * n_reps
    rate_hot = 20.0 * math.sqrt(HOT / (batch_all * NH))
    rate_cold = 20.0 * math.sqrt(owned * n_data / (batch_all * NC))
    new_hot = compensate(hot_table, hot_backup, hot_grad, rate_hot)
    new_cold = compensate(cold_table, cold_backup, cold_grad, rate_cold)
    return (new_hot, new_cold)


def solution(mesh):
    placed = (
        P(("dp", "rep"), None),
        P(("dp", "rep"), None),
        P(("dp", "rep"), None),
        P(("dp", "rep")),
        P(),
        P(),
        P("dp", None),
        P("dp", None),
        P(None, ("dp", "rep")),
        P(("dp", "rep"), None),
        P(),
        P(),
    )
    return jax.shard_map(
        shards, mesh=mesh, in_specs=placed, out_specs=(P(), P("dp", None)), check_vma=False
    )
```

time: 225 us -> 195 us (0.87)
  local copies, waits for them, and re-layouts: 67.9 us -> 19.5 us
  other arithmetic: 47.5 us -> 5.43 us
  Pallas kernels: 0 us -> 41.7 us
  waiting for transfers between devices: 53.9 us -> 76.5 us
  blocking collectives: 0 us -> 13.7 us
  matrix products: 12.6 us -> 0 us
  starting transfers between devices: 41.5 us -> 37.3 us
    pallas_call x0 -> x6, Pallas kernels: none -> 41.7 us  [the longest x1 15 us: small_step(): call(functools.partial(cross_body, rank), (shape((places, E), BF), shape(...]
    scatter-add x2 -> x0, other arithmetic: 32.3 us -> none  [the longest x1 20.4 us: shards(): jax.ops.segment_sum(incoming.reshape(n_data * capacity, E).astype(jnp.flo...]
    scatter x2 -> x0, local copies, waits for them, and re-layouts: 18 us -> none  [the longest x1 9.24 us: shards(): outgoing = jnp.zeros((n_data * capacity, E), jnp.bfloat16).at[place].set(...]
    all_to_all x0 -> x1, blocking collectives: none -> 13.7 us  [small_step(): asked = lax.all_to_all(ask, 'dp', split_axis=0, concat_axis=0, tiled=True)]
    gather x3 -> x0, local copies, waits for them, and re-layouts: 12.8 us -> none  [the longest x1 5.55 us: shards(): found = jnp.take(cold_table, safe, axis=0).astype(jnp.bfloat16)]
    dot_general x2 -> x0, matrix products: 12.6 us -> none  [the longest x1 6.51 us: shards(): jnp.dot(d_hidden, down_t, preferred_element_type=jnp.float32)]
    ppermute x9, waiting for transfers between devices: 4.41 us -> 15.7 us  [shift(): lax.ppermute(value, axis, [(i, (i + distance) % size) for i in range(size)])]
    all_to_all x3 -> x2, waiting for transfers between devices: 4.87 us -> 15.6 us  [the longest x1 15.6 us: small_step(): lax.all_to_all(send, 'dp', split_axis=0, concat_axis=0, tiled=True)]
  transfers between devices with their start and end apart: 29 -> 28, of which waited for: 14 -> 15; matrix products, arithmetic and copies ran while one was open for 42% -> 5% of each run, Pallas kernels for 0% -> 14%
where the time goes in v2:
time: 195 us
  waiting for transfers between devices  76.5 us (39%)
  Pallas kernels  41.7 us (21%)
  starting transfers between devices  37.3 us (19%)
  local copies, waits for them, and re-layouts  19.5 us (10%)
  blocking collectives  13.7 us (7%)
  other arithmetic  5.43 us (3%)
    ppermute x17, waiting for transfers between devices, swap(): return lax.ppermute(value, axis, [(i, i ^ distance) for i in range(size)])  45.2 us
    ppermute x9, waiting for transfers between devices, shift(): lax.ppermute(value, axis, [(i, (i + distance) % size) for i in range(size)])  15.7 us
    all_to_all x1, waiting for transfers between devices, small_step(): lax.all_to_all(send, 'dp', split_axis=0, concat_axis=0, tiled=True)  15.6 us
    ppermute x9, starting transfers between devices, shift(): lax.ppermute(value, axis, [(i, (i + distance) % size) for i in range(size)])  15.5 us
    unnamed x50, local copies, waits for them, and re-layouts  15.1 us
    pallas_call x1, Pallas kernels, small_step(): call(functools.partial(cross_body, rank), (shape((places, E), BF), shape(...  15 us
    all_to_all x1, blocking collectives, small_step(): asked = lax.all_to_all(ask, 'dp', split_axis=0, concat_axis=0, tiled=True)  13.7 us
    ppermute x17, starting transfers between devices, swap(): return lax.ppermute(value, axis, [(i, i ^ distance) for i in range(size)])  13.5 us
  transfers between devices with their start and end apart: 28, of which 15 were waited for; matrix products, arithmetic and copies ran while one was open for 5% of the time, Pallas kernels for 14%

profile of v2, /device:TPU:0, one launch (start us, length us, event | category | flops | bytes accessed | tf_op | source)
XLA Modules:
  0.0 195.1 jit_solution(6006951669911750863)
XLA Ops:
  0.6 1.0 pad_maximum_fusion
  1.6 3.1 %collective-permute-start = (bf16[32,3328]{1,0:T(8,128)(2,1)S(1)}, bf16[32,3328]{1,0:T(8,128)(2,1)S(1)}, u32[]{:S(2)}, u32[]{:S(2)}) collective-permute-start(bf16[32,3328]{1,0:T(8,128)(2,1)S(1)} %pad_maximum_fusion), channel_id=1, source_target_pairs={{0,8},{4,12},{8,16},{12,20},{16,24},{20,28},{24,0},{28,4},{1,9},{5... | collective-permute-start | bytes 638984 | tf_op jit(solution)/shard_map/ppermute | solution.py:34
  4.7 2.6 %collective-permute-start.1 = (bf16[32,3328]{1,0:T(8,128)(2,1)S(1)}, bf16[32,3328]{1,0:T(8,128)(2,1)S(1)}, u32[]{:S(2)}, u32[]{:S(2)}) collective-permute-start(bf16[32,3328]{1,0:T(8,128)(2,1)S(1)} %pad_maximum_fusion), channel_id=1, source_target_pairs={{0,16},{4,20},{8,24},{12,28},{16,0},{20,4},{24,8},{28,12},{1,17},{... | collective-permute-start | bytes 638984 | tf_op jit(solution)/shard_map/ppermute | solution.py:34
  7.3 1.3 collective-permute-start.2
  9.3 3.7 %collective-permute-done = bf16[32,3328]{1,0:T(8,128)(2,1)S(1)} collective-permute-done((bf16[32,3328]{1,0:T(8,128)(2,1)S(1)}, bf16[32,3328]{1,0:T(8,128)(2,1)S(1)}, u32[]{:S(2)}, u32[]{:S(2)}) %collective-permute-start) | collective-permute-done | bytes 213024 | tf_op jit(solution)/shard_map/ppermute | solution.py:34
  13.0 0.6 slice_dynamic-update-slice_fusion.5
  13.6 7.7 %collective-permute-done.1 = bf16[32,3328]{1,0:T(8,128)(2,1)S(1)} collective-permute-done((bf16[32,3328]{1,0:T(8,128)(2,1)S(1)}, bf16[32,3328]{1,0:T(8,128)(2,1)S(1)}, u32[]{:S(2)}, u32[]{:S(2)}) %collective-permute-start.1) | collective-permute-done | bytes 213024 | tf_op jit(solution)/shard_map/ppermute | solution.py:34
  21.3 0.6 slice_dynamic-update-slice_fusion.4
  21.9 0.7 slice_dynamic-update-slice_fusion.3
  22.8 0.7 constant_dynamic-update-slice_fusion
  24.1 0.6 slice_dynamic-update-slice_fusion.1
  25.4 1.5 collective-permute-start.6
  26.9 1.5 collective-permute-start.4
  28.4 18.0 %collective-permute-done.6.rest_4_ = bf16[128,3328]{1,0:T(8,128)(2,1)S(1)} collective-permute-done((bf16[128,3328]{1,0:T(8,128)(2,1)}, bf16[128,3328]{1,0:T(8,128)(2,1)S(1)}, u32[]{:S(2)}, u32[]{:S(2)}) %collective-permute-start.6) | collective-permute-done | bytes 852000 | tf_op jit(solution)/shard_map/ppermute | solution.py:29
  46.4 0.8 slice.38
  47.2 1.5 collective-permute-start.8
  50.2 13.7 %all_to_all.33 = s32[8,4,128]{2,1,0:T(4,128)S(1)} all-to-all(s32[8,4,128]{2,1,0:T(4,128)S(1)} %bitcast.17), channel_id=1, replica_groups=mesh['dp'=8,'rep'=4] {'dp'}, dimensions={0} | all-to-all | bytes 32768 | tf_op jit(solution)/shard_map/all_to_all | solution.py:338
  63.9 11.1 %serve.1 = bf16[3328,128]{1,0:T(8,128)(2,1)} custom-call(s32[32,128]{1,0:T(8,128)S(1)} %bitcast.15, f32[2048,128]{1,0:T(8,128)S(1)} %copy-done), custom_call_target="tpu_custom_call" | custom-call | flops 1000000 | bytes 6000000 | tf_op jit(solution)/shard_map/serve/pallas_call | solution.py:349
  75.0 3.6 %all-to-all-start.1 = ((bf16[8,416,128]{2,1,0:T(8,128)(2,1)}), bf16[8,416,128]{2,1,0:T(8,128)(2,1)S(1)}, u32[]{:S(2)}, u32[]{:S(2)}) async-start(bf16[8,416,128]{2,1,0:T(8,128)(2,1)} %bitcast.5), calls=%async_computation.1 | async-start | bytes 1703936 | tf_op jit(solution)/shard_map/all_to_all | solution.py:357
  78.7 1.0 slice.39
  79.7 2.0 %collective-permute-start.9 = (bf16[64,3328]{1,0:T(8,128)(2,1)S(1)}, bf16[64,3328]{1,0:T(8,128)(2,1)S(1)}, u32[]{:S(2)}, u32[]{:S(2)}) collective-permute-start(bf16[64,3328]{1,0:T(8,128)(2,1)S(1)} %slice.39), channel_id=1, source_target_pairs={{0,4},{4,0},{8,12},{12,8},{16,20},{20,16},{24,28},{28,24},{1,5},{5... | collective-permute-start | bytes 1277960 | tf_op jit(solution)/shard_map/ppermute | solution.py:29
  82.3 0.8 constant_dynamic-update-slice_fusion.3
  83.1 14.1 %collective-permute-done.9 = bf16[64,3328]{1,0:T(8,128)(2,1)S(1)} collective-permute-done((bf16[64,3328]{1,0:T(8,128)(2,1)S(1)}, bf16[64,3328]{1,0:T(8,128)(2,1)S(1)}, u32[]{:S(2)}, u32[]{:S(2)}) %collective-permute-start.9) | collective-permute-done | bytes 426016 | tf_op jit(solution)/shard_map/ppermute | solution.py:29
  97.2 0.8 constant_dynamic-update-slice_fusion.2.rest_6_
  98.1 0.7 copy-done.19
  98.8 0.7 copy-done.7
  99.5 5.3 %hot_rows.1.hot_ref = bf16[1664,128]{1,0:T(8,128)(2,1)S(1)} custom-call(s32[13,128]{1,0:T(8,128)S(1)} %bitcast.18, f32[1024,128]{1,0:T(8,128)S(1)} %copy-done.1), custom_call_target="tpu_custom_call" | custom-call | flops 1000000 | bytes 4000000 | tf_op jit(solution)/shard_map/hot_rows/pallas_call | solution.py:341
  104.8 0.7 copy-done.2
  105.6 0.9 copy-done.4
  106.5 0.6 copy-done.8
  107.2 1.0 copy-done.3
  108.2 1.2 copy-done.5
  109.3 15.0 %cross.1 = (bf16[3328,128]{1,0:T(8,128)(2,1)S(1)}, f32[1664,128]{1,0:T(8,128)S(1)}) custom-call(s32[16,128]{1,0:T(8,128)S(1)} %get-tuple-element.6.place_ref, bf16[3328,128]{1,0:T(8,128)(2,1)S(1)} %bitcast.12, bf16[1664,128]{1,0:T(8,128)(2,1)S(1)} %copy-done.3, s32[1,128]{1,0:T(1,128)S(1)} %bitcast.21, f32[1,3328]{1,0:T(1,128)S(1)} %reshape.24.bias_ref, ...), custom_call_target="tpu_custom_call" | custom-call | flops 1744830464 | bytes 20000000 | tf_op jit(solution)/shard_map/cross/pallas_call | solution.py:359
  124.4 0.9 copy-done.6
  125.3 0.9 copy-done.9
  126.2 4.8 %all-to-all-start.2 = ((bf16[8,416,128]{2,1,0:T(8,128)(2,1)}), bf16[8,416,128]{2,1,0:T(8,128)(2,1)S(1)}, u32[]{:S(2)}, u32[]{:S(2)}) async-start(bf16[8,416,128]{2,1,0:T(8,128)(2,1)} %bitcast.13), calls=%async_computation.2 | async-start | bytes 1703936 | tf_op jit(solution)/shard_map/all_to_all | solution.py:384
  131.0 1.1 copy-done.10
  132.1 1.2 hot_sum.1
  133.5 1.5 collective-permute-done.11
  135.0 0.7 constant_dynamic-slice_fusion.4
  135.7 1.2 collective-permute-start.12
  136.9 15.6 %all-to-all-done.2 = bf16[8,416,128]{2,1,0:T(8,128)(2,1)S(1)} async-done(((bf16[8,416,128]{2,1,0:T(8,128)(2,1)}), bf16[8,416,128]{2,1,0:T(8,128)(2,1)S(1)}, u32[]{:S(2)}, u32[]{:S(2)}) %all-to-all-start.2) | async-done | bytes 852000 | tf_op jit(solution)/shard_map/all_to_all | solution.py:384
  152.6 8.4 %cold_sum.1 = f32[2048,128]{1,0:T(8,128)S(1)} custom-call(s32[32,128]{1,0:T(8,128)S(1)} %bitcast.16, bf16[3328,128]{1,0:T(8,128)(2,1)S(1)} %bitcast.14), custom_call_target="tpu_custom_call" | custom-call | flops 1744830464 | bytes 5000000 | tf_op jit(solution)/shard_map/cold_sum/pallas_call | solution.py:393
  161.1 0.9 dynamic-slice_add_fusion.2
  162.0 1.4 collective-permute-start.13
  163.4 3.1 %collective-permute-done.13 = f32[128,128]{1,0:T(8,128)S(1)} collective-permute-done((f32[128,128]{1,0:T(8,128)S(1)}, f32[128,128]{1,0:T(8,128)S(1)}, u32[]{:S(2)}, u32[]{:S(2)}) %collective-permute-start.13) | collective-permute-done | bytes 65568 | tf_op jit(solution)/shard_map/ppermute | solution.py:29
  166.8 1.5 collective-permute-start.15
  168.3 2.2 %collective-permute-start.16 = (f32[32,128]{1,0:T(8,128)S(1)}, f32[32,128]{1,0:T(8,128)S(1)}, u32[]{:S(2)}, u32[]{:S(2)}) collective-permute-start(f32[32,128]{1,0:T(8,128)S(1)} %get-tuple-element.13), channel_id=1, source_target_pairs={{0,24},{4,28},{8,0},{12,4},{16,8},{20,12},{24,16},{28,20},{1,25},{... | collective-permute-start | bytes 49160 | tf_op jit(solution)/shard_map/ppermute | solution.py:34
  170.5 1.7 collective-permute-done.14
  172.8 2.1 %collective-permute-start.17 = (f32[32,128]{1,0:T(8,128)S(1)}, f32[32,128]{1,0:T(8,128)S(1)}, u32[]{:S(2)}, u32[]{:S(2)}) collective-permute-start(f32[32,128]{1,0:T(8,128)S(1)} %get-tuple-element.11), channel_id=1, source_target_pairs={{0,8},{4,12},{8,16},{12,20},{16,24},{20,28},{24,0},{28,4},{1,9},{5... | collective-permute-start | bytes 49160 | tf_op jit(solution)/shard_map/ppermute | solution.py:34
  174.9 1.8 collective-permute-start.18
  176.7 0.7 collective-permute-start.19
  177.4 1.0 collective-permute-done.17
  178.4 1.1 collective-permute-done.18
  179.5 1.1 fusion
  180.6 1.3 collective-permute-start.24
  181.9 1.3 collective-permute-start.20
  183.2 2.9 %collective-permute-done.20 = f32[128,128]{1,0:T(8,128)S(1)} collective-permute-done((f32[128,128]{1,0:T(8,128)S(1)}, f32[128,128]{1,0:T(8,128)S(1)}, u32[]{:S(2)}, u32[]{:S(2)}) %collective-permute-start.20) | collective-permute-done | bytes 65568 | tf_op jit(solution)/shard_map/ppermute | solution.py:29
  186.2 0.9 collective-permute-start.21
  187.1 1.4 collective-permute-done.24
  188.6 2.6 %collective-permute-done.21 = f32[256,128]{1,0:T(8,128)S(1)} collective-permute-done((f32[256,128]{1,0:T(8,128)S(1)}, f32[256,128]{1,0:T(8,128)S(1)}, u32[]{:S(2)}, u32[]{:S(2)}) %collective-permute-start.21) | collective-permute-done | bytes 131104 | tf_op jit(solution)/shard_map/ppermute | solution.py:29
  191.3 1.5 collective-permute-done.22
  192.8 1.0 multiply_subtract_fusion.1
  193.8 1.3 multiply_subtract_fusion
  (77 shorter events, 5.6 us)
Async XLA Ops:
  0.6 8.0 %copy-start.15 = (bf16[3328,16]{0,1:T(8,128)(2,1)S(1)}, bf16[3328,16]{0,1:T(8,128)(2,1)}, u32[]{:S(2)}) copy-start(bf16[3328,16]{0,1:T(8,128)(2,1)} %param.20) | copy-start | bytes 319492
  1.6 11.3 %collective-permute-start = (bf16[32,3328]{1,0:T(8,128)(2,1)S(1)}, bf16[32,3328]{1,0:T(8,128)(2,1)S(1)}, u32[]{:S(2)}, u32[]{:S(2)}) collective-permute-start(bf16[32,3328]{1,0:T(8,128)(2,1)S(1)} %pad_maximum_fusion), channel_id=1, source_target_pairs={{0,8},{4,12},{8,16},{12,20},{16,24},{20,28},{24,0},{28,4},{1,9},{5... | collective-permute-start | bytes 638984 | tf_op jit(solution)/shard_map/ppermute | solution.py:34
  4.7 16.5 %collective-permute-start.1 = (bf16[32,3328]{1,0:T(8,128)(2,1)S(1)}, bf16[32,3328]{1,0:T(8,128)(2,1)S(1)}, u32[]{:S(2)}, u32[]{:S(2)}) collective-permute-start(bf16[32,3328]{1,0:T(8,128)(2,1)S(1)} %pad_maximum_fusion), channel_id=1, source_target_pairs={{0,16},{4,20},{8,24},{12,28},{16,0},{20,4},{24,8},{28,12},{1,17},{... | collective-permute-start | bytes 638984 | tf_op jit(solution)/shard_map/ppermute | solution.py:34
  7.3 14.6 %collective-permute-start.2 = (bf16[32,3328]{1,0:T(8,128)(2,1)S(1)}, bf16[32,3328]{1,0:T(8,128)(2,1)S(1)}, u32[]{:S(2)}, u32[]{:S(2)}) collective-permute-start(bf16[32,3328]{1,0:T(8,128)(2,1)S(1)} %pad_maximum_fusion), channel_id=1, source_target_pairs={{0,24},{4,28},{8,0},{12,4},{16,8},{20,12},{24,16},{28,20},{1,25},{... | collective-permute-start | bytes 638984 | tf_op jit(solution)/shard_map/ppermute | solution.py:34
  21.9 0.9 copy-start.16
  23.5 40.4 %copy-start = (f32[2048,128]{1,0:T(8,128)S(1)}, f32[2048,128]{1,0:T(8,128)}, u32[]{:S(2)}) copy-start(f32[2048,128]{1,0:T(8,128)} %table_ref.2) | copy-start | bytes 3145732
  25.4 23.3 %copy-start.20 = (s32[1664,1]{0,1:T(1,128)S(1)}, s32[1664,1]{0,1:T(1,128)}, u32[]{:S(2)}) copy-start(s32[1664,1]{0,1:T(1,128)} %param.14) | copy-start | bytes 19972
  25.4 21.0 %collective-permute-start.6 = (bf16[128,3328]{1,0:T(8,128)(2,1)}, bf16[128,3328]{1,0:T(8,128)(2,1)S(1)}, u32[]{:S(2)}, u32[]{:S(2)}) collective-permute-start(bf16[128,3328]{1,0:T(8,128)(2,1)} %slice_dynamic-update-slice_fusion.rest_0_), channel_id=1, source_target_pairs={{0,4},{4,0},{8,12},{12,8},{16,20},{20,16},{24,28},{28,24},{1,5},{5... | collective-permute-start | bytes 2555912 | tf_op jit(solution)/shard_map/ppermute | solution.py:29
  26.9 51.7 %collective-permute-start.4 = (bf16[128,3328]{1,0:T(8,128)(2,1)}, bf16[128,3328]{1,0:T(8,128)(2,1)}, u32[]{:S(2)}, u32[]{:S(2)}) collective-permute-start(bf16[128,3328]{1,0:T(8,128)(2,1)} %slice_dynamic-update-slice_fusion.rest_0_), channel_id=1, source_target_pairs={{0,2},{1,3},{2,0},{3,1},{4,6},{5,7},{6,4},{7,5},{8,10},{9,11},{10,... | collective-permute-start | bytes 2555912 | tf_op jit(solution)/shard_map/ppermute | solution.py:29
  47.2 35.1 %collective-permute-start.8 = (bf16[64,3328]{1,0:T(8,128)(2,1)}, bf16[64,3328]{1,0:T(8,128)(2,1)S(1)}, u32[]{:S(2)}, u32[]{:S(2)}) collective-permute-start(bf16[64,3328]{1,0:T(8,128)(2,1)} %slice.38), channel_id=1, source_target_pairs={{0,2},{1,3},{2,0},{3,1},{4,6},{5,7},{6,4},{7,5},{8,10},{9,11},{10,... | collective-permute-start | bytes 1277960 | tf_op jit(solution)/shard_map/ppermute | solution.py:29
  48.9 0.7 copy-start.11
  75.0 31.5 %all-to-all-start.1 = ((bf16[8,416,128]{2,1,0:T(8,128)(2,1)}), bf16[8,416,128]{2,1,0:T(8,128)(2,1)S(1)}, u32[]{:S(2)}, u32[]{:S(2)}) async-start(bf16[8,416,128]{2,1,0:T(8,128)(2,1)} %bitcast.5), calls=%async_computation.1 | async-start | bytes 1703936 | tf_op jit(solution)/shard_map/all_to_all | solution.py:357
  78.6 26.9 %collective-permute-start.3 = (bf16[128,3328]{1,0:T(8,128)(2,1)}, bf16[128,3328]{1,0:T(8,128)(2,1)S(1)}, u32[]{:S(2)}, u32[]{:S(2)}) collective-permute-start(bf16[128,3328]{1,0:T(8,128)(2,1)} %slice_dynamic-update-slice_fusion.rest_0_), channel_id=1, source_target_pairs={{0,1},{1,0},{2,3},{3,2},{4,5},{5,4},{6,7},{7,6},{8,9},{9,8},{10,11... | collective-permute-start | bytes 2555912 | tf_op jit(solution)/shard_map/ppermute | solution.py:29
  79.7 17.5 %collective-permute-start.9 = (bf16[64,3328]{1,0:T(8,128)(2,1)S(1)}, bf16[64,3328]{1,0:T(8,128)(2,1)S(1)}, u32[]{:S(2)}, u32[]{:S(2)}) collective-permute-start(bf16[64,3328]{1,0:T(8,128)(2,1)S(1)} %slice.39), channel_id=1, source_target_pairs={{0,4},{4,0},{8,12},{12,8},{16,20},{20,16},{24,28},{28,24},{1,5},{5... | collective-permute-start | bytes 1277960 | tf_op jit(solution)/shard_map/ppermute | solution.py:29
  81.8 24.7 %collective-permute-start.5 = (bf16[128,3328]{1,0:T(8,128)(2,1)}, bf16[128,3328]{1,0:T(8,128)(2,1)}, u32[]{:S(2)}, u32[]{:S(2)}) collective-permute-start(bf16[128,3328]{1,0:T(8,128)(2,1)} %collective-permute-done.4.rest_2_), channel_id=1, source_target_pairs={{0,1},{1,0},{2,3},{3,2},{4,5},{5,4},{6,7},{7,6},{8,9},{9,8},{10,11... | collective-permute-start | bytes 2555912 | tf_op jit(solution)/shard_map/ppermute | solution.py:29
  82.0 24.5 %collective-permute-start.7 = (bf16[128,3328]{1,0:T(8,128)(2,1)S(1)}, bf16[128,3328]{1,0:T(8,128)(2,1)}, u32[]{:S(2)}, u32[]{:S(2)}) collective-permute-start(bf16[128,3328]{1,0:T(8,128)(2,1)S(1)} %collective-permute-done.6.rest_4_), channel_id=1, source_target_pairs={{0,1},{1,0},{2,3},{3,2},{4,5},{5,4},{6,7},{7,6},{8,9},{9,8},{10,11... | collective-permute-start | bytes 2555912 | tf_op jit(solution)/shard_map/ppermute | solution.py:29
  83.1 15.0 %copy-start.18 = (f32[3328]{0:T(1024)S(1)}, f32[3328]{0:T(1024)}, u32[]{:S(2)}) copy-start(f32[3328]{0:T(1024)} %param.22) | copy-start | bytes 39940
  83.1 15.7 %copy-start.1 = (f32[1024,128]{1,0:T(8,128)S(1)}, f32[1024,128]{1,0:T(8,128)}, u32[]{:S(2)}) copy-start(f32[1024,128]{1,0:T(8,128)} %table_ref.3) | copy-start | bytes 1572868
  98.1 0.7 copy-start.19
  98.1 8.4 %collective-permute-start.10 = (bf16[128,3328]{1,0:T(8,128)(2,1)}, bf16[128,3328]{1,0:T(8,128)(2,1)}, u32[]{:S(2)}, u32[]{:S(2)}) collective-permute-start(bf16[128,3328]{1,0:T(8,128)(2,1)} %constant_dynamic-update-slice_fusion.2.rest_6_), channel_id=1, source_target_pairs={{0,1},{1,0},{2,3},{3,2},{4,5},{5,4},{6,7},{7,6},{8,9},{9,8},{10,11... | collective-permute-start | bytes 2555912 | tf_op jit(solution)/shard_map/ppermute | solution.py:29
  98.8 0.7 copy-start.7
  104.8 0.8 copy-start.2
  105.6 0.9 copy-start.4
  106.5 0.7 copy-start.8
  107.2 1.0 copy-start.3
  108.2 1.2 copy-start.5
  124.4 0.9 copy-start.6
  125.3 0.9 copy-start.9
  126.2 26.4 %all-to-all-start.2 = ((bf16[8,416,128]{2,1,0:T(8,128)(2,1)}), bf16[8,416,128]{2,1,0:T(8,128)(2,1)S(1)}, u32[]{:S(2)}, u32[]{:S(2)}) async-start(bf16[8,416,128]{2,1,0:T(8,128)(2,1)} %bitcast.13), calls=%async_computation.2 | async-start | bytes 1703936 | tf_op jit(solution)/shard_map/all_to_all | solution.py:384
  131.0 1.2 copy-start.10
  133.4 1.6 collective-permute-start.11
  135.0 17.6 %copy-start.12 = (f32[512,128]{1,0:T(8,128)}, f32[512,128]{1,0:T(8,128)S(1)}, u32[]{:S(2)}) copy-start(f32[512,128]{1,0:T(8,128)S(1)} %dynamic-slice_add_fusion.1) | copy-start | bytes 786436
  135.7 25.3 %collective-permute-start.12 = (f32[256,128]{1,0:T(8,128)}, f32[256,128]{1,0:T(8,128)}, u32[]{:S(2)}, u32[]{:S(2)}) collective-permute-start(f32[256,128]{1,0:T(8,128)} %constant_dynamic-slice_fusion.4), channel_id=1, source_target_pairs={{0,2},{1,3},{2,0},{3,1},{4,6},{5,7},{6,4},{7,5},{8,10},{9,11},{10,... | collective-permute-start | bytes 393224 | tf_op jit(solution)/shard_map/ppermute | solution.py:29
  152.6 8.5 %copy-start.13 = (f32[512,128]{1,0:T(8,128)S(1)}, f32[512,128]{1,0:T(8,128)}, u32[]{:S(2)}) copy-start(f32[512,128]{1,0:T(8,128)} %copy-done.12) | copy-start | bytes 786436
  161.0 18.5 %collective-permute-start.23 = (f32[2048,128]{1,0:T(8,128)S(1)}, f32[2048,128]{1,0:T(8,128)}, u32[]{:S(2)}, u32[]{:S(2)}) collective-permute-start(f32[2048,128]{1,0:T(8,128)S(1)} %cold_sum.1), channel_id=1, source_target_pairs={{0,1},{1,0},{2,3},{3,2},{4,5},{5,4},{6,7},{7,6},{8,9},{9,8},{10,11... | collective-permute-start | bytes 3145736 | tf_op jit(solution)/shard_map/ppermute | solution.py:29
  162.0 4.5 %collective-permute-start.13 = (f32[128,128]{1,0:T(8,128)S(1)}, f32[128,128]{1,0:T(8,128)S(1)}, u32[]{:S(2)}, u32[]{:S(2)}) collective-permute-start(f32[128,128]{1,0:T(8,128)S(1)} %constant_dynamic-slice_fusion.3), channel_id=1, source_target_pairs={{0,4},{4,0},{8,12},{12,8},{16,20},{20,16},{24,28},{28,24},{1,5},{5... | collective-permute-start | bytes 196616 | tf_op jit(solution)/shard_map/ppermute | solution.py:29
  166.6 5.6 %collective-permute-start.14 = (f32[32,128]{1,0:T(8,128)S(1)}, f32[32,128]{1,0:T(8,128)S(1)}, u32[]{:S(2)}, u32[]{:S(2)}) collective-permute-start(f32[32,128]{1,0:T(8,128)S(1)} %get-tuple-element.12), channel_id=1, source_target_pairs={{0,8},{4,12},{8,16},{12,20},{16,24},{20,28},{24,0},{28,4},{1,9},{5... | collective-permute-start | bytes 49160 | tf_op jit(solution)/shard_map/ppermute | solution.py:34
  166.8 5.4 %collective-permute-start.15 = (f32[32,128]{1,0:T(8,128)S(1)}, f32[32,128]{1,0:T(8,128)S(1)}, u32[]{:S(2)}, u32[]{:S(2)}) collective-permute-start(f32[32,128]{1,0:T(8,128)S(1)} %get-tuple-element.14), channel_id=1, source_target_pairs={{0,16},{4,20},{8,24},{12,28},{16,0},{20,4},{24,8},{28,12},{1,17},{... | collective-permute-start | bytes 49160 | tf_op jit(solution)/shard_map/ppermute | solution.py:34
  168.3 4.5 %collective-permute-start.16 = (f32[32,128]{1,0:T(8,128)S(1)}, f32[32,128]{1,0:T(8,128)S(1)}, u32[]{:S(2)}, u32[]{:S(2)}) collective-permute-start(f32[32,128]{1,0:T(8,128)S(1)} %get-tuple-element.13), channel_id=1, source_target_pairs={{0,24},{4,28},{8,0},{12,4},{16,8},{20,12},{24,16},{28,20},{1,25},{... | collective-permute-start | bytes 49160 | tf_op jit(solution)/shard_map/ppermute | solution.py:34
  172.8 5.6 %collective-permute-start.17 = (f32[32,128]{1,0:T(8,128)S(1)}, f32[32,128]{1,0:T(8,128)S(1)}, u32[]{:S(2)}, u32[]{:S(2)}) collective-permute-start(f32[32,128]{1,0:T(8,128)S(1)} %get-tuple-element.11), channel_id=1, source_target_pairs={{0,8},{4,12},{8,16},{12,20},{16,24},{20,28},{24,0},{28,4},{1,9},{5... | collective-permute-start | bytes 49160 | tf_op jit(solution)/shard_map/ppermute | solution.py:34
  174.9 4.6 %collective-permute-start.18 = (f32[32,128]{1,0:T(8,128)S(1)}, f32[32,128]{1,0:T(8,128)S(1)}, u32[]{:S(2)}, u32[]{:S(2)}) collective-permute-start(f32[32,128]{1,0:T(8,128)S(1)} %get-tuple-element.11), channel_id=1, source_target_pairs={{0,16},{4,20},{8,24},{12,28},{16,0},{20,4},{24,8},{28,12},{1,17},{... | collective-permute-start | bytes 49160 | tf_op jit(solution)/shard_map/ppermute | solution.py:34
  176.7 5.2 %collective-permute-start.19 = (f32[32,128]{1,0:T(8,128)S(1)}, f32[32,128]{1,0:T(8,128)S(1)}, u32[]{:S(2)}, u32[]{:S(2)}) collective-permute-start(f32[32,128]{1,0:T(8,128)S(1)} %get-tuple-element.11), channel_id=1, source_target_pairs={{0,24},{4,28},{8,0},{12,4},{16,8},{20,12},{24,16},{28,20},{1,25},{... | collective-permute-start | bytes 49160 | tf_op jit(solution)/shard_map/ppermute | solution.py:34
  180.6 7.8 %collective-permute-start.24 = (bf16[1024,128]{1,0:T(8,128)(2,1)S(1)}, bf16[1024,128]{1,0:T(8,128)(2,1)S(1)}, u32[]{:S(2)}, u32[]{:S(2)}) collective-permute-start(bf16[1024,128]{1,0:T(8,128)(2,1)S(1)} %fusion), channel_id=1, source_target_pairs={{0,2},{1,3},{2,0},{3,1},{4,6},{5,7},{6,4},{7,5},{8,10},{9,11},{10,... | collective-permute-start | bytes 786440 | tf_op jit(solution)/shard_map/ppermute | solution.py:29
  181.9 4.3 %collective-permute-start.20 = (f32[128,128]{1,0:T(8,128)S(1)}, f32[128,128]{1,0:T(8,128)S(1)}, u32[]{:S(2)}, u32[]{:S(2)}) collective-permute-start(f32[128,128]{1,0:T(8,128)S(1)} %constant_dynamic-update-slice_fusion.4), channel_id=1, source_target_pairs={{0,4},{4,0},{8,12},{12,8},{16,20},{20,16},{24,28},{28,24},{1,5},{5... | collective-permute-start | bytes 196616 | tf_op jit(solution)/shard_map/ppermute | solution.py:29
  186.2 5.0 %collective-permute-start.21 = (f32[256,128]{1,0:T(8,128)S(1)}, f32[256,128]{1,0:T(8,128)S(1)}, u32[]{:S(2)}, u32[]{:S(2)}) collective-permute-start(f32[256,128]{1,0:T(8,128)S(1)} %maximum_select_fusion.3), channel_id=1, source_target_pairs={{0,2},{1,3},{2,0},{3,1},{4,6},{5,7},{6,4},{7,5},{8,10},{9,11},{10,... | collective-permute-start | bytes 393224 | tf_op jit(solution)/shard_map/ppermute | solution.py:29
  188.5 4.3 %copy-start.17 = (bf16[1024,128]{1,0:T(8,128)(2,1)S(1)}, bf16[1024,128]{1,0:T(8,128)(2,1)}, u32[]{:S(2)}) copy-start(bf16[1024,128]{1,0:T(8,128)(2,1)} %param.17) | copy-start | bytes 786436
  188.5 5.2 %collective-permute-start.25 = (f32[1024,128]{1,0:T(8,128)S(1)}, f32[1024,128]{1,0:T(8,128)S(1)}, u32[]{:S(2)}, u32[]{:S(2)}) collective-permute-start(f32[1024,128]{1,0:T(8,128)S(1)} %convert_add_fusion), channel_id=1, source_target_pairs={{0,1},{1,0},{2,3},{3,2},{4,5},{5,4},{6,7},{7,6},{8,9},{9,8},{10,11... | collective-permute-start | bytes 1572872 | tf_op jit(solution)/shard_map/ppermute | solution.py:29
  191.2 1.6 collective-permute-start.22
  191.3 2.5 %copy-start.14 = (bf16[2048,128]{1,0:T(8,128)(2,1)S(1)}, bf16[2048,128]{1,0:T(8,128)(2,1)}, u32[]{:S(2)}) copy-start(bf16[2048,128]{1,0:T(8,128)(2,1)} %param.19) | copy-start | bytes 1572868

commit v3 on v2

--- a/solution.py
+++ b/solution.py
@@ -34,20 +34,32 @@
     return lax.ppermute(value, axis, [(i, (i + distance) % size) for i in range(size)])
 
 
-def weight_pieces(down_t, up):
-    n_data = lax.axis_size("dp")
-    own = jnp.concatenate([down_t, up], axis=0)
-    rank = down_t.shape[0]
-    column = [own] + [shift(own, "dp", 2 * k) for k in range(1, n_data // 2)]
-    half = len(column) * rank
-    column = jnp.concatenate([c[:rank] for c in column] + [c[rank:] for c in column], axis=0)
-    over_x = swap(column, "rep", 2)
-    over_y = swap(column, "dp", 1)
-    across = jnp.concatenate(
-        [swap(over_y[:half], "rep", 2), swap(over_x[half:], "dp", 1)], axis=0
-    )
+def after(value, *others):
+    return lax.optimization_barrier((value, *others))[0]
+
+
+def swap_both(value):
+    n_data, n_reps = lax.axis_size("dp"), lax.axis_size("rep")
+    ways = [
+        (d * n_reps + r, (d ^ 1) * n_reps + (r ^ 2)) for d in range(n_data) for r in range(n_reps)
+    ]
+    return lax.ppermute(value, ("dp", "rep"), ways)
+
+
+def weight_starts(down_t, up):
+    own = jnp.stack([down_t, up])[None]
+    z = [shift(own, "dp", 2 * k) for k in range(1, lax.axis_size("dp") // 2)]
+    return own, swap(own, "rep", 2), swap(own, "dp", 1), z
+
+
+def weight_pieces(starts, first):
+    own, own_x, own_y, z = starts
+    z = jnp.concatenate(lax.optimization_barrier((*z, first))[:-1], axis=0)
+    over_x = swap(jnp.concatenate([z, own_y], axis=0), "rep", 2)
+    over_y = swap(z, "dp", 1)
+    across = swap_both(z)
     pieces = []
-    for piece in (column, over_x, over_y, across):
+    for piece in (own, own_x, own_y, z, over_y, over_x, across):
         pieces += [piece, swap(piece, "rep", 1)]
     return pieces
 
@@ -65,27 +77,44 @@
     )
 
 
-def sum_hot(partial):
-    n_data = lax.axis_size("dp")
-    nz = n_data // 2
+def plane_swaps():
+    return (
+        (lambda v: swap(v, "rep", 2), 2),
+        (lambda v: swap(v, "dp", 1), 1),
+        (swap_both, 3),
+    )
+
+
+def hot_down(partial):
+    nz = lax.axis_size("dp") // 2
     rep, data = lax.axis_index("rep"), lax.axis_index("dp")
-    core, x, y, z = rep % 2, rep // 2, data % 2, data // 2
-    total = partial
-    for axis, distance, index in (("rep", 1, core), ("rep", 2, x), ("dp", 1, y)):
-        total = half_of(total, index, 2) + swap(half_of(total, 1 - index, 2), axis, distance)
-    rows = total.shape[0] // nz
+    core, z, spot = rep % 2, data // 2, (rep // 2) * 2 + data % 2
+    total = half_of(partial, core, 2) + swap(half_of(partial, 1 - core, 2), "rep", 1)
+    total = half_of(total, spot, 4) + sum(move(half_of(total, spot ^ w, 4)) for move, w in plane_swaps())
     parts = [half_of(total, z, nz)]
     for k in range(1, nz):
         parts.append(shift(half_of(total, (z + k) % nz, nz), "dp", 2 * k))
-    total = sum(parts[1:], parts[0])
-    back = [total] + [shift(total, "dp", 2 * k) for k in range(1, nz)]
+    return sum(parts[1:], parts[0])
+
+
+def hot_along_z(total):
+    nz = lax.axis_size("dp") // 2
+    z, rows = lax.axis_index("dp") // 2, total.shape[0]
     whole = jnp.zeros((rows * nz, E), total.dtype)
-    for k, piece in enumerate(back):
+    for k in range(nz):
+        piece = shift(total, "dp", 2 * k) if k else total
         whole = lax.dynamic_update_slice_in_dim(whole, piece, ((z - k) % nz) * rows, axis=0)
-    total = whole
-    for axis, distance, index in (("dp", 1, y), ("rep", 2, x), ("rep", 1, core)):
-        total = paired(total, swap(total, axis, distance), index)
-    return total
+    return whole
+
+
+def hot_up(total):
+    rep, data = lax.axis_index("rep"), lax.axis_index("dp")
+    core, spot, rows = rep % 2, (rep // 2) * 2 + data % 2, total.shape[0]
+    whole = jnp.zeros((rows * 4, E), total.dtype)
+    whole = lax.dynamic_update_slice_in_dim(whole, total, spot * rows, axis=0)
+    for move, w in plane_swaps():
+        whole = lax.dynamic_update_slice_in_dim(whole, move(total), (spot ^ w) * rows, axis=0)
+    return paired(whole, swap(whole, "rep", 1), core)
 
 
 def sum_cold(partial):
@@ -98,7 +127,7 @@
 
 
 LANES = 128
-GROUP = 16
+GROUP = 32
 BF = jnp.bfloat16
 F32 = jnp.float32
 VMEM = pl.BlockSpec(memory_space=pltpu.VMEM)
@@ -159,7 +188,6 @@
                 [
                     jnp.where(hit, (row // 16).astype(F32), zero),
                     jnp.where(hit, (row % 16).astype(F32), zero),
-                    jnp.where(hit, 1.0, zero),
                 ],
                 axis=0,
             ).astype(BF)
@@ -171,7 +199,7 @@
         NT,
         preferred_element_type=F32,
     )
-    asked = found[:asks] * 16.0 + found[asks : 2 * asks] + found[2 * asks :] - 1.0
+    asked = found[:asks] * 16.0 + found[asks:]
     lane = lax.broadcasted_iota(jnp.int32, (asks, LANES), 1)
     for d in range(n_data):
         total = jnp.sum(sums[d * padded : (d + 1) * padded], axis=0, keepdims=True)
@@ -180,41 +208,53 @@
 
 
 def serve_body(n_data, capacity, ask_ref, table_ref, out_ref, found):
-    blocks = ask_ref.shape[0] // n_data
+    block = ask_ref.shape[0] // n_data
     found[...] = jnp.zeros_like(found)
     for d in range(n_data):
-        asked = ask_ref[d * blocks + blocks - 1, LANES - 1]
 
         def group(g, carry, d=d):
-            line, lane = d * blocks + g // 8, (g % 8) * GROUP
             start = pl.multiple_of(d * capacity + g * GROUP, GROUP)
+            rows = [ask_ref[d * block + g * GROUP + k] for k in range(GROUP)]
+            taken = [table_ref[pl.ds(row, 1), :] for row in rows]
             for k in range(GROUP):
-                row = jnp.maximum(ask_ref[line, lane + k], 0)
-                found[pl.ds(start + k, 1), :] = table_ref[pl.ds(row, 1), :]
+                found[pl.ds(start + k, 1), :] = taken[k]
             return carry
 
+        asked = ask_ref[(d + 1) * block - 1]
         lax.fori_loop(0, (asked + GROUP - 1) // GROUP, group, 0)
     out_ref[...] = found[...].astype(BF)
 
 
-def pick(index_ref, source, into, lines):
+def pick(index_ref, source, into):
     def group(g, carry):
-        line, lane = g // 8, (g % 8) * GROUP
         start = pl.multiple_of(g * GROUP, GROUP)
+        rows = [index_ref[start + k] for k in range(GROUP)]
+        taken = [source[pl.ds(row, 1), :] for row in rows]
         for k in range(GROUP):
-            into[pl.ds(start + k, 1), :] = source[pl.ds(index_ref[line, lane + k], 1), :]
+            into[pl.ds(start + k, 1), :] = taken[k]
         return carry
 
-    lax.fori_loop(0, lines * 8, group, 0)
+    lax.fori_loop(0, into.shape[0] // GROUP, group, 0)
+
+
+def put(index_ref, source, into):
+    def group(g, carry):
+        start = pl.multiple_of(g * GROUP, GROUP)
+        rows = [index_ref[start + k] for k in range(GROUP)]
+        taken = [source[pl.ds(start + k, 1), :] for k in range(GROUP)]
+        for k in range(GROUP):
+            into[pl.ds(rows[k], 1), :] = taken[k]
+        return carry
+
+    lax.fori_loop(0, source.shape[0] // GROUP, group, 0)
 
 
 def hot_rows_body(id_ref, table_ref, out_ref, found):
-    pick(id_ref, table_ref, found, NH)
+    pick(id_ref, table_ref, found)
     out_ref[...] = found[...].astype(BF)
 
 
 def cross_body(
-    rank,
     place_ref,
     back_ref,
     hot_ref,
@@ -225,20 +265,22 @@
 ):
     n_pieces = len(rest) - 10
     pieces = rest[:n_pieces]
-    send_ref, hot_grad_ref, down, up, back, cold, upper, x_all, du_all, sem = rest[n_pieces:]
-    half = pieces[0].shape[0] // 2
+    send_ref, hot_grad_ref, downs, ups, back, cold, upper, x_all, du_all, sem = rest[n_pieces:]
     copies = []
-    for part, target in ((0, down), (1, up)):
+    for part, target in ((0, downs), (1, ups)):
+        first = 0
         for i, piece in enumerate(pieces):
+            count = piece.shape[0]
             copy = pltpu.make_async_copy(
-                piece.at[pl.ds(part * half, half)],
-                target.at[pl.ds(i * half, half)],
-                sem.at[part, i],
+                piece.at[:, part], target.at[pl.ds(first, count)], sem.at[part, i]
             )
             copy.start()
             copies.append(copy)
+            first += count
+    down = downs.reshape(downs.shape[0] * downs.shape[1], F)
+    up = ups.reshape(ups.shape[0] * ups.shape[1], F)
     back[...] = back_ref[...].astype(F32)
-    pick(place_ref, back, cold, NC)
+    pick(place_ref, back, cold)
     rows = LANES
     for s in range(NH):
         x_all[:, s * E : (s + 1) * E] = hot_ref[s * rows : (s + 1) * rows, :]
@@ -277,15 +319,7 @@
                 hot_grad_ref[s * rows : (s + 1) * rows, :] = piece
             else:
                 cold[(s - NH) * rows : (s - NH + 1) * rows, :] = piece
-
-    def group(g, carry):
-        line, lane = g // 8, (g % 8) * GROUP
-        start = pl.multiple_of(g * GROUP, GROUP)
-        for k in range(GROUP):
-            back[pl.ds(place_ref[line, lane + k], 1), :] = cold[pl.ds(start + k, 1), :]
-        return carry
-
-    lax.fori_loop(0, NC * 8, group, 0)
+    put(place_ref, cold, back)
     send_ref[...] = back[...].astype(BF)
 
 
@@ -305,13 +339,17 @@
 def cold_sum_body(n_data, capacity, ask_ref, grad_ref, out_ref, hits):
     owned = out_ref.shape[0]
     blocks = ask_ref.shape[0] // n_data
-    names = lax.broadcasted_iota(jnp.int32, (owned, LANES), 0)
+    lines = []
     for d in range(n_data):
         for b in range(blocks):
             wide = min(LANES, capacity - b * LANES)
-            hit = (names == ask_ref[d * blocks + b : d * blocks + b + 1, :]).astype(F32).astype(BF)
-            start = d * capacity + b * LANES
-            hits[:, start : start + wide] = hit[:, :wide]
+            lines.append(ask_ref[d * blocks + b : d * blocks + b + 1, :wide])
+    ids = jnp.concatenate(lines, axis=1)
+    names = lax.broadcasted_iota(jnp.int32, (owned, LANES), 0)
+    for start in range(0, n_data * capacity, LANES):
+        hits[:, start : start + LANES] = (
+            (names == ids[:, start : start + LANES]).astype(F32).astype(BF)
+        )
     out_ref[...] = jnp.dot(hits[...], grad_ref[...], preferred_element_type=F32)
 
 
@@ -336,8 +374,9 @@
         "route",
     )(owner_t, cold_rows.T)
     asked = lax.all_to_all(ask, "dp", split_axis=0, concat_axis=0, tiled=True)
-    pieces = weight_pieces(cross_down.T, cross_up)
+    starts = weight_starts(cross_down.T, cross_up)
     hot_t = hot_ids.T
+    place = place.reshape(-1)
     hot_rows = call(
         hot_rows_body,
         shape((NH * rows, E), BF),
@@ -345,7 +384,8 @@
         [pltpu.VMEM((NH * rows, E), F32)],
         (10**6, 4 * 10**6),
         "hot_rows",
-    )(hot_t, hot_table)
+    )(hot_t.reshape(-1), hot_table)
+    asked = after(asked, hot_rows)
     found = call(
         functools.partial(serve_body, n_data, capacity),
         shape((places, E), BF),
@@ -353,16 +393,19 @@
         [pltpu.VMEM((places, E), F32)],
         (10**6, 6 * 10**6),
         "serve",
-    )(asked, cold_table)
+    )(asked.reshape(-1), cold_table)
     returned = lax.all_to_all(found, "dp", split_axis=0, concat_axis=0, tiled=True)
-    rank = sum(p.shape[0] for p in pieces) // 2
+    pieces = weight_pieces(starts, found)
+    n_shards = sum(p.shape[0] for p in pieces)
+    depth = cross_up.shape[0]
+    rank = n_shards * depth
     send, hot_grad = call(
-        functools.partial(cross_body, rank),
+        cross_body,
         (shape((places, E), BF), shape((NH * rows, E), F32)),
         [SMEM] + [VMEM] * 5 + [ANY] * len(pieces),
         [
-            pltpu.VMEM((rank, F), BF),
-            pltpu.VMEM((rank, F), BF),
+            pltpu.VMEM((n_shards, depth, F), BF),
+            pltpu.VMEM((n_shards, depth, F), BF),
             pltpu.VMEM((places, E), F32),
             pltpu.VMEM((NC * rows, E), F32),
             pltpu.VMEM((rows, F), F32),
@@ -390,6 +433,8 @@
         (2 * HOT * NH * rows * 2 * E, 5 * 10**6),
         "hot_sum",
     )(hot_t, hot_grad)
+    hot_share = hot_along_z(hot_down(hot_partial))
+    incoming = after(incoming, hot_share)
     cold_partial = call(
         functools.partial(cold_sum_body, n_data, capacity),
         shape((owned, E), F32),
@@ -398,7 +443,7 @@
         (2 * owned * places * E, 5 * 10**6),
         "cold_sum",
     )(asked, incoming)
-    return sum_hot(hot_partial), sum_cold(cold_partial)
+    return hot_up(hot_share), sum_cold(cold_partial)
 
 
 def large_step(

time: 195 us -> 158 us (0.81)
  Pallas kernels: 41.7 us -> 23.1 us
  blocking collectives: 13.7 us -> 0 us
  waiting for transfers between devices: 76.5 us -> 66.6 us
  starting transfers between devices: 37.3 us -> 46.8 us
  local copies, waits for them, and re-layouts: 19.5 us -> 12.4 us
  other arithmetic: 5.43 us -> 7.79 us
    all_to_all x1, waiting for transfers between devices: 15.6 us -> 0.01 us  [small_step(): lax.all_to_all(send, 'dp', split_axis=0, concat_axis=0, tiled=True)]
    all_to_all x1 -> x0, blocking collectives: 13.7 us -> none  [small_step(): asked = lax.all_to_all(ask, 'dp', split_axis=0, concat_axis=0, tiled=True)]
    ppermute x9, waiting for transfers between devices: 15.7 us -> 7.61 us  [shift(): lax.ppermute(value, axis, [(i, (i + distance) % size) for i in range(size)])]
    unnamed x50 -> x34, local copies, waits for them, and re-layouts: 15.1 us -> 7.04 us
    all_to_all x0 -> x1, waiting for transfers between devices: none -> 7.41 us  [small_step(): asked = lax.all_to_all(ask, 'dp', split_axis=0, concat_axis=0, tiled=True)]
    ppermute x17 -> x20, waiting for transfers between devices: 45.2 us -> 51.6 us  [swap(): return lax.ppermute(value, axis, [(i, i ^ distance) for i in range(size)])]
    pallas_call x1, Pallas kernels: 15 us -> 8.91 us  [small_step(): call(cross_body, (shape((places, E), BF), shape((NH * rows, E), F32)), [S...]
    pallas_call x1, Pallas kernels: 11.1 us -> 5.05 us  [small_step(): call(functools.partial(serve_body, n_data, capacity), shape((places, E),...]
  transfers between devices with their start and end apart: 28 -> 35, of which waited for: 15 -> 12; matrix products, arithmetic and copies ran while one was open for 5% -> 7% of each run, Pallas kernels for 14% -> 5%
where the time goes in v3:
time: 158 us
  waiting for transfers between devices  66.6 us (42%)
  starting transfers between devices  46.8 us (30%)
  Pallas kernels  23.1 us (15%)
  local copies, waits for them, and re-layouts  12.4 us (8%)
  other arithmetic  7.79 us (5%)
    ppermute x20, waiting for transfers between devices, swap(): return lax.ppermute(value, axis, [(i, i ^ distance) for i in range(size)])  51.6 us
    ppermute x20, starting transfers between devices, swap(): return lax.ppermute(value, axis, [(i, i ^ distance) for i in range(size)])  17.6 us
    ppermute x9, starting transfers between devices, shift(): lax.ppermute(value, axis, [(i, (i + distance) % size) for i in range(size)])  16 us
    pallas_call x1, Pallas kernels, small_step(): call(cross_body, (shape((places, E), BF), shape((NH * rows, E), F32)), [S...  8.91 us
    ppermute x9, waiting for transfers between devices, shift(): lax.ppermute(value, axis, [(i, (i + distance) % size) for i in range(size)])  7.61 us
    all_to_all x1, waiting for transfers between devices, small_step(): asked = lax.all_to_all(ask, 'dp', split_axis=0, concat_axis=0, tiled=True)  7.41 us
    unnamed x34, local copies, waits for them, and re-layouts  7.04 us
    all_to_all x1, starting transfers between devices, small_step(): lax.all_to_all(send, 'dp', split_axis=0, concat_axis=0, tiled=True)  5.66 us
  transfers between devices with their start and end apart: 35, of which 12 were waited for; matrix products, arithmetic and copies ran while one was open for 7% of the time, Pallas kernels for 5%

profile of v3, /device:TPU:0, one launch (start us, length us, event | category | flops | bytes accessed | tf_op | source)
XLA Modules:
  0.0 157.6 jit_solution(7937422447739019081)
XLA Ops:
  0.7 1.8 %maximum_bitcast_fusion.rest_0_ = bf16[1,2,16,3328]{3,2,1,0:T(8,128)(2,1)} fusion(bf16[1,16,3328]{2,1,0:T(8,128)(2,1)} %bitcast.31, bf16[1,16,3328]{2,1,0:T(8,128)(2,1)} %bitcast.32), kind=kLoop, calls=%fused_computation.9 | loop fusion | flops 106496 | bytes 425984 | tf_op jit(solution)/shard_map/broadcast_in_dim | solution.py:50
  2.4 3.0 %collective-permute-start.5 = (bf16[1,2,16,3328]{3,2,1,0:T(8,128)(2,1)}, bf16[1,2,16,3328]{3,2,1,0:T(8,128)(2,1)}, u32[]{:S(2)}, u32[]{:S(2)}) collective-permute-start(bf16[1,2,16,3328]{3,2,1,0:T(8,128)(2,1)} %maximum_bitcast_fusion.rest_0_), channel_id=1, source_target_pairs={{0,8},{4,12},{8,16},{12,20},{16,24},{20,28},{24,0},{28,4},{1,9},{5... | collective-permute-start | bytes 638984 | tf_op jit(solution)/shard_map/ppermute | solution.py:34
  5.4 2.6 %collective-permute-start.6 = (bf16[1,2,16,3328]{3,2,1,0:T(8,128)(2,1)}, bf16[1,2,16,3328]{3,2,1,0:T(8,128)(2,1)S(1)}, u32[]{:S(2)}, u32[]{:S(2)}) collective-permute-start(bf16[1,2,16,3328]{3,2,1,0:T(8,128)(2,1)} %maximum_bitcast_fusion.rest_0_), channel_id=1, source_target_pairs={{0,16},{4,20},{8,24},{12,28},{16,0},{20,4},{24,8},{28,12},{1,17},{... | collective-permute-start | bytes 638984 | tf_op jit(solution)/shard_map/ppermute | solution.py:34
  8.0 1.3 collective-permute-start.7
  9.4 0.7 reduce
  10.4 0.7 copy-done.10
  11.1 1.2 route.1
  12.3 3.3 %all-to-all-start = ((s32[8,4,128]{2,1,0:T(4,128)}), s32[8,4,128]{2,1,0:T(4,128)S(1)}, u32[]{:S(2)}, u32[]{:S(2)}) async-start(s32[8,4,128]{2,1,0:T(4,128)} %bitcast.4), calls=%async_computation | async-start | bytes 32768 | tf_op jit(solution)/shard_map/all_to_all | solution.py:376
  15.6 1.9 %collective-permute-start.3 = (bf16[1,2,16,3328]{3,2,1,0:T(8,128)(2,1)}, bf16[1,2,16,3328]{3,2,1,0:T(8,128)(2,1)}, u32[]{:S(2)}, u32[]{:S(2)}) collective-permute-start(bf16[1,2,16,3328]{3,2,1,0:T(8,128)(2,1)} %maximum_bitcast_fusion.rest_0_), channel_id=1, source_target_pairs={{0,4},{4,0},{8,12},{12,8},{16,20},{20,16},{24,28},{28,24},{1,5},{5... | collective-permute-start | bytes 638984 | tf_op jit(solution)/shard_map/ppermute | solution.py:29
  17.6 0.7 copy-done.7
  18.3 2.2 %hot_rows.1.hot_ref = bf16[1664,128]{1,0:T(8,128)(2,1)S(1)} custom-call(s32[1664]{0:T(1024)S(1)} %bitcast.25, f32[1024,128]{1,0:T(8,128)S(1)} %copy-done.1), custom_call_target="tpu_custom_call" | custom-call | flops 1000000 | bytes 4000000 | tf_op jit(solution)/shard_map/hot_rows/pallas_call | solution.py:380
  20.5 7.4 %all-to-all-done = s32[8,4,128]{2,1,0:T(4,128)S(1)} async-done(((s32[8,4,128]{2,1,0:T(4,128)}), s32[8,4,128]{2,1,0:T(4,128)S(1)}, u32[]{:S(2)}, u32[]{:S(2)}) %all-to-all-start) | async-done | bytes 16416 | tf_op jit(solution)/shard_map/all_to_all | solution.py:376
  27.9 5.0 %serve.1 = bf16[3328,128]{1,0:T(8,128)(2,1)} custom-call(s32[4096]{0:T(1024)S(1)} %bitcast.23, f32[2048,128]{1,0:T(8,128)S(1)} %copy-done), custom_call_target="tpu_custom_call" | custom-call | flops 1000000 | bytes 6000000 | tf_op jit(solution)/shard_map/serve/pallas_call | solution.py:389
  32.9 3.6 %all-to-all-start.1 = ((bf16[8,416,128]{2,1,0:T(8,128)(2,1)}), bf16[8,416,128]{2,1,0:T(8,128)(2,1)S(1)}, u32[]{:S(2)}, u32[]{:S(2)}) async-start(bf16[8,416,128]{2,1,0:T(8,128)(2,1)} %bitcast.8), calls=%async_computation.1 | async-start | bytes 1703936 | tf_op jit(solution)/shard_map/all_to_all | solution.py:397
  36.5 0.7 copy-done.11
  37.2 1.0 constant_dynamic-update-slice_fusion.2
  38.2 1.2 pad_maximum_fusion
  39.5 1.6 collective-permute-start.11
  41.1 0.9 constant_dynamic-update-slice_fusion.rest_6_
  42.0 2.0 %collective-permute-start.9 = (bf16[3,2,16,3328]{3,2,1,0:T(8,128)(2,1)S(1)}, bf16[3,2,16,3328]{3,2,1,0:T(8,128)(2,1)}, u32[]{:S(2)}, u32[]{:S(2)}) collective-permute-start(bf16[3,2,16,3328]{3,2,1,0:T(8,128)(2,1)S(1)} %constant_dynamic-update-slice_fusion.rest_6_), channel_id=1, source_target_pairs={{0,4},{4,0},{8,12},{12,8},{16,20},{20,16},{24,28},{28,24},{1,5},{5... | collective-permute-start | bytes 1916936 | tf_op jit(solution)/shard_map/ppermute | solution.py:29
  44.1 1.5 collective-permute-start.1
  45.6 15.9 %collective-permute-done.11.rest_10_ = bf16[4,2,16,3328]{3,2,1,0:T(8,128)(2,1)} collective-permute-done((bf16[4,2,16,3328]{3,2,1,0:T(8,128)(2,1)S(1)}, bf16[4,2,16,3328]{3,2,1,0:T(8,128)(2,1)}, u32[]{:S(2)}, u32[]{:S(2)}) %collective-permute-start.11) | collective-permute-done | bytes 852000 | tf_op jit(solution)/shard_map/ppermute | solution.py:29
  61.5 0.5 collective-permute-start
  62.0 16.4 %collective-permute-done.1.rest_2_ = bf16[1,2,16,3328]{3,2,1,0:T(8,128)(2,1)} collective-permute-done((bf16[1,2,16,3328]{3,2,1,0:T(8,128)(2,1)}, bf16[1,2,16,3328]{3,2,1,0:T(8,128)(2,1)}, u32[]{:S(2)}, u32[]{:S(2)}) %collective-permute-start.1) | collective-permute-done | bytes 213024 | tf_op jit(solution)/shard_map/ppermute | solution.py:29
  78.5 0.5 collective-permute-start.10
  79.1 0.7 copy-done.3
  80.2 2.0 %collective-permute-done.4.rest_5_ = bf16[1,2,16,3328]{3,2,1,0:T(8,128)(2,1)S(1)} collective-permute-done((bf16[1,2,16,3328]{3,2,1,0:T(8,128)(2,1)}, bf16[1,2,16,3328]{3,2,1,0:T(8,128)(2,1)S(1)}, u32[]{:S(2)}, u32[]{:S(2)}) %collective-permute-start.4) | collective-permute-done | bytes 213024 | tf_op jit(solution)/shard_map/ppermute | solution.py:29
  82.2 0.7 copy-done.5
  83.0 0.7 reshape.37.weight_ref
  83.8 0.9 collective-permute-done.2.rest_3_
  84.7 0.6 copy-done.9
  85.4 0.9 copy-done.4
  86.3 0.9 copy-done.6
  87.3 8.9 %cross.1 = (bf16[3328,128]{1,0:T(8,128)(2,1)S(1)}, f32[1664,128]{1,0:T(8,128)S(1)}) custom-call(s32[2048]{0:T(1024)S(1)} %bitcast.27, bf16[3328,128]{1,0:T(8,128)(2,1)S(1)} %bitcast.20, bf16[1664,128]{1,0:T(8,128)(2,1)S(1)} %hot_rows.1.hot_ref, s32[1,128]{1,0:T(1,128)S(1)} %bitcast.29, f32[1,3328]{1,0:T(1,128)S(1)} %reshape.36.bias_ref, ...), custom_call_target="tpu_custom_call" | custom-call | flops 1744830464 | bytes 20000000 | tf_op jit(solution)/shard_map/cross/pallas_call | solution.py:402
  96.2 1.2 hot_sum.1
  97.7 5.7 %all-to-all-start.2 = ((bf16[8,416,128]{2,1,0:T(8,128)(2,1)}), bf16[8,416,128]{2,1,0:T(8,128)(2,1)S(1)}, u32[]{:S(2)}, u32[]{:S(2)}) async-start(bf16[8,416,128]{2,1,0:T(8,128)(2,1)} %bitcast.21), calls=%async_computation.2 | async-start | bytes 1703936 | tf_op jit(solution)/shard_map/all_to_all | solution.py:427
  103.4 1.6 collective-permute-start.16
  105.0 2.0 %collective-permute-start.17 = (f32[128,128]{1,0:T(8,128)S(1)}, f32[128,128]{1,0:T(8,128)S(1)}, u32[]{:S(2)}, u32[]{:S(2)}) collective-permute-start(f32[128,128]{1,0:T(8,128)S(1)} %get-tuple-element.22), channel_id=1, source_target_pairs={{0,4},{4,0},{8,12},{12,8},{16,20},{20,16},{24,28},{28,24},{1,5},{5... | collective-permute-start | bytes 196616 | tf_op jit(solution)/shard_map/ppermute | solution.py:29
  107.0 0.8 collective-permute-done.16
  107.7 7.8 %collective-permute-done.17 = f32[128,128]{1,0:T(8,128)S(1)} collective-permute-done((f32[128,128]{1,0:T(8,128)S(1)}, f32[128,128]{1,0:T(8,128)S(1)}, u32[]{:S(2)}, u32[]{:S(2)}) %collective-permute-start.17) | collective-permute-done | bytes 65568 | tf_op jit(solution)/shard_map/ppermute | solution.py:29
  115.7 5.1 %collective-permute-start.20 = (f32[32,128]{1,0:T(8,128)S(1)}, f32[32,128]{1,0:T(8,128)S(1)}, u32[]{:S(2)}, u32[]{:S(2)}) collective-permute-start(f32[32,128]{1,0:T(8,128)S(1)} %get-tuple-element.27), channel_id=1, source_target_pairs={{0,16},{4,20},{8,24},{12,28},{16,0},{20,4},{24,8},{28,12},{1,17},{... | collective-permute-start | bytes 49160 | tf_op jit(solution)/shard_map/ppermute | solution.py:34
  120.8 1.7 %collective-permute-done.19 = f32[32,128]{1,0:T(8,128)S(1)} collective-permute-done((f32[32,128]{1,0:T(8,128)S(1)}, f32[32,128]{1,0:T(8,128)S(1)}, u32[]{:S(2)}, u32[]{:S(2)}) %collective-permute-start.19) | collective-permute-done | bytes 16416 | tf_op jit(solution)/shard_map/ppermute | solution.py:34
  122.5 4.1 %collective-permute-done.20 = f32[32,128]{1,0:T(8,128)S(1)} collective-permute-done((f32[32,128]{1,0:T(8,128)S(1)}, f32[32,128]{1,0:T(8,128)S(1)}, u32[]{:S(2)}, u32[]{:S(2)}) %collective-permute-start.20) | collective-permute-done | bytes 16416 | tf_op jit(solution)/shard_map/ppermute | solution.py:34
  126.7 0.6 broadcast_in_dim.10
  127.3 0.6 constant_dynamic-update-slice_fusion.10
  127.9 0.7 collective-permute-start.22
  128.6 1.7 %collective-permute-start.23 = (f32[32,128]{1,0:T(8,128)S(1)}, f32[32,128]{1,0:T(8,128)S(1)}, u32[]{:S(2)}, u32[]{:S(2)}) collective-permute-start(f32[32,128]{1,0:T(8,128)S(1)} %get-tuple-element.21), channel_id=1, source_target_pairs={{0,16},{4,20},{8,24},{12,28},{16,0},{20,4},{24,8},{28,12},{1,17},{... | collective-permute-start | bytes 49160 | tf_op jit(solution)/shard_map/ppermute | solution.py:34
  130.3 1.4 collective-permute-start.24
  131.7 1.7 %collective-permute-done.22 = f32[32,128]{1,0:T(8,128)S(1)} collective-permute-done((f32[32,128]{1,0:T(8,128)S(1)}, f32[32,128]{1,0:T(8,128)S(1)}, u32[]{:S(2)}, u32[]{:S(2)}) %collective-permute-start.22) | collective-permute-done | bytes 16416 | tf_op jit(solution)/shard_map/ppermute | solution.py:34
  133.5 0.6 constant_dynamic-update-slice_fusion.9
  134.1 0.6 constant_dynamic-update-slice_fusion.8
  134.7 0.6 constant_dynamic-update-slice_fusion.7
  135.3 4.5 %cold_sum.1 = f32[2048,128]{1,0:T(8,128)S(1)} custom-call(s32[32,128]{1,0:T(8,128)S(1)} %bitcast.24, bf16[3328,128]{1,0:T(8,128)(2,1)S(1)} %bitcast.22), custom_call_target="tpu_custom_call" | custom-call | flops 1744830464 | bytes 5000000 | tf_op jit(solution)/shard_map/cold_sum/pallas_call | solution.py:438
  139.8 1.6 collective-permute-start.25
  141.4 1.4 collective-permute-start.26
  142.8 0.6 collective-permute-start.27
  143.4 1.1 fusion
  144.5 1.6 collective-permute-start.30
  146.1 0.9 constant_dynamic-update-slice_fusion.6
  147.0 6.0 %collective-permute-done.30 = bf16[1024,128]{1,0:T(8,128)(2,1)S(1)} collective-permute-done((bf16[1024,128]{1,0:T(8,128)(2,1)S(1)}, bf16[1024,128]{1,0:T(8,128)(2,1)S(1)}, u32[]{:S(2)}, u32[]{:S(2)}) %collective-permute-start.30) | collective-permute-done | bytes 262176 | tf_op jit(solution)/shard_map/ppermute | solution.py:29
  153.1 0.5 collective-permute-start.28
  153.7 1.7 %collective-permute-done.28 = f32[512,128]{1,0:T(8,128)S(1)} collective-permute-done((f32[512,128]{1,0:T(8,128)S(1)}, f32[512,128]{1,0:T(8,128)S(1)}, u32[]{:S(2)}, u32[]{:S(2)}) %collective-permute-start.28) | collective-permute-done | bytes 262176 | tf_op jit(solution)/shard_map/ppermute | solution.py:29
  155.4 1.0 multiply_subtract_fusion.1
  156.3 1.3 multiply_subtract_fusion
  (73 shorter events, 1.8 us)
Async XLA Ops:
  0.6 16.9 %copy-start.1 = (f32[1024,128]{1,0:T(8,128)S(1)}, f32[1024,128]{1,0:T(8,128)}, u32[]{:S(2)}) copy-start(f32[1024,128]{1,0:T(8,128)} %table_ref.2) | copy-start | bytes 1572868
  0.6 27.3 %copy-start = (f32[2048,128]{1,0:T(8,128)S(1)}, f32[2048,128]{1,0:T(8,128)}, u32[]{:S(2)}) copy-start(f32[2048,128]{1,0:T(8,128)} %table_ref.3) | copy-start | bytes 3145732
  2.4 34.1 %collective-permute-start.5 = (bf16[1,2,16,3328]{3,2,1,0:T(8,128)(2,1)}, bf16[1,2,16,3328]{3,2,1,0:T(8,128)(2,1)}, u32[]{:S(2)}, u32[]{:S(2)}) collective-permute-start(bf16[1,2,16,3328]{3,2,1,0:T(8,128)(2,1)} %maximum_bitcast_fusion.rest_0_), channel_id=1, source_target_pairs={{0,8},{4,12},{8,16},{12,20},{16,24},{20,28},{24,0},{28,4},{1,9},{5... | collective-permute-start | bytes 638984 | tf_op jit(solution)/shard_map/ppermute | solution.py:34
  5.4 31.1 %collective-permute-start.6 = (bf16[1,2,16,3328]{3,2,1,0:T(8,128)(2,1)}, bf16[1,2,16,3328]{3,2,1,0:T(8,128)(2,1)S(1)}, u32[]{:S(2)}, u32[]{:S(2)}) collective-permute-start(bf16[1,2,16,3328]{3,2,1,0:T(8,128)(2,1)} %maximum_bitcast_fusion.rest_0_), channel_id=1, source_target_pairs={{0,16},{4,20},{8,24},{12,28},{16,0},{20,4},{24,8},{28,12},{1,17},{... | collective-permute-start | bytes 638984 | tf_op jit(solution)/shard_map/ppermute | solution.py:34
  8.0 29.2 %collective-permute-start.7 = (bf16[1,2,16,3328]{3,2,1,0:T(8,128)(2,1)}, bf16[1,2,16,3328]{3,2,1,0:T(8,128)(2,1)}, u32[]{:S(2)}, u32[]{:S(2)}) collective-permute-start(bf16[1,2,16,3328]{3,2,1,0:T(8,128)(2,1)} %maximum_bitcast_fusion.rest_0_), channel_id=1, source_target_pairs={{0,24},{4,28},{8,0},{12,4},{16,8},{20,12},{24,16},{28,20},{1,25},{... | collective-permute-start | bytes 638984 | tf_op jit(solution)/shard_map/ppermute | solution.py:34
  10.4 0.7 copy-start.10
  12.3 15.6 %all-to-all-start = ((s32[8,4,128]{2,1,0:T(4,128)}), s32[8,4,128]{2,1,0:T(4,128)S(1)}, u32[]{:S(2)}, u32[]{:S(2)}) async-start(s32[8,4,128]{2,1,0:T(4,128)} %bitcast.4), calls=%async_computation | async-start | bytes 32768 | tf_op jit(solution)/shard_map/all_to_all | solution.py:376
  15.6 22.6 %collective-permute-start.3 = (bf16[1,2,16,3328]{3,2,1,0:T(8,128)(2,1)}, bf16[1,2,16,3328]{3,2,1,0:T(8,128)(2,1)}, u32[]{:S(2)}, u32[]{:S(2)}) collective-permute-start(bf16[1,2,16,3328]{3,2,1,0:T(8,128)(2,1)} %maximum_bitcast_fusion.rest_0_), channel_id=1, source_target_pairs={{0,4},{4,0},{8,12},{12,8},{16,20},{20,16},{24,28},{28,24},{1,5},{5... | collective-permute-start | bytes 638984 | tf_op jit(solution)/shard_map/ppermute | solution.py:29
  17.6 0.7 copy-start.7
  32.9 51.8 %all-to-all-start.1 = ((bf16[8,416,128]{2,1,0:T(8,128)(2,1)}), bf16[8,416,128]{2,1,0:T(8,128)(2,1)S(1)}, u32[]{:S(2)}, u32[]{:S(2)}) async-start(bf16[8,416,128]{2,1,0:T(8,128)(2,1)} %bitcast.8), calls=%async_computation.1 | async-start | bytes 1703936 | tf_op jit(solution)/shard_map/all_to_all | solution.py:397
  36.5 0.7 copy-start.11
  37.2 1.0 copy-start.12
  39.5 22.0 %collective-permute-start.11 = (bf16[4,2,16,3328]{3,2,1,0:T(8,128)(2,1)S(1)}, bf16[4,2,16,3328]{3,2,1,0:T(8,128)(2,1)}, u32[]{:S(2)}, u32[]{:S(2)}) collective-permute-start(bf16[4,2,16,3328]{3,2,1,0:T(8,128)(2,1)S(1)} %pad_maximum_fusion), channel_id=1, source_target_pairs={{0,2},{1,3},{2,0},{3,1},{4,6},{5,7},{6,4},{7,5},{8,10},{9,11},{10,... | collective-permute-start | bytes 2555912 | tf_op jit(solution)/shard_map/ppermute | solution.py:29
  42.0 41.0 %copy-start.15 = (f32[3328]{0:T(1024)S(1)}, f32[3328]{0:T(1024)}, u32[]{:S(2)}) copy-start(f32[3328]{0:T(1024)} %param.22) | copy-start | bytes 39940
  42.0 36.5 %collective-permute-start.9 = (bf16[3,2,16,3328]{3,2,1,0:T(8,128)(2,1)S(1)}, bf16[3,2,16,3328]{3,2,1,0:T(8,128)(2,1)}, u32[]{:S(2)}, u32[]{:S(2)}) collective-permute-start(bf16[3,2,16,3328]{3,2,1,0:T(8,128)(2,1)S(1)} %constant_dynamic-update-slice_fusion.rest_6_), channel_id=1, source_target_pairs={{0,4},{4,0},{8,12},{12,8},{16,20},{20,16},{24,28},{28,24},{1,5},{5... | collective-permute-start | bytes 1916936 | tf_op jit(solution)/shard_map/ppermute | solution.py:29
  44.0 35.0 %collective-permute-start.13 = (bf16[3,2,16,3328]{3,2,1,0:T(8,128)(2,1)S(1)}, bf16[3,2,16,3328]{3,2,1,0:T(8,128)(2,1)}, u32[]{:S(2)}, u32[]{:S(2)}) collective-permute-start(bf16[3,2,16,3328]{3,2,1,0:T(8,128)(2,1)S(1)} %constant_dynamic-update-slice_fusion.rest_6_), channel_id=1, source_target_pairs={{0,6},{1,7},{2,4},{3,5},{4,2},{5,3},{6,0},{7,1},{8,14},{9,15},{10,... | collective-permute-start | bytes 1916936 | tf_op jit(solution)/shard_map/ppermute | solution.py:46
  44.1 34.4 %collective-permute-start.1 = (bf16[1,2,16,3328]{3,2,1,0:T(8,128)(2,1)}, bf16[1,2,16,3328]{3,2,1,0:T(8,128)(2,1)}, u32[]{:S(2)}, u32[]{:S(2)}) collective-permute-start(bf16[1,2,16,3328]{3,2,1,0:T(8,128)(2,1)} %maximum_bitcast_fusion.rest_0_), channel_id=1, source_target_pairs={{0,2},{1,3},{2,0},{3,1},{4,6},{5,7},{6,4},{7,5},{8,10},{9,11},{10,... | collective-permute-start | bytes 638984 | tf_op jit(solution)/shard_map/ppermute | solution.py:29
  61.5 23.2 %collective-permute-start.12 = (bf16[4,2,16,3328]{3,2,1,0:T(8,128)(2,1)}, bf16[4,2,16,3328]{3,2,1,0:T(8,128)(2,1)}, u32[]{:S(2)}, u32[]{:S(2)}) collective-permute-start(bf16[4,2,16,3328]{3,2,1,0:T(8,128)(2,1)} %collective-permute-done.11.rest_10_), channel_id=1, source_target_pairs={{0,1},{1,0},{2,3},{3,2},{4,5},{5,4},{6,7},{7,6},{8,9},{9,8},{10,11... | collective-permute-start | bytes 2555912 | tf_op jit(solution)/shard_map/ppermute | solution.py:29
  61.5 17.5 %collective-permute-start = (bf16[1,2,16,3328]{3,2,1,0:T(8,128)(2,1)}, bf16[1,2,16,3328]{3,2,1,0:T(8,128)(2,1)S(1)}, u32[]{:S(2)}, u32[]{:S(2)}) collective-permute-start(bf16[1,2,16,3328]{3,2,1,0:T(8,128)(2,1)} %maximum_bitcast_fusion.rest_0_), channel_id=1, source_target_pairs={{0,1},{1,0},{2,3},{3,2},{4,5},{5,4},{6,7},{7,6},{8,9},{9,8},{10,11... | collective-permute-start | bytes 638984 | tf_op jit(solution)/shard_map/ppermute | solution.py:29
  78.5 6.2 %collective-permute-start.8 = (bf16[3,2,16,3328]{3,2,1,0:T(8,128)(2,1)S(1)}, bf16[3,2,16,3328]{3,2,1,0:T(8,128)(2,1)}, u32[]{:S(2)}, u32[]{:S(2)}) collective-permute-start(bf16[3,2,16,3328]{3,2,1,0:T(8,128)(2,1)S(1)} %constant_dynamic-update-slice_fusion.rest_6_), channel_id=1, source_target_pairs={{0,1},{1,0},{2,3},{3,2},{4,5},{5,4},{6,7},{7,6},{8,9},{9,8},{10,11... | collective-permute-start | bytes 1916936 | tf_op jit(solution)/shard_map/ppermute | solution.py:29
  78.5 6.2 %collective-permute-start.10 = (bf16[3,2,16,3328]{3,2,1,0:T(8,128)(2,1)}, bf16[3,2,16,3328]{3,2,1,0:T(8,128)(2,1)}, u32[]{:S(2)}, u32[]{:S(2)}) collective-permute-start(bf16[3,2,16,3328]{3,2,1,0:T(8,128)(2,1)} %collective-permute-done.9.rest_8_), channel_id=1, source_target_pairs={{0,1},{1,0},{2,3},{3,2},{4,5},{5,4},{6,7},{7,6},{8,9},{9,8},{10,11... | collective-permute-start | bytes 1916936 | tf_op jit(solution)/shard_map/ppermute | solution.py:29
  79.0 5.7 %collective-permute-start.14 = (bf16[3,2,16,3328]{3,2,1,0:T(8,128)(2,1)}, bf16[3,2,16,3328]{3,2,1,0:T(8,128)(2,1)}, u32[]{:S(2)}, u32[]{:S(2)}) collective-permute-start(bf16[3,2,16,3328]{3,2,1,0:T(8,128)(2,1)} %collective-permute-done.13.rest_12_), channel_id=1, source_target_pairs={{0,1},{1,0},{2,3},{3,2},{4,5},{5,4},{6,7},{7,6},{8,9},{9,8},{10,11... | collective-permute-start | bytes 1916936 | tf_op jit(solution)/shard_map/ppermute | solution.py:29
  79.1 0.7 copy-start.3
  79.7 2.5 %collective-permute-start.4 = (bf16[1,2,16,3328]{3,2,1,0:T(8,128)(2,1)}, bf16[1,2,16,3328]{3,2,1,0:T(8,128)(2,1)S(1)}, u32[]{:S(2)}, u32[]{:S(2)}) collective-permute-start(bf16[1,2,16,3328]{3,2,1,0:T(8,128)(2,1)} %collective-permute-done.3.rest_4_), channel_id=1, source_target_pairs={{0,1},{1,0},{2,3},{3,2},{4,5},{5,4},{6,7},{7,6},{8,9},{9,8},{10,11... | collective-permute-start | bytes 638984 | tf_op jit(solution)/shard_map/ppermute | solution.py:29
  82.2 0.7 copy-start.5
  82.9 1.8 %collective-permute-start.2 = (bf16[1,2,16,3328]{3,2,1,0:T(8,128)(2,1)}, bf16[1,2,16,3328]{3,2,1,0:T(8,128)(2,1)}, u32[]{:S(2)}, u32[]{:S(2)}) collective-permute-start(bf16[1,2,16,3328]{3,2,1,0:T(8,128)(2,1)} %collective-permute-done.1.rest_2_), channel_id=1, source_target_pairs={{0,1},{1,0},{2,3},{3,2},{4,5},{5,4},{6,7},{7,6},{8,9},{9,8},{10,11... | collective-permute-start | bytes 638984 | tf_op jit(solution)/shard_map/ppermute | solution.py:29
  84.7 0.7 copy-start.9
  85.4 0.9 copy-start.4
  86.3 0.9 copy-start.6
  87.3 8.9 %copy-start.8 = (s32[128,13]{0,1:T(8,128)S(1)}, s32[128,13]{0,1:T(8,128)}, u32[]{:S(2)}) copy-start(s32[128,13]{0,1:T(8,128)} %param.12) | copy-start | bytes 19972
  96.2 1.3 copy-start.2
  97.5 5.9 %collective-permute-start.15 = (f32[512,128]{1,0:T(8,128)S(1)}, f32[512,128]{1,0:T(8,128)S(1)}, u32[]{:S(2)}, u32[]{:S(2)}) collective-permute-start(f32[512,128]{1,0:T(8,128)S(1)} %constant_dynamic-slice_fusion.6), channel_id=1, source_target_pairs={{0,1},{1,0},{2,3},{3,2},{4,5},{5,4},{6,7},{7,6},{8,9},{9,8},{10,11... | collective-permute-start | bytes 786440 | tf_op jit(solution)/shard_map/ppermute | solution.py:29
  97.7 37.6 %all-to-all-start.2 = ((bf16[8,416,128]{2,1,0:T(8,128)(2,1)}), bf16[8,416,128]{2,1,0:T(8,128)(2,1)S(1)}, u32[]{:S(2)}, u32[]{:S(2)}) async-start(bf16[8,416,128]{2,1,0:T(8,128)(2,1)} %bitcast.21), calls=%async_computation.2 | async-start | bytes 1703936 | tf_op jit(solution)/shard_map/all_to_all | solution.py:427
  103.4 4.3 %collective-permute-start.16 = (f32[128,128]{1,0:T(8,128)S(1)}, f32[128,128]{1,0:T(8,128)S(1)}, u32[]{:S(2)}, u32[]{:S(2)}) collective-permute-start(f32[128,128]{1,0:T(8,128)S(1)} %get-tuple-element.24), channel_id=1, source_target_pairs={{0,2},{1,3},{2,0},{3,1},{4,6},{5,7},{6,4},{7,5},{8,10},{9,11},{10,... | collective-permute-start | bytes 196616 | tf_op jit(solution)/shard_map/ppermute | solution.py:29
  105.0 10.6 %collective-permute-start.17 = (f32[128,128]{1,0:T(8,128)S(1)}, f32[128,128]{1,0:T(8,128)S(1)}, u32[]{:S(2)}, u32[]{:S(2)}) collective-permute-start(f32[128,128]{1,0:T(8,128)S(1)} %get-tuple-element.22), channel_id=1, source_target_pairs={{0,4},{4,0},{8,12},{12,8},{16,20},{20,16},{24,28},{28,24},{1,5},{5... | collective-permute-start | bytes 196616 | tf_op jit(solution)/shard_map/ppermute | solution.py:29
  107.0 8.6 %collective-permute-start.18 = (f32[128,128]{1,0:T(8,128)S(1)}, f32[128,128]{1,0:T(8,128)S(1)}, u32[]{:S(2)}, u32[]{:S(2)}) collective-permute-start(f32[128,128]{1,0:T(8,128)S(1)} %get-tuple-element.23), channel_id=1, source_target_pairs={{0,6},{1,7},{2,4},{3,5},{4,2},{5,3},{6,0},{7,1},{8,14},{9,15},{10,... | collective-permute-start | bytes 196616 | tf_op jit(solution)/shard_map/ppermute | solution.py:46
  115.6 6.9 %collective-permute-start.19 = (f32[32,128]{1,0:T(8,128)S(1)}, f32[32,128]{1,0:T(8,128)S(1)}, u32[]{:S(2)}, u32[]{:S(2)}) collective-permute-start(f32[32,128]{1,0:T(8,128)S(1)} %get-tuple-element.25), channel_id=1, source_target_pairs={{0,8},{4,12},{8,16},{12,20},{16,24},{20,28},{24,0},{28,4},{1,9},{5... | collective-permute-start | bytes 49160 | tf_op jit(solution)/shard_map/ppermute | solution.py:34
  115.7 11.0 %collective-permute-start.20 = (f32[32,128]{1,0:T(8,128)S(1)}, f32[32,128]{1,0:T(8,128)S(1)}, u32[]{:S(2)}, u32[]{:S(2)}) collective-permute-start(f32[32,128]{1,0:T(8,128)S(1)} %get-tuple-element.27), channel_id=1, source_target_pairs={{0,16},{4,20},{8,24},{12,28},{16,0},{20,4},{24,8},{28,12},{1,17},{... | collective-permute-start | bytes 49160 | tf_op jit(solution)/shard_map/ppermute | solution.py:34
  120.8 5.9 %collective-permute-start.21 = (f32[32,128]{1,0:T(8,128)S(1)}, f32[32,128]{1,0:T(8,128)S(1)}, u32[]{:S(2)}, u32[]{:S(2)}) collective-permute-start(f32[32,128]{1,0:T(8,128)S(1)} %get-tuple-element.26), channel_id=1, source_target_pairs={{0,24},{4,28},{8,0},{12,4},{16,8},{20,12},{24,16},{28,20},{1,25},{... | collective-permute-start | bytes 49160 | tf_op jit(solution)/shard_map/ppermute | solution.py:34
  127.9 5.5 %collective-permute-start.22 = (f32[32,128]{1,0:T(8,128)S(1)}, f32[32,128]{1,0:T(8,128)S(1)}, u32[]{:S(2)}, u32[]{:S(2)}) collective-permute-start(f32[32,128]{1,0:T(8,128)S(1)} %get-tuple-element.21), channel_id=1, source_target_pairs={{0,8},{4,12},{8,16},{12,20},{16,24},{20,28},{24,0},{28,4},{1,9},{5... | collective-permute-start | bytes 49160 | tf_op jit(solution)/shard_map/ppermute | solution.py:34
  128.6 5.4 %collective-permute-start.23 = (f32[32,128]{1,0:T(8,128)S(1)}, f32[32,128]{1,0:T(8,128)S(1)}, u32[]{:S(2)}, u32[]{:S(2)}) collective-permute-start(f32[32,128]{1,0:T(8,128)S(1)} %get-tuple-element.21), channel_id=1, source_target_pairs={{0,16},{4,20},{8,24},{12,28},{16,0},{20,4},{24,8},{28,12},{1,17},{... | collective-permute-start | bytes 49160 | tf_op jit(solution)/shard_map/ppermute | solution.py:34
  130.3 4.3 %collective-permute-start.24 = (f32[32,128]{1,0:T(8,128)S(1)}, f32[32,128]{1,0:T(8,128)S(1)}, u32[]{:S(2)}, u32[]{:S(2)}) collective-permute-start(f32[32,128]{1,0:T(8,128)S(1)} %get-tuple-element.21), channel_id=1, source_target_pairs={{0,24},{4,28},{8,0},{12,4},{16,8},{20,12},{24,16},{28,20},{1,25},{... | collective-permute-start | bytes 49160 | tf_op jit(solution)/shard_map/ppermute | solution.py:34
  139.8 3.6 %collective-permute-start.29 = (f32[2048,128]{1,0:T(8,128)S(1)}, f32[2048,128]{1,0:T(8,128)}, u32[]{:S(2)}, u32[]{:S(2)}) collective-permute-start(f32[2048,128]{1,0:T(8,128)S(1)} %cold_sum.1), channel_id=1, source_target_pairs={{0,1},{1,0},{2,3},{3,2},{4,5},{5,4},{6,7},{7,6},{8,9},{9,8},{10,11... | collective-permute-start | bytes 3145736 | tf_op jit(solution)/shard_map/ppermute | solution.py:29
  139.8 7.1 %collective-permute-start.25 = (f32[128,128]{1,0:T(8,128)}, f32[128,128]{1,0:T(8,128)S(1)}, u32[]{:S(2)}, u32[]{:S(2)}) collective-permute-start(f32[128,128]{1,0:T(8,128)} %constant_dynamic-update-slice_fusion.7), channel_id=1, source_target_pairs={{0,2},{1,3},{2,0},{3,1},{4,6},{5,7},{6,4},{7,5},{8,10},{9,11},{10,... | collective-permute-start | bytes 196616 | tf_op jit(solution)/shard_map/ppermute | solution.py:29
  141.4 5.6 %collective-permute-start.26 = (f32[128,128]{1,0:T(8,128)}, f32[128,128]{1,0:T(8,128)S(1)}, u32[]{:S(2)}, u32[]{:S(2)}) collective-permute-start(f32[128,128]{1,0:T(8,128)} %constant_dynamic-update-slice_fusion.7), channel_id=1, source_target_pairs={{0,4},{4,0},{8,12},{12,8},{16,20},{20,16},{24,28},{28,24},{1,5},{5... | collective-permute-start | bytes 196616 | tf_op jit(solution)/shard_map/ppermute | solution.py:29
  142.8 10.3 %collective-permute-start.27 = (f32[128,128]{1,0:T(8,128)}, f32[128,128]{1,0:T(8,128)S(1)}, u32[]{:S(2)}, u32[]{:S(2)}) collective-permute-start(f32[128,128]{1,0:T(8,128)} %constant_dynamic-update-slice_fusion.7), channel_id=1, source_target_pairs={{0,6},{1,7},{2,4},{3,5},{4,2},{5,3},{6,0},{7,1},{8,14},{9,15},{10,... | collective-permute-start | bytes 196616 | tf_op jit(solution)/shard_map/ppermute | solution.py:46
  144.5 8.5 %collective-permute-start.30 = (bf16[1024,128]{1,0:T(8,128)(2,1)S(1)}, bf16[1024,128]{1,0:T(8,128)(2,1)S(1)}, u32[]{:S(2)}, u32[]{:S(2)}) collective-permute-start(bf16[1024,128]{1,0:T(8,128)(2,1)S(1)} %fusion), channel_id=1, source_target_pairs={{0,2},{1,3},{2,0},{3,1},{4,6},{5,7},{6,4},{7,5},{8,10},{9,11},{10,... | collective-permute-start | bytes 786440 | tf_op jit(solution)/shard_map/ppermute | solution.py:29
  153.0 2.4 %copy-start.14 = (bf16[1024,128]{1,0:T(8,128)(2,1)S(1)}, bf16[1024,128]{1,0:T(8,128)(2,1)}, u32[]{:S(2)}) copy-start(bf16[1024,128]{1,0:T(8,128)(2,1)} %param.17) | copy-start | bytes 786436
  153.0 3.3 %collective-permute-start.31 = (f32[1024,128]{1,0:T(8,128)S(1)}, f32[1024,128]{1,0:T(8,128)S(1)}, u32[]{:S(2)}, u32[]{:S(2)}) collective-permute-start(f32[1024,128]{1,0:T(8,128)S(1)} %convert_add_fusion), channel_id=1, source_target_pairs={{0,1},{1,0},{2,3},{3,2},{4,5},{5,4},{6,7},{7,6},{8,9},{9,8},{10,11... | collective-permute-start | bytes 1572872 | tf_op jit(solution)/shard_map/ppermute | solution.py:29
  153.1 2.2 %collective-permute-start.28 = (f32[512,128]{1,0:T(8,128)S(1)}, f32[512,128]{1,0:T(8,128)S(1)}, u32[]{:S(2)}, u32[]{:S(2)}) collective-permute-start(f32[512,128]{1,0:T(8,128)S(1)} %constant_dynamic-update-slice_fusion.3), channel_id=1, source_target_pairs={{0,1},{1,0},{2,3},{3,2},{4,5},{5,4},{6,7},{7,6},{8,9},{9,8},{10,11... | collective-permute-start | bytes 786440 | tf_op jit(solution)/shard_map/ppermute | solution.py:29
  153.7 2.7 %copy-start.13 = (bf16[2048,128]{1,0:T(8,128)(2,1)S(1)}, bf16[2048,128]{1,0:T(8,128)(2,1)}, u32[]{:S(2)}) copy-start(bf16[2048,128]{1,0:T(8,128)(2,1)} %param.19) | copy-start | bytes 1572868

commit v4 on v3

--- a/solution.py
+++ b/solution.py
@@ -21,7 +21,7 @@
 
 
 def is_small(n_data, n_reps):
-    return n_reps == 4 and n_data % 2 == 0 and n_data <= 16
+    return n_reps == 4 and n_data in (4, 8, 16)
 
 
 def swap(value, axis, distance):
@@ -49,17 +49,15 @@
 def weight_starts(down_t, up):
     own = jnp.stack([down_t, up])[None]
     z = [shift(own, "dp", 2 * k) for k in range(1, lax.axis_size("dp") // 2)]
-    return own, swap(own, "rep", 2), swap(own, "dp", 1), z
-
-
-def weight_pieces(starts, first):
-    own, own_x, own_y, z = starts
-    z = jnp.concatenate(lax.optimization_barrier((*z, first))[:-1], axis=0)
-    over_x = swap(jnp.concatenate([z, own_y], axis=0), "rep", 2)
+    return [own, swap(own, "rep", 2), swap(own, "dp", 1), swap_both(own)], jnp.concatenate(z, axis=0)
+
+
+def weight_pieces(plane, z):
+    over_x = swap(z, "rep", 2)
     over_y = swap(z, "dp", 1)
-    across = swap_both(z)
+    across = swap(over_y, "rep", 2)
     pieces = []
-    for piece in (own, own_x, own_y, z, over_y, over_x, across):
+    for piece in (*plane, z, over_x, over_y, across):
         pieces += [piece, swap(piece, "rep", 1)]
     return pieces
 
@@ -77,44 +75,23 @@
     )
 
 
-def plane_swaps():
-    return (
-        (lambda v: swap(v, "rep", 2), 2),
-        (lambda v: swap(v, "dp", 1), 1),
-        (swap_both, 3),
-    )
-
-
-def hot_down(partial):
-    nz = lax.axis_size("dp") // 2
+def hot_early(partial):
     rep, data = lax.axis_index("rep"), lax.axis_index("dp")
-    core, z, spot = rep % 2, data // 2, (rep // 2) * 2 + data % 2
-    total = half_of(partial, core, 2) + swap(half_of(partial, 1 - core, 2), "rep", 1)
-    total = half_of(total, spot, 4) + sum(move(half_of(total, spot ^ w, 4)) for move, w in plane_swaps())
-    parts = [half_of(total, z, nz)]
-    for k in range(1, nz):
-        parts.append(shift(half_of(total, (z + k) % nz, nz), "dp", 2 * k))
-    return sum(parts[1:], parts[0])
-
-
-def hot_along_z(total):
-    nz = lax.axis_size("dp") // 2
-    z, rows = lax.axis_index("dp") // 2, total.shape[0]
-    whole = jnp.zeros((rows * nz, E), total.dtype)
-    for k in range(nz):
-        piece = shift(total, "dp", 2 * k) if k else total
-        whole = lax.dynamic_update_slice_in_dim(whole, piece, ((z - k) % nz) * rows, axis=0)
-    return whole
-
-
-def hot_up(total):
+    total = partial
+    for axis, distance, index in (("rep", 1, rep % 2), ("rep", 2, rep // 2), ("dp", 1, data % 2)):
+        total = half_of(total, index, 2) + swap(half_of(total, 1 - index, 2), axis, distance)
+    return total + swap(total, "dp", 2)
+
+
+def hot_late(total):
     rep, data = lax.axis_index("rep"), lax.axis_index("dp")
-    core, spot, rows = rep % 2, (rep // 2) * 2 + data % 2, total.shape[0]
-    whole = jnp.zeros((rows * 4, E), total.dtype)
-    whole = lax.dynamic_update_slice_in_dim(whole, total, spot * rows, axis=0)
-    for move, w in plane_swaps():
-        whole = lax.dynamic_update_slice_in_dim(whole, move(total), (spot ^ w) * rows, axis=0)
-    return paired(whole, swap(whole, "rep", 1), core)
+    distance = 4
+    while distance < lax.axis_size("dp"):
+        total = total + swap(total, "dp", distance)
+        distance *= 2
+    for axis, distance, index in (("dp", 1, data % 2), ("rep", 2, rep // 2), ("rep", 1, rep % 2)):
+        total = paired(total, swap(total, axis, distance), index)
+    return total
 
 
 def sum_cold(partial):
@@ -370,11 +347,11 @@
         (shape((16, LANES), jnp.int32), shape((n_data * blocks, LANES), jnp.int32)),
         [VMEM, VMEM],
         [],
-        (10**8, 10**5),
+        (1, 1),
         "route",
     )(owner_t, cold_rows.T)
     asked = lax.all_to_all(ask, "dp", split_axis=0, concat_axis=0, tiled=True)
-    starts = weight_starts(cross_down.T, cross_up)
+    plane, z = weight_starts(cross_down.T, cross_up)
     hot_t = hot_ids.T
     place = place.reshape(-1)
     hot_rows = call(
@@ -382,20 +359,20 @@
         shape((NH * rows, E), BF),
         [SMEM, VMEM],
         [pltpu.VMEM((NH * rows, E), F32)],
-        (10**6, 4 * 10**6),
+        (1, 1),
         "hot_rows",
     )(hot_t.reshape(-1), hot_table)
-    asked = after(asked, hot_rows)
+    asked, hot_rows, z, *plane = lax.optimization_barrier((asked, hot_rows, z, *plane))
     found = call(
         functools.partial(serve_body, n_data, capacity),
         shape((places, E), BF),
         [SMEM, VMEM],
         [pltpu.VMEM((places, E), F32)],
-        (10**6, 6 * 10**6),
+        (1, 1),
         "serve",
     )(asked.reshape(-1), cold_table)
     returned = lax.all_to_all(found, "dp", split_axis=0, concat_axis=0, tiled=True)
-    pieces = weight_pieces(starts, found)
+    pieces = weight_pieces(plane, z)
     n_shards = sum(p.shape[0] for p in pieces)
     depth = cross_up.shape[0]
     rank = n_shards * depth
@@ -415,6 +392,7 @@
         ],
         (8 * rows * F * rank, 20 * 10**6),
         "cross",
+        58,
     )(
         place,
         returned,
@@ -433,8 +411,8 @@
         (2 * HOT * NH * rows * 2 * E, 5 * 10**6),
         "hot_sum",
     )(hot_t, hot_grad)
-    hot_share = hot_along_z(hot_down(hot_partial))
-    incoming = after(incoming, hot_share)
+    hot_share = hot_early(hot_partial)
+    incoming, hot_share = lax.optimization_barrier((incoming, hot_share))
     cold_partial = call(
         functools.partial(cold_sum_body, n_data, capacity),
         shape((owned, E), F32),
@@ -443,7 +421,7 @@
         (2 * owned * places * E, 5 * 10**6),
         "cold_sum",
     )(asked, incoming)
-    return hot_up(hot_share), sum_cold(cold_partial)
+    return hot_late(hot_share), sum_cold(cold_partial)
 
 
 def large_step(

time: 158 us -> 141 us (0.89)
  starting transfers between devices: 46.8 us -> 40.5 us
  local copies, waits for them, and re-layouts: 12.4 us -> 6.58 us
  waiting for transfers between devices: 66.6 us -> 62.1 us
    ppermute x9 -> x3, starting transfers between devices: 16 us -> 7.01 us  [shift(): lax.ppermute(value, axis, [(i, (i + distance) % size) for i in range(size)])]
    ppermute x9 -> x3, waiting for transfers between devices: 7.61 us -> 0.01 us  [shift(): lax.ppermute(value, axis, [(i, (i + distance) % size) for i in range(size)])]
    ppermute x20 -> x24, waiting for transfers between devices: 51.6 us -> 58.1 us  [swap(): return lax.ppermute(value, axis, [(i, i ^ distance) for i in range(size)])]
    all_to_all x1, waiting for transfers between devices: 7.41 us -> 2.6 us  [small_step(): asked = lax.all_to_all(ask, 'dp', split_axis=0, concat_axis=0, tiled=True)]
    dynamic_update_slice x7 -> x0, local copies, waits for them, and re-layouts: 2.7 us -> none  [the longest x3 1.82 us: hot_along_z(): lax.dynamic_update_slice_in_dim(whole, piece, (z - k) % nz * rows, axis=0)]
    unnamed x34 -> x44, local copies, waits for them, and re-layouts: 7.04 us -> 5.05 us
    ppermute x20 -> x24, starting transfers between devices: 17.6 us -> 17.5 us  [swap(): return lax.ppermute(value, axis, [(i, i ^ distance) for i in range(size)])]
  transfers between devices with their start and end apart: 35 -> 31, of which waited for: 12 -> 17; matrix products, arithmetic and copies ran while one was open for 7% -> 4% of each run, Pallas kernels for 5% -> 6%
where the time goes in v4:
time: 141 us; the launch traced here: 140 us
  waiting for transfers between devices  62.1 us (44%)
  starting transfers between devices  40.5 us (29%)
  Pallas kernels  23 us (16%)
  other arithmetic  6.82 us (5%)
  local copies, waits for them, and re-layouts  6.58 us (5%)
    ppermute x24, waiting for transfers between devices, swap(): return lax.ppermute(value, axis, [(i, i ^ distance) for i in range(size)])  58.1 us
    ppermute x24, starting transfers between devices, swap(): return lax.ppermute(value, axis, [(i, i ^ distance) for i in range(size)])  17.5 us
    pallas_call x1, Pallas kernels, small_step(): call(cross_body, (shape((places, E), BF), shape((NH * rows, E), F32)), [S...  10.3 us
    ppermute x3, starting transfers between devices, shift(): lax.ppermute(value, axis, [(i, (i + distance) % size) for i in range(size)])  7.01 us
    all_to_all x1, starting transfers between devices, small_step(): lax.all_to_all(send, 'dp', split_axis=0, concat_axis=0, tiled=True)  5.65 us
    unnamed x44, local copies, waits for them, and re-layouts  5.05 us
    all_to_all x1, starting transfers between devices, small_step(): lax.all_to_all(found, 'dp', split_axis=0, concat_axis=0, tiled=True)  4.95 us
    pallas_call x1, Pallas kernels, small_step(): call(functools.partial(cold_sum_body, n_data, capacity), shape((owned, E)...  4.5 us
  transfers between devices with their start and end apart: 31, of which 17 were waited for; matrix products, arithmetic and copies ran while one was open for 4% of the time, Pallas kernels for 6%

profile of v4, /device:TPU:0, one launch (start us, length us, event | category | flops | bytes accessed | tf_op | source)
XLA Modules:
  0.0 139.9 jit_solution(18136478680100612485)
XLA Ops:
  0.6 1.0 maximum_bitcast_fusion.rest_0_
  1.7 3.1 %collective-permute-start = (bf16[1,2,16,3328]{3,2,1,0:T(8,128)(2,1)S(1)}, bf16[1,2,16,3328]{3,2,1,0:T(8,128)(2,1)S(1)}, u32[]{:S(2)}, u32[]{:S(2)}) collective-permute-start(bf16[1,2,16,3328]{3,2,1,0:T(8,128)(2,1)S(1)} %maximum_bitcast_fusion.rest_0_), channel_id=1, source_target_pairs={{0,8},{4,12},{8,16},{12,20},{16,24},{20,28},{24,0},{28,4},{1,9},{5... | collective-permute-start | bytes 638984 | tf_op jit(solution)/shard_map/ppermute | solution.py:34
  4.8 2.6 %collective-permute-start.1 = (bf16[1,2,16,3328]{3,2,1,0:T(8,128)(2,1)S(1)}, bf16[1,2,16,3328]{3,2,1,0:T(8,128)(2,1)S(1)}, u32[]{:S(2)}, u32[]{:S(2)}) collective-permute-start(bf16[1,2,16,3328]{3,2,1,0:T(8,128)(2,1)S(1)} %maximum_bitcast_fusion.rest_0_), channel_id=1, source_target_pairs={{0,16},{4,20},{8,24},{12,28},{16,0},{20,4},{24,8},{28,12},{1,17},{... | collective-permute-start | bytes 638984 | tf_op jit(solution)/shard_map/ppermute | solution.py:34
  7.3 1.3 collective-permute-start.2
  8.7 1.5 %collective-permute-start.3 = (bf16[1,2,16,3328]{3,2,1,0:T(8,128)(2,1)S(1)}, bf16[1,2,16,3328]{3,2,1,0:T(8,128)(2,1)S(1)}, u32[]{:S(2)}, u32[]{:S(2)}) collective-permute-start(bf16[1,2,16,3328]{3,2,1,0:T(8,128)(2,1)S(1)} %maximum_bitcast_fusion.rest_0_), channel_id=1, source_target_pairs={{0,2},{1,3},{2,0},{3,1},{4,6},{5,7},{6,4},{7,5},{8,10},{9,11},{10,... | collective-permute-start | bytes 638984 | tf_op jit(solution)/shard_map/ppermute | solution.py:29
  10.2 1.5 %collective-permute-start.4 = (bf16[1,2,16,3328]{3,2,1,0:T(8,128)(2,1)S(1)}, bf16[1,2,16,3328]{3,2,1,0:T(8,128)(2,1)S(1)}, u32[]{:S(2)}, u32[]{:S(2)}) collective-permute-start(bf16[1,2,16,3328]{3,2,1,0:T(8,128)(2,1)S(1)} %maximum_bitcast_fusion.rest_0_), channel_id=1, source_target_pairs={{0,4},{4,0},{8,12},{12,8},{16,20},{20,16},{24,28},{28,24},{1,5},{5... | collective-permute-start | bytes 638984 | tf_op jit(solution)/shard_map/ppermute | solution.py:29
  11.7 0.7 reduce
  12.4 0.2 reshape.31
  12.7 0.6 copy-done.5
  13.3 1.2 route.1
  14.5 0.6 copy-done.4
  15.1 3.5 %all-to-all-start = ((s32[8,4,128]{2,1,0:T(4,128)}), s32[8,4,128]{2,1,0:T(4,128)S(1)}, u32[]{:S(2)}, u32[]{:S(2)}) async-start(s32[8,4,128]{2,1,0:T(4,128)} %bitcast.3), calls=%async_computation | async-start | bytes 32768 | tf_op jit(solution)/shard_map/all_to_all | solution.py:353
  18.7 2.2 %hot_rows.1.hot_ref = bf16[1664,128]{1,0:T(8,128)(2,1)S(1)} custom-call(s32[1664]{0:T(1024)S(1)} %bitcast.24, f32[1024,128]{1,0:T(8,128)S(1)} %copy-done.1), custom_call_target="tpu_custom_call" | custom-call | flops 1 | bytes 1 | tf_op jit(solution)/shard_map/hot_rows/pallas_call | solution.py:357
  20.9 0.7 copy-done.2
  21.6 1.9 %collective-permute-start.5 = (bf16[1,2,16,3328]{3,2,1,0:T(8,128)(2,1)S(1)}, bf16[1,2,16,3328]{3,2,1,0:T(8,128)(2,1)S(1)}, u32[]{:S(2)}, u32[]{:S(2)}) collective-permute-start(bf16[1,2,16,3328]{3,2,1,0:T(8,128)(2,1)S(1)} %maximum_bitcast_fusion.rest_0_), channel_id=1, source_target_pairs={{0,6},{1,7},{2,4},{3,5},{4,2},{5,3},{6,0},{7,1},{8,14},{9,15},{10,... | collective-permute-start | bytes 638984 | tf_op jit(solution)/shard_map/ppermute | solution.py:46
  23.5 0.9 pad_maximum_fusion.rest_8_
  24.4 2.6 %all-to-all-done = s32[8,4,128]{2,1,0:T(4,128)S(1)} async-done(((s32[8,4,128]{2,1,0:T(4,128)}), s32[8,4,128]{2,1,0:T(4,128)S(1)}, u32[]{:S(2)}, u32[]{:S(2)}) %all-to-all-start) | async-done | bytes 16416 | tf_op jit(solution)/shard_map/all_to_all | solution.py:353
  27.1 1.4 collective-permute-done.5.rest_6_
  28.4 0.7 copy-done.15
  29.1 1.9 %collective-permute-start.13 = (bf16[3,2,16,3328]{3,2,1,0:T(8,128)(2,1)}, bf16[3,2,16,3328]{3,2,1,0:T(8,128)(2,1)S(1)}, u32[]{:S(2)}, u32[]{:S(2)}) collective-permute-start(bf16[3,2,16,3328]{3,2,1,0:T(8,128)(2,1)} %pad_maximum_fusion.rest_8_), channel_id=1, source_target_pairs={{0,4},{4,0},{8,12},{12,8},{16,20},{20,16},{24,28},{28,24},{1,5},{5... | collective-permute-start | bytes 1916936 | tf_op jit(solution)/shard_map/ppermute | solution.py:29
  31.0 3.5 %serve.1 = bf16[3328,128]{1,0:T(8,128)(2,1)} custom-call(s32[4096]{0:T(1024)S(1)} %bitcast.21, f32[2048,128]{1,0:T(8,128)S(1)} %copy-done), custom_call_target="tpu_custom_call" | custom-call | flops 1 | bytes 1 | tf_op jit(solution)/shard_map/serve/pallas_call | solution.py:366
  34.5 5.0 %all-to-all-start.1 = ((bf16[8,416,128]{2,1,0:T(8,128)(2,1)}), bf16[8,416,128]{2,1,0:T(8,128)(2,1)S(1)}, u32[]{:S(2)}, u32[]{:S(2)}) async-start(bf16[8,416,128]{2,1,0:T(8,128)(2,1)} %bitcast.12), calls=%async_computation.1 | async-start | bytes 1703936 | tf_op jit(solution)/shard_map/all_to_all | solution.py:374
  39.5 0.5 collective-permute-start.11
  40.0 11.5 %collective-permute-done.13.rest_12_ = bf16[3,2,16,3328]{3,2,1,0:T(8,128)(2,1)S(1)} collective-permute-done((bf16[3,2,16,3328]{3,2,1,0:T(8,128)(2,1)}, bf16[3,2,16,3328]{3,2,1,0:T(8,128)(2,1)S(1)}, u32[]{:S(2)}, u32[]{:S(2)}) %collective-permute-start.13) | collective-permute-done | bytes 639008 | tf_op jit(solution)/shard_map/ppermute | solution.py:29
  51.4 1.5 %collective-permute-start.15 = (bf16[3,2,16,3328]{3,2,1,0:T(8,128)(2,1)S(1)}, bf16[3,2,16,3328]{3,2,1,0:T(8,128)(2,1)}, u32[]{:S(2)}, u32[]{:S(2)}) collective-permute-start(bf16[3,2,16,3328]{3,2,1,0:T(8,128)(2,1)S(1)} %collective-permute-done.13.rest_12_), channel_id=1, source_target_pairs={{0,2},{1,3},{2,0},{3,1},{4,6},{5,7},{6,4},{7,5},{8,10},{9,11},{10,... | collective-permute-start | bytes 1916936 | tf_op jit(solution)/shard_map/ppermute | solution.py:29
  52.9 0.5 collective-permute-start.7
  53.5 0.9 collective-permute-done.6.rest_1_
  54.4 0.1 collective-permute-start.14
  54.5 0.8 collective-permute-done.11.rest_10_
  55.3 11.0 %collective-permute-done.15.rest_14_ = bf16[3,2,16,3328]{3,2,1,0:T(8,128)(2,1)} collective-permute-done((bf16[3,2,16,3328]{3,2,1,0:T(8,128)(2,1)S(1)}, bf16[3,2,16,3328]{3,2,1,0:T(8,128)(2,1)}, u32[]{:S(2)}, u32[]{:S(2)}) %collective-permute-start.15) | collective-permute-done | bytes 639008 | tf_op jit(solution)/shard_map/ppermute | solution.py:29
  66.3 0.6 collective-permute-start.8
  66.9 0.1 copy-done.17
  67.0 1.9 %collective-permute-done.8.rest_5_ = bf16[1,2,16,3328]{3,2,1,0:T(8,128)(2,1)S(1)} collective-permute-done((bf16[1,2,16,3328]{3,2,1,0:T(8,128)(2,1)}, bf16[1,2,16,3328]{3,2,1,0:T(8,128)(2,1)S(1)}, u32[]{:S(2)}, u32[]{:S(2)}) %collective-permute-start.8) | collective-permute-done | bytes 213024 | tf_op jit(solution)/shard_map/ppermute | solution.py:29
  68.9 0.1 collective-permute-start.9
  69.0 0.6 reshape.36.bias_ref
  69.6 0.1 copy-done.21
  69.7 0.6 reshape.37.weight_ref
  70.4 0.2 collective-permute-done.9.rest_7_
  70.6 0.6 copy-done.19
  71.3 0.3 copy-done.7
  71.5 10.3 %cross.1 = (bf16[3328,128]{1,0:T(8,128)(2,1)}, f32[1664,128]{1,0:T(8,128)}) custom-call(s32[2048]{0:T(1024)} %bitcast.26, bf16[3328,128]{1,0:T(8,128)(2,1)} %bitcast.28, bf16[1664,128]{1,0:T(8,128)(2,1)} %copy-done.2, s32[1,128]{1,0:T(1,128)} %bitcast.32, f32[1,3328]{1,0:T(1,128)} %reshape.36.bias_ref, f32[1,3328]{1,0:T(1,128)} %reshape.37.weight_ref, ...), custom_call_target="tpu_custom_call" | custom-call | flops 1744830464 | bytes 20000000 | tf_op jit(solution)/shard_map/cross/pallas_call | solution.py:379
  81.9 5.6 %all-to-all-start.2 = ((bf16[8,416,128]{2,1,0:T(8,128)(2,1)}), bf16[8,416,128]{2,1,0:T(8,128)(2,1)S(1)}, u32[]{:S(2)}, u32[]{:S(2)}) async-start(bf16[8,416,128]{2,1,0:T(8,128)(2,1)} %bitcast.29), calls=%async_computation.2 | async-start | bytes 1703936 | tf_op jit(solution)/shard_map/all_to_all | solution.py:405
  87.5 1.2 copy-done.6
  88.7 1.2 hot_sum.1
  90.0 1.5 %collective-permute-done.17 = f32[512,128]{1,0:T(8,128)S(1)} collective-permute-done((f32[512,128]{1,0:T(8,128)S(1)}, f32[512,128]{1,0:T(8,128)S(1)}, u32[]{:S(2)}, u32[]{:S(2)}) %collective-permute-start.17) | collective-permute-done | bytes 262176 | tf_op jit(solution)/shard_map/ppermute | solution.py:29
  91.6 1.6 %collective-permute-start.18 = (f32[256,128]{1,0:T(8,128)S(1)}, f32[256,128]{1,0:T(8,128)S(1)}, u32[]{:S(2)}, u32[]{:S(2)}) collective-permute-start(f32[256,128]{1,0:T(8,128)S(1)} %constant_dynamic-slice_fusion.1), channel_id=1, source_target_pairs={{0,2},{1,3},{2,0},{3,1},{4,6},{5,7},{6,4},{7,5},{8,10},{9,11},{10,... | collective-permute-start | bytes 393224 | tf_op jit(solution)/shard_map/ppermute | solution.py:29
  93.1 4.0 %collective-permute-done.18 = f32[256,128]{1,0:T(8,128)S(1)} collective-permute-done((f32[256,128]{1,0:T(8,128)S(1)}, f32[256,128]{1,0:T(8,128)S(1)}, u32[]{:S(2)}, u32[]{:S(2)}) %collective-permute-start.18) | collective-permute-done | bytes 131104 | tf_op jit(solution)/shard_map/ppermute | solution.py:29
  97.2 2.1 %collective-permute-start.19 = (f32[128,128]{1,0:T(8,128)S(1)}, f32[128,128]{1,0:T(8,128)S(1)}, u32[]{:S(2)}, u32[]{:S(2)}) collective-permute-start(f32[128,128]{1,0:T(8,128)S(1)} %constant_dynamic-slice_fusion), channel_id=1, source_target_pairs={{0,4},{4,0},{8,12},{12,8},{16,20},{20,16},{24,28},{28,24},{1,5},{5... | collective-permute-start | bytes 196616 | tf_op jit(solution)/shard_map/ppermute | solution.py:29
  99.3 2.8 %collective-permute-done.19 = f32[128,128]{1,0:T(8,128)S(1)} collective-permute-done((f32[128,128]{1,0:T(8,128)S(1)}, f32[128,128]{1,0:T(8,128)S(1)}, u32[]{:S(2)}, u32[]{:S(2)}) %collective-permute-start.19) | collective-permute-done | bytes 65568 | tf_op jit(solution)/shard_map/ppermute | solution.py:29
  102.1 2.8 %collective-permute-start.20 = (f32[128,128]{1,0:T(8,128)S(1)}, f32[128,128]{1,0:T(8,128)S(1)}, u32[]{:S(2)}, u32[]{:S(2)}) collective-permute-start(f32[128,128]{1,0:T(8,128)S(1)} %dynamic-slice_add_fusion.3), channel_id=1, source_target_pairs={{0,8},{4,12},{8,0},{12,4},{16,24},{20,28},{24,16},{28,20},{1,9},{5... | collective-permute-start | bytes 196616 | tf_op jit(solution)/shard_map/ppermute | solution.py:29
  104.9 5.6 %collective-permute-done.20 = f32[128,128]{1,0:T(8,128)S(1)} collective-permute-done((f32[128,128]{1,0:T(8,128)S(1)}, f32[128,128]{1,0:T(8,128)S(1)}, u32[]{:S(2)}, u32[]{:S(2)}) %collective-permute-start.20) | collective-permute-done | bytes 65568 | tf_op jit(solution)/shard_map/ppermute | solution.py:29
  110.5 0.6 add.64
  111.1 4.5 %cold_sum.1 = f32[2048,128]{1,0:T(8,128)S(1)} custom-call(s32[32,128]{1,0:T(8,128)S(1)} %bitcast.22, bf16[3328,128]{1,0:T(8,128)(2,1)S(1)} %bitcast.20), custom_call_target="tpu_custom_call" | custom-call | flops 1744830464 | bytes 5000000 | tf_op jit(solution)/shard_map/cold_sum/pallas_call | solution.py:416
  115.7 2.8 %collective-permute-done.25 = f32[2048,128]{1,0:T(8,128)} collective-permute-done((f32[2048,128]{1,0:T(8,128)S(1)}, f32[2048,128]{1,0:T(8,128)}, u32[]{:S(2)}, u32[]{:S(2)}) %collective-permute-start.25) | collective-permute-done | bytes 1048608 | tf_op jit(solution)/shard_map/ppermute | solution.py:29
  118.5 1.1 fusion
  119.6 1.6 %collective-permute-start.26 = (bf16[1024,128]{1,0:T(8,128)(2,1)S(1)}, bf16[1024,128]{1,0:T(8,128)(2,1)S(1)}, u32[]{:S(2)}, u32[]{:S(2)}) collective-permute-start(bf16[1024,128]{1,0:T(8,128)(2,1)S(1)} %fusion), channel_id=1, source_target_pairs={{0,2},{1,3},{2,0},{3,1},{4,6},{5,7},{6,4},{7,5},{8,10},{9,11},{10,... | collective-permute-start | bytes 786440 | tf_op jit(solution)/shard_map/ppermute | solution.py:29
  121.2 5.5 %collective-permute-done.21 = f32[128,128]{1,0:T(8,128)S(1)} collective-permute-done((f32[128,128]{1,0:T(8,128)S(1)}, f32[128,128]{1,0:T(8,128)S(1)}, u32[]{:S(2)}, u32[]{:S(2)}) %collective-permute-start.21) | collective-permute-done | bytes 65568 | tf_op jit(solution)/shard_map/ppermute | solution.py:29
  126.7 0.4 collective-permute-start.22
  127.1 3.9 %collective-permute-done.22 = f32[128,128]{1,0:T(8,128)S(1)} collective-permute-done((f32[128,128]{1,0:T(8,128)S(1)}, f32[128,128]{1,0:T(8,128)S(1)}, u32[]{:S(2)}, u32[]{:S(2)}) %collective-permute-start.22) | collective-permute-done | bytes 65568 | tf_op jit(solution)/shard_map/ppermute | solution.py:29
  131.0 0.6 collective-permute-start.23
  131.7 4.3 %collective-permute-done.23 = f32[256,128]{1,0:T(8,128)S(1)} collective-permute-done((f32[256,128]{1,0:T(8,128)S(1)}, f32[256,128]{1,0:T(8,128)S(1)}, u32[]{:S(2)}, u32[]{:S(2)}) %collective-permute-start.23) | collective-permute-done | bytes 131104 | tf_op jit(solution)/shard_map/ppermute | solution.py:29
  136.2 1.5 %collective-permute-done.24 = f32[512,128]{1,0:T(8,128)S(1)} collective-permute-done((f32[512,128]{1,0:T(8,128)S(1)}, f32[512,128]{1,0:T(8,128)S(1)}, u32[]{:S(2)}, u32[]{:S(2)}) %collective-permute-start.24) | collective-permute-done | bytes 262176 | tf_op jit(solution)/shard_map/ppermute | solution.py:29
  137.7 1.0 multiply_subtract_fusion.1
  138.6 1.3 multiply_subtract_fusion
  (69 shorter events, 0.8 us)
Async XLA Ops:
  0.6 18.0 %copy-start.1 = (f32[1024,128]{1,0:T(8,128)S(1)}, f32[1024,128]{1,0:T(8,128)}, u32[]{:S(2)}) copy-start(f32[1024,128]{1,0:T(8,128)} %table_ref.2) | copy-start | bytes 1572868
  1.7 51.2 %copy-start.8 = (bf16[1,2,16,3328]{3,2,1,0:T(8,128)(2,1)}, bf16[1,2,16,3328]{3,2,1,0:T(8,128)(2,1)S(1)}, u32[]{:S(2)}) copy-start(bf16[1,2,16,3328]{3,2,1,0:T(8,128)(2,1)S(1)} %maximum_bitcast_fusion.rest_0_) | copy-start | bytes 638980
  1.7 20.0 %collective-permute-start = (bf16[1,2,16,3328]{3,2,1,0:T(8,128)(2,1)S(1)}, bf16[1,2,16,3328]{3,2,1,0:T(8,128)(2,1)S(1)}, u32[]{:S(2)}, u32[]{:S(2)}) collective-permute-start(bf16[1,2,16,3328]{3,2,1,0:T(8,128)(2,1)S(1)} %maximum_bitcast_fusion.rest_0_), channel_id=1, source_target_pairs={{0,8},{4,12},{8,16},{12,20},{16,24},{20,28},{24,0},{28,4},{1,9},{5... | collective-permute-start | bytes 638984 | tf_op jit(solution)/shard_map/ppermute | solution.py:34
  4.8 18.8 %collective-permute-start.1 = (bf16[1,2,16,3328]{3,2,1,0:T(8,128)(2,1)S(1)}, bf16[1,2,16,3328]{3,2,1,0:T(8,128)(2,1)S(1)}, u32[]{:S(2)}, u32[]{:S(2)}) collective-permute-start(bf16[1,2,16,3328]{3,2,1,0:T(8,128)(2,1)S(1)} %maximum_bitcast_fusion.rest_0_), channel_id=1, source_target_pairs={{0,16},{4,20},{8,24},{12,28},{16,0},{20,4},{24,8},{28,12},{1,17},{... | collective-permute-start | bytes 638984 | tf_op jit(solution)/shard_map/ppermute | solution.py:34
  7.3 16.2 %collective-permute-start.2 = (bf16[1,2,16,3328]{3,2,1,0:T(8,128)(2,1)S(1)}, bf16[1,2,16,3328]{3,2,1,0:T(8,128)(2,1)S(1)}, u32[]{:S(2)}, u32[]{:S(2)}) collective-permute-start(bf16[1,2,16,3328]{3,2,1,0:T(8,128)(2,1)S(1)} %maximum_bitcast_fusion.rest_0_), channel_id=1, source_target_pairs={{0,24},{4,28},{8,0},{12,4},{16,8},{20,12},{24,16},{28,20},{1,25},{... | collective-permute-start | bytes 638984 | tf_op jit(solution)/shard_map/ppermute | solution.py:34
  8.7 18.4 %collective-permute-start.3 = (bf16[1,2,16,3328]{3,2,1,0:T(8,128)(2,1)S(1)}, bf16[1,2,16,3328]{3,2,1,0:T(8,128)(2,1)S(1)}, u32[]{:S(2)}, u32[]{:S(2)}) collective-permute-start(bf16[1,2,16,3328]{3,2,1,0:T(8,128)(2,1)S(1)} %maximum_bitcast_fusion.rest_0_), channel_id=1, source_target_pairs={{0,2},{1,3},{2,0},{3,1},{4,6},{5,7},{6,4},{7,5},{8,10},{9,11},{10,... | collective-permute-start | bytes 638984 | tf_op jit(solution)/shard_map/ppermute | solution.py:29
  10.2 16.9 %collective-permute-start.4 = (bf16[1,2,16,3328]{3,2,1,0:T(8,128)(2,1)S(1)}, bf16[1,2,16,3328]{3,2,1,0:T(8,128)(2,1)S(1)}, u32[]{:S(2)}, u32[]{:S(2)}) collective-permute-start(bf16[1,2,16,3328]{3,2,1,0:T(8,128)(2,1)S(1)} %maximum_bitcast_fusion.rest_0_), channel_id=1, source_target_pairs={{0,4},{4,0},{8,12},{12,8},{16,20},{20,16},{24,28},{28,24},{1,5},{5... | collective-permute-start | bytes 638984 | tf_op jit(solution)/shard_map/ppermute | solution.py:29
  12.6 0.7 copy-start.5
  14.5 0.6 copy-start.4
  15.1 3.5 %copy-start.3 = (s32[128,13]{0,1:T(8,128)S(1)}, s32[128,13]{0,1:T(8,128)}, u32[]{:S(2)}) copy-start(s32[128,13]{0,1:T(8,128)} %param.12) | copy-start | bytes 19972
  15.1 11.9 %all-to-all-start = ((s32[8,4,128]{2,1,0:T(4,128)}), s32[8,4,128]{2,1,0:T(4,128)S(1)}, u32[]{:S(2)}, u32[]{:S(2)}) async-start(s32[8,4,128]{2,1,0:T(4,128)} %bitcast.3), calls=%async_computation | async-start | bytes 32768 | tf_op jit(solution)/shard_map/all_to_all | solution.py:353
  18.6 12.4 %copy-start = (f32[2048,128]{1,0:T(8,128)S(1)}, f32[2048,128]{1,0:T(8,128)}, u32[]{:S(2)}) copy-start(f32[2048,128]{1,0:T(8,128)} %table_ref.3) | copy-start | bytes 3145732
  20.9 0.8 copy-start.2
  21.6 6.8 %collective-permute-start.5 = (bf16[1,2,16,3328]{3,2,1,0:T(8,128)(2,1)S(1)}, bf16[1,2,16,3328]{3,2,1,0:T(8,128)(2,1)S(1)}, u32[]{:S(2)}, u32[]{:S(2)}) collective-permute-start(bf16[1,2,16,3328]{3,2,1,0:T(8,128)(2,1)S(1)} %maximum_bitcast_fusion.rest_0_), channel_id=1, source_target_pairs={{0,6},{1,7},{2,4},{3,5},{4,2},{5,3},{6,0},{7,1},{8,14},{9,15},{10,... | collective-permute-start | bytes 638984 | tf_op jit(solution)/shard_map/ppermute | solution.py:46
  27.0 25.9 %copy-start.13 = (bf16[1,2,16,3328]{3,2,1,0:T(8,128)(2,1)}, bf16[1,2,16,3328]{3,2,1,0:T(8,128)(2,1)S(1)}, u32[]{:S(2)}) copy-start(bf16[1,2,16,3328]{3,2,1,0:T(8,128)(2,1)S(1)} %collective-permute-done.3.rest_2_) | copy-start | bytes 638980
  27.1 1.4 copy-start.14
  28.4 0.7 copy-start.15
  29.1 22.3 %collective-permute-start.13 = (bf16[3,2,16,3328]{3,2,1,0:T(8,128)(2,1)}, bf16[3,2,16,3328]{3,2,1,0:T(8,128)(2,1)S(1)}, u32[]{:S(2)}, u32[]{:S(2)}) collective-permute-start(bf16[3,2,16,3328]{3,2,1,0:T(8,128)(2,1)} %pad_maximum_fusion.rest_8_), channel_id=1, source_target_pairs={{0,4},{4,0},{8,12},{12,8},{16,20},{20,16},{24,28},{28,24},{1,5},{5... | collective-permute-start | bytes 1916936 | tf_op jit(solution)/shard_map/ppermute | solution.py:29
  34.5 36.1 %all-to-all-start.1 = ((bf16[8,416,128]{2,1,0:T(8,128)(2,1)}), bf16[8,416,128]{2,1,0:T(8,128)(2,1)S(1)}, u32[]{:S(2)}, u32[]{:S(2)}) async-start(bf16[8,416,128]{2,1,0:T(8,128)(2,1)} %bitcast.12), calls=%async_computation.1 | async-start | bytes 1703936 | tf_op jit(solution)/shard_map/all_to_all | solution.py:374
  39.4 29.6 %copy-start.20 = (f32[3328]{0:T(1024)S(1)}, f32[3328]{0:T(1024)}, u32[]{:S(2)}) copy-start(f32[3328]{0:T(1024)} %param.22) | copy-start | bytes 39940
  39.5 15.9 %collective-permute-start.11 = (bf16[3,2,16,3328]{3,2,1,0:T(8,128)(2,1)}, bf16[3,2,16,3328]{3,2,1,0:T(8,128)(2,1)}, u32[]{:S(2)}, u32[]{:S(2)}) collective-permute-start(bf16[3,2,16,3328]{3,2,1,0:T(8,128)(2,1)} %pad_maximum_fusion.rest_8_), channel_id=1, source_target_pairs={{0,2},{1,3},{2,0},{3,1},{4,6},{5,7},{6,4},{7,5},{8,10},{9,11},{10,... | collective-permute-start | bytes 1916936 | tf_op jit(solution)/shard_map/ppermute | solution.py:29
  51.4 19.2 %copy-start.9 = (bf16[3,2,16,3328]{3,2,1,0:T(8,128)(2,1)}, bf16[3,2,16,3328]{3,2,1,0:T(8,128)(2,1)S(1)}, u32[]{:S(2)}) copy-start(bf16[3,2,16,3328]{3,2,1,0:T(8,128)(2,1)S(1)} %collective-permute-done.13.rest_12_) | copy-start | bytes 1916932
  51.4 14.9 %collective-permute-start.15 = (bf16[3,2,16,3328]{3,2,1,0:T(8,128)(2,1)S(1)}, bf16[3,2,16,3328]{3,2,1,0:T(8,128)(2,1)}, u32[]{:S(2)}, u32[]{:S(2)}) collective-permute-start(bf16[3,2,16,3328]{3,2,1,0:T(8,128)(2,1)S(1)} %collective-permute-done.13.rest_12_), channel_id=1, source_target_pairs={{0,2},{1,3},{2,0},{3,1},{4,6},{5,7},{6,4},{7,5},{8,10},{9,11},{10,... | collective-permute-start | bytes 1916936 | tf_op jit(solution)/shard_map/ppermute | solution.py:29
  52.9 1.5 %collective-permute-start.6 = (bf16[1,2,16,3328]{3,2,1,0:T(8,128)(2,1)S(1)}, bf16[1,2,16,3328]{3,2,1,0:T(8,128)(2,1)S(1)}, u32[]{:S(2)}, u32[]{:S(2)}) collective-permute-start(bf16[1,2,16,3328]{3,2,1,0:T(8,128)(2,1)S(1)} %maximum_bitcast_fusion.rest_0_), channel_id=1, source_target_pairs={{0,1},{1,0},{2,3},{3,2},{4,5},{5,4},{6,7},{7,6},{8,9},{9,8},{10,11... | collective-permute-start | bytes 638984 | tf_op jit(solution)/shard_map/ppermute | solution.py:29
  52.9 13.4 %collective-permute-start.7 = (bf16[1,2,16,3328]{3,2,1,0:T(8,128)(2,1)S(1)}, bf16[1,2,16,3328]{3,2,1,0:T(8,128)(2,1)S(1)}, u32[]{:S(2)}, u32[]{:S(2)}) collective-permute-start(bf16[1,2,16,3328]{3,2,1,0:T(8,128)(2,1)S(1)} %collective-permute-done.3.rest_2_), channel_id=1, source_target_pairs={{0,1},{1,0},{2,3},{3,2},{4,5},{5,4},{6,7},{7,6},{8,9},{9,8},{10,11... | collective-permute-start | bytes 638984 | tf_op jit(solution)/shard_map/ppermute | solution.py:29
  53.4 17.2 %collective-permute-start.10 = (bf16[3,2,16,3328]{3,2,1,0:T(8,128)(2,1)}, bf16[3,2,16,3328]{3,2,1,0:T(8,128)(2,1)}, u32[]{:S(2)}, u32[]{:S(2)}) collective-permute-start(bf16[3,2,16,3328]{3,2,1,0:T(8,128)(2,1)} %pad_maximum_fusion.rest_8_), channel_id=1, source_target_pairs={{0,1},{1,0},{2,3},{3,2},{4,5},{5,4},{6,7},{7,6},{8,9},{9,8},{10,11... | collective-permute-start | bytes 1916936 | tf_op jit(solution)/shard_map/ppermute | solution.py:29
  54.4 11.9 %copy-start.16 = (bf16[1,2,16,3328]{3,2,1,0:T(8,128)(2,1)}, bf16[1,2,16,3328]{3,2,1,0:T(8,128)(2,1)S(1)}, u32[]{:S(2)}) copy-start(bf16[1,2,16,3328]{3,2,1,0:T(8,128)(2,1)S(1)} %collective-permute-done.6.rest_1_) | copy-start | bytes 638980
  54.4 16.2 %collective-permute-start.14 = (bf16[3,2,16,3328]{3,2,1,0:T(8,128)(2,1)S(1)}, bf16[3,2,16,3328]{3,2,1,0:T(8,128)(2,1)}, u32[]{:S(2)}, u32[]{:S(2)}) collective-permute-start(bf16[3,2,16,3328]{3,2,1,0:T(8,128)(2,1)S(1)} %collective-permute-done.13.rest_12_), channel_id=1, source_target_pairs={{0,1},{1,0},{2,3},{3,2},{4,5},{5,4},{6,7},{7,6},{8,9},{9,8},{10,11... | collective-permute-start | bytes 1916936 | tf_op jit(solution)/shard_map/ppermute | solution.py:29
  55.3 15.3 %collective-permute-start.12 = (bf16[3,2,16,3328]{3,2,1,0:T(8,128)(2,1)}, bf16[3,2,16,3328]{3,2,1,0:T(8,128)(2,1)}, u32[]{:S(2)}, u32[]{:S(2)}) collective-permute-start(bf16[3,2,16,3328]{3,2,1,0:T(8,128)(2,1)} %collective-permute-done.11.rest_10_), channel_id=1, source_target_pairs={{0,1},{1,0},{2,3},{3,2},{4,5},{5,4},{6,7},{7,6},{8,9},{9,8},{10,11... | collective-permute-start | bytes 1916936 | tf_op jit(solution)/shard_map/ppermute | solution.py:29
  66.3 4.3 %collective-permute-start.16 = (bf16[3,2,16,3328]{3,2,1,0:T(8,128)(2,1)}, bf16[3,2,16,3328]{3,2,1,0:T(8,128)(2,1)}, u32[]{:S(2)}, u32[]{:S(2)}) collective-permute-start(bf16[3,2,16,3328]{3,2,1,0:T(8,128)(2,1)} %collective-permute-done.15.rest_14_), channel_id=1, source_target_pairs={{0,1},{1,0},{2,3},{3,2},{4,5},{5,4},{6,7},{7,6},{8,9},{9,8},{10,11... | collective-permute-start | bytes 1916936 | tf_op jit(solution)/shard_map/ppermute | solution.py:29
  66.3 0.7 copy-start.17
  66.3 2.6 %collective-permute-start.8 = (bf16[1,2,16,3328]{3,2,1,0:T(8,128)(2,1)}, bf16[1,2,16,3328]{3,2,1,0:T(8,128)(2,1)S(1)}, u32[]{:S(2)}, u32[]{:S(2)}) collective-permute-start(bf16[1,2,16,3328]{3,2,1,0:T(8,128)(2,1)} %copy-done.14), channel_id=1, source_target_pairs={{0,1},{1,0},{2,3},{3,2},{4,5},{5,4},{6,7},{7,6},{8,9},{9,8},{10,11... | collective-permute-start | bytes 638984 | tf_op jit(solution)/shard_map/ppermute | solution.py:29
  68.9 1.7 %copy-start.18 = (bf16[1,2,16,3328]{3,2,1,0:T(8,128)(2,1)}, bf16[1,2,16,3328]{3,2,1,0:T(8,128)(2,1)S(1)}, u32[]{:S(2)}) copy-start(bf16[1,2,16,3328]{3,2,1,0:T(8,128)(2,1)S(1)} %collective-permute-done.8.rest_5_) | copy-start | bytes 638980
  68.9 1.7 %collective-permute-start.9 = (bf16[1,2,16,3328]{3,2,1,0:T(8,128)(2,1)}, bf16[1,2,16,3328]{3,2,1,0:T(8,128)(2,1)S(1)}, u32[]{:S(2)}, u32[]{:S(2)}) collective-permute-start(bf16[1,2,16,3328]{3,2,1,0:T(8,128)(2,1)} %copy-done.15), channel_id=1, source_target_pairs={{0,1},{1,0},{2,3},{3,2},{4,5},{5,4},{6,7},{7,6},{8,9},{9,8},{10,11... | collective-permute-start | bytes 638984 | tf_op jit(solution)/shard_map/ppermute | solution.py:29
  69.0 0.7 copy-start.21
  70.6 0.7 copy-start.19
  70.6 0.9 copy-start.7
  81.9 29.3 %all-to-all-start.2 = ((bf16[8,416,128]{2,1,0:T(8,128)(2,1)}), bf16[8,416,128]{2,1,0:T(8,128)(2,1)S(1)}, u32[]{:S(2)}, u32[]{:S(2)}) async-start(bf16[8,416,128]{2,1,0:T(8,128)(2,1)} %bitcast.29), calls=%async_computation.2 | async-start | bytes 1703936 | tf_op jit(solution)/shard_map/all_to_all | solution.py:405
  87.5 1.2 copy-start.6
  89.9 1.6 %collective-permute-start.17 = (f32[512,128]{1,0:T(8,128)S(1)}, f32[512,128]{1,0:T(8,128)S(1)}, u32[]{:S(2)}, u32[]{:S(2)}) collective-permute-start(f32[512,128]{1,0:T(8,128)S(1)} %constant_dynamic-slice_fusion.2), channel_id=1, source_target_pairs={{0,1},{1,0},{2,3},{3,2},{4,5},{5,4},{6,7},{7,6},{8,9},{9,8},{10,11... | collective-permute-start | bytes 786440 | tf_op jit(solution)/shard_map/ppermute | solution.py:29
  91.6 5.6 %collective-permute-start.18 = (f32[256,128]{1,0:T(8,128)S(1)}, f32[256,128]{1,0:T(8,128)S(1)}, u32[]{:S(2)}, u32[]{:S(2)}) collective-permute-start(f32[256,128]{1,0:T(8,128)S(1)} %constant_dynamic-slice_fusion.1), channel_id=1, source_target_pairs={{0,2},{1,3},{2,0},{3,1},{4,6},{5,7},{6,4},{7,5},{8,10},{9,11},{10,... | collective-permute-start | bytes 393224 | tf_op jit(solution)/shard_map/ppermute | solution.py:29
  97.2 4.9 %collective-permute-start.19 = (f32[128,128]{1,0:T(8,128)S(1)}, f32[128,128]{1,0:T(8,128)S(1)}, u32[]{:S(2)}, u32[]{:S(2)}) collective-permute-start(f32[128,128]{1,0:T(8,128)S(1)} %constant_dynamic-slice_fusion), channel_id=1, source_target_pairs={{0,4},{4,0},{8,12},{12,8},{16,20},{20,16},{24,28},{28,24},{1,5},{5... | collective-permute-start | bytes 196616 | tf_op jit(solution)/shard_map/ppermute | solution.py:29
  102.1 8.4 %collective-permute-start.20 = (f32[128,128]{1,0:T(8,128)S(1)}, f32[128,128]{1,0:T(8,128)S(1)}, u32[]{:S(2)}, u32[]{:S(2)}) collective-permute-start(f32[128,128]{1,0:T(8,128)S(1)} %dynamic-slice_add_fusion.3), channel_id=1, source_target_pairs={{0,8},{4,12},{8,0},{12,4},{16,24},{20,28},{24,16},{28,20},{1,9},{5... | collective-permute-start | bytes 196616 | tf_op jit(solution)/shard_map/ppermute | solution.py:29
  115.6 2.9 %collective-permute-start.25 = (f32[2048,128]{1,0:T(8,128)S(1)}, f32[2048,128]{1,0:T(8,128)}, u32[]{:S(2)}, u32[]{:S(2)}) collective-permute-start(f32[2048,128]{1,0:T(8,128)S(1)} %cold_sum.1), channel_id=1, source_target_pairs={{0,1},{1,0},{2,3},{3,2},{4,5},{5,4},{6,7},{7,6},{8,9},{9,8},{10,11... | collective-permute-start | bytes 3145736 | tf_op jit(solution)/shard_map/ppermute | solution.py:29
  115.7 5.5 %copy-start.11 = (f32[128,128]{1,0:T(8,128)S(1)}, f32[128,128]{1,0:T(8,128)}, u32[]{:S(2)}) copy-start(f32[128,128]{1,0:T(8,128)} %add.64) | copy-start | bytes 196612
  119.6 12.0 %collective-permute-start.26 = (bf16[1024,128]{1,0:T(8,128)(2,1)S(1)}, bf16[1024,128]{1,0:T(8,128)(2,1)S(1)}, u32[]{:S(2)}, u32[]{:S(2)}) collective-permute-start(bf16[1024,128]{1,0:T(8,128)(2,1)S(1)} %fusion), channel_id=1, source_target_pairs={{0,2},{1,3},{2,0},{3,1},{4,6},{5,7},{6,4},{7,5},{8,10},{9,11},{10,... | collective-permute-start | bytes 786440 | tf_op jit(solution)/shard_map/ppermute | solution.py:29
  121.2 5.5 %collective-permute-start.21 = (f32[128,128]{1,0:T(8,128)S(1)}, f32[128,128]{1,0:T(8,128)S(1)}, u32[]{:S(2)}, u32[]{:S(2)}) collective-permute-start(f32[128,128]{1,0:T(8,128)S(1)} %copy-done.11), channel_id=1, source_target_pairs={{0,16},{4,20},{8,24},{12,28},{16,0},{20,4},{24,8},{28,12},{1,17},{... | collective-permute-start | bytes 196616 | tf_op jit(solution)/shard_map/ppermute | solution.py:29
  126.7 4.3 %collective-permute-start.22 = (f32[128,128]{1,0:T(8,128)S(1)}, f32[128,128]{1,0:T(8,128)S(1)}, u32[]{:S(2)}, u32[]{:S(2)}) collective-permute-start(f32[128,128]{1,0:T(8,128)S(1)} %add.65), channel_id=1, source_target_pairs={{0,4},{4,0},{8,12},{12,8},{16,20},{20,16},{24,28},{28,24},{1,5},{5... | collective-permute-start | bytes 196616 | tf_op jit(solution)/shard_map/ppermute | solution.py:29
  131.0 5.0 %collective-permute-start.23 = (f32[256,128]{1,0:T(8,128)S(1)}, f32[256,128]{1,0:T(8,128)S(1)}, u32[]{:S(2)}, u32[]{:S(2)}) collective-permute-start(f32[256,128]{1,0:T(8,128)S(1)} %maximum_select_fusion.3), channel_id=1, source_target_pairs={{0,2},{1,3},{2,0},{3,1},{4,6},{5,7},{6,4},{7,5},{8,10},{9,11},{10,... | collective-permute-start | bytes 393224 | tf_op jit(solution)/shard_map/ppermute | solution.py:29
  131.7 6.0 %copy-start.12 = (bf16[1024,128]{1,0:T(8,128)(2,1)S(1)}, bf16[1024,128]{1,0:T(8,128)(2,1)}, u32[]{:S(2)}) copy-start(bf16[1024,128]{1,0:T(8,128)(2,1)} %param.17) | copy-start | bytes 786436
  131.7 7.0 %collective-permute-start.27 = (f32[1024,128]{1,0:T(8,128)S(1)}, f32[1024,128]{1,0:T(8,128)S(1)}, u32[]{:S(2)}, u32[]{:S(2)}) collective-permute-start(f32[1024,128]{1,0:T(8,128)S(1)} %convert_add_fusion), channel_id=1, source_target_pairs={{0,1},{1,0},{2,3},{3,2},{4,5},{5,4},{6,7},{7,6},{8,9},{9,8},{10,11... | collective-permute-start | bytes 1572872 | tf_op jit(solution)/shard_map/ppermute | solution.py:29
  136.1 1.6 %collective-permute-start.24 = (f32[512,128]{1,0:T(8,128)S(1)}, f32[512,128]{1,0:T(8,128)S(1)}, u32[]{:S(2)}, u32[]{:S(2)}) collective-permute-start(f32[512,128]{1,0:T(8,128)S(1)} %maximum_select_fusion.2), channel_id=1, source_target_pairs={{0,1},{1,0},{2,3},{3,2},{4,5},{5,4},{6,7},{7,6},{8,9},{9,8},{10,11... | collective-permute-start | bytes 786440 | tf_op jit(solution)/shard_map/ppermute | solution.py:29
  136.2 2.5 %copy-start.10 = (bf16[2048,128]{1,0:T(8,128)(2,1)S(1)}, bf16[2048,128]{1,0:T(8,128)(2,1)}, u32[]{:S(2)}) copy-start(bf16[2048,128]{1,0:T(8,128)(2,1)} %param.19) | copy-start | bytes 1572868

commit v5 on v4

--- a/solution.py
+++ b/solution.py
@@ -21,7 +21,7 @@
 
 
 def is_small(n_data, n_reps):
-    return n_reps == 4 and n_data in (4, 8, 16)
+    return n_reps == 4 and n_data == 8
 
 
 def swap(value, axis, distance):
@@ -47,19 +47,18 @@
 
 
 def weight_starts(down_t, up):
-    own = jnp.stack([down_t, up])[None]
-    z = [shift(own, "dp", 2 * k) for k in range(1, lax.axis_size("dp") // 2)]
-    return [own, swap(own, "rep", 2), swap(own, "dp", 1), swap_both(own)], jnp.concatenate(z, axis=0)
+    own = jnp.stack([down_t, up])[:, None]
+    z = [swap(own, "dp", 2 * k) for k in range(1, lax.axis_size("dp") // 2)]
+    over_x, over_y = swap(own, "rep", 2), swap(own, "dp", 1)
+    return [own, over_x, over_y, swap_both(own)], z
 
 
 def weight_pieces(plane, z):
-    over_x = swap(z, "rep", 2)
-    over_y = swap(z, "dp", 1)
-    across = swap(over_y, "rep", 2)
-    pieces = []
-    for piece in (*plane, z, over_x, over_y, across):
-        pieces += [piece, swap(piece, "rep", 1)]
-    return pieces
+    over_x, over_y = swap(z, "rep", 2), swap(z, "dp", 1)
+    across = swap(over_y[0], "rep", 2), swap(over_x[1], "dp", 1)
+    whole = [*plane, z, over_x, over_y]
+    whole += [swap(piece, "rep", 1) for piece in whole]
+    return whole, [(piece, swap(piece, "rep", 1)) for piece in across]
 
 
 def half_of(value, index, count):
@@ -80,27 +79,9 @@
     total = partial
     for axis, distance, index in (("rep", 1, rep % 2), ("rep", 2, rep // 2), ("dp", 1, data % 2)):
         total = half_of(total, index, 2) + swap(half_of(total, 1 - index, 2), axis, distance)
-    return total + swap(total, "dp", 2)
-
-
-def hot_late(total):
-    rep, data = lax.axis_index("rep"), lax.axis_index("dp")
-    distance = 4
-    while distance < lax.axis_size("dp"):
+    for distance in (2, 4):
         total = total + swap(total, "dp", distance)
-        distance *= 2
-    for axis, distance, index in (("dp", 1, data % 2), ("rep", 2, rep // 2), ("rep", 1, rep % 2)):
-        total = paired(total, swap(total, axis, distance), index)
     return total
-
-
-def sum_cold(partial):
-    rep = lax.axis_index("rep")
-    core = rep % 2
-    chip = partial + swap(partial, "rep", 1)
-    mine = half_of(chip, core, 2).astype(jnp.bfloat16)
-    mine = mine.astype(jnp.float32) + swap(mine, "rep", 2).astype(jnp.float32)
-    return paired(mine, swap(mine, "rep", 1), core)
 
 
 LANES = 128
@@ -214,18 +195,6 @@
     lax.fori_loop(0, into.shape[0] // GROUP, group, 0)
 
 
-def put(index_ref, source, into):
-    def group(g, carry):
-        start = pl.multiple_of(g * GROUP, GROUP)
-        rows = [index_ref[start + k] for k in range(GROUP)]
-        taken = [source[pl.ds(start + k, 1), :] for k in range(GROUP)]
-        for k in range(GROUP):
-            into[pl.ds(rows[k], 1), :] = taken[k]
-        return carry
-
-    lax.fori_loop(0, source.shape[0] // GROUP, group, 0)
-
-
 def hot_rows_body(id_ref, table_ref, out_ref, found):
     pick(id_ref, table_ref, found)
     out_ref[...] = found[...].astype(BF)
@@ -233,6 +202,7 @@
 
 def cross_body(
     place_ref,
+    id_ref,
     back_ref,
     hot_ref,
     label_ref,
@@ -240,22 +210,31 @@
     weight_ref,
     *rest,
 ):
-    n_pieces = len(rest) - 10
+    n_pieces = len(rest) - 12
     pieces = rest[:n_pieces]
-    send_ref, hot_grad_ref, downs, ups, back, cold, upper, x_all, du_all, sem = rest[n_pieces:]
+    send_ref, hot_sum_ref, downs, ups, back, cold, upper, x_all, du_all, hits, hot_grad, sem = rest[
+        n_pieces:
+    ]
     copies = []
+    whole = [piece for piece in pieces if len(piece.shape) == 4]
+    parts = [piece for piece in pieces if len(piece.shape) == 3]
+    n_parts = len(parts) // 2
     for part, target in ((0, downs), (1, ups)):
+        sources = [piece.at[part] for piece in whole]
+        sources += parts[part * n_parts : (part + 1) * n_parts]
         first = 0
-        for i, piece in enumerate(pieces):
-            count = piece.shape[0]
-            copy = pltpu.make_async_copy(
-                piece.at[:, part], target.at[pl.ds(first, count)], sem.at[part, i]
-            )
+        for i, source in enumerate(sources):
+            count = source.shape[0]
+            copy = pltpu.make_async_copy(source, target.at[pl.ds(first, count)], sem.at[part, i])
             copy.start()
             copies.append(copy)
             first += count
+    n_copies = len(copies) // 2
     down = downs.reshape(downs.shape[0] * downs.shape[1], F)
     up = ups.reshape(ups.shape[0] * ups.shape[1], F)
+    names = lax.broadcasted_iota(jnp.int32, (HOT, LANES), 0)
+    for s in range(NH):
+        hits[:, s * LANES : (s + 1) * LANES] = (names == id_ref[s : s + 1, :]).astype(F32).astype(BF)
     back[...] = back_ref[...].astype(F32)
     pick(place_ref, back, cold)
     rows = LANES
@@ -263,57 +242,50 @@
         x_all[:, s * E : (s + 1) * E] = hot_ref[s * rows : (s + 1) * rows, :]
     for s in range(NC):
         x_all[:, (NH + s) * E : (NH + s + 1) * E] = cold[s * rows : (s + 1) * rows, :].astype(BF)
-    for copy in copies[:n_pieces]:
+    for copy in copies[:n_copies]:
         copy.wait()
     hidden = lax.dot_general(x_all[...], down[...], NT, preferred_element_type=F32).astype(BF)
-    for copy in copies[n_pieces:]:
+    for copy in copies[n_copies:]:
         copy.wait()
     wide = 2 * E
     chunks = [pl.ds(c * wide, wide) for c in range(F // wide)]
     logit = jnp.zeros((rows, wide), F32)
     for c in chunks:
-        u = jnp.dot(hidden, up[:, c], preferred_element_type=F32) + bias_ref[:, c]
+        u = jnp.dot(hidden, up[:, c], preferred_element_type=F32) + bias_ref[c][None, :]
         upper[:, c] = u
         x = x_all[:, c].astype(F32)
-        logit = logit + (x * u + x) * weight_ref[:, c]
+        logit = logit + (x * u + x) * weight_ref[c][None, :]
     logit = jnp.sum(logit, axis=1, keepdims=True)
     at = lax.broadcasted_iota(jnp.int32, (rows, rows), 0)
     to = lax.broadcasted_iota(jnp.int32, (rows, rows), 1)
     label = jnp.sum(jnp.where(at == to, label_ref[...].astype(F32), 0.0), axis=1, keepdims=True)
     delta = 1.0 / (1.0 + jnp.exp(-logit)) - label
     for c in chunks:
-        du_all[:, c] = (delta * weight_ref[:, c] * x_all[:, c].astype(F32)).astype(BF)
+        du_all[:, c] = (delta * weight_ref[c][None, :] * x_all[:, c].astype(F32)).astype(BF)
     dh = lax.dot_general(du_all[...], up[...], NT, preferred_element_type=F32).astype(BF)
     back[...] = jnp.zeros_like(back)
     for i, c in enumerate(chunks):
-        grad = delta * weight_ref[:, c] * (upper[:, c] + 1.0) + jnp.dot(
+        grad = delta * weight_ref[c][None, :] * (upper[:, c] + 1.0) + jnp.dot(
             dh, down[:, c], preferred_element_type=F32
         )
         for j in range(2):
             s = 2 * i + j
             piece = grad[:, j * E : (j + 1) * E]
             if s < NH:
-                hot_grad_ref[s * rows : (s + 1) * rows, :] = piece
+                first = piece.astype(BF)
+                hot_grad[s * rows : (s + 1) * rows, :E] = first
+                hot_grad[s * rows : (s + 1) * rows, E:] = (piece - first.astype(F32)).astype(BF)
             else:
-                cold[(s - NH) * rows : (s - NH + 1) * rows, :] = piece
-    put(place_ref, cold, back)
+                start = (s - NH) * rows
+                cold[start : start + rows, :] = piece
+                for k in range(start, start + rows):
+                    back[pl.ds(place_ref[k], 1), :] = cold[pl.ds(k, 1), :]
     send_ref[...] = back[...].astype(BF)
-
-
-def hot_sum_body(id_ref, grad_ref, out_ref, hits):
-    names = lax.broadcasted_iota(jnp.int32, (HOT, LANES), 0)
-    for s in range(NH):
-        hits[:, s * LANES : (s + 1) * LANES] = (names == id_ref[s : s + 1, :]).astype(F32).astype(BF)
-    grad = grad_ref[...]
-    first = grad.astype(BF)
-    rest = (grad - first.astype(F32)).astype(BF)
-    both = jnp.dot(
-        hits[...], jnp.concatenate([first, rest], axis=1), preferred_element_type=F32
-    )
-    out_ref[...] = both[:, :E] + both[:, E:]
-
-
-def cold_sum_body(n_data, capacity, ask_ref, grad_ref, out_ref, hits):
+    both = jnp.dot(hits[...], hot_grad[...], preferred_element_type=F32)
+    hot_sum_ref[...] = both[:, :E] + both[:, E:]
+
+
+def cold_sum_body(n_data, capacity, first_ref, ask_ref, grad_ref, out_ref, hits):
     owned = out_ref.shape[0]
     blocks = ask_ref.shape[0] // n_data
     lines = []
@@ -322,7 +294,7 @@
             wide = min(LANES, capacity - b * LANES)
             lines.append(ask_ref[d * blocks + b : d * blocks + b + 1, :wide])
     ids = jnp.concatenate(lines, axis=1)
-    names = lax.broadcasted_iota(jnp.int32, (owned, LANES), 0)
+    names = lax.broadcasted_iota(jnp.int32, (owned, LANES), 0) + first_ref[0]
     for start in range(0, n_data * capacity, LANES):
         hits[:, start : start + LANES] = (
             (names == ids[:, start : start + LANES]).astype(F32).astype(BF)
@@ -351,7 +323,6 @@
         "route",
     )(owner_t, cold_rows.T)
     asked = lax.all_to_all(ask, "dp", split_axis=0, concat_axis=0, tiled=True)
-    plane, z = weight_starts(cross_down.T, cross_up)
     hot_t = hot_ids.T
     place = place.reshape(-1)
     hot_rows = call(
@@ -362,7 +333,9 @@
         (1, 1),
         "hot_rows",
     )(hot_t.reshape(-1), hot_table)
-    asked, hot_rows, z, *plane = lax.optimization_barrier((asked, hot_rows, z, *plane))
+    plane, z = weight_starts(cross_down.T, cross_up)
+    asked = after(asked, hot_rows, *plane)
+    z = jnp.concatenate(lax.optimization_barrier((*z, asked))[:-1], axis=1)
     found = call(
         functools.partial(serve_body, n_data, capacity),
         shape((places, E), BF),
@@ -372,14 +345,15 @@
         "serve",
     )(asked.reshape(-1), cold_table)
     returned = lax.all_to_all(found, "dp", split_axis=0, concat_axis=0, tiled=True)
-    pieces = weight_pieces(plane, z)
-    n_shards = sum(p.shape[0] for p in pieces)
+    whole, (down_rest, up_rest) = weight_pieces(plane, z)
+    pieces = [*whole, *down_rest, *up_rest]
+    n_shards = sum(p.shape[-3] for p in (*whole, *down_rest))
     depth = cross_up.shape[0]
     rank = n_shards * depth
-    send, hot_grad = call(
+    send, hot_partial = call(
         cross_body,
-        (shape((places, E), BF), shape((NH * rows, E), F32)),
-        [SMEM] + [VMEM] * 5 + [ANY] * len(pieces),
+        (shape((places, E), BF), shape((HOT, E), F32)),
+        [SMEM] + [VMEM] * 6 + [ANY] * len(pieces),
         [
             pltpu.VMEM((n_shards, depth, F), BF),
             pltpu.VMEM((n_shards, depth, F), BF),
@@ -388,40 +362,47 @@
             pltpu.VMEM((rows, F), F32),
             pltpu.VMEM((rows, F), BF),
             pltpu.VMEM((rows, F), BF),
-            pltpu.SemaphoreType.DMA((2, len(pieces))),
+            pltpu.VMEM((HOT, NH * rows), BF),
+            pltpu.VMEM((NH * rows, 2 * E), BF),
+            pltpu.SemaphoreType.DMA((2, len(whole) + len(down_rest))),
         ],
         (8 * rows * F * rank, 20 * 10**6),
         "cross",
         58,
     )(
         place,
+        hot_t,
         returned,
         hot_rows,
         labels.reshape(1, rows),
-        cross_bias.reshape(1, F),
-        out_weight.reshape(1, F),
+        cross_bias,
+        out_weight,
         *pieces,
     )
     incoming = lax.all_to_all(send, "dp", split_axis=0, concat_axis=0, tiled=True)
-    hot_partial = call(
-        hot_sum_body,
-        shape((HOT, E), F32),
-        [VMEM, VMEM],
-        [pltpu.VMEM((HOT, NH * rows), BF)],
-        (2 * HOT * NH * rows * 2 * E, 5 * 10**6),
-        "hot_sum",
-    )(hot_t, hot_grad)
     hot_share = hot_early(hot_partial)
+    core = lax.axis_index("rep") % 2
     incoming, hot_share = lax.optimization_barrier((incoming, hot_share))
-    cold_partial = call(
-        functools.partial(cold_sum_body, n_data, capacity),
-        shape((owned, E), F32),
-        [VMEM, VMEM],
-        [pltpu.VMEM((owned, places), BF)],
-        (2 * owned * places * E, 5 * 10**6),
-        "cold_sum",
-    )(asked, incoming)
-    return hot_late(hot_share), sum_cold(cold_partial)
+
+    def cold_sum(rows_of, grads):
+        return call(
+            functools.partial(cold_sum_body, n_data, capacity),
+            shape((owned // 2, E), F32),
+            [SMEM, VMEM, VMEM],
+            [pltpu.VMEM((owned // 2, places), BF)],
+            (10**9, 10**7),
+            "cold_sum",
+        )((rows_of * (owned // 2)).reshape(1), asked, grads)
+
+    others = cold_sum(1 - core, incoming)
+    incoming = after(incoming, others)
+    mine = cold_sum(core, incoming)
+    hot_share = paired(hot_share, swap(hot_share, "dp", 1), lax.axis_index("dp") % 2)
+    mine = (mine + swap(others, "rep", 1)).astype(BF)
+    mine, hot_share = lax.optimization_barrier((mine, hot_share))
+    mine = mine.astype(F32) + swap(mine, "rep", 2).astype(F32)
+    hot_share = paired(hot_share, swap(hot_share, "rep", 2), lax.axis_index("rep") // 2)
+    return tuple(paired(half, swap(half, "rep", 1), core) for half in (hot_share, mine))
 
 
 def large_step(

time: 141 us -> 136 us (0.965)
  waiting for transfers between devices: 62.1 us -> 51.6 us
  starting transfers between devices: 40.5 us -> 45.7 us
    ppermute x24 -> x29, starting transfers between devices: 17.5 us -> 32.2 us  [swap(): return lax.ppermute(value, axis, [(i, i ^ distance) for i in range(size)])]
    ppermute x24 -> x29, waiting for transfers between devices: 58.1 us -> 46.6 us  [swap(): return lax.ppermute(value, axis, [(i, i ^ distance) for i in range(size)])]
    ppermute x3 -> x0, starting transfers between devices: 7.01 us -> none  [shift(): lax.ppermute(value, axis, [(i, (i + distance) % size) for i in range(size)])]
    all_to_all x1, waiting for transfers between devices: 2.6 us -> 5.01 us  [small_step(): asked = lax.all_to_all(ask, 'dp', split_axis=0, concat_axis=0, tiled=True)]
    ppermute x1, starting transfers between devices: 1.87 us -> 0.02 us  [swap_both(): return lax.ppermute(value, ('dp', 'rep'), ways)]
    pallas_call x1, Pallas kernels: 3.48 us -> 5.05 us  [small_step(): call(functools.partial(serve_body, n_data, capacity), shape((places, E),...]
    unnamed x44 -> x34, local copies, waits for them, and re-layouts: 5.05 us -> 4.38 us
  transfers between devices with their start and end apart: 31 -> 33, of which waited for: 17 -> 14; matrix products, arithmetic and copies ran while one was open for 4% -> 3% of each run, Pallas kernels for 6% -> 8%
where the time goes in v5:
time: 136 us; the launch traced here: 135 us
  waiting for transfers between devices  51.6 us (38%)
  starting transfers between devices  45.7 us (34%)
  Pallas kernels  23.2 us (17%)
  local copies, waits for them, and re-layouts  7.36 us (5%)
  other arithmetic  6.3 us (5%)
    ppermute x29, waiting for transfers between devices, swap(): return lax.ppermute(value, axis, [(i, i ^ distance) for i in range(size)])  46.6 us
    ppermute x29, starting transfers between devices, swap(): return lax.ppermute(value, axis, [(i, i ^ distance) for i in range(size)])  32.2 us
    pallas_call x1, Pallas kernels, small_step(): call(cross_body, (shape((places, E), BF), shape((HOT, E), F32)), [SMEM] +...  10.7 us
    all_to_all x1, starting transfers between devices, small_step(): lax.all_to_all(send, 'dp', split_axis=0, concat_axis=0, tiled=True)  6.48 us
    pallas_call x1, Pallas kernels, small_step(): call(functools.partial(serve_body, n_data, capacity), shape((places, E),...  5.05 us
    all_to_all x1, waiting for transfers between devices, small_step(): asked = lax.all_to_all(ask, 'dp', split_axis=0, concat_axis=0, tiled=True)  5.01 us
    unnamed x34, local copies, waits for them, and re-layouts  4.38 us
    pallas_call x2, Pallas kernels, cold_sum(): call(functools.partial(cold_sum_body, n_data, capacity), shape((owned //...  3.98 us
  transfers between devices with their start and end apart: 33, of which 14 were waited for; matrix products, arithmetic and copies ran while one was open for 3% of the time, Pallas kernels for 8%

profile of v5, /device:TPU:0, one launch (start us, length us, event | category | flops | bytes accessed | tf_op | source)
XLA Modules:
  0.0 135.2 jit_solution(17988997493494313839)
XLA Ops:
  0.6 1.0 maximum_bitcast_fusion.rest_0_
  1.7 3.0 %collective-permute-start = (bf16[2,1,16,3328]{3,2,1,0:T(8,128)(2,1)S(1)}, bf16[2,1,16,3328]{3,2,1,0:T(8,128)(2,1)}, u32[]{:S(2)}, u32[]{:S(2)}) collective-permute-start(bf16[2,1,16,3328]{3,2,1,0:T(8,128)(2,1)S(1)} %maximum_bitcast_fusion.rest_0_), channel_id=1, source_target_pairs={{0,2},{1,3},{2,0},{3,1},{4,6},{5,7},{6,4},{7,5},{8,10},{9,11},{10,... | collective-permute-start | bytes 638984 | tf_op jit(solution)/shard_map/ppermute | solution.py:29
  4.7 1.5 %collective-permute-start.1 = (bf16[2,1,16,3328]{3,2,1,0:T(8,128)(2,1)S(1)}, bf16[2,1,16,3328]{3,2,1,0:T(8,128)(2,1)}, u32[]{:S(2)}, u32[]{:S(2)}) collective-permute-start(bf16[2,1,16,3328]{3,2,1,0:T(8,128)(2,1)S(1)} %maximum_bitcast_fusion.rest_0_), channel_id=1, source_target_pairs={{0,4},{4,0},{8,12},{12,8},{16,20},{20,16},{24,28},{28,24},{1,5},{5... | collective-permute-start | bytes 638984 | tf_op jit(solution)/shard_map/ppermute | solution.py:29
  6.2 2.0 %collective-permute-start.3 = (bf16[2,1,16,3328]{3,2,1,0:T(8,128)(2,1)S(1)}, bf16[2,1,16,3328]{3,2,1,0:T(8,128)(2,1)S(1)}, u32[]{:S(2)}, u32[]{:S(2)}) collective-permute-start(bf16[2,1,16,3328]{3,2,1,0:T(8,128)(2,1)S(1)} %maximum_bitcast_fusion.rest_0_), channel_id=1, source_target_pairs={{0,8},{4,12},{8,0},{12,4},{16,24},{20,28},{24,16},{28,20},{1,9},{5... | collective-permute-start | bytes 638984 | tf_op jit(solution)/shard_map/ppermute | solution.py:29
  8.3 2.6 %collective-permute-start.4 = (bf16[2,1,16,3328]{3,2,1,0:T(8,128)(2,1)S(1)}, bf16[2,1,16,3328]{3,2,1,0:T(8,128)(2,1)S(1)}, u32[]{:S(2)}, u32[]{:S(2)}) collective-permute-start(bf16[2,1,16,3328]{3,2,1,0:T(8,128)(2,1)S(1)} %maximum_bitcast_fusion.rest_0_), channel_id=1, source_target_pairs={{0,16},{4,20},{8,24},{12,28},{16,0},{20,4},{24,8},{28,12},{1,17},{... | collective-permute-start | bytes 638984 | tf_op jit(solution)/shard_map/ppermute | solution.py:29
  10.9 4.2 %collective-permute-start.5 = (bf16[2,1,16,3328]{3,2,1,0:T(8,128)(2,1)S(1)}, bf16[2,1,16,3328]{3,2,1,0:T(8,128)(2,1)S(1)}, u32[]{:S(2)}, u32[]{:S(2)}) collective-permute-start(bf16[2,1,16,3328]{3,2,1,0:T(8,128)(2,1)S(1)} %maximum_bitcast_fusion.rest_0_), channel_id=1, source_target_pairs={{0,24},{4,28},{8,16},{12,20},{16,8},{20,12},{24,0},{28,4},{1,25},{... | collective-permute-start | bytes 638984 | tf_op jit(solution)/shard_map/ppermute | solution.py:29
  15.0 0.7 reduce
  15.8 0.2 reshape.32
  16.0 0.1 copy.14
  16.0 0.6 copy-done.4
  16.7 1.2 route.1
  17.9 0.6 copy-done.5
  18.5 3.5 %all-to-all-start = ((s32[8,4,128]{2,1,0:T(4,128)}), s32[8,4,128]{2,1,0:T(4,128)S(1)}, u32[]{:S(2)}, u32[]{:S(2)}) async-start(s32[8,4,128]{2,1,0:T(4,128)} %bitcast.3), calls=%async_computation | async-start | bytes 32768 | tf_op jit(solution)/shard_map/all_to_all | solution.py:325
  22.0 2.2 %hot_rows.1.hot_ref = bf16[1664,128]{1,0:T(8,128)(2,1)S(1)} custom-call(s32[1664]{0:T(1024)S(1)} %bitcast.33, f32[1024,128]{1,0:T(8,128)S(1)} %copy-done.1), custom_call_target="tpu_custom_call" | custom-call | flops 1 | bytes 1 | tf_op jit(solution)/shard_map/hot_rows/pallas_call | solution.py:328
  24.2 0.8 copy-done.2
  25.0 5.0 %all-to-all-done = s32[8,4,128]{2,1,0:T(4,128)S(1)} async-done(((s32[8,4,128]{2,1,0:T(4,128)}), s32[8,4,128]{2,1,0:T(4,128)S(1)}, u32[]{:S(2)}, u32[]{:S(2)}) %all-to-all-start) | async-done | bytes 16416 | tf_op jit(solution)/shard_map/all_to_all | solution.py:325
  30.0 0.7 constant_dynamic-update-slice_fusion.2
  30.8 0.7 constant_dynamic-update-slice_fusion.1
  31.5 0.7 constant_dynamic-update-slice_fusion.rest_4_
  32.2 0.6 collective-permute-start.7
  32.8 1.5 %collective-permute-start.6 = (bf16[2,3,16,3328]{3,2,1,0:T(8,128)(2,1)}, bf16[2,3,16,3328]{3,2,1,0:T(8,128)(2,1)}, u32[]{:S(2)}, u32[]{:S(2)}) collective-permute-start(bf16[2,3,16,3328]{3,2,1,0:T(8,128)(2,1)} %constant_dynamic-update-slice_fusion.rest_4_), channel_id=1, source_target_pairs={{0,2},{1,3},{2,0},{3,1},{4,6},{5,7},{6,4},{7,5},{8,10},{9,11},{10,... | collective-permute-start | bytes 1916936 | tf_op jit(solution)/shard_map/ppermute | solution.py:29
  34.3 0.2 collective-permute-start.12
  34.5 5.0 %serve.1 = bf16[3328,128]{1,0:T(8,128)(2,1)} custom-call(s32[4096]{0:T(1024)S(1)} %bitcast.28, f32[2048,128]{1,0:T(8,128)S(1)} %copy-done), custom_call_target="tpu_custom_call" | custom-call | flops 1 | bytes 1 | tf_op jit(solution)/shard_map/serve/pallas_call | solution.py:339
  39.6 3.6 %all-to-all-start.1 = ((bf16[8,416,128]{2,1,0:T(8,128)(2,1)}), bf16[8,416,128]{2,1,0:T(8,128)(2,1)S(1)}, u32[]{:S(2)}, u32[]{:S(2)}) async-start(bf16[8,416,128]{2,1,0:T(8,128)(2,1)} %bitcast.13), calls=%async_computation.1 | async-start | bytes 1703936 | tf_op jit(solution)/shard_map/all_to_all | solution.py:347
  43.1 0.3 collective-permute-start.10
  43.5 2.9 %collective-permute-done.7.rest_6_ = bf16[2,3,16,3328]{3,2,1,0:T(8,128)(2,1)S(1)} collective-permute-done((bf16[2,3,16,3328]{3,2,1,0:T(8,128)(2,1)}, bf16[2,3,16,3328]{3,2,1,0:T(8,128)(2,1)S(1)}, u32[]{:S(2)}, u32[]{:S(2)}) %collective-permute-start.7) | collective-permute-done | bytes 639008 | tf_op jit(solution)/shard_map/ppermute | solution.py:29
  46.4 3.5 %collective-permute-done.6.rest_5_ = bf16[2,3,16,3328]{3,2,1,0:T(8,128)(2,1)} collective-permute-done((bf16[2,3,16,3328]{3,2,1,0:T(8,128)(2,1)}, bf16[2,3,16,3328]{3,2,1,0:T(8,128)(2,1)}, u32[]{:S(2)}, u32[]{:S(2)}) %collective-permute-start.6) | collective-permute-done | bytes 639008 | tf_op jit(solution)/shard_map/ppermute | solution.py:29
  49.9 1.0 slice_bitcast_fusion
  50.9 1.6 %collective-permute-start.15 = (bf16[3,16,3328]{2,1,0:T(8,128)(2,1)S(1)}, bf16[3,16,3328]{2,1,0:T(8,128)(2,1)S(1)}, u32[]{:S(2)}, u32[]{:S(2)}) collective-permute-start(bf16[3,16,3328]{2,1,0:T(8,128)(2,1)S(1)} %slice_bitcast_fusion.1), channel_id=1, source_target_pairs={{0,2},{1,3},{2,0},{3,1},{4,6},{5,7},{6,4},{7,5},{8,10},{9,11},{10,... | collective-permute-start | bytes 958472 | tf_op jit(solution)/shard_map/ppermute | solution.py:29
  52.5 0.2 collective-permute-start.13
  52.7 0.3 collective-permute-start.14
  53.0 1.6 %collective-permute-start.17 = (bf16[3,16,3328]{2,1,0:T(8,128)(2,1)S(1)}, bf16[3,16,3328]{2,1,0:T(8,128)(2,1)}, u32[]{:S(2)}, u32[]{:S(2)}) collective-permute-start(bf16[3,16,3328]{2,1,0:T(8,128)(2,1)S(1)} %slice_bitcast_fusion), channel_id=1, source_target_pairs={{0,4},{4,0},{8,12},{12,8},{16,20},{20,16},{24,28},{28,24},{1,5},{5... | collective-permute-start | bytes 958472 | tf_op jit(solution)/shard_map/ppermute | solution.py:29
  54.6 6.4 %collective-permute-done.15.rest_14_ = bf16[3,16,3328]{2,1,0:T(8,128)(2,1)S(1)} collective-permute-done((bf16[3,16,3328]{2,1,0:T(8,128)(2,1)S(1)}, bf16[3,16,3328]{2,1,0:T(8,128)(2,1)S(1)}, u32[]{:S(2)}, u32[]{:S(2)}) %collective-permute-start.15) | collective-permute-done | bytes 319520 | tf_op jit(solution)/shard_map/ppermute | solution.py:29
  60.9 4.1 %collective-permute-done.17.rest_16_ = bf16[3,16,3328]{2,1,0:T(8,128)(2,1)} collective-permute-done((bf16[3,16,3328]{2,1,0:T(8,128)(2,1)S(1)}, bf16[3,16,3328]{2,1,0:T(8,128)(2,1)}, u32[]{:S(2)}, u32[]{:S(2)}) %collective-permute-start.17) | collective-permute-done | bytes 319520 | tf_op jit(solution)/shard_map/ppermute | solution.py:29
  65.2 1.9 %collective-permute-done.18.rest_17_ = bf16[3,16,3328]{2,1,0:T(8,128)(2,1)} collective-permute-done((bf16[3,16,3328]{2,1,0:T(8,128)(2,1)}, bf16[3,16,3328]{2,1,0:T(8,128)(2,1)}, u32[]{:S(2)}, u32[]{:S(2)}) %collective-permute-start.18) | collective-permute-done | bytes 319520 | tf_op jit(solution)/shard_map/ppermute | solution.py:29
  67.1 0.9 copy-done.6
  67.9 10.7 %cross.1 = (bf16[3328,128]{1,0:T(8,128)(2,1)}, f32[1024,128]{1,0:T(8,128)}) custom-call(s32[2048]{0:T(1024)} %bitcast.35, s32[13,128]{1,0:T(8,128)} %bitcast.32, bf16[3328,128]{1,0:T(8,128)(2,1)} %bitcast.36, bf16[1664,128]{1,0:T(8,128)(2,1)} %copy-done.2, s32[1,128]{1,0:T(1,128)} %bitcast.40, f32[3328]{0:T(1024)} %bias_ref.1, f32[3328]{0:T(1024)} %weight_ref.1, ...), custom_call_target="tpu_custom_call" | custom-call | flops 1744830464 | bytes 20000000 | tf_op jit(solution)/shard_map/cross/pallas_call | solution.py:353
  78.7 1.0 constant_dynamic-slice_fusion.2
  79.7 0.2 collective-permute-start.19
  79.9 6.5 %all-to-all-start.2 = ((bf16[8,416,128]{2,1,0:T(8,128)(2,1)}), bf16[8,416,128]{2,1,0:T(8,128)(2,1)S(1)}, u32[]{:S(2)}, u32[]{:S(2)}) async-start(bf16[8,416,128]{2,1,0:T(8,128)(2,1)} %bitcast.37), calls=%async_computation.2 | async-start | bytes 1703936 | tf_op jit(solution)/shard_map/all_to_all | solution.py:382
  86.4 0.2 collective-permute-start.20
  86.6 5.4 %collective-permute-done.20 = f32[256,128]{1,0:T(8,128)S(1)} collective-permute-done((f32[256,128]{1,0:T(8,128)S(1)}, f32[256,128]{1,0:T(8,128)S(1)}, u32[]{:S(2)}, u32[]{:S(2)}) %collective-permute-start.20) | collective-permute-done | bytes 131104 | tf_op jit(solution)/shard_map/ppermute | solution.py:29
  92.0 1.8 %collective-permute-start.21 = (f32[128,128]{1,0:T(8,128)S(1)}, f32[128,128]{1,0:T(8,128)S(1)}, u32[]{:S(2)}, u32[]{:S(2)}) collective-permute-start(f32[128,128]{1,0:T(8,128)S(1)} %constant_dynamic-slice_fusion), channel_id=1, source_target_pairs={{0,4},{4,0},{8,12},{12,8},{16,20},{20,16},{24,28},{28,24},{1,5},{5... | collective-permute-start | bytes 196616 | tf_op jit(solution)/shard_map/ppermute | solution.py:29
  93.8 3.9 %collective-permute-done.21 = f32[128,128]{1,0:T(8,128)S(1)} collective-permute-done((f32[128,128]{1,0:T(8,128)S(1)}, f32[128,128]{1,0:T(8,128)S(1)}, u32[]{:S(2)}, u32[]{:S(2)}) %collective-permute-start.21) | collective-permute-done | bytes 65568 | tf_op jit(solution)/shard_map/ppermute | solution.py:29
  97.7 0.4 collective-permute-start.22
  98.1 4.6 %collective-permute-done.22 = f32[128,128]{1,0:T(8,128)S(1)} collective-permute-done((f32[128,128]{1,0:T(8,128)S(1)}, f32[128,128]{1,0:T(8,128)S(1)}, u32[]{:S(2)}, u32[]{:S(2)}) %collective-permute-start.22) | collective-permute-done | bytes 65568 | tf_op jit(solution)/shard_map/ppermute | solution.py:29
  102.7 6.7 %collective-permute-start.23 = (f32[128,128]{1,0:T(8,128)S(1)}, f32[128,128]{1,0:T(8,128)S(1)}, u32[]{:S(2)}, u32[]{:S(2)}) collective-permute-start(f32[128,128]{1,0:T(8,128)S(1)} %add.60), channel_id=1, source_target_pairs={{0,16},{4,20},{8,24},{12,28},{16,0},{20,4},{24,8},{28,12},{1,17},{... | collective-permute-start | bytes 196616 | tf_op jit(solution)/shard_map/ppermute | solution.py:29
  109.4 2.2 %collective-permute-done.23 = f32[128,128]{1,0:T(8,128)S(1)} collective-permute-done((f32[128,128]{1,0:T(8,128)S(1)}, f32[128,128]{1,0:T(8,128)S(1)}, u32[]{:S(2)}, u32[]{:S(2)}) %collective-permute-start.23) | collective-permute-done | bytes 65568 | tf_op jit(solution)/shard_map/ppermute | solution.py:29
  111.7 2.0 %cold_sum.2 = f32[1024,128]{1,0:T(8,128)S(1)} custom-call(s32[1]{0:T(128)} %bitcast.20.first_ref, s32[32,128]{1,0:T(8,128)S(1)} %bitcast.29, bf16[3328,128]{1,0:T(8,128)(2,1)S(1)} %bitcast.26), custom_call_target="tpu_custom_call" | custom-call | flops 1000000000 | bytes 10000000 | tf_op jit(solution)/shard_map/cold_sum/pallas_call | solution.py:388
  113.7 0.1 collective-permute-start.24
  113.8 1.0 collective-permute-start.25
  114.8 2.0 %cold_sum.3 = f32[1024,128]{1,0:T(8,128)S(1)} custom-call(s32[1]{0:T(128)} %bitcast.first_ref, s32[32,128]{1,0:T(8,128)S(1)} %bitcast.30, bf16[3328,128]{1,0:T(8,128)(2,1)S(1)} %bitcast.27), custom_call_target="tpu_custom_call" | custom-call | flops 1000000000 | bytes 10000000 | tf_op jit(solution)/shard_map/cold_sum/pallas_call | solution.py:388
  116.8 1.5 %collective-permute-done.25 = f32[128,128]{1,0:T(8,128)S(1)} collective-permute-done((f32[128,128]{1,0:T(8,128)S(1)}, f32[128,128]{1,0:T(8,128)S(1)}, u32[]{:S(2)}, u32[]{:S(2)}) %collective-permute-start.25) | collective-permute-done | bytes 65568 | tf_op jit(solution)/shard_map/ppermute | solution.py:29
  118.3 1.1 add_convert_fusion
  119.4 0.4 collective-permute-start.28
  119.8 1.7 %collective-permute-start.26 = (f32[256,128]{1,0:T(8,128)S(1)}, f32[256,128]{1,0:T(8,128)S(1)}, u32[]{:S(2)}, u32[]{:S(2)}) collective-permute-start(f32[256,128]{1,0:T(8,128)S(1)} %maximum_select_fusion.3), channel_id=1, source_target_pairs={{0,2},{1,3},{2,0},{3,1},{4,6},{5,7},{6,4},{7,5},{8,10},{9,11},{10,... | collective-permute-start | bytes 393224 | tf_op jit(solution)/shard_map/ppermute | solution.py:29
  121.5 7.2 %collective-permute-done.28 = bf16[1024,128]{1,0:T(8,128)(2,1)S(1)} collective-permute-done((bf16[1024,128]{1,0:T(8,128)(2,1)S(1)}, bf16[1024,128]{1,0:T(8,128)(2,1)S(1)}, u32[]{:S(2)}, u32[]{:S(2)}) %collective-permute-start.28) | collective-permute-done | bytes 262176 | tf_op jit(solution)/shard_map/ppermute | solution.py:29
  128.7 0.1 convert_add_fusion
  128.7 0.1 collective-permute-start.29
  128.8 1.3 collective-permute-done.26
  130.2 0.1 collective-permute-start.27
  130.2 1.6 %collective-permute-done.27 = f32[512,128]{1,0:T(8,128)} collective-permute-done((f32[512,128]{1,0:T(8,128)S(1)}, f32[512,128]{1,0:T(8,128)}, u32[]{:S(2)}, u32[]{:S(2)}) %collective-permute-start.27) | collective-permute-done | bytes 262176 | tf_op jit(solution)/shard_map/ppermute | solution.py:29
  131.9 2.0 %multiply_subtract_fusion.1 = f32[1024,128]{1,0:T(8,128)} fusion(f32[1024,128]{1,0:T(8,128)S(1)} %copy-done.1, bf16[1024,128]{1,0:T(8,128)(2,1)S(1)} %copy-done.12, f32[512,128]{1,0:T(8,128)S(1)} %maximum_select_fusion.2, f32[512,128]{1,0:T(8,128)} %collective-permute-done.27, pred[]{:T(512)S(6)} %eq.15), kind=kLoop, calls=%fused_computation.4 | loop fusion | flops 1441792 | bytes 1835009 | tf_op jit(solution)/shard_map/sub | solution.py:20
  133.9 1.3 multiply_subtract_fusion
  (63 shorter events, 0.3 us)
Async XLA Ops:
  0.6 21.3 %copy-start.1 = (f32[1024,128]{1,0:T(8,128)S(1)}, f32[1024,128]{1,0:T(8,128)}, u32[]{:S(2)}) copy-start(f32[1024,128]{1,0:T(8,128)} %table_ref.2) | copy-start | bytes 1572868
  1.7 31.1 %copy-start.8 = (bf16[2,1,16,3328]{3,2,1,0:T(8,128)(2,1)}, bf16[2,1,16,3328]{3,2,1,0:T(8,128)(2,1)S(1)}, u32[]{:S(2)}) copy-start(bf16[2,1,16,3328]{3,2,1,0:T(8,128)(2,1)S(1)} %maximum_bitcast_fusion.rest_0_) | copy-start | bytes 638980
  1.7 9.2 %collective-permute-start = (bf16[2,1,16,3328]{3,2,1,0:T(8,128)(2,1)S(1)}, bf16[2,1,16,3328]{3,2,1,0:T(8,128)(2,1)}, u32[]{:S(2)}, u32[]{:S(2)}) collective-permute-start(bf16[2,1,16,3328]{3,2,1,0:T(8,128)(2,1)S(1)} %maximum_bitcast_fusion.rest_0_), channel_id=1, source_target_pairs={{0,2},{1,3},{2,0},{3,1},{4,6},{5,7},{6,4},{7,5},{8,10},{9,11},{10,... | collective-permute-start | bytes 638984 | tf_op jit(solution)/shard_map/ppermute | solution.py:29
  4.7 25.3 %collective-permute-start.1 = (bf16[2,1,16,3328]{3,2,1,0:T(8,128)(2,1)S(1)}, bf16[2,1,16,3328]{3,2,1,0:T(8,128)(2,1)}, u32[]{:S(2)}, u32[]{:S(2)}) collective-permute-start(bf16[2,1,16,3328]{3,2,1,0:T(8,128)(2,1)S(1)} %maximum_bitcast_fusion.rest_0_), channel_id=1, source_target_pairs={{0,4},{4,0},{8,12},{12,8},{16,20},{20,16},{24,28},{28,24},{1,5},{5... | collective-permute-start | bytes 638984 | tf_op jit(solution)/shard_map/ppermute | solution.py:29
  6.2 23.8 %collective-permute-start.2 = (bf16[2,1,16,3328]{3,2,1,0:T(8,128)(2,1)S(1)}, bf16[2,1,16,3328]{3,2,1,0:T(8,128)(2,1)}, u32[]{:S(2)}, u32[]{:S(2)}) collective-permute-start(bf16[2,1,16,3328]{3,2,1,0:T(8,128)(2,1)S(1)} %maximum_bitcast_fusion.rest_0_), channel_id=1, source_target_pairs={{0,6},{1,7},{2,4},{3,5},{4,2},{5,3},{6,0},{7,1},{8,14},{9,15},{10,... | collective-permute-start | bytes 638984 | tf_op jit(solution)/shard_map/ppermute | solution.py:46
  6.2 23.8 %collective-permute-start.3 = (bf16[2,1,16,3328]{3,2,1,0:T(8,128)(2,1)S(1)}, bf16[2,1,16,3328]{3,2,1,0:T(8,128)(2,1)S(1)}, u32[]{:S(2)}, u32[]{:S(2)}) collective-permute-start(bf16[2,1,16,3328]{3,2,1,0:T(8,128)(2,1)S(1)} %maximum_bitcast_fusion.rest_0_), channel_id=1, source_target_pairs={{0,8},{4,12},{8,0},{12,4},{16,24},{20,28},{24,16},{28,20},{1,9},{5... | collective-permute-start | bytes 638984 | tf_op jit(solution)/shard_map/ppermute | solution.py:29
  8.3 21.8 %collective-permute-start.4 = (bf16[2,1,16,3328]{3,2,1,0:T(8,128)(2,1)S(1)}, bf16[2,1,16,3328]{3,2,1,0:T(8,128)(2,1)S(1)}, u32[]{:S(2)}, u32[]{:S(2)}) collective-permute-start(bf16[2,1,16,3328]{3,2,1,0:T(8,128)(2,1)S(1)} %maximum_bitcast_fusion.rest_0_), channel_id=1, source_target_pairs={{0,16},{4,20},{8,24},{12,28},{16,0},{20,4},{24,8},{28,12},{1,17},{... | collective-permute-start | bytes 638984 | tf_op jit(solution)/shard_map/ppermute | solution.py:29
  10.9 19.2 %collective-permute-start.5 = (bf16[2,1,16,3328]{3,2,1,0:T(8,128)(2,1)S(1)}, bf16[2,1,16,3328]{3,2,1,0:T(8,128)(2,1)S(1)}, u32[]{:S(2)}, u32[]{:S(2)}) collective-permute-start(bf16[2,1,16,3328]{3,2,1,0:T(8,128)(2,1)S(1)} %maximum_bitcast_fusion.rest_0_), channel_id=1, source_target_pairs={{0,24},{4,28},{8,16},{12,20},{16,8},{20,12},{24,0},{28,4},{1,25},{... | collective-permute-start | bytes 638984 | tf_op jit(solution)/shard_map/ppermute | solution.py:29
  16.0 0.7 copy-start.4
  17.9 0.6 copy-start.5
  18.5 3.5 %copy-start.3 = (s32[128,13]{0,1:T(8,128)S(1)}, s32[128,13]{0,1:T(8,128)}, u32[]{:S(2)}) copy-start(s32[128,13]{0,1:T(8,128)} %param.12) | copy-start | bytes 19972
  18.5 11.5 %all-to-all-start = ((s32[8,4,128]{2,1,0:T(4,128)}), s32[8,4,128]{2,1,0:T(4,128)S(1)}, u32[]{:S(2)}, u32[]{:S(2)}) async-start(s32[8,4,128]{2,1,0:T(4,128)} %bitcast.3), calls=%async_computation | async-start | bytes 32768 | tf_op jit(solution)/shard_map/all_to_all | solution.py:325
  22.0 12.6 %copy-start = (f32[2048,128]{1,0:T(8,128)S(1)}, f32[2048,128]{1,0:T(8,128)}, u32[]{:S(2)}) copy-start(f32[2048,128]{1,0:T(8,128)} %table_ref.3) | copy-start | bytes 3145732
  24.2 0.8 copy-start.2
  32.2 14.3 %collective-permute-start.7 = (bf16[2,3,16,3328]{3,2,1,0:T(8,128)(2,1)}, bf16[2,3,16,3328]{3,2,1,0:T(8,128)(2,1)S(1)}, u32[]{:S(2)}, u32[]{:S(2)}) collective-permute-start(bf16[2,3,16,3328]{3,2,1,0:T(8,128)(2,1)} %constant_dynamic-update-slice_fusion.rest_4_), channel_id=1, source_target_pairs={{0,4},{4,0},{8,12},{12,8},{16,20},{20,16},{24,28},{28,24},{1,5},{5... | collective-permute-start | bytes 1916936 | tf_op jit(solution)/shard_map/ppermute | solution.py:29
  32.8 18.1 %collective-permute-start.8 = (bf16[2,1,16,3328]{3,2,1,0:T(8,128)(2,1)S(1)}, bf16[2,1,16,3328]{3,2,1,0:T(8,128)(2,1)}, u32[]{:S(2)}, u32[]{:S(2)}) collective-permute-start(bf16[2,1,16,3328]{3,2,1,0:T(8,128)(2,1)S(1)} %maximum_bitcast_fusion.rest_0_), channel_id=1, source_target_pairs={{0,1},{1,0},{2,3},{3,2},{4,5},{5,4},{6,7},{7,6},{8,9},{9,8},{10,11... | collective-permute-start | bytes 638984 | tf_op jit(solution)/shard_map/ppermute | solution.py:29
  32.8 17.1 %collective-permute-start.6 = (bf16[2,3,16,3328]{3,2,1,0:T(8,128)(2,1)}, bf16[2,3,16,3328]{3,2,1,0:T(8,128)(2,1)}, u32[]{:S(2)}, u32[]{:S(2)}) collective-permute-start(bf16[2,3,16,3328]{3,2,1,0:T(8,128)(2,1)} %constant_dynamic-update-slice_fusion.rest_4_), channel_id=1, source_target_pairs={{0,2},{1,3},{2,0},{3,1},{4,6},{5,7},{6,4},{7,5},{8,10},{9,11},{10,... | collective-permute-start | bytes 1916936 | tf_op jit(solution)/shard_map/ppermute | solution.py:29
  34.3 30.8 %collective-permute-start.12 = (bf16[2,3,16,3328]{3,2,1,0:T(8,128)(2,1)}, bf16[2,3,16,3328]{3,2,1,0:T(8,128)(2,1)}, u32[]{:S(2)}, u32[]{:S(2)}) collective-permute-start(bf16[2,3,16,3328]{3,2,1,0:T(8,128)(2,1)} %constant_dynamic-update-slice_fusion.rest_4_), channel_id=1, source_target_pairs={{0,1},{1,0},{2,3},{3,2},{4,5},{5,4},{6,7},{7,6},{8,9},{9,8},{10,11... | collective-permute-start | bytes 1916936 | tf_op jit(solution)/shard_map/ppermute | solution.py:29
  39.6 27.5 %all-to-all-start.1 = ((bf16[8,416,128]{2,1,0:T(8,128)(2,1)}), bf16[8,416,128]{2,1,0:T(8,128)(2,1)S(1)}, u32[]{:S(2)}, u32[]{:S(2)}) async-start(bf16[8,416,128]{2,1,0:T(8,128)(2,1)} %bitcast.13), calls=%async_computation.1 | async-start | bytes 1703936 | tf_op jit(solution)/shard_map/all_to_all | solution.py:347
  43.1 9.3 %collective-permute-start.10 = (bf16[2,1,16,3328]{3,2,1,0:T(8,128)(2,1)}, bf16[2,1,16,3328]{3,2,1,0:T(8,128)(2,1)S(1)}, u32[]{:S(2)}, u32[]{:S(2)}) collective-permute-start(bf16[2,1,16,3328]{3,2,1,0:T(8,128)(2,1)} %collective-permute-done.1.rest_2_), channel_id=1, source_target_pairs={{0,1},{1,0},{2,3},{3,2},{4,5},{5,4},{6,7},{7,6},{8,9},{9,8},{10,11... | collective-permute-start | bytes 638984 | tf_op jit(solution)/shard_map/ppermute | solution.py:29
  46.4 18.7 %copy-start.7 = (bf16[2,3,16,3328]{3,2,1,0:T(8,128)(2,1)}, bf16[2,3,16,3328]{3,2,1,0:T(8,128)(2,1)S(1)}, u32[]{:S(2)}) copy-start(bf16[2,3,16,3328]{3,2,1,0:T(8,128)(2,1)S(1)} %collective-permute-done.7.rest_6_) | copy-start | bytes 1916932
  46.4 6.3 %collective-permute-start.11 = (bf16[2,1,16,3328]{3,2,1,0:T(8,128)(2,1)}, bf16[2,1,16,3328]{3,2,1,0:T(8,128)(2,1)S(1)}, u32[]{:S(2)}, u32[]{:S(2)}) collective-permute-start(bf16[2,1,16,3328]{3,2,1,0:T(8,128)(2,1)} %collective-permute-done.2.rest_3_), channel_id=1, source_target_pairs={{0,1},{1,0},{2,3},{3,2},{4,5},{5,4},{6,7},{7,6},{8,9},{9,8},{10,11... | collective-permute-start | bytes 638984 | tf_op jit(solution)/shard_map/ppermute | solution.py:29
  49.9 3.1 %collective-permute-start.9 = (bf16[2,1,16,3328]{3,2,1,0:T(8,128)(2,1)}, bf16[2,1,16,3328]{3,2,1,0:T(8,128)(2,1)S(1)}, u32[]{:S(2)}, u32[]{:S(2)}) collective-permute-start(bf16[2,1,16,3328]{3,2,1,0:T(8,128)(2,1)} %collective-permute-done.rest_1_), channel_id=1, source_target_pairs={{0,1},{1,0},{2,3},{3,2},{4,5},{5,4},{6,7},{7,6},{8,9},{9,8},{10,11... | collective-permute-start | bytes 638984 | tf_op jit(solution)/shard_map/ppermute | solution.py:29
  50.9 10.0 %collective-permute-start.15 = (bf16[3,16,3328]{2,1,0:T(8,128)(2,1)S(1)}, bf16[3,16,3328]{2,1,0:T(8,128)(2,1)S(1)}, u32[]{:S(2)}, u32[]{:S(2)}) collective-permute-start(bf16[3,16,3328]{2,1,0:T(8,128)(2,1)S(1)} %slice_bitcast_fusion.1), channel_id=1, source_target_pairs={{0,2},{1,3},{2,0},{3,1},{4,6},{5,7},{6,4},{7,5},{8,10},{9,11},{10,... | collective-permute-start | bytes 958472 | tf_op jit(solution)/shard_map/ppermute | solution.py:29
  52.5 12.6 %copy-start.13 = (bf16[2,1,16,3328]{3,2,1,0:T(8,128)(2,1)}, bf16[2,1,16,3328]{3,2,1,0:T(8,128)(2,1)S(1)}, u32[]{:S(2)}) copy-start(bf16[2,1,16,3328]{3,2,1,0:T(8,128)(2,1)S(1)} %collective-permute-done.10.rest_9_) | copy-start | bytes 638980
  52.5 12.7 %collective-permute-start.13 = (bf16[2,3,16,3328]{3,2,1,0:T(8,128)(2,1)}, bf16[2,3,16,3328]{3,2,1,0:T(8,128)(2,1)}, u32[]{:S(2)}, u32[]{:S(2)}) collective-permute-start(bf16[2,3,16,3328]{3,2,1,0:T(8,128)(2,1)} %collective-permute-done.6.rest_5_), channel_id=1, source_target_pairs={{0,1},{1,0},{2,3},{3,2},{4,5},{5,4},{6,7},{7,6},{8,9},{9,8},{10,11... | collective-permute-start | bytes 1916936 | tf_op jit(solution)/shard_map/ppermute | solution.py:29
  52.7 12.4 %copy-start.14 = (bf16[2,1,16,3328]{3,2,1,0:T(8,128)(2,1)}, bf16[2,1,16,3328]{3,2,1,0:T(8,128)(2,1)S(1)}, u32[]{:S(2)}) copy-start(bf16[2,1,16,3328]{3,2,1,0:T(8,128)(2,1)S(1)} %collective-permute-done.11.rest_10_) | copy-start | bytes 638980
  52.7 12.4 %collective-permute-start.14 = (bf16[2,3,16,3328]{3,2,1,0:T(8,128)(2,1)S(1)}, bf16[2,3,16,3328]{3,2,1,0:T(8,128)(2,1)}, u32[]{:S(2)}, u32[]{:S(2)}) collective-permute-start(bf16[2,3,16,3328]{3,2,1,0:T(8,128)(2,1)S(1)} %collective-permute-done.7.rest_6_), channel_id=1, source_target_pairs={{0,1},{1,0},{2,3},{3,2},{4,5},{5,4},{6,7},{7,6},{8,9},{9,8},{10,11... | collective-permute-start | bytes 1916936 | tf_op jit(solution)/shard_map/ppermute | solution.py:29
  53.0 12.1 %copy-start.15 = (bf16[2,1,16,3328]{3,2,1,0:T(8,128)(2,1)}, bf16[2,1,16,3328]{3,2,1,0:T(8,128)(2,1)S(1)}, u32[]{:S(2)}) copy-start(bf16[2,1,16,3328]{3,2,1,0:T(8,128)(2,1)S(1)} %collective-permute-done.9.rest_8_) | copy-start | bytes 638980
  53.0 12.1 %collective-permute-start.17 = (bf16[3,16,3328]{2,1,0:T(8,128)(2,1)S(1)}, bf16[3,16,3328]{2,1,0:T(8,128)(2,1)}, u32[]{:S(2)}, u32[]{:S(2)}) collective-permute-start(bf16[3,16,3328]{2,1,0:T(8,128)(2,1)S(1)} %slice_bitcast_fusion), channel_id=1, source_target_pairs={{0,4},{4,0},{8,12},{12,8},{16,20},{20,16},{24,28},{28,24},{1,5},{5... | collective-permute-start | bytes 958472 | tf_op jit(solution)/shard_map/ppermute | solution.py:29
  60.9 6.1 %copy-start.11 = (bf16[3,16,3328]{2,1,0:T(8,128)(2,1)}, bf16[3,16,3328]{2,1,0:T(8,128)(2,1)S(1)}, u32[]{:S(2)}) copy-start(bf16[3,16,3328]{2,1,0:T(8,128)(2,1)S(1)} %collective-permute-done.15.rest_14_) | copy-start | bytes 958468
  60.9 4.2 %collective-permute-start.16 = (bf16[3,16,3328]{2,1,0:T(8,128)(2,1)S(1)}, bf16[3,16,3328]{2,1,0:T(8,128)(2,1)}, u32[]{:S(2)}, u32[]{:S(2)}) collective-permute-start(bf16[3,16,3328]{2,1,0:T(8,128)(2,1)S(1)} %collective-permute-done.15.rest_14_), channel_id=1, source_target_pairs={{0,1},{1,0},{2,3},{3,2},{4,5},{5,4},{6,7},{7,6},{8,9},{9,8},{10,11... | collective-permute-start | bytes 958472 | tf_op jit(solution)/shard_map/ppermute | solution.py:29
  65.1 2.0 %collective-permute-start.18 = (bf16[3,16,3328]{2,1,0:T(8,128)(2,1)}, bf16[3,16,3328]{2,1,0:T(8,128)(2,1)}, u32[]{:S(2)}, u32[]{:S(2)}) collective-permute-start(bf16[3,16,3328]{2,1,0:T(8,128)(2,1)} %collective-permute-done.17.rest_16_), channel_id=1, source_target_pairs={{0,1},{1,0},{2,3},{3,2},{4,5},{5,4},{6,7},{7,6},{8,9},{9,8},{10,11... | collective-permute-start | bytes 958472 | tf_op jit(solution)/shard_map/ppermute | solution.py:29
  67.0 0.9 copy-start.6
  79.7 6.7 %collective-permute-start.19 = (f32[512,128]{1,0:T(8,128)S(1)}, f32[512,128]{1,0:T(8,128)S(1)}, u32[]{:S(2)}, u32[]{:S(2)}) collective-permute-start(f32[512,128]{1,0:T(8,128)S(1)} %constant_dynamic-slice_fusion.2), channel_id=1, source_target_pairs={{0,1},{1,0},{2,3},{3,2},{4,5},{5,4},{6,7},{7,6},{8,9},{9,8},{10,11... | collective-permute-start | bytes 786440 | tf_op jit(solution)/shard_map/ppermute | solution.py:29
  79.8 6.5 %copy-start.9 = (f32[1024,128]{1,0:T(8,128)S(1)}, f32[1024,128]{1,0:T(8,128)}, u32[]{:S(2)}) copy-start(f32[1024,128]{1,0:T(8,128)} %get-tuple-element.22) | copy-start | bytes 1572868
  79.9 31.8 %all-to-all-start.2 = ((bf16[8,416,128]{2,1,0:T(8,128)(2,1)}), bf16[8,416,128]{2,1,0:T(8,128)(2,1)S(1)}, u32[]{:S(2)}, u32[]{:S(2)}) async-start(bf16[8,416,128]{2,1,0:T(8,128)(2,1)} %bitcast.37), calls=%async_computation.2 | async-start | bytes 1703936 | tf_op jit(solution)/shard_map/all_to_all | solution.py:382
  86.4 5.5 %collective-permute-start.20 = (f32[256,128]{1,0:T(8,128)S(1)}, f32[256,128]{1,0:T(8,128)S(1)}, u32[]{:S(2)}, u32[]{:S(2)}) collective-permute-start(f32[256,128]{1,0:T(8,128)S(1)} %constant_dynamic-slice_fusion.1), channel_id=1, source_target_pairs={{0,2},{1,3},{2,0},{3,1},{4,6},{5,7},{6,4},{7,5},{8,10},{9,11},{10,... | collective-permute-start | bytes 393224 | tf_op jit(solution)/shard_map/ppermute | solution.py:29
  92.0 5.7 %collective-permute-start.21 = (f32[128,128]{1,0:T(8,128)S(1)}, f32[128,128]{1,0:T(8,128)S(1)}, u32[]{:S(2)}, u32[]{:S(2)}) collective-permute-start(f32[128,128]{1,0:T(8,128)S(1)} %constant_dynamic-slice_fusion), channel_id=1, source_target_pairs={{0,4},{4,0},{8,12},{12,8},{16,20},{20,16},{24,28},{28,24},{1,5},{5... | collective-permute-start | bytes 196616 | tf_op jit(solution)/shard_map/ppermute | solution.py:29
  97.7 5.0 %collective-permute-start.22 = (f32[128,128]{1,0:T(8,128)S(1)}, f32[128,128]{1,0:T(8,128)S(1)}, u32[]{:S(2)}, u32[]{:S(2)}) collective-permute-start(f32[128,128]{1,0:T(8,128)S(1)} %dynamic-slice_add_fusion.2), channel_id=1, source_target_pairs={{0,8},{4,12},{8,0},{12,4},{16,24},{20,28},{24,16},{28,20},{1,9},{5... | collective-permute-start | bytes 196616 | tf_op jit(solution)/shard_map/ppermute | solution.py:29
  102.7 8.9 %collective-permute-start.23 = (f32[128,128]{1,0:T(8,128)S(1)}, f32[128,128]{1,0:T(8,128)S(1)}, u32[]{:S(2)}, u32[]{:S(2)}) collective-permute-start(f32[128,128]{1,0:T(8,128)S(1)} %add.60), channel_id=1, source_target_pairs={{0,16},{4,20},{8,24},{12,28},{16,0},{20,4},{24,8},{28,12},{1,17},{... | collective-permute-start | bytes 196616 | tf_op jit(solution)/shard_map/ppermute | solution.py:29
  113.7 4.6 %collective-permute-start.24 = (f32[1024,128]{1,0:T(8,128)S(1)}, f32[1024,128]{1,0:T(8,128)}, u32[]{:S(2)}, u32[]{:S(2)}) collective-permute-start(f32[1024,128]{1,0:T(8,128)S(1)} %cold_sum.2), channel_id=1, source_target_pairs={{0,1},{1,0},{2,3},{3,2},{4,5},{5,4},{6,7},{7,6},{8,9},{9,8},{10,11... | collective-permute-start | bytes 1572872 | tf_op jit(solution)/shard_map/ppermute | solution.py:29
  113.8 4.5 %collective-permute-start.25 = (f32[128,128]{1,0:T(8,128)S(1)}, f32[128,128]{1,0:T(8,128)S(1)}, u32[]{:S(2)}, u32[]{:S(2)}) collective-permute-start(f32[128,128]{1,0:T(8,128)S(1)} %add.61), channel_id=1, source_target_pairs={{0,4},{4,0},{8,12},{12,8},{16,20},{20,16},{24,28},{28,24},{1,5},{5... | collective-permute-start | bytes 196616 | tf_op jit(solution)/shard_map/ppermute | solution.py:29
  119.4 9.3 %collective-permute-start.28 = (bf16[1024,128]{1,0:T(8,128)(2,1)S(1)}, bf16[1024,128]{1,0:T(8,128)(2,1)S(1)}, u32[]{:S(2)}, u32[]{:S(2)}) collective-permute-start(bf16[1024,128]{1,0:T(8,128)(2,1)S(1)} %add_convert_fusion), channel_id=1, source_target_pairs={{0,2},{1,3},{2,0},{3,1},{4,6},{5,7},{6,4},{7,5},{8,10},{9,11},{10,... | collective-permute-start | bytes 786440 | tf_op jit(solution)/shard_map/ppermute | solution.py:29
  119.8 10.3 %collective-permute-start.26 = (f32[256,128]{1,0:T(8,128)S(1)}, f32[256,128]{1,0:T(8,128)S(1)}, u32[]{:S(2)}, u32[]{:S(2)}) collective-permute-start(f32[256,128]{1,0:T(8,128)S(1)} %maximum_select_fusion.3), channel_id=1, source_target_pairs={{0,2},{1,3},{2,0},{3,1},{4,6},{5,7},{6,4},{7,5},{8,10},{9,11},{10,... | collective-permute-start | bytes 393224 | tf_op jit(solution)/shard_map/ppermute | solution.py:29
  128.7 3.2 %copy-start.12 = (bf16[1024,128]{1,0:T(8,128)(2,1)S(1)}, bf16[1024,128]{1,0:T(8,128)(2,1)}, u32[]{:S(2)}) copy-start(bf16[1024,128]{1,0:T(8,128)(2,1)} %param.17) | copy-start | bytes 786436
  128.7 5.1 %collective-permute-start.29 = (f32[1024,128]{1,0:T(8,128)S(1)}, f32[1024,128]{1,0:T(8,128)S(1)}, u32[]{:S(2)}, u32[]{:S(2)}) collective-permute-start(f32[1024,128]{1,0:T(8,128)S(1)} %convert_add_fusion), channel_id=1, source_target_pairs={{0,1},{1,0},{2,3},{3,2},{4,5},{5,4},{6,7},{7,6},{8,9},{9,8},{10,11... | collective-permute-start | bytes 1572872 | tf_op jit(solution)/shard_map/ppermute | solution.py:29
  130.2 1.7 %collective-permute-start.27 = (f32[512,128]{1,0:T(8,128)S(1)}, f32[512,128]{1,0:T(8,128)}, u32[]{:S(2)}, u32[]{:S(2)}) collective-permute-start(f32[512,128]{1,0:T(8,128)S(1)} %maximum_select_fusion.2), channel_id=1, source_target_pairs={{0,1},{1,0},{2,3},{3,2},{4,5},{5,4},{6,7},{7,6},{8,9},{9,8},{10,11... | collective-permute-start | bytes 786440 | tf_op jit(solution)/shard_map/ppermute | solution.py:29
  130.2 3.6 %copy-start.10 = (bf16[2048,128]{1,0:T(8,128)(2,1)S(1)}, bf16[2048,128]{1,0:T(8,128)(2,1)}, u32[]{:S(2)}) copy-start(bf16[2048,128]{1,0:T(8,128)(2,1)} %param.19) | copy-start | bytes 1572868

commit v6 on v5

--- a/solution.py
+++ b/solution.py
@@ -74,10 +74,12 @@
     )
 
 
-def hot_early(partial):
-    rep, data = lax.axis_index("rep"), lax.axis_index("dp")
-    total = partial
-    for axis, distance, index in (("rep", 1, rep % 2), ("rep", 2, rep // 2), ("dp", 1, data % 2)):
+def hot_early(mine, other):
+    total = mine + swap(other, "rep", 1)
+    for axis, distance, index in (
+        ("rep", 2, lax.axis_index("rep") // 2),
+        ("dp", 1, lax.axis_index("dp") % 2),
+    ):
         total = half_of(total, index, 2) + swap(half_of(total, 1 - index, 2), axis, distance)
     for distance in (2, 4):
         total = total + swap(total, "dp", distance)
@@ -201,6 +203,7 @@
 
 
 def cross_body(
+    core_ref,
     place_ref,
     id_ref,
     back_ref,
@@ -210,11 +213,10 @@
     weight_ref,
     *rest,
 ):
-    n_pieces = len(rest) - 12
+    n_pieces = len(rest) - 13
     pieces = rest[:n_pieces]
-    send_ref, hot_sum_ref, downs, ups, back, cold, upper, x_all, du_all, hits, hot_grad, sem = rest[
-        n_pieces:
-    ]
+    send_ref, hot_other_ref, hot_mine_ref, *scratch = rest[n_pieces:]
+    downs, ups, back, cold, upper, x_all, du_all, hits, hot_grad, sem = scratch
     copies = []
     whole = [piece for piece in pieces if len(piece.shape) == 4]
     parts = [piece for piece in pieces if len(piece.shape) == 3]
@@ -281,8 +283,11 @@
                 for k in range(start, start + rows):
                     back[pl.ds(place_ref[k], 1), :] = cold[pl.ds(k, 1), :]
     send_ref[...] = back[...].astype(BF)
-    both = jnp.dot(hits[...], hot_grad[...], preferred_element_type=F32)
-    hot_sum_ref[...] = both[:, :E] + both[:, E:]
+    half = HOT // 2
+    for core, out_ref in ((1 - core_ref[0], hot_other_ref), (core_ref[0], hot_mine_ref)):
+        rows_of = pl.ds(pl.multiple_of(core * half, half), half)
+        both = jnp.dot(hits[rows_of, :], hot_grad[...], preferred_element_type=F32)
+        out_ref[...] = both[:, :E] + both[:, E:]
 
 
 def cold_sum_body(n_data, capacity, first_ref, ask_ref, grad_ref, out_ref, hits):
@@ -350,10 +355,11 @@
     n_shards = sum(p.shape[-3] for p in (*whole, *down_rest))
     depth = cross_up.shape[0]
     rank = n_shards * depth
-    send, hot_partial = call(
+    core = lax.axis_index("rep") % 2
+    send, hot_other, hot_mine = call(
         cross_body,
-        (shape((places, E), BF), shape((HOT, E), F32)),
-        [SMEM] + [VMEM] * 6 + [ANY] * len(pieces),
+        (shape((places, E), BF), shape((HOT // 2, E), F32), shape((HOT // 2, E), F32)),
+        [SMEM, SMEM] + [VMEM] * 6 + [ANY] * len(pieces),
         [
             pltpu.VMEM((n_shards, depth, F), BF),
             pltpu.VMEM((n_shards, depth, F), BF),
@@ -370,6 +376,7 @@
         "cross",
         58,
     )(
+        core.reshape(1),
         place,
         hot_t,
         returned,
@@ -380,8 +387,7 @@
         *pieces,
     )
     incoming = lax.all_to_all(send, "dp", split_axis=0, concat_axis=0, tiled=True)
-    hot_share = hot_early(hot_partial)
-    core = lax.axis_index("rep") % 2
+    hot_share = hot_early(hot_mine, hot_other)
     incoming, hot_share = lax.optimization_barrier((incoming, hot_share))
 
     def cold_sum(rows_of, grads):
@@ -399,7 +405,6 @@
     mine = cold_sum(core, incoming)
     hot_share = paired(hot_share, swap(hot_share, "dp", 1), lax.axis_index("dp") % 2)
     mine = (mine + swap(others, "rep", 1)).astype(BF)
-    mine, hot_share = lax.optimization_barrier((mine, hot_share))
     mine = mine.astype(F32) + swap(mine, "rep", 2).astype(F32)
     hot_share = paired(hot_share, swap(hot_share, "rep", 2), lax.axis_index("rep") // 2)
     return tuple(paired(half, swap(half, "rep", 1), core) for half in (hot_share, mine))

time: 136 us -> 131 us (0.963)
  waiting for transfers between devices: 51.6 us -> 47.4 us
  starting transfers between devices: 45.7 us -> 49.2 us
  other arithmetic: 6.3 us -> 4.21 us
    ppermute x29, waiting for transfers between devices: 46.6 us -> 42.4 us  [swap(): return lax.ppermute(value, axis, [(i, i ^ distance) for i in range(size)])]
    ppermute x29, starting transfers between devices: 32.2 us -> 35.9 us  [swap(): return lax.ppermute(value, axis, [(i, i ^ distance) for i in range(size)])]
    pallas_call x1, Pallas kernels: 5.05 us -> 3.63 us  [small_step(): call(functools.partial(serve_body, n_data, capacity), shape((places, E),...]
    unnamed x34 -> x36, local copies, waits for them, and re-layouts: 4.38 us -> 4.33 us
  transfers between devices with their start and end apart: 33 -> 33, of which waited for: 14 -> 15; matrix products, arithmetic and copies ran while one was open for 3% -> 2% of each run, Pallas kernels for 8% -> 7%
where the time goes in v6:
time: 131 us; the launch traced here: 130 us
  starting transfers between devices  49.2 us (38%)
  waiting for transfers between devices  47.4 us (36%)
  Pallas kernels  21.9 us (17%)
  local copies, waits for them, and re-layouts  6.33 us (5%)
  other arithmetic  4.21 us (3%)
    ppermute x29, waiting for transfers between devices, swap(): return lax.ppermute(value, axis, [(i, i ^ distance) for i in range(size)])  42.4 us
    ppermute x29, starting transfers between devices, swap(): return lax.ppermute(value, axis, [(i, i ^ distance) for i in range(size)])  35.9 us
    pallas_call x1, Pallas kernels, small_step(): call(cross_body, (shape((places, E), BF), shape((HOT // 2, E), F32), shap...  10.8 us
    all_to_all x1, starting transfers between devices, small_step(): lax.all_to_all(send, 'dp', split_axis=0, concat_axis=0, tiled=True)  5.66 us
    all_to_all x1, waiting for transfers between devices, small_step(): asked = lax.all_to_all(ask, 'dp', split_axis=0, concat_axis=0, tiled=True)  5.05 us
    unnamed x36, local copies, waits for them, and re-layouts  4.33 us
    all_to_all x1, starting transfers between devices, small_step(): lax.all_to_all(found, 'dp', split_axis=0, concat_axis=0, tiled=True)  4.13 us
    pallas_call x2, Pallas kernels, cold_sum(): call(functools.partial(cold_sum_body, n_data, capacity), shape((owned //...  3.98 us
  transfers between devices with their start and end apart: 33, of which 15 were waited for; matrix products, arithmetic and copies ran while one was open for 2% of the time, Pallas kernels for 7%

profile of v6, /device:TPU:0, one launch (start us, length us, event | category | flops | bytes accessed | tf_op | source)
XLA Modules:
  0.0 130.1 jit_solution(14261690305269672409)
XLA Ops:
  0.6 1.0 maximum_bitcast_fusion.rest_0_
  1.7 3.0 %collective-permute-start = (bf16[2,1,16,3328]{3,2,1,0:T(8,128)(2,1)S(1)}, bf16[2,1,16,3328]{3,2,1,0:T(8,128)(2,1)}, u32[]{:S(2)}, u32[]{:S(2)}) collective-permute-start(bf16[2,1,16,3328]{3,2,1,0:T(8,128)(2,1)S(1)} %maximum_bitcast_fusion.rest_0_), channel_id=1, source_target_pairs={{0,2},{1,3},{2,0},{3,1},{4,6},{5,7},{6,4},{7,5},{8,10},{9,11},{10,... | collective-permute-start | bytes 638984 | tf_op jit(solution)/shard_map/ppermute | solution.py:29
  4.7 1.5 %collective-permute-start.1 = (bf16[2,1,16,3328]{3,2,1,0:T(8,128)(2,1)S(1)}, bf16[2,1,16,3328]{3,2,1,0:T(8,128)(2,1)}, u32[]{:S(2)}, u32[]{:S(2)}) collective-permute-start(bf16[2,1,16,3328]{3,2,1,0:T(8,128)(2,1)S(1)} %maximum_bitcast_fusion.rest_0_), channel_id=1, source_target_pairs={{0,4},{4,0},{8,12},{12,8},{16,20},{20,16},{24,28},{28,24},{1,5},{5... | collective-permute-start | bytes 638984 | tf_op jit(solution)/shard_map/ppermute | solution.py:29
  6.2 2.0 %collective-permute-start.3 = (bf16[2,1,16,3328]{3,2,1,0:T(8,128)(2,1)S(1)}, bf16[2,1,16,3328]{3,2,1,0:T(8,128)(2,1)S(1)}, u32[]{:S(2)}, u32[]{:S(2)}) collective-permute-start(bf16[2,1,16,3328]{3,2,1,0:T(8,128)(2,1)S(1)} %maximum_bitcast_fusion.rest_0_), channel_id=1, source_target_pairs={{0,8},{4,12},{8,0},{12,4},{16,24},{20,28},{24,16},{28,20},{1,9},{5... | collective-permute-start | bytes 638984 | tf_op jit(solution)/shard_map/ppermute | solution.py:29
  8.3 2.6 %collective-permute-start.4 = (bf16[2,1,16,3328]{3,2,1,0:T(8,128)(2,1)S(1)}, bf16[2,1,16,3328]{3,2,1,0:T(8,128)(2,1)S(1)}, u32[]{:S(2)}, u32[]{:S(2)}) collective-permute-start(bf16[2,1,16,3328]{3,2,1,0:T(8,128)(2,1)S(1)} %maximum_bitcast_fusion.rest_0_), channel_id=1, source_target_pairs={{0,16},{4,20},{8,24},{12,28},{16,0},{20,4},{24,8},{28,12},{1,17},{... | collective-permute-start | bytes 638984 | tf_op jit(solution)/shard_map/ppermute | solution.py:29
  10.8 0.0 collective-permute-done.rest_1_
  10.9 4.2 %collective-permute-start.5 = (bf16[2,1,16,3328]{3,2,1,0:T(8,128)(2,1)S(1)}, bf16[2,1,16,3328]{3,2,1,0:T(8,128)(2,1)S(1)}, u32[]{:S(2)}, u32[]{:S(2)}) collective-permute-start(bf16[2,1,16,3328]{3,2,1,0:T(8,128)(2,1)S(1)} %maximum_bitcast_fusion.rest_0_), channel_id=1, source_target_pairs={{0,24},{4,28},{8,16},{12,20},{16,8},{20,12},{24,0},{28,4},{1,25},{... | collective-permute-start | bytes 638984 | tf_op jit(solution)/shard_map/ppermute | solution.py:29
  15.0 0.7 reduce
  15.8 0.2 reshape.35
  16.0 0.1 copy.14
  16.0 0.6 copy-done.4
  16.7 1.2 route.1
  17.9 0.6 copy-done.5
  18.5 3.5 %all-to-all-start = ((s32[8,4,128]{2,1,0:T(4,128)}), s32[8,4,128]{2,1,0:T(4,128)S(1)}, u32[]{:S(2)}, u32[]{:S(2)}) async-start(s32[8,4,128]{2,1,0:T(4,128)} %bitcast.5), calls=%async_computation | async-start | bytes 32768 | tf_op jit(solution)/shard_map/all_to_all | solution.py:330
  22.0 2.2 %hot_rows.1.hot_ref = bf16[1664,128]{1,0:T(8,128)(2,1)S(1)} custom-call(s32[1664]{0:T(1024)S(1)} %bitcast.34, f32[1024,128]{1,0:T(8,128)S(1)} %copy-done.1), custom_call_target="tpu_custom_call" | custom-call | flops 1 | bytes 1 | tf_op jit(solution)/shard_map/hot_rows/pallas_call | solution.py:333
  24.2 0.7 copy-done.2
  25.0 5.0 %all-to-all-done = s32[8,4,128]{2,1,0:T(4,128)S(1)} async-done(((s32[8,4,128]{2,1,0:T(4,128)}), s32[8,4,128]{2,1,0:T(4,128)S(1)}, u32[]{:S(2)}, u32[]{:S(2)}) %all-to-all-start) | async-done | bytes 16416 | tf_op jit(solution)/shard_map/all_to_all | solution.py:330
  30.0 0.7 constant_dynamic-update-slice_fusion.2
  30.7 0.7 constant_dynamic-update-slice_fusion.1
  31.4 0.7 constant_dynamic-update-slice_fusion.rest_4_
  32.1 0.6 collective-permute-start.7
  32.8 1.5 %collective-permute-start.6 = (bf16[2,3,16,3328]{3,2,1,0:T(8,128)(2,1)}, bf16[2,3,16,3328]{3,2,1,0:T(8,128)(2,1)}, u32[]{:S(2)}, u32[]{:S(2)}) collective-permute-start(bf16[2,3,16,3328]{3,2,1,0:T(8,128)(2,1)} %constant_dynamic-update-slice_fusion.rest_4_), channel_id=1, source_target_pairs={{0,2},{1,3},{2,0},{3,1},{4,6},{5,7},{6,4},{7,5},{8,10},{9,11},{10,... | collective-permute-start | bytes 1916936 | tf_op jit(solution)/shard_map/ppermute | solution.py:29
  34.3 0.2 collective-permute-start.12
  34.5 3.6 %serve.1 = bf16[3328,128]{1,0:T(8,128)(2,1)} custom-call(s32[4096]{0:T(1024)S(1)} %bitcast.29, f32[2048,128]{1,0:T(8,128)S(1)} %copy-done), custom_call_target="tpu_custom_call" | custom-call | flops 1 | bytes 1 | tf_op jit(solution)/shard_map/serve/pallas_call | solution.py:344
  38.1 4.1 %all-to-all-start.1 = ((bf16[8,416,128]{2,1,0:T(8,128)(2,1)}), bf16[8,416,128]{2,1,0:T(8,128)(2,1)S(1)}, u32[]{:S(2)}, u32[]{:S(2)}) async-start(bf16[8,416,128]{2,1,0:T(8,128)(2,1)} %bitcast.13), calls=%async_computation.1 | async-start | bytes 1703936 | tf_op jit(solution)/shard_map/all_to_all | solution.py:352
  42.3 0.0 collective-permute-start.10
  42.3 6.4 %collective-permute-done.7.rest_6_ = bf16[2,3,16,3328]{3,2,1,0:T(8,128)(2,1)S(1)} collective-permute-done((bf16[2,3,16,3328]{3,2,1,0:T(8,128)(2,1)}, bf16[2,3,16,3328]{3,2,1,0:T(8,128)(2,1)S(1)}, u32[]{:S(2)}, u32[]{:S(2)}) %collective-permute-start.7) | collective-permute-done | bytes 639008 | tf_op jit(solution)/shard_map/ppermute | solution.py:29
  48.8 1.1 collective-permute-done.6.rest_5_
  49.9 1.0 slice_bitcast_fusion
  50.9 3.0 %collective-permute-start.15 = (bf16[3,16,3328]{2,1,0:T(8,128)(2,1)S(1)}, bf16[3,16,3328]{2,1,0:T(8,128)(2,1)S(1)}, u32[]{:S(2)}, u32[]{:S(2)}) collective-permute-start(bf16[3,16,3328]{2,1,0:T(8,128)(2,1)S(1)} %slice_bitcast_fusion.1), channel_id=1, source_target_pairs={{0,2},{1,3},{2,0},{3,1},{4,6},{5,7},{6,4},{7,5},{8,10},{9,11},{10,... | collective-permute-start | bytes 958472 | tf_op jit(solution)/shard_map/ppermute | solution.py:29
  54.0 0.5 collective-permute-start.14
  54.5 2.4 %collective-permute-start.17 = (bf16[3,16,3328]{2,1,0:T(8,128)(2,1)S(1)}, bf16[3,16,3328]{2,1,0:T(8,128)(2,1)}, u32[]{:S(2)}, u32[]{:S(2)}) collective-permute-start(bf16[3,16,3328]{2,1,0:T(8,128)(2,1)S(1)} %slice_bitcast_fusion), channel_id=1, source_target_pairs={{0,4},{4,0},{8,12},{12,8},{16,20},{20,16},{24,28},{28,24},{1,5},{5... | collective-permute-start | bytes 958472 | tf_op jit(solution)/shard_map/ppermute | solution.py:29
  56.8 4.8 %collective-permute-done.15.rest_14_ = bf16[3,16,3328]{2,1,0:T(8,128)(2,1)S(1)} collective-permute-done((bf16[3,16,3328]{2,1,0:T(8,128)(2,1)S(1)}, bf16[3,16,3328]{2,1,0:T(8,128)(2,1)S(1)}, u32[]{:S(2)}, u32[]{:S(2)}) %collective-permute-start.15) | collective-permute-done | bytes 319520 | tf_op jit(solution)/shard_map/ppermute | solution.py:29
  61.7 4.5 %collective-permute-done.17.rest_16_ = bf16[3,16,3328]{2,1,0:T(8,128)(2,1)} collective-permute-done((bf16[3,16,3328]{2,1,0:T(8,128)(2,1)S(1)}, bf16[3,16,3328]{2,1,0:T(8,128)(2,1)}, u32[]{:S(2)}, u32[]{:S(2)}) %collective-permute-start.17) | collective-permute-done | bytes 319520 | tf_op jit(solution)/shard_map/ppermute | solution.py:29
  66.2 1.9 %collective-permute-done.18.rest_17_ = bf16[3,16,3328]{2,1,0:T(8,128)(2,1)} collective-permute-done((bf16[3,16,3328]{2,1,0:T(8,128)(2,1)}, bf16[3,16,3328]{2,1,0:T(8,128)(2,1)}, u32[]{:S(2)}, u32[]{:S(2)}) %collective-permute-start.18) | collective-permute-done | bytes 319520 | tf_op jit(solution)/shard_map/ppermute | solution.py:29
  68.1 0.9 copy-done.6
  69.0 10.8 %cross.1 = (bf16[3328,128]{1,0:T(8,128)(2,1)}, f32[512,128]{1,0:T(8,128)}, f32[512,128]{1,0:T(8,128)}) custom-call(s32[1]{0:T(128)} %bitcast.core_ref, s32[2048]{0:T(1024)} %bitcast.36, s32[13,128]{1,0:T(8,128)} %bitcast.33, bf16[3328,128]{1,0:T(8,128)(2,1)} %bitcast.37, bf16[1664,128]{1,0:T(8,128)(2,1)} %copy-done.2, s32[1,128]{1,0:T(1,128)} %bitcast.41, ...), custom_call_target="tpu_custom_call" | custom-call | flops 1744830464 | bytes 20000000 | tf_op jit(solution)/shard_map/cross/pallas_call | solution.py:359
  79.8 5.7 %all-to-all-start.2 = ((bf16[8,416,128]{2,1,0:T(8,128)(2,1)}), bf16[8,416,128]{2,1,0:T(8,128)(2,1)S(1)}, u32[]{:S(2)}, u32[]{:S(2)}) async-start(bf16[8,416,128]{2,1,0:T(8,128)(2,1)} %bitcast.38), calls=%async_computation.2 | async-start | bytes 1703936 | tf_op jit(solution)/shard_map/all_to_all | solution.py:389
  85.5 0.1 collective-permute-start.19
  85.6 1.5 %collective-permute-done.19 = f32[512,128]{1,0:T(8,128)S(1)} collective-permute-done((f32[512,128]{1,0:T(8,128)S(1)}, f32[512,128]{1,0:T(8,128)S(1)}, u32[]{:S(2)}, u32[]{:S(2)}) %collective-permute-start.19) | collective-permute-done | bytes 262176 | tf_op jit(solution)/shard_map/ppermute | solution.py:29
  87.2 0.5 collective-permute-start.20
  87.6 5.1 %collective-permute-done.20 = f32[256,128]{1,0:T(8,128)S(1)} collective-permute-done((f32[256,128]{1,0:T(8,128)S(1)}, f32[256,128]{1,0:T(8,128)S(1)}, u32[]{:S(2)}, u32[]{:S(2)}) %collective-permute-start.20) | collective-permute-done | bytes 131104 | tf_op jit(solution)/shard_map/ppermute | solution.py:29
  92.8 2.0 %collective-permute-start.21 = (f32[128,128]{1,0:T(8,128)S(1)}, f32[128,128]{1,0:T(8,128)S(1)}, u32[]{:S(2)}, u32[]{:S(2)}) collective-permute-start(f32[128,128]{1,0:T(8,128)S(1)} %constant_dynamic-slice_fusion), channel_id=1, source_target_pairs={{0,4},{4,0},{8,12},{12,8},{16,20},{20,16},{24,28},{28,24},{1,5},{5... | collective-permute-start | bytes 196616 | tf_op jit(solution)/shard_map/ppermute | solution.py:29
  94.8 2.8 %collective-permute-done.21 = f32[128,128]{1,0:T(8,128)S(1)} collective-permute-done((f32[128,128]{1,0:T(8,128)S(1)}, f32[128,128]{1,0:T(8,128)S(1)}, u32[]{:S(2)}, u32[]{:S(2)}) %collective-permute-start.21) | collective-permute-done | bytes 65568 | tf_op jit(solution)/shard_map/ppermute | solution.py:29
  97.6 3.8 %collective-permute-start.22 = (f32[128,128]{1,0:T(8,128)S(1)}, f32[128,128]{1,0:T(8,128)S(1)}, u32[]{:S(2)}, u32[]{:S(2)}) collective-permute-start(f32[128,128]{1,0:T(8,128)S(1)} %dynamic-slice_add_fusion.1), channel_id=1, source_target_pairs={{0,8},{4,12},{8,0},{12,4},{16,24},{20,28},{24,16},{28,20},{1,9},{5... | collective-permute-start | bytes 196616 | tf_op jit(solution)/shard_map/ppermute | solution.py:29
  101.4 2.2 %collective-permute-done.22 = f32[128,128]{1,0:T(8,128)S(1)} collective-permute-done((f32[128,128]{1,0:T(8,128)S(1)}, f32[128,128]{1,0:T(8,128)S(1)}, u32[]{:S(2)}, u32[]{:S(2)}) %collective-permute-start.22) | collective-permute-done | bytes 65568 | tf_op jit(solution)/shard_map/ppermute | solution.py:29
  103.7 4.5 %collective-permute-start.23 = (f32[128,128]{1,0:T(8,128)S(1)}, f32[128,128]{1,0:T(8,128)S(1)}, u32[]{:S(2)}, u32[]{:S(2)}) collective-permute-start(f32[128,128]{1,0:T(8,128)S(1)} %add.51), channel_id=1, source_target_pairs={{0,16},{4,20},{8,24},{12,28},{16,0},{20,4},{24,8},{28,12},{1,17},{... | collective-permute-start | bytes 196616 | tf_op jit(solution)/shard_map/ppermute | solution.py:29
  108.2 2.3 %collective-permute-done.23 = f32[128,128]{1,0:T(8,128)S(1)} collective-permute-done((f32[128,128]{1,0:T(8,128)S(1)}, f32[128,128]{1,0:T(8,128)S(1)}, u32[]{:S(2)}, u32[]{:S(2)}) %collective-permute-start.23) | collective-permute-done | bytes 65568 | tf_op jit(solution)/shard_map/ppermute | solution.py:29
  110.5 2.0 %cold_sum.2 = f32[1024,128]{1,0:T(8,128)S(1)} custom-call(s32[1]{0:T(128)} %bitcast.21.first_ref, s32[32,128]{1,0:T(8,128)S(1)} %bitcast.30, bf16[3328,128]{1,0:T(8,128)(2,1)S(1)} %bitcast.27), custom_call_target="tpu_custom_call" | custom-call | flops 1000000000 | bytes 10000000 | tf_op jit(solution)/shard_map/cold_sum/pallas_call | solution.py:394
  112.5 0.1 collective-permute-start.27
  112.6 2.0 %cold_sum.3 = f32[1024,128]{1,0:T(8,128)S(1)} custom-call(s32[1]{0:T(128)} %bitcast.20.first_ref, s32[32,128]{1,0:T(8,128)S(1)} %bitcast.31, bf16[3328,128]{1,0:T(8,128)(2,1)S(1)} %bitcast.28), custom_call_target="tpu_custom_call" | custom-call | flops 1000000000 | bytes 10000000 | tf_op jit(solution)/shard_map/cold_sum/pallas_call | solution.py:394
  114.6 0.1 add_convert_fusion
  114.6 0.5 collective-permute-start.28
  115.1 1.1 collective-permute-start.24
  116.2 3.2 %collective-permute-done.24 = f32[128,128]{1,0:T(8,128)S(1)} collective-permute-done((f32[128,128]{1,0:T(8,128)S(1)}, f32[128,128]{1,0:T(8,128)S(1)}, u32[]{:S(2)}, u32[]{:S(2)}) %collective-permute-start.24) | collective-permute-done | bytes 65568 | tf_op jit(solution)/shard_map/ppermute | solution.py:29
  119.4 1.7 %collective-permute-start.25 = (f32[256,128]{1,0:T(8,128)S(1)}, f32[256,128]{1,0:T(8,128)S(1)}, u32[]{:S(2)}, u32[]{:S(2)}) collective-permute-start(f32[256,128]{1,0:T(8,128)S(1)} %maximum_select_fusion.3), channel_id=1, source_target_pairs={{0,2},{1,3},{2,0},{3,1},{4,6},{5,7},{6,4},{7,5},{8,10},{9,11},{10,... | collective-permute-start | bytes 393224 | tf_op jit(solution)/shard_map/ppermute | solution.py:29
  121.1 2.7 %collective-permute-done.28 = bf16[1024,128]{1,0:T(8,128)(2,1)S(1)} collective-permute-done((bf16[1024,128]{1,0:T(8,128)(2,1)S(1)}, bf16[1024,128]{1,0:T(8,128)(2,1)S(1)}, u32[]{:S(2)}, u32[]{:S(2)}) %collective-permute-start.28) | collective-permute-done | bytes 262176 | tf_op jit(solution)/shard_map/ppermute | solution.py:29
  123.8 0.1 convert_add_fusion
  123.9 0.1 collective-permute-start.29
  124.0 2.3 %collective-permute-done.25 = f32[256,128]{1,0:T(8,128)S(1)} collective-permute-done((f32[256,128]{1,0:T(8,128)S(1)}, f32[256,128]{1,0:T(8,128)S(1)}, u32[]{:S(2)}, u32[]{:S(2)}) %collective-permute-start.25) | collective-permute-done | bytes 131104 | tf_op jit(solution)/shard_map/ppermute | solution.py:29
  126.2 0.1 collective-permute-start.26
  126.3 1.5 %collective-permute-done.26 = f32[512,128]{1,0:T(8,128)S(1)} collective-permute-done((f32[512,128]{1,0:T(8,128)S(1)}, f32[512,128]{1,0:T(8,128)S(1)}, u32[]{:S(2)}, u32[]{:S(2)}) %collective-permute-start.26) | collective-permute-done | bytes 262176 | tf_op jit(solution)/shard_map/ppermute | solution.py:29
  127.8 1.0 multiply_subtract_fusion.1
  128.8 1.3 %multiply_subtract_fusion = f32[2048,128]{1,0:T(8,128)} fusion(f32[2048,128]{1,0:T(8,128)S(1)} %copy-done, bf16[2048,128]{1,0:T(8,128)(2,1)S(1)} %copy-done.9, f32[1024,128]{1,0:T(8,128)S(1)} %convert_add_fusion, f32[1024,128]{1,0:T(8,128)S(1)} %collective-permute-done.29, pred[]{:T(512)S(6)} %eq.14), kind=kLoop, calls=%fused_computation.1 | loop fusion | flops 2883584 | bytes 3670017 | tf_op jit(solution)/shard_map/sub | solution.py:20
  (64 shorter events, 0.3 us)
Async XLA Ops:
  0.6 21.3 %copy-start.1 = (f32[1024,128]{1,0:T(8,128)S(1)}, f32[1024,128]{1,0:T(8,128)}, u32[]{:S(2)}) copy-start(f32[1024,128]{1,0:T(8,128)} %table_ref.2) | copy-start | bytes 1572868
  1.7 31.1 %copy-start.8 = (bf16[2,1,16,3328]{3,2,1,0:T(8,128)(2,1)}, bf16[2,1,16,3328]{3,2,1,0:T(8,128)(2,1)S(1)}, u32[]{:S(2)}) copy-start(bf16[2,1,16,3328]{3,2,1,0:T(8,128)(2,1)S(1)} %maximum_bitcast_fusion.rest_0_) | copy-start | bytes 638980
  1.7 9.2 %collective-permute-start = (bf16[2,1,16,3328]{3,2,1,0:T(8,128)(2,1)S(1)}, bf16[2,1,16,3328]{3,2,1,0:T(8,128)(2,1)}, u32[]{:S(2)}, u32[]{:S(2)}) collective-permute-start(bf16[2,1,16,3328]{3,2,1,0:T(8,128)(2,1)S(1)} %maximum_bitcast_fusion.rest_0_), channel_id=1, source_target_pairs={{0,2},{1,3},{2,0},{3,1},{4,6},{5,7},{6,4},{7,5},{8,10},{9,11},{10,... | collective-permute-start | bytes 638984 | tf_op jit(solution)/shard_map/ppermute | solution.py:29
  4.7 25.3 %collective-permute-start.1 = (bf16[2,1,16,3328]{3,2,1,0:T(8,128)(2,1)S(1)}, bf16[2,1,16,3328]{3,2,1,0:T(8,128)(2,1)}, u32[]{:S(2)}, u32[]{:S(2)}) collective-permute-start(bf16[2,1,16,3328]{3,2,1,0:T(8,128)(2,1)S(1)} %maximum_bitcast_fusion.rest_0_), channel_id=1, source_target_pairs={{0,4},{4,0},{8,12},{12,8},{16,20},{20,16},{24,28},{28,24},{1,5},{5... | collective-permute-start | bytes 638984 | tf_op jit(solution)/shard_map/ppermute | solution.py:29
  6.2 23.8 %collective-permute-start.2 = (bf16[2,1,16,3328]{3,2,1,0:T(8,128)(2,1)S(1)}, bf16[2,1,16,3328]{3,2,1,0:T(8,128)(2,1)}, u32[]{:S(2)}, u32[]{:S(2)}) collective-permute-start(bf16[2,1,16,3328]{3,2,1,0:T(8,128)(2,1)S(1)} %maximum_bitcast_fusion.rest_0_), channel_id=1, source_target_pairs={{0,6},{1,7},{2,4},{3,5},{4,2},{5,3},{6,0},{7,1},{8,14},{9,15},{10,... | collective-permute-start | bytes 638984 | tf_op jit(solution)/shard_map/ppermute | solution.py:46
  6.2 23.8 %collective-permute-start.3 = (bf16[2,1,16,3328]{3,2,1,0:T(8,128)(2,1)S(1)}, bf16[2,1,16,3328]{3,2,1,0:T(8,128)(2,1)S(1)}, u32[]{:S(2)}, u32[]{:S(2)}) collective-permute-start(bf16[2,1,16,3328]{3,2,1,0:T(8,128)(2,1)S(1)} %maximum_bitcast_fusion.rest_0_), channel_id=1, source_target_pairs={{0,8},{4,12},{8,0},{12,4},{16,24},{20,28},{24,16},{28,20},{1,9},{5... | collective-permute-start | bytes 638984 | tf_op jit(solution)/shard_map/ppermute | solution.py:29
  8.3 21.8 %collective-permute-start.4 = (bf16[2,1,16,3328]{3,2,1,0:T(8,128)(2,1)S(1)}, bf16[2,1,16,3328]{3,2,1,0:T(8,128)(2,1)S(1)}, u32[]{:S(2)}, u32[]{:S(2)}) collective-permute-start(bf16[2,1,16,3328]{3,2,1,0:T(8,128)(2,1)S(1)} %maximum_bitcast_fusion.rest_0_), channel_id=1, source_target_pairs={{0,16},{4,20},{8,24},{12,28},{16,0},{20,4},{24,8},{28,12},{1,17},{... | collective-permute-start | bytes 638984 | tf_op jit(solution)/shard_map/ppermute | solution.py:29
  10.9 19.2 %collective-permute-start.5 = (bf16[2,1,16,3328]{3,2,1,0:T(8,128)(2,1)S(1)}, bf16[2,1,16,3328]{3,2,1,0:T(8,128)(2,1)S(1)}, u32[]{:S(2)}, u32[]{:S(2)}) collective-permute-start(bf16[2,1,16,3328]{3,2,1,0:T(8,128)(2,1)S(1)} %maximum_bitcast_fusion.rest_0_), channel_id=1, source_target_pairs={{0,24},{4,28},{8,16},{12,20},{16,8},{20,12},{24,0},{28,4},{1,25},{... | collective-permute-start | bytes 638984 | tf_op jit(solution)/shard_map/ppermute | solution.py:29
  16.0 0.7 copy-start.4
  17.9 0.6 copy-start.5
  18.5 3.5 %copy-start.3 = (s32[128,13]{0,1:T(8,128)S(1)}, s32[128,13]{0,1:T(8,128)}, u32[]{:S(2)}) copy-start(s32[128,13]{0,1:T(8,128)} %param.12) | copy-start | bytes 19972
  18.5 11.5 %all-to-all-start = ((s32[8,4,128]{2,1,0:T(4,128)}), s32[8,4,128]{2,1,0:T(4,128)S(1)}, u32[]{:S(2)}, u32[]{:S(2)}) async-start(s32[8,4,128]{2,1,0:T(4,128)} %bitcast.5), calls=%async_computation | async-start | bytes 32768 | tf_op jit(solution)/shard_map/all_to_all | solution.py:330
  22.0 12.5 %copy-start = (f32[2048,128]{1,0:T(8,128)S(1)}, f32[2048,128]{1,0:T(8,128)}, u32[]{:S(2)}) copy-start(f32[2048,128]{1,0:T(8,128)} %table_ref.3) | copy-start | bytes 3145732
  24.2 0.8 copy-start.2
  32.1 16.6 %collective-permute-start.7 = (bf16[2,3,16,3328]{3,2,1,0:T(8,128)(2,1)}, bf16[2,3,16,3328]{3,2,1,0:T(8,128)(2,1)S(1)}, u32[]{:S(2)}, u32[]{:S(2)}) collective-permute-start(bf16[2,3,16,3328]{3,2,1,0:T(8,128)(2,1)} %constant_dynamic-update-slice_fusion.rest_4_), channel_id=1, source_target_pairs={{0,4},{4,0},{8,12},{12,8},{16,20},{20,16},{24,28},{28,24},{1,5},{5... | collective-permute-start | bytes 1916936 | tf_op jit(solution)/shard_map/ppermute | solution.py:29
  32.8 18.1 %collective-permute-start.8 = (bf16[2,1,16,3328]{3,2,1,0:T(8,128)(2,1)S(1)}, bf16[2,1,16,3328]{3,2,1,0:T(8,128)(2,1)}, u32[]{:S(2)}, u32[]{:S(2)}) collective-permute-start(bf16[2,1,16,3328]{3,2,1,0:T(8,128)(2,1)S(1)} %maximum_bitcast_fusion.rest_0_), channel_id=1, source_target_pairs={{0,1},{1,0},{2,3},{3,2},{4,5},{5,4},{6,7},{7,6},{8,9},{9,8},{10,11... | collective-permute-start | bytes 638984 | tf_op jit(solution)/shard_map/ppermute | solution.py:29
  32.8 17.1 %collective-permute-start.6 = (bf16[2,3,16,3328]{3,2,1,0:T(8,128)(2,1)}, bf16[2,3,16,3328]{3,2,1,0:T(8,128)(2,1)}, u32[]{:S(2)}, u32[]{:S(2)}) collective-permute-start(bf16[2,3,16,3328]{3,2,1,0:T(8,128)(2,1)} %constant_dynamic-update-slice_fusion.rest_4_), channel_id=1, source_target_pairs={{0,2},{1,3},{2,0},{3,1},{4,6},{5,7},{6,4},{7,5},{8,10},{9,11},{10,... | collective-permute-start | bytes 1916936 | tf_op jit(solution)/shard_map/ppermute | solution.py:29
  34.3 31.9 %collective-permute-start.12 = (bf16[2,3,16,3328]{3,2,1,0:T(8,128)(2,1)}, bf16[2,3,16,3328]{3,2,1,0:T(8,128)(2,1)}, u32[]{:S(2)}, u32[]{:S(2)}) collective-permute-start(bf16[2,3,16,3328]{3,2,1,0:T(8,128)(2,1)} %constant_dynamic-update-slice_fusion.rest_4_), channel_id=1, source_target_pairs={{0,1},{1,0},{2,3},{3,2},{4,5},{5,4},{6,7},{7,6},{8,9},{9,8},{10,11... | collective-permute-start | bytes 1916936 | tf_op jit(solution)/shard_map/ppermute | solution.py:29
  38.1 29.9 %all-to-all-start.1 = ((bf16[8,416,128]{2,1,0:T(8,128)(2,1)}), bf16[8,416,128]{2,1,0:T(8,128)(2,1)S(1)}, u32[]{:S(2)}, u32[]{:S(2)}) async-start(bf16[8,416,128]{2,1,0:T(8,128)(2,1)} %bitcast.13), calls=%async_computation.1 | async-start | bytes 1703936 | tf_op jit(solution)/shard_map/all_to_all | solution.py:352
  42.3 11.7 %collective-permute-start.10 = (bf16[2,1,16,3328]{3,2,1,0:T(8,128)(2,1)}, bf16[2,1,16,3328]{3,2,1,0:T(8,128)(2,1)S(1)}, u32[]{:S(2)}, u32[]{:S(2)}) collective-permute-start(bf16[2,1,16,3328]{3,2,1,0:T(8,128)(2,1)} %collective-permute-done.1.rest_2_), channel_id=1, source_target_pairs={{0,1},{1,0},{2,3},{3,2},{4,5},{5,4},{6,7},{7,6},{8,9},{9,8},{10,11... | collective-permute-start | bytes 638984 | tf_op jit(solution)/shard_map/ppermute | solution.py:29
  48.7 17.4 %copy-start.7 = (bf16[2,3,16,3328]{3,2,1,0:T(8,128)(2,1)}, bf16[2,3,16,3328]{3,2,1,0:T(8,128)(2,1)S(1)}, u32[]{:S(2)}) copy-start(bf16[2,3,16,3328]{3,2,1,0:T(8,128)(2,1)S(1)} %collective-permute-done.7.rest_6_) | copy-start | bytes 1916932
  48.7 5.2 %collective-permute-start.11 = (bf16[2,1,16,3328]{3,2,1,0:T(8,128)(2,1)}, bf16[2,1,16,3328]{3,2,1,0:T(8,128)(2,1)S(1)}, u32[]{:S(2)}, u32[]{:S(2)}) collective-permute-start(bf16[2,1,16,3328]{3,2,1,0:T(8,128)(2,1)} %collective-permute-done.2.rest_3_), channel_id=1, source_target_pairs={{0,1},{1,0},{2,3},{3,2},{4,5},{5,4},{6,7},{7,6},{8,9},{9,8},{10,11... | collective-permute-start | bytes 638984 | tf_op jit(solution)/shard_map/ppermute | solution.py:29
  49.9 4.6 %collective-permute-start.9 = (bf16[2,1,16,3328]{3,2,1,0:T(8,128)(2,1)}, bf16[2,1,16,3328]{3,2,1,0:T(8,128)(2,1)S(1)}, u32[]{:S(2)}, u32[]{:S(2)}) collective-permute-start(bf16[2,1,16,3328]{3,2,1,0:T(8,128)(2,1)} %collective-permute-done.rest_1_), channel_id=1, source_target_pairs={{0,1},{1,0},{2,3},{3,2},{4,5},{5,4},{6,7},{7,6},{8,9},{9,8},{10,11... | collective-permute-start | bytes 638984 | tf_op jit(solution)/shard_map/ppermute | solution.py:29
  50.9 10.7 %collective-permute-start.15 = (bf16[3,16,3328]{2,1,0:T(8,128)(2,1)S(1)}, bf16[3,16,3328]{2,1,0:T(8,128)(2,1)S(1)}, u32[]{:S(2)}, u32[]{:S(2)}) collective-permute-start(bf16[3,16,3328]{2,1,0:T(8,128)(2,1)S(1)} %slice_bitcast_fusion.1), channel_id=1, source_target_pairs={{0,2},{1,3},{2,0},{3,1},{4,6},{5,7},{6,4},{7,5},{8,10},{9,11},{10,... | collective-permute-start | bytes 958472 | tf_op jit(solution)/shard_map/ppermute | solution.py:29
  53.9 12.2 %copy-start.13 = (bf16[2,1,16,3328]{3,2,1,0:T(8,128)(2,1)}, bf16[2,1,16,3328]{3,2,1,0:T(8,128)(2,1)S(1)}, u32[]{:S(2)}) copy-start(bf16[2,1,16,3328]{3,2,1,0:T(8,128)(2,1)S(1)} %collective-permute-done.10.rest_9_) | copy-start | bytes 638980
  53.9 12.2 %collective-permute-start.13 = (bf16[2,3,16,3328]{3,2,1,0:T(8,128)(2,1)}, bf16[2,3,16,3328]{3,2,1,0:T(8,128)(2,1)}, u32[]{:S(2)}, u32[]{:S(2)}) collective-permute-start(bf16[2,3,16,3328]{3,2,1,0:T(8,128)(2,1)} %collective-permute-done.6.rest_5_), channel_id=1, source_target_pairs={{0,1},{1,0},{2,3},{3,2},{4,5},{5,4},{6,7},{7,6},{8,9},{9,8},{10,11... | collective-permute-start | bytes 1916936 | tf_op jit(solution)/shard_map/ppermute | solution.py:29
  54.0 12.2 %copy-start.14 = (bf16[2,1,16,3328]{3,2,1,0:T(8,128)(2,1)}, bf16[2,1,16,3328]{3,2,1,0:T(8,128)(2,1)S(1)}, u32[]{:S(2)}) copy-start(bf16[2,1,16,3328]{3,2,1,0:T(8,128)(2,1)S(1)} %collective-permute-done.11.rest_10_) | copy-start | bytes 638980
  54.0 12.2 %collective-permute-start.14 = (bf16[2,3,16,3328]{3,2,1,0:T(8,128)(2,1)S(1)}, bf16[2,3,16,3328]{3,2,1,0:T(8,128)(2,1)}, u32[]{:S(2)}, u32[]{:S(2)}) collective-permute-start(bf16[2,3,16,3328]{3,2,1,0:T(8,128)(2,1)S(1)} %collective-permute-done.7.rest_6_), channel_id=1, source_target_pairs={{0,1},{1,0},{2,3},{3,2},{4,5},{5,4},{6,7},{7,6},{8,9},{9,8},{10,11... | collective-permute-start | bytes 1916936 | tf_op jit(solution)/shard_map/ppermute | solution.py:29
  54.5 11.7 %copy-start.15 = (bf16[2,1,16,3328]{3,2,1,0:T(8,128)(2,1)}, bf16[2,1,16,3328]{3,2,1,0:T(8,128)(2,1)S(1)}, u32[]{:S(2)}) copy-start(bf16[2,1,16,3328]{3,2,1,0:T(8,128)(2,1)S(1)} %collective-permute-done.9.rest_8_) | copy-start | bytes 638980
  54.5 11.6 %collective-permute-start.17 = (bf16[3,16,3328]{2,1,0:T(8,128)(2,1)S(1)}, bf16[3,16,3328]{2,1,0:T(8,128)(2,1)}, u32[]{:S(2)}, u32[]{:S(2)}) collective-permute-start(bf16[3,16,3328]{2,1,0:T(8,128)(2,1)S(1)} %slice_bitcast_fusion), channel_id=1, source_target_pairs={{0,4},{4,0},{8,12},{12,8},{16,20},{20,16},{24,28},{28,24},{1,5},{5... | collective-permute-start | bytes 958472 | tf_op jit(solution)/shard_map/ppermute | solution.py:29
  61.6 6.4 %copy-start.10 = (bf16[3,16,3328]{2,1,0:T(8,128)(2,1)}, bf16[3,16,3328]{2,1,0:T(8,128)(2,1)S(1)}, u32[]{:S(2)}) copy-start(bf16[3,16,3328]{2,1,0:T(8,128)(2,1)S(1)} %collective-permute-done.15.rest_14_) | copy-start | bytes 958468
  61.6 4.5 %collective-permute-start.16 = (bf16[3,16,3328]{2,1,0:T(8,128)(2,1)S(1)}, bf16[3,16,3328]{2,1,0:T(8,128)(2,1)}, u32[]{:S(2)}, u32[]{:S(2)}) collective-permute-start(bf16[3,16,3328]{2,1,0:T(8,128)(2,1)S(1)} %collective-permute-done.15.rest_14_), channel_id=1, source_target_pairs={{0,1},{1,0},{2,3},{3,2},{4,5},{5,4},{6,7},{7,6},{8,9},{9,8},{10,11... | collective-permute-start | bytes 958472 | tf_op jit(solution)/shard_map/ppermute | solution.py:29
  66.1 2.0 %collective-permute-start.18 = (bf16[3,16,3328]{2,1,0:T(8,128)(2,1)}, bf16[3,16,3328]{2,1,0:T(8,128)(2,1)}, u32[]{:S(2)}, u32[]{:S(2)}) collective-permute-start(bf16[3,16,3328]{2,1,0:T(8,128)(2,1)} %collective-permute-done.17.rest_16_), channel_id=1, source_target_pairs={{0,1},{1,0},{2,3},{3,2},{4,5},{5,4},{6,7},{7,6},{8,9},{9,8},{10,11... | collective-permute-start | bytes 958472 | tf_op jit(solution)/shard_map/ppermute | solution.py:29
  68.1 0.9 copy-start.6
  79.8 5.7 %copy-start.16 = (f32[512,128]{1,0:T(8,128)S(1)}, f32[512,128]{1,0:T(8,128)}, u32[]{:S(2)}) copy-start(f32[512,128]{1,0:T(8,128)} %get-tuple-element.22) | copy-start | bytes 786436
  79.8 7.3 %copy-start.11 = (f32[512,128]{1,0:T(8,128)S(1)}, f32[512,128]{1,0:T(8,128)}, u32[]{:S(2)}) copy-start(f32[512,128]{1,0:T(8,128)} %get-tuple-element.21) | copy-start | bytes 786436
  79.8 30.6 %all-to-all-start.2 = ((bf16[8,416,128]{2,1,0:T(8,128)(2,1)}), bf16[8,416,128]{2,1,0:T(8,128)(2,1)S(1)}, u32[]{:S(2)}, u32[]{:S(2)}) async-start(bf16[8,416,128]{2,1,0:T(8,128)(2,1)} %bitcast.38), calls=%async_computation.2 | async-start | bytes 1703936 | tf_op jit(solution)/shard_map/all_to_all | solution.py:389
  85.5 1.6 %collective-permute-start.19 = (f32[512,128]{1,0:T(8,128)S(1)}, f32[512,128]{1,0:T(8,128)S(1)}, u32[]{:S(2)}, u32[]{:S(2)}) collective-permute-start(f32[512,128]{1,0:T(8,128)S(1)} %copy-done.16), channel_id=1, source_target_pairs={{0,1},{1,0},{2,3},{3,2},{4,5},{5,4},{6,7},{7,6},{8,9},{9,8},{10,11... | collective-permute-start | bytes 786440 | tf_op jit(solution)/shard_map/ppermute | solution.py:29
  87.2 5.6 %collective-permute-start.20 = (f32[256,128]{1,0:T(8,128)S(1)}, f32[256,128]{1,0:T(8,128)S(1)}, u32[]{:S(2)}, u32[]{:S(2)}) collective-permute-start(f32[256,128]{1,0:T(8,128)S(1)} %constant_dynamic-slice_fusion.1), channel_id=1, source_target_pairs={{0,2},{1,3},{2,0},{3,1},{4,6},{5,7},{6,4},{7,5},{8,10},{9,11},{10,... | collective-permute-start | bytes 393224 | tf_op jit(solution)/shard_map/ppermute | solution.py:29
  92.8 4.8 %collective-permute-start.21 = (f32[128,128]{1,0:T(8,128)S(1)}, f32[128,128]{1,0:T(8,128)S(1)}, u32[]{:S(2)}, u32[]{:S(2)}) collective-permute-start(f32[128,128]{1,0:T(8,128)S(1)} %constant_dynamic-slice_fusion), channel_id=1, source_target_pairs={{0,4},{4,0},{8,12},{12,8},{16,20},{20,16},{24,28},{28,24},{1,5},{5... | collective-permute-start | bytes 196616 | tf_op jit(solution)/shard_map/ppermute | solution.py:29
  97.6 6.0 %collective-permute-start.22 = (f32[128,128]{1,0:T(8,128)S(1)}, f32[128,128]{1,0:T(8,128)S(1)}, u32[]{:S(2)}, u32[]{:S(2)}) collective-permute-start(f32[128,128]{1,0:T(8,128)S(1)} %dynamic-slice_add_fusion.1), channel_id=1, source_target_pairs={{0,8},{4,12},{8,0},{12,4},{16,24},{20,28},{24,16},{28,20},{1,9},{5... | collective-permute-start | bytes 196616 | tf_op jit(solution)/shard_map/ppermute | solution.py:29
  103.7 6.8 %collective-permute-start.23 = (f32[128,128]{1,0:T(8,128)S(1)}, f32[128,128]{1,0:T(8,128)S(1)}, u32[]{:S(2)}, u32[]{:S(2)}) collective-permute-start(f32[128,128]{1,0:T(8,128)S(1)} %add.51), channel_id=1, source_target_pairs={{0,16},{4,20},{8,24},{12,28},{16,0},{20,4},{24,8},{28,12},{1,17},{... | collective-permute-start | bytes 196616 | tf_op jit(solution)/shard_map/ppermute | solution.py:29
  112.5 2.1 %collective-permute-start.27 = (f32[1024,128]{1,0:T(8,128)S(1)}, f32[1024,128]{1,0:T(8,128)S(1)}, u32[]{:S(2)}, u32[]{:S(2)}) collective-permute-start(f32[1024,128]{1,0:T(8,128)S(1)} %cold_sum.2), channel_id=1, source_target_pairs={{0,1},{1,0},{2,3},{3,2},{4,5},{5,4},{6,7},{7,6},{8,9},{9,8},{10,11... | collective-permute-start | bytes 1572872 | tf_op jit(solution)/shard_map/ppermute | solution.py:29
  114.6 9.2 %collective-permute-start.28 = (bf16[1024,128]{1,0:T(8,128)(2,1)S(1)}, bf16[1024,128]{1,0:T(8,128)(2,1)S(1)}, u32[]{:S(2)}, u32[]{:S(2)}) collective-permute-start(bf16[1024,128]{1,0:T(8,128)(2,1)S(1)} %add_convert_fusion), channel_id=1, source_target_pairs={{0,2},{1,3},{2,0},{3,1},{4,6},{5,7},{6,4},{7,5},{8,10},{9,11},{10,... | collective-permute-start | bytes 786440 | tf_op jit(solution)/shard_map/ppermute | solution.py:29
  115.1 4.3 %collective-permute-start.24 = (f32[128,128]{1,0:T(8,128)S(1)}, f32[128,128]{1,0:T(8,128)S(1)}, u32[]{:S(2)}, u32[]{:S(2)}) collective-permute-start(f32[128,128]{1,0:T(8,128)S(1)} %add.52), channel_id=1, source_target_pairs={{0,4},{4,0},{8,12},{12,8},{16,20},{20,16},{24,28},{28,24},{1,5},{5... | collective-permute-start | bytes 196616 | tf_op jit(solution)/shard_map/ppermute | solution.py:29
  119.4 6.8 %collective-permute-start.25 = (f32[256,128]{1,0:T(8,128)S(1)}, f32[256,128]{1,0:T(8,128)S(1)}, u32[]{:S(2)}, u32[]{:S(2)}) collective-permute-start(f32[256,128]{1,0:T(8,128)S(1)} %maximum_select_fusion.3), channel_id=1, source_target_pairs={{0,2},{1,3},{2,0},{3,1},{4,6},{5,7},{6,4},{7,5},{8,10},{9,11},{10,... | collective-permute-start | bytes 393224 | tf_op jit(solution)/shard_map/ppermute | solution.py:29
  123.9 4.0 %copy-start.12 = (bf16[1024,128]{1,0:T(8,128)(2,1)S(1)}, bf16[1024,128]{1,0:T(8,128)(2,1)}, u32[]{:S(2)}) copy-start(bf16[1024,128]{1,0:T(8,128)(2,1)} %param.17) | copy-start | bytes 786436
  123.9 4.9 %collective-permute-start.29 = (f32[1024,128]{1,0:T(8,128)S(1)}, f32[1024,128]{1,0:T(8,128)S(1)}, u32[]{:S(2)}, u32[]{:S(2)}) collective-permute-start(f32[1024,128]{1,0:T(8,128)S(1)} %convert_add_fusion), channel_id=1, source_target_pairs={{0,1},{1,0},{2,3},{3,2},{4,5},{5,4},{6,7},{7,6},{8,9},{9,8},{10,11... | collective-permute-start | bytes 1572872 | tf_op jit(solution)/shard_map/ppermute | solution.py:29
  126.2 1.6 %collective-permute-start.26 = (f32[512,128]{1,0:T(8,128)S(1)}, f32[512,128]{1,0:T(8,128)S(1)}, u32[]{:S(2)}, u32[]{:S(2)}) collective-permute-start(f32[512,128]{1,0:T(8,128)S(1)} %maximum_select_fusion.2), channel_id=1, source_target_pairs={{0,1},{1,0},{2,3},{3,2},{4,5},{5,4},{6,7},{7,6},{8,9},{9,8},{10,11... | collective-permute-start | bytes 786440 | tf_op jit(solution)/shard_map/ppermute | solution.py:29
  126.3 2.5 %copy-start.9 = (bf16[2048,128]{1,0:T(8,128)(2,1)S(1)}, bf16[2048,128]{1,0:T(8,128)(2,1)}, u32[]{:S(2)}) copy-start(bf16[2048,128]{1,0:T(8,128)(2,1)} %param.19) | copy-start | bytes 1572868

commit v7 on v6

--- a/solution.py
+++ b/solution.py
@@ -339,8 +339,8 @@
         "hot_rows",
     )(hot_t.reshape(-1), hot_table)
     plane, z = weight_starts(cross_down.T, cross_up)
-    asked = after(asked, hot_rows, *plane)
-    z = jnp.concatenate(lax.optimization_barrier((*z, asked))[:-1], axis=1)
+    z = jnp.concatenate(z, axis=1)
+    asked, z = lax.optimization_barrier((asked, z, hot_rows, *plane))[:2]
     found = call(
         functools.partial(serve_body, n_data, capacity),
         shape((places, E), BF),

time: 131 us -> 129 us (0.985); the launches traced: 130 us -> 130 us
  waiting for transfers between devices: 47.4 us -> 54 us
  starting transfers between devices: 49.2 us -> 43.7 us
    ppermute x29, starting transfers between devices: 35.9 us -> 24 us  [swap(): return lax.ppermute(value, axis, [(i, i ^ distance) for i in range(size)])]
    ppermute x29, waiting for transfers between devices: 42.4 us -> 49.2 us  [swap(): return lax.ppermute(value, axis, [(i, i ^ distance) for i in range(size)])]
    all_to_all x1, starting transfers between devices: 4.13 us -> 6.29 us  [small_step(): lax.all_to_all(found, 'dp', split_axis=0, concat_axis=0, tiled=True)]
    ppermute x1, starting transfers between devices: 0.02 us -> 1.99 us  [swap_both(): return lax.ppermute(value, ('dp', 'rep'), ways)]
    all_to_all x1, waiting for transfers between devices: 5.05 us -> 3.25 us  [small_step(): asked = lax.all_to_all(ask, 'dp', split_axis=0, concat_axis=0, tiled=True)]
    all_to_all x1, starting transfers between devices: 3.47 us -> 5.01 us  [small_step(): asked = lax.all_to_all(ask, 'dp', split_axis=0, concat_axis=0, tiled=True)]
    ppermute x1, waiting for transfers between devices: 0.01 us -> 1.55 us  [swap_both(): return lax.ppermute(value, ('dp', 'rep'), ways)]
    unnamed x36 -> x34, local copies, waits for them, and re-layouts: 4.33 us -> 2.93 us
  transfers between devices with their start and end apart: 33 -> 33, of which waited for: 15 -> 16; matrix products, arithmetic and copies ran while one was open for 2% -> 3% of each run, Pallas kernels for 7% -> 7%
where the time goes in v7:
time: 129 us; the launch traced here: 130 us
  waiting for transfers between devices  54 us (42%)
  starting transfers between devices  43.7 us (34%)
  Pallas kernels  21.3 us (17%)
  local copies, waits for them, and re-layouts  5.2 us (4%)
  other arithmetic  4.28 us (3%)
    ppermute x29, waiting for transfers between devices, swap(): return lax.ppermute(value, axis, [(i, i ^ distance) for i in range(size)])  49.2 us
    ppermute x29, starting transfers between devices, swap(): return lax.ppermute(value, axis, [(i, i ^ distance) for i in range(size)])  24 us
    pallas_call x1, Pallas kernels, small_step(): call(cross_body, (shape((places, E), BF), shape((HOT // 2, E), F32), shap...  10.8 us
    all_to_all x1, starting transfers between devices, small_step(): lax.all_to_all(send, 'dp', split_axis=0, concat_axis=0, tiled=True)  6.36 us
    all_to_all x1, starting transfers between devices, small_step(): lax.all_to_all(found, 'dp', split_axis=0, concat_axis=0, tiled=True)  6.29 us
    all_to_all x1, starting transfers between devices, small_step(): asked = lax.all_to_all(ask, 'dp', split_axis=0, concat_axis=0, tiled=True)  5.01 us
    pallas_call x2, Pallas kernels, cold_sum(): call(functools.partial(cold_sum_body, n_data, capacity), shape((owned //...  3.98 us
    all_to_all x1, waiting for transfers between devices, small_step(): asked = lax.all_to_all(ask, 'dp', split_axis=0, concat_axis=0, tiled=True)  3.25 us
  transfers between devices with their start and end apart: 33, of which 16 were waited for; matrix products, arithmetic and copies ran while one was open for 3% of the time, Pallas kernels for 7%

profile of v7, /device:TPU:0, one launch (start us, length us, event | category | flops | bytes accessed | tf_op | source)
XLA Modules:
  0.0 129.5 jit_solution(17666255771187741797)
XLA Ops:
  0.6 1.0 maximum_bitcast_fusion.rest_0_
  1.7 3.1 %collective-permute-start = (bf16[2,1,16,3328]{3,2,1,0:T(8,128)(2,1)S(1)}, bf16[2,1,16,3328]{3,2,1,0:T(8,128)(2,1)S(1)}, u32[]{:S(2)}, u32[]{:S(2)}) collective-permute-start(bf16[2,1,16,3328]{3,2,1,0:T(8,128)(2,1)S(1)} %maximum_bitcast_fusion.rest_0_), channel_id=1, source_target_pairs={{0,8},{4,12},{8,0},{12,4},{16,24},{20,28},{24,16},{28,20},{1,9},{5... | collective-permute-start | bytes 638984 | tf_op jit(solution)/shard_map/ppermute | solution.py:29
  4.8 2.6 %collective-permute-start.1 = (bf16[2,1,16,3328]{3,2,1,0:T(8,128)(2,1)S(1)}, bf16[2,1,16,3328]{3,2,1,0:T(8,128)(2,1)S(1)}, u32[]{:S(2)}, u32[]{:S(2)}) collective-permute-start(bf16[2,1,16,3328]{3,2,1,0:T(8,128)(2,1)S(1)} %maximum_bitcast_fusion.rest_0_), channel_id=1, source_target_pairs={{0,16},{4,20},{8,24},{12,28},{16,0},{20,4},{24,8},{28,12},{1,17},{... | collective-permute-start | bytes 638984 | tf_op jit(solution)/shard_map/ppermute | solution.py:29
  7.4 1.7 %collective-permute-start.3 = (bf16[2,1,16,3328]{3,2,1,0:T(8,128)(2,1)S(1)}, bf16[2,1,16,3328]{3,2,1,0:T(8,128)(2,1)}, u32[]{:S(2)}, u32[]{:S(2)}) collective-permute-start(bf16[2,1,16,3328]{3,2,1,0:T(8,128)(2,1)S(1)} %maximum_bitcast_fusion.rest_0_), channel_id=1, source_target_pairs={{0,2},{1,3},{2,0},{3,1},{4,6},{5,7},{6,4},{7,5},{8,10},{9,11},{10,... | collective-permute-start | bytes 638984 | tf_op jit(solution)/shard_map/ppermute | solution.py:29
  9.1 1.5 %collective-permute-start.4 = (bf16[2,1,16,3328]{3,2,1,0:T(8,128)(2,1)S(1)}, bf16[2,1,16,3328]{3,2,1,0:T(8,128)(2,1)}, u32[]{:S(2)}, u32[]{:S(2)}) collective-permute-start(bf16[2,1,16,3328]{3,2,1,0:T(8,128)(2,1)S(1)} %maximum_bitcast_fusion.rest_0_), channel_id=1, source_target_pairs={{0,4},{4,0},{8,12},{12,8},{16,20},{20,16},{24,28},{28,24},{1,5},{5... | collective-permute-start | bytes 638984 | tf_op jit(solution)/shard_map/ppermute | solution.py:29
  10.6 0.7 reduce
  11.3 0.2 reshape.35
  11.5 0.1 copy.14
  11.6 0.6 copy-done.4
  12.2 1.2 route.1
  13.4 0.6 copy-done.5
  14.0 5.0 %all-to-all-start = ((s32[8,4,128]{2,1,0:T(4,128)}), s32[8,4,128]{2,1,0:T(4,128)S(1)}, u32[]{:S(2)}, u32[]{:S(2)}) async-start(s32[8,4,128]{2,1,0:T(4,128)} %bitcast.5), calls=%async_computation | async-start | bytes 32768 | tf_op jit(solution)/shard_map/all_to_all | solution.py:330
  19.1 2.2 %hot_rows.1.hot_ref = bf16[1664,128]{1,0:T(8,128)(2,1)S(1)} custom-call(s32[1664]{0:T(1024)S(1)} %bitcast.34, f32[1024,128]{1,0:T(8,128)S(1)} %copy-done.1), custom_call_target="tpu_custom_call" | custom-call | flops 1 | bytes 1 | tf_op jit(solution)/shard_map/hot_rows/pallas_call | solution.py:333
  21.3 0.7 copy-done.2
  22.1 2.0 %collective-permute-start.5 = (bf16[2,1,16,3328]{3,2,1,0:T(8,128)(2,1)S(1)}, bf16[2,1,16,3328]{3,2,1,0:T(8,128)(2,1)}, u32[]{:S(2)}, u32[]{:S(2)}) collective-permute-start(bf16[2,1,16,3328]{3,2,1,0:T(8,128)(2,1)S(1)} %maximum_bitcast_fusion.rest_0_), channel_id=1, source_target_pairs={{0,6},{1,7},{2,4},{3,5},{4,2},{5,3},{6,0},{7,1},{8,14},{9,15},{10,... | collective-permute-start | bytes 638984 | tf_op jit(solution)/shard_map/ppermute | solution.py:46
  24.0 0.1 pad_maximum_fusion.rest_4_
  24.1 3.2 %all-to-all-done = s32[8,4,128]{2,1,0:T(4,128)S(1)} async-done(((s32[8,4,128]{2,1,0:T(4,128)}), s32[8,4,128]{2,1,0:T(4,128)S(1)}, u32[]{:S(2)}, u32[]{:S(2)}) %all-to-all-start) | async-done | bytes 16416 | tf_op jit(solution)/shard_map/all_to_all | solution.py:330
  27.4 1.5 %collective-permute-done.5.rest_3_ = bf16[2,1,16,3328]{3,2,1,0:T(8,128)(2,1)} collective-permute-done((bf16[2,1,16,3328]{3,2,1,0:T(8,128)(2,1)S(1)}, bf16[2,1,16,3328]{3,2,1,0:T(8,128)(2,1)}, u32[]{:S(2)}, u32[]{:S(2)}) %collective-permute-start.5) | collective-permute-done | bytes 213024 | tf_op jit(solution)/shard_map/ppermute | solution.py:46
  28.9 2.0 %collective-permute-start.7 = (bf16[2,3,16,3328]{3,2,1,0:T(8,128)(2,1)S(1)}, bf16[2,3,16,3328]{3,2,1,0:T(8,128)(2,1)}, u32[]{:S(2)}, u32[]{:S(2)}) collective-permute-start(bf16[2,3,16,3328]{3,2,1,0:T(8,128)(2,1)S(1)} %pad_maximum_fusion.rest_4_), channel_id=1, source_target_pairs={{0,4},{4,0},{8,12},{12,8},{16,20},{20,16},{24,28},{28,24},{1,5},{5... | collective-permute-start | bytes 1916936 | tf_op jit(solution)/shard_map/ppermute | solution.py:29
  31.0 0.6 collective-permute-start.6
  31.5 0.2 collective-permute-start.12
  31.8 3.1 %serve.1 = bf16[3328,128]{1,0:T(8,128)(2,1)} custom-call(s32[4096]{0:T(1024)S(1)} %bitcast.29, f32[2048,128]{1,0:T(8,128)S(1)} %copy-done), custom_call_target="tpu_custom_call" | custom-call | flops 1 | bytes 1 | tf_op jit(solution)/shard_map/serve/pallas_call | solution.py:344
  34.9 6.3 %all-to-all-start.1 = ((bf16[8,416,128]{2,1,0:T(8,128)(2,1)}), bf16[8,416,128]{2,1,0:T(8,128)(2,1)S(1)}, u32[]{:S(2)}, u32[]{:S(2)}) async-start(bf16[8,416,128]{2,1,0:T(8,128)(2,1)} %bitcast.13), calls=%async_computation.1 | async-start | bytes 1703936 | tf_op jit(solution)/shard_map/all_to_all | solution.py:352
  41.2 1.5 %collective-permute-done.7.rest_6_ = bf16[2,3,16,3328]{3,2,1,0:T(8,128)(2,1)} collective-permute-done((bf16[2,3,16,3328]{3,2,1,0:T(8,128)(2,1)S(1)}, bf16[2,3,16,3328]{3,2,1,0:T(8,128)(2,1)}, u32[]{:S(2)}, u32[]{:S(2)}) %collective-permute-start.7) | collective-permute-done | bytes 639008 | tf_op jit(solution)/shard_map/ppermute | solution.py:29
  42.6 1.0 slice_bitcast_fusion.1
  43.6 4.2 %collective-permute-done.6.rest_5_ = bf16[2,3,16,3328]{3,2,1,0:T(8,128)(2,1)} collective-permute-done((bf16[2,3,16,3328]{3,2,1,0:T(8,128)(2,1)S(1)}, bf16[2,3,16,3328]{3,2,1,0:T(8,128)(2,1)}, u32[]{:S(2)}, u32[]{:S(2)}) %collective-permute-start.6) | collective-permute-done | bytes 639008 | tf_op jit(solution)/shard_map/ppermute | solution.py:29
  47.9 1.0 slice_bitcast_fusion
  48.9 0.6 collective-permute-start.15
  49.5 0.2 collective-permute-start.13
  49.8 0.3 collective-permute-start.14
  50.0 0.0 collective-permute-start.17
  50.1 8.8 %collective-permute-done.15.rest_14_ = bf16[3,16,3328]{2,1,0:T(8,128)(2,1)S(1)} collective-permute-done((bf16[3,16,3328]{2,1,0:T(8,128)(2,1)S(1)}, bf16[3,16,3328]{2,1,0:T(8,128)(2,1)S(1)}, u32[]{:S(2)}, u32[]{:S(2)}) %collective-permute-start.15) | collective-permute-done | bytes 319520 | tf_op jit(solution)/shard_map/ppermute | solution.py:29
  58.9 3.3 %collective-permute-done.17.rest_16_ = bf16[3,16,3328]{2,1,0:T(8,128)(2,1)} collective-permute-done((bf16[3,16,3328]{2,1,0:T(8,128)(2,1)S(1)}, bf16[3,16,3328]{2,1,0:T(8,128)(2,1)}, u32[]{:S(2)}, u32[]{:S(2)}) %collective-permute-start.17) | collective-permute-done | bytes 319520 | tf_op jit(solution)/shard_map/ppermute | solution.py:29
  62.3 1.9 %collective-permute-done.18.rest_17_ = bf16[3,16,3328]{2,1,0:T(8,128)(2,1)} collective-permute-done((bf16[3,16,3328]{2,1,0:T(8,128)(2,1)}, bf16[3,16,3328]{2,1,0:T(8,128)(2,1)}, u32[]{:S(2)}, u32[]{:S(2)}) %collective-permute-start.18) | collective-permute-done | bytes 319520 | tf_op jit(solution)/shard_map/ppermute | solution.py:29
  64.2 0.9 copy-done.6
  65.1 10.8 %cross.1 = (bf16[3328,128]{1,0:T(8,128)(2,1)}, f32[512,128]{1,0:T(8,128)}, f32[512,128]{1,0:T(8,128)}) custom-call(s32[1]{0:T(128)} %bitcast.core_ref, s32[2048]{0:T(1024)} %bitcast.36, s32[13,128]{1,0:T(8,128)} %bitcast.33, bf16[3328,128]{1,0:T(8,128)(2,1)} %bitcast.37, bf16[1664,128]{1,0:T(8,128)(2,1)} %copy-done.2, s32[1,128]{1,0:T(1,128)} %bitcast.41, ...), custom_call_target="tpu_custom_call" | custom-call | flops 1744830464 | bytes 20000000 | tf_op jit(solution)/shard_map/cross/pallas_call | solution.py:359
  75.9 6.4 %all-to-all-start.2 = ((bf16[8,416,128]{2,1,0:T(8,128)(2,1)}), bf16[8,416,128]{2,1,0:T(8,128)(2,1)S(1)}, u32[]{:S(2)}, u32[]{:S(2)}) async-start(bf16[8,416,128]{2,1,0:T(8,128)(2,1)} %bitcast.38), calls=%async_computation.2 | async-start | bytes 1703936 | tf_op jit(solution)/shard_map/all_to_all | solution.py:389
  82.3 0.1 collective-permute-start.19
  82.4 1.5 %collective-permute-done.19 = f32[512,128]{1,0:T(8,128)S(1)} collective-permute-done((f32[512,128]{1,0:T(8,128)S(1)}, f32[512,128]{1,0:T(8,128)S(1)}, u32[]{:S(2)}, u32[]{:S(2)}) %collective-permute-start.19) | collective-permute-done | bytes 262176 | tf_op jit(solution)/shard_map/ppermute | solution.py:29
  84.0 2.0 %collective-permute-start.20 = (f32[256,128]{1,0:T(8,128)S(1)}, f32[256,128]{1,0:T(8,128)S(1)}, u32[]{:S(2)}, u32[]{:S(2)}) collective-permute-start(f32[256,128]{1,0:T(8,128)S(1)} %constant_dynamic-slice_fusion.1), channel_id=1, source_target_pairs={{0,2},{1,3},{2,0},{3,1},{4,6},{5,7},{6,4},{7,5},{8,10},{9,11},{10,... | collective-permute-start | bytes 393224 | tf_op jit(solution)/shard_map/ppermute | solution.py:29
  85.9 3.8 %collective-permute-done.20 = f32[256,128]{1,0:T(8,128)S(1)} collective-permute-done((f32[256,128]{1,0:T(8,128)S(1)}, f32[256,128]{1,0:T(8,128)S(1)}, u32[]{:S(2)}, u32[]{:S(2)}) %collective-permute-start.20) | collective-permute-done | bytes 131104 | tf_op jit(solution)/shard_map/ppermute | solution.py:29
  89.8 2.0 %collective-permute-start.21 = (f32[128,128]{1,0:T(8,128)S(1)}, f32[128,128]{1,0:T(8,128)S(1)}, u32[]{:S(2)}, u32[]{:S(2)}) collective-permute-start(f32[128,128]{1,0:T(8,128)S(1)} %constant_dynamic-slice_fusion), channel_id=1, source_target_pairs={{0,4},{4,0},{8,12},{12,8},{16,20},{20,16},{24,28},{28,24},{1,5},{5... | collective-permute-start | bytes 196616 | tf_op jit(solution)/shard_map/ppermute | solution.py:29
  91.8 2.8 %collective-permute-done.21 = f32[128,128]{1,0:T(8,128)S(1)} collective-permute-done((f32[128,128]{1,0:T(8,128)S(1)}, f32[128,128]{1,0:T(8,128)S(1)}, u32[]{:S(2)}, u32[]{:S(2)}) %collective-permute-start.21) | collective-permute-done | bytes 65568 | tf_op jit(solution)/shard_map/ppermute | solution.py:29
  94.6 3.9 %collective-permute-start.22 = (f32[128,128]{1,0:T(8,128)S(1)}, f32[128,128]{1,0:T(8,128)S(1)}, u32[]{:S(2)}, u32[]{:S(2)}) collective-permute-start(f32[128,128]{1,0:T(8,128)S(1)} %dynamic-slice_add_fusion.1), channel_id=1, source_target_pairs={{0,8},{4,12},{8,0},{12,4},{16,24},{20,28},{24,16},{28,20},{1,9},{5... | collective-permute-start | bytes 196616 | tf_op jit(solution)/shard_map/ppermute | solution.py:29
  98.5 5.8 %collective-permute-done.22 = f32[128,128]{1,0:T(8,128)S(1)} collective-permute-done((f32[128,128]{1,0:T(8,128)S(1)}, f32[128,128]{1,0:T(8,128)S(1)}, u32[]{:S(2)}, u32[]{:S(2)}) %collective-permute-start.22) | collective-permute-done | bytes 65568 | tf_op jit(solution)/shard_map/ppermute | solution.py:29
  104.3 0.7 collective-permute-start.23
  105.0 4.9 %collective-permute-done.23 = f32[128,128]{1,0:T(8,128)S(1)} collective-permute-done((f32[128,128]{1,0:T(8,128)S(1)}, f32[128,128]{1,0:T(8,128)S(1)}, u32[]{:S(2)}, u32[]{:S(2)}) %collective-permute-start.23) | collective-permute-done | bytes 65568 | tf_op jit(solution)/shard_map/ppermute | solution.py:29
  109.9 2.0 %cold_sum.2 = f32[1024,128]{1,0:T(8,128)S(1)} custom-call(s32[1]{0:T(128)} %bitcast.21.first_ref, s32[32,128]{1,0:T(8,128)S(1)} %bitcast.30, bf16[3328,128]{1,0:T(8,128)(2,1)S(1)} %bitcast.27), custom_call_target="tpu_custom_call" | custom-call | flops 1000000000 | bytes 10000000 | tf_op jit(solution)/shard_map/cold_sum/pallas_call | solution.py:394
  111.9 0.1 collective-permute-start.27
  112.0 2.0 %cold_sum.3 = f32[1024,128]{1,0:T(8,128)S(1)} custom-call(s32[1]{0:T(128)} %bitcast.20.first_ref, s32[32,128]{1,0:T(8,128)S(1)} %bitcast.31, bf16[3328,128]{1,0:T(8,128)(2,1)S(1)} %bitcast.28), custom_call_target="tpu_custom_call" | custom-call | flops 1000000000 | bytes 10000000 | tf_op jit(solution)/shard_map/cold_sum/pallas_call | solution.py:394
  114.0 0.1 add_convert_fusion
  114.1 0.1 collective-permute-start.28
  114.2 0.4 collective-permute-start.24
  114.5 4.2 %collective-permute-done.24 = f32[128,128]{1,0:T(8,128)S(1)} collective-permute-done((f32[128,128]{1,0:T(8,128)S(1)}, f32[128,128]{1,0:T(8,128)S(1)}, u32[]{:S(2)}, u32[]{:S(2)}) %collective-permute-start.24) | collective-permute-done | bytes 65568 | tf_op jit(solution)/shard_map/ppermute | solution.py:29
  118.7 1.8 %collective-permute-start.25 = (f32[256,128]{1,0:T(8,128)S(1)}, f32[256,128]{1,0:T(8,128)S(1)}, u32[]{:S(2)}, u32[]{:S(2)}) collective-permute-start(f32[256,128]{1,0:T(8,128)S(1)} %maximum_select_fusion.3), channel_id=1, source_target_pairs={{0,2},{1,3},{2,0},{3,1},{4,6},{5,7},{6,4},{7,5},{8,10},{9,11},{10,... | collective-permute-start | bytes 393224 | tf_op jit(solution)/shard_map/ppermute | solution.py:29
  120.5 2.7 %collective-permute-done.28 = bf16[1024,128]{1,0:T(8,128)(2,1)S(1)} collective-permute-done((bf16[1024,128]{1,0:T(8,128)(2,1)S(1)}, bf16[1024,128]{1,0:T(8,128)(2,1)S(1)}, u32[]{:S(2)}, u32[]{:S(2)}) %collective-permute-start.28) | collective-permute-done | bytes 262176 | tf_op jit(solution)/shard_map/ppermute | solution.py:29
  123.2 0.1 convert_add_fusion
  123.3 0.0 copy-start.12
  123.3 0.1 collective-permute-start.29
  123.4 2.3 %collective-permute-done.25 = f32[256,128]{1,0:T(8,128)S(1)} collective-permute-done((f32[256,128]{1,0:T(8,128)S(1)}, f32[256,128]{1,0:T(8,128)S(1)}, u32[]{:S(2)}, u32[]{:S(2)}) %collective-permute-start.25) | collective-permute-done | bytes 131104 | tf_op jit(solution)/shard_map/ppermute | solution.py:29
  125.7 0.1 collective-permute-start.26
  125.8 1.5 %collective-permute-done.26 = f32[512,128]{1,0:T(8,128)S(1)} collective-permute-done((f32[512,128]{1,0:T(8,128)S(1)}, f32[512,128]{1,0:T(8,128)S(1)}, u32[]{:S(2)}, u32[]{:S(2)}) %collective-permute-start.26) | collective-permute-done | bytes 262176 | tf_op jit(solution)/shard_map/ppermute | solution.py:29
  127.3 1.0 multiply_subtract_fusion.1
  128.2 1.3 %multiply_subtract_fusion = f32[2048,128]{1,0:T(8,128)} fusion(f32[2048,128]{1,0:T(8,128)S(1)} %copy-done, bf16[2048,128]{1,0:T(8,128)(2,1)S(1)} %copy-done.9, f32[1024,128]{1,0:T(8,128)S(1)} %convert_add_fusion, f32[1024,128]{1,0:T(8,128)S(1)} %collective-permute-done.29, pred[]{:T(512)S(6)} %eq.14), kind=kLoop, calls=%fused_computation.1 | loop fusion | flops 2883584 | bytes 3670017 | tf_op jit(solution)/shard_map/sub | solution.py:20
  (62 shorter events, 0.3 us)
Async XLA Ops:
  0.6 18.4 %copy-start.1 = (f32[1024,128]{1,0:T(8,128)S(1)}, f32[1024,128]{1,0:T(8,128)}, u32[]{:S(2)}) copy-start(f32[1024,128]{1,0:T(8,128)} %table_ref.2) | copy-start | bytes 1572868
  1.7 29.3 %copy-start.8 = (bf16[2,1,16,3328]{3,2,1,0:T(8,128)(2,1)}, bf16[2,1,16,3328]{3,2,1,0:T(8,128)(2,1)S(1)}, u32[]{:S(2)}) copy-start(bf16[2,1,16,3328]{3,2,1,0:T(8,128)(2,1)S(1)} %maximum_bitcast_fusion.rest_0_) | copy-start | bytes 638980
  1.7 20.4 %collective-permute-start = (bf16[2,1,16,3328]{3,2,1,0:T(8,128)(2,1)S(1)}, bf16[2,1,16,3328]{3,2,1,0:T(8,128)(2,1)S(1)}, u32[]{:S(2)}, u32[]{:S(2)}) collective-permute-start(bf16[2,1,16,3328]{3,2,1,0:T(8,128)(2,1)S(1)} %maximum_bitcast_fusion.rest_0_), channel_id=1, source_target_pairs={{0,8},{4,12},{8,0},{12,4},{16,24},{20,28},{24,16},{28,20},{1,9},{5... | collective-permute-start | bytes 638984 | tf_op jit(solution)/shard_map/ppermute | solution.py:29
  4.8 19.3 %collective-permute-start.1 = (bf16[2,1,16,3328]{3,2,1,0:T(8,128)(2,1)S(1)}, bf16[2,1,16,3328]{3,2,1,0:T(8,128)(2,1)S(1)}, u32[]{:S(2)}, u32[]{:S(2)}) collective-permute-start(bf16[2,1,16,3328]{3,2,1,0:T(8,128)(2,1)S(1)} %maximum_bitcast_fusion.rest_0_), channel_id=1, source_target_pairs={{0,16},{4,20},{8,24},{12,28},{16,0},{20,4},{24,8},{28,12},{1,17},{... | collective-permute-start | bytes 638984 | tf_op jit(solution)/shard_map/ppermute | solution.py:29
  7.4 16.7 %collective-permute-start.2 = (bf16[2,1,16,3328]{3,2,1,0:T(8,128)(2,1)S(1)}, bf16[2,1,16,3328]{3,2,1,0:T(8,128)(2,1)S(1)}, u32[]{:S(2)}, u32[]{:S(2)}) collective-permute-start(bf16[2,1,16,3328]{3,2,1,0:T(8,128)(2,1)S(1)} %maximum_bitcast_fusion.rest_0_), channel_id=1, source_target_pairs={{0,24},{4,28},{8,16},{12,20},{16,8},{20,12},{24,0},{28,4},{1,25},{... | collective-permute-start | bytes 638984 | tf_op jit(solution)/shard_map/ppermute | solution.py:29
  7.4 20.0 %collective-permute-start.3 = (bf16[2,1,16,3328]{3,2,1,0:T(8,128)(2,1)S(1)}, bf16[2,1,16,3328]{3,2,1,0:T(8,128)(2,1)}, u32[]{:S(2)}, u32[]{:S(2)}) collective-permute-start(bf16[2,1,16,3328]{3,2,1,0:T(8,128)(2,1)S(1)} %maximum_bitcast_fusion.rest_0_), channel_id=1, source_target_pairs={{0,2},{1,3},{2,0},{3,1},{4,6},{5,7},{6,4},{7,5},{8,10},{9,11},{10,... | collective-permute-start | bytes 638984 | tf_op jit(solution)/shard_map/ppermute | solution.py:29
  9.1 18.3 %collective-permute-start.4 = (bf16[2,1,16,3328]{3,2,1,0:T(8,128)(2,1)S(1)}, bf16[2,1,16,3328]{3,2,1,0:T(8,128)(2,1)}, u32[]{:S(2)}, u32[]{:S(2)}) collective-permute-start(bf16[2,1,16,3328]{3,2,1,0:T(8,128)(2,1)S(1)} %maximum_bitcast_fusion.rest_0_), channel_id=1, source_target_pairs={{0,4},{4,0},{8,12},{12,8},{16,20},{20,16},{24,28},{28,24},{1,5},{5... | collective-permute-start | bytes 638984 | tf_op jit(solution)/shard_map/ppermute | solution.py:29
  11.5 0.7 copy-start.4
  13.4 0.6 copy-start.5
  14.0 5.0 %copy-start.3 = (s32[128,13]{0,1:T(8,128)S(1)}, s32[128,13]{0,1:T(8,128)}, u32[]{:S(2)}) copy-start(s32[128,13]{0,1:T(8,128)} %param.12) | copy-start | bytes 19972
  14.0 13.4 %all-to-all-start = ((s32[8,4,128]{2,1,0:T(4,128)}), s32[8,4,128]{2,1,0:T(4,128)S(1)}, u32[]{:S(2)}, u32[]{:S(2)}) async-start(s32[8,4,128]{2,1,0:T(4,128)} %bitcast.5), calls=%async_computation | async-start | bytes 32768 | tf_op jit(solution)/shard_map/all_to_all | solution.py:330
  19.1 12.7 %copy-start = (f32[2048,128]{1,0:T(8,128)S(1)}, f32[2048,128]{1,0:T(8,128)}, u32[]{:S(2)}) copy-start(f32[2048,128]{1,0:T(8,128)} %table_ref.3) | copy-start | bytes 3145732
  21.3 0.8 copy-start.2
  22.1 6.9 %collective-permute-start.5 = (bf16[2,1,16,3328]{3,2,1,0:T(8,128)(2,1)S(1)}, bf16[2,1,16,3328]{3,2,1,0:T(8,128)(2,1)}, u32[]{:S(2)}, u32[]{:S(2)}) collective-permute-start(bf16[2,1,16,3328]{3,2,1,0:T(8,128)(2,1)S(1)} %maximum_bitcast_fusion.rest_0_), channel_id=1, source_target_pairs={{0,6},{1,7},{2,4},{3,5},{4,2},{5,3},{6,0},{7,1},{8,14},{9,15},{10,... | collective-permute-start | bytes 638984 | tf_op jit(solution)/shard_map/ppermute | solution.py:46
  24.1 10.7 %copy-start.7 = (bf16[2,3,16,3328]{3,2,1,0:T(8,128)(2,1)}, bf16[2,3,16,3328]{3,2,1,0:T(8,128)(2,1)S(1)}, u32[]{:S(2)}) copy-start(bf16[2,3,16,3328]{3,2,1,0:T(8,128)(2,1)S(1)} %pad_maximum_fusion.rest_4_) | copy-start | bytes 1916932
  28.9 13.7 %collective-permute-start.7 = (bf16[2,3,16,3328]{3,2,1,0:T(8,128)(2,1)S(1)}, bf16[2,3,16,3328]{3,2,1,0:T(8,128)(2,1)}, u32[]{:S(2)}, u32[]{:S(2)}) collective-permute-start(bf16[2,3,16,3328]{3,2,1,0:T(8,128)(2,1)S(1)} %pad_maximum_fusion.rest_4_), channel_id=1, source_target_pairs={{0,4},{4,0},{8,12},{12,8},{16,20},{20,16},{24,28},{28,24},{1,5},{5... | collective-permute-start | bytes 1916936 | tf_op jit(solution)/shard_map/ppermute | solution.py:29
  31.0 17.9 %collective-permute-start.8 = (bf16[2,1,16,3328]{3,2,1,0:T(8,128)(2,1)S(1)}, bf16[2,1,16,3328]{3,2,1,0:T(8,128)(2,1)}, u32[]{:S(2)}, u32[]{:S(2)}) collective-permute-start(bf16[2,1,16,3328]{3,2,1,0:T(8,128)(2,1)S(1)} %maximum_bitcast_fusion.rest_0_), channel_id=1, source_target_pairs={{0,1},{1,0},{2,3},{3,2},{4,5},{5,4},{6,7},{7,6},{8,9},{9,8},{10,11... | collective-permute-start | bytes 638984 | tf_op jit(solution)/shard_map/ppermute | solution.py:29
  31.0 16.9 %collective-permute-start.6 = (bf16[2,3,16,3328]{3,2,1,0:T(8,128)(2,1)S(1)}, bf16[2,3,16,3328]{3,2,1,0:T(8,128)(2,1)}, u32[]{:S(2)}, u32[]{:S(2)}) collective-permute-start(bf16[2,3,16,3328]{3,2,1,0:T(8,128)(2,1)S(1)} %pad_maximum_fusion.rest_4_), channel_id=1, source_target_pairs={{0,2},{1,3},{2,0},{3,1},{4,6},{5,7},{6,4},{7,5},{8,10},{9,11},{10,... | collective-permute-start | bytes 1916936 | tf_op jit(solution)/shard_map/ppermute | solution.py:29
  31.5 30.7 %collective-permute-start.12 = (bf16[2,3,16,3328]{3,2,1,0:T(8,128)(2,1)S(1)}, bf16[2,3,16,3328]{3,2,1,0:T(8,128)(2,1)}, u32[]{:S(2)}, u32[]{:S(2)}) collective-permute-start(bf16[2,3,16,3328]{3,2,1,0:T(8,128)(2,1)S(1)} %pad_maximum_fusion.rest_4_), channel_id=1, source_target_pairs={{0,1},{1,0},{2,3},{3,2},{4,5},{5,4},{6,7},{7,6},{8,9},{9,8},{10,11... | collective-permute-start | bytes 1916936 | tf_op jit(solution)/shard_map/ppermute | solution.py:29
  34.9 29.3 %all-to-all-start.1 = ((bf16[8,416,128]{2,1,0:T(8,128)(2,1)}), bf16[8,416,128]{2,1,0:T(8,128)(2,1)S(1)}, u32[]{:S(2)}, u32[]{:S(2)}) async-start(bf16[8,416,128]{2,1,0:T(8,128)(2,1)} %bitcast.13), calls=%async_computation.1 | async-start | bytes 1703936 | tf_op jit(solution)/shard_map/all_to_all | solution.py:352
  41.1 8.4 %collective-permute-start.10 = (bf16[2,1,16,3328]{3,2,1,0:T(8,128)(2,1)}, bf16[2,1,16,3328]{3,2,1,0:T(8,128)(2,1)S(1)}, u32[]{:S(2)}, u32[]{:S(2)}) collective-permute-start(bf16[2,1,16,3328]{3,2,1,0:T(8,128)(2,1)} %collective-permute-done.4.rest_2_), channel_id=1, source_target_pairs={{0,1},{1,0},{2,3},{3,2},{4,5},{5,4},{6,7},{7,6},{8,9},{9,8},{10,11... | collective-permute-start | bytes 638984 | tf_op jit(solution)/shard_map/ppermute | solution.py:29
  42.6 7.1 %collective-permute-start.11 = (bf16[2,1,16,3328]{3,2,1,0:T(8,128)(2,1)}, bf16[2,1,16,3328]{3,2,1,0:T(8,128)(2,1)S(1)}, u32[]{:S(2)}, u32[]{:S(2)}) collective-permute-start(bf16[2,1,16,3328]{3,2,1,0:T(8,128)(2,1)} %collective-permute-done.5.rest_3_), channel_id=1, source_target_pairs={{0,1},{1,0},{2,3},{3,2},{4,5},{5,4},{6,7},{7,6},{8,9},{9,8},{10,11... | collective-permute-start | bytes 638984 | tf_op jit(solution)/shard_map/ppermute | solution.py:29
  47.9 2.2 %collective-permute-start.9 = (bf16[2,1,16,3328]{3,2,1,0:T(8,128)(2,1)}, bf16[2,1,16,3328]{3,2,1,0:T(8,128)(2,1)S(1)}, u32[]{:S(2)}, u32[]{:S(2)}) collective-permute-start(bf16[2,1,16,3328]{3,2,1,0:T(8,128)(2,1)} %collective-permute-done.3.rest_1_), channel_id=1, source_target_pairs={{0,1},{1,0},{2,3},{3,2},{4,5},{5,4},{6,7},{7,6},{8,9},{9,8},{10,11... | collective-permute-start | bytes 638984 | tf_op jit(solution)/shard_map/ppermute | solution.py:29
  48.9 10.0 %collective-permute-start.15 = (bf16[3,16,3328]{2,1,0:T(8,128)(2,1)S(1)}, bf16[3,16,3328]{2,1,0:T(8,128)(2,1)S(1)}, u32[]{:S(2)}, u32[]{:S(2)}) collective-permute-start(bf16[3,16,3328]{2,1,0:T(8,128)(2,1)S(1)} %slice_bitcast_fusion.1), channel_id=1, source_target_pairs={{0,2},{1,3},{2,0},{3,1},{4,6},{5,7},{6,4},{7,5},{8,10},{9,11},{10,... | collective-permute-start | bytes 958472 | tf_op jit(solution)/shard_map/ppermute | solution.py:29
  49.5 12.7 %copy-start.13 = (bf16[2,1,16,3328]{3,2,1,0:T(8,128)(2,1)}, bf16[2,1,16,3328]{3,2,1,0:T(8,128)(2,1)S(1)}, u32[]{:S(2)}) copy-start(bf16[2,1,16,3328]{3,2,1,0:T(8,128)(2,1)S(1)} %collective-permute-done.10.rest_9_) | copy-start | bytes 638980
  49.5 12.7 %collective-permute-start.13 = (bf16[2,3,16,3328]{3,2,1,0:T(8,128)(2,1)}, bf16[2,3,16,3328]{3,2,1,0:T(8,128)(2,1)}, u32[]{:S(2)}, u32[]{:S(2)}) collective-permute-start(bf16[2,3,16,3328]{3,2,1,0:T(8,128)(2,1)} %collective-permute-done.6.rest_5_), channel_id=1, source_target_pairs={{0,1},{1,0},{2,3},{3,2},{4,5},{5,4},{6,7},{7,6},{8,9},{9,8},{10,11... | collective-permute-start | bytes 1916936 | tf_op jit(solution)/shard_map/ppermute | solution.py:29
  49.8 12.4 %copy-start.14 = (bf16[2,1,16,3328]{3,2,1,0:T(8,128)(2,1)}, bf16[2,1,16,3328]{3,2,1,0:T(8,128)(2,1)S(1)}, u32[]{:S(2)}) copy-start(bf16[2,1,16,3328]{3,2,1,0:T(8,128)(2,1)S(1)} %collective-permute-done.11.rest_10_) | copy-start | bytes 638980
  49.8 12.5 %collective-permute-start.14 = (bf16[2,3,16,3328]{3,2,1,0:T(8,128)(2,1)}, bf16[2,3,16,3328]{3,2,1,0:T(8,128)(2,1)}, u32[]{:S(2)}, u32[]{:S(2)}) collective-permute-start(bf16[2,3,16,3328]{3,2,1,0:T(8,128)(2,1)} %collective-permute-done.7.rest_6_), channel_id=1, source_target_pairs={{0,1},{1,0},{2,3},{3,2},{4,5},{5,4},{6,7},{7,6},{8,9},{9,8},{10,11... | collective-permute-start | bytes 1916936 | tf_op jit(solution)/shard_map/ppermute | solution.py:29
  50.0 12.2 %copy-start.15 = (bf16[2,1,16,3328]{3,2,1,0:T(8,128)(2,1)}, bf16[2,1,16,3328]{3,2,1,0:T(8,128)(2,1)S(1)}, u32[]{:S(2)}) copy-start(bf16[2,1,16,3328]{3,2,1,0:T(8,128)(2,1)S(1)} %collective-permute-done.9.rest_8_) | copy-start | bytes 638980
  50.0 12.1 %collective-permute-start.17 = (bf16[3,16,3328]{2,1,0:T(8,128)(2,1)S(1)}, bf16[3,16,3328]{2,1,0:T(8,128)(2,1)}, u32[]{:S(2)}, u32[]{:S(2)}) collective-permute-start(bf16[3,16,3328]{2,1,0:T(8,128)(2,1)S(1)} %slice_bitcast_fusion), channel_id=1, source_target_pairs={{0,4},{4,0},{8,12},{12,8},{16,20},{20,16},{24,28},{28,24},{1,5},{5... | collective-permute-start | bytes 958472 | tf_op jit(solution)/shard_map/ppermute | solution.py:29
  58.9 5.3 %copy-start.10 = (bf16[3,16,3328]{2,1,0:T(8,128)(2,1)}, bf16[3,16,3328]{2,1,0:T(8,128)(2,1)S(1)}, u32[]{:S(2)}) copy-start(bf16[3,16,3328]{2,1,0:T(8,128)(2,1)S(1)} %collective-permute-done.15.rest_14_) | copy-start | bytes 958468
  58.9 3.4 %collective-permute-start.16 = (bf16[3,16,3328]{2,1,0:T(8,128)(2,1)S(1)}, bf16[3,16,3328]{2,1,0:T(8,128)(2,1)}, u32[]{:S(2)}, u32[]{:S(2)}) collective-permute-start(bf16[3,16,3328]{2,1,0:T(8,128)(2,1)S(1)} %collective-permute-done.15.rest_14_), channel_id=1, source_target_pairs={{0,1},{1,0},{2,3},{3,2},{4,5},{5,4},{6,7},{7,6},{8,9},{9,8},{10,11... | collective-permute-start | bytes 958472 | tf_op jit(solution)/shard_map/ppermute | solution.py:29
  62.2 2.0 %collective-permute-start.18 = (bf16[3,16,3328]{2,1,0:T(8,128)(2,1)}, bf16[3,16,3328]{2,1,0:T(8,128)(2,1)}, u32[]{:S(2)}, u32[]{:S(2)}) collective-permute-start(bf16[3,16,3328]{2,1,0:T(8,128)(2,1)} %collective-permute-done.17.rest_16_), channel_id=1, source_target_pairs={{0,1},{1,0},{2,3},{3,2},{4,5},{5,4},{6,7},{7,6},{8,9},{9,8},{10,11... | collective-permute-start | bytes 958472 | tf_op jit(solution)/shard_map/ppermute | solution.py:29
  64.2 0.9 copy-start.6
  75.9 6.4 %copy-start.16 = (f32[512,128]{1,0:T(8,128)S(1)}, f32[512,128]{1,0:T(8,128)}, u32[]{:S(2)}) copy-start(f32[512,128]{1,0:T(8,128)} %get-tuple-element.18) | copy-start | bytes 786436
  75.9 8.0 %copy-start.11 = (f32[512,128]{1,0:T(8,128)S(1)}, f32[512,128]{1,0:T(8,128)}, u32[]{:S(2)}) copy-start(f32[512,128]{1,0:T(8,128)} %get-tuple-element.17) | copy-start | bytes 786436
  75.9 34.0 %all-to-all-start.2 = ((bf16[8,416,128]{2,1,0:T(8,128)(2,1)}), bf16[8,416,128]{2,1,0:T(8,128)(2,1)S(1)}, u32[]{:S(2)}, u32[]{:S(2)}) async-start(bf16[8,416,128]{2,1,0:T(8,128)(2,1)} %bitcast.38), calls=%async_computation.2 | async-start | bytes 1703936 | tf_op jit(solution)/shard_map/all_to_all | solution.py:389
  82.3 1.6 %collective-permute-start.19 = (f32[512,128]{1,0:T(8,128)S(1)}, f32[512,128]{1,0:T(8,128)S(1)}, u32[]{:S(2)}, u32[]{:S(2)}) collective-permute-start(f32[512,128]{1,0:T(8,128)S(1)} %copy-done.16), channel_id=1, source_target_pairs={{0,1},{1,0},{2,3},{3,2},{4,5},{5,4},{6,7},{7,6},{8,9},{9,8},{10,11... | collective-permute-start | bytes 786440 | tf_op jit(solution)/shard_map/ppermute | solution.py:29
  84.0 5.8 %collective-permute-start.20 = (f32[256,128]{1,0:T(8,128)S(1)}, f32[256,128]{1,0:T(8,128)S(1)}, u32[]{:S(2)}, u32[]{:S(2)}) collective-permute-start(f32[256,128]{1,0:T(8,128)S(1)} %constant_dynamic-slice_fusion.1), channel_id=1, source_target_pairs={{0,2},{1,3},{2,0},{3,1},{4,6},{5,7},{6,4},{7,5},{8,10},{9,11},{10,... | collective-permute-start | bytes 393224 | tf_op jit(solution)/shard_map/ppermute | solution.py:29
  89.8 4.8 %collective-permute-start.21 = (f32[128,128]{1,0:T(8,128)S(1)}, f32[128,128]{1,0:T(8,128)S(1)}, u32[]{:S(2)}, u32[]{:S(2)}) collective-permute-start(f32[128,128]{1,0:T(8,128)S(1)} %constant_dynamic-slice_fusion), channel_id=1, source_target_pairs={{0,4},{4,0},{8,12},{12,8},{16,20},{20,16},{24,28},{28,24},{1,5},{5... | collective-permute-start | bytes 196616 | tf_op jit(solution)/shard_map/ppermute | solution.py:29
  94.6 9.7 %collective-permute-start.22 = (f32[128,128]{1,0:T(8,128)S(1)}, f32[128,128]{1,0:T(8,128)S(1)}, u32[]{:S(2)}, u32[]{:S(2)}) collective-permute-start(f32[128,128]{1,0:T(8,128)S(1)} %dynamic-slice_add_fusion.1), channel_id=1, source_target_pairs={{0,8},{4,12},{8,0},{12,4},{16,24},{20,28},{24,16},{28,20},{1,9},{5... | collective-permute-start | bytes 196616 | tf_op jit(solution)/shard_map/ppermute | solution.py:29
  104.3 5.6 %collective-permute-start.23 = (f32[128,128]{1,0:T(8,128)S(1)}, f32[128,128]{1,0:T(8,128)S(1)}, u32[]{:S(2)}, u32[]{:S(2)}) collective-permute-start(f32[128,128]{1,0:T(8,128)S(1)} %add.51), channel_id=1, source_target_pairs={{0,16},{4,20},{8,24},{12,28},{16,0},{20,4},{24,8},{28,12},{1,17},{... | collective-permute-start | bytes 196616 | tf_op jit(solution)/shard_map/ppermute | solution.py:29
  111.9 2.1 %collective-permute-start.27 = (f32[1024,128]{1,0:T(8,128)S(1)}, f32[1024,128]{1,0:T(8,128)S(1)}, u32[]{:S(2)}, u32[]{:S(2)}) collective-permute-start(f32[1024,128]{1,0:T(8,128)S(1)} %cold_sum.2), channel_id=1, source_target_pairs={{0,1},{1,0},{2,3},{3,2},{4,5},{5,4},{6,7},{7,6},{8,9},{9,8},{10,11... | collective-permute-start | bytes 1572872 | tf_op jit(solution)/shard_map/ppermute | solution.py:29
  114.1 9.2 %collective-permute-start.28 = (bf16[1024,128]{1,0:T(8,128)(2,1)S(1)}, bf16[1024,128]{1,0:T(8,128)(2,1)S(1)}, u32[]{:S(2)}, u32[]{:S(2)}) collective-permute-start(bf16[1024,128]{1,0:T(8,128)(2,1)S(1)} %add_convert_fusion), channel_id=1, source_target_pairs={{0,2},{1,3},{2,0},{3,1},{4,6},{5,7},{6,4},{7,5},{8,10},{9,11},{10,... | collective-permute-start | bytes 786440 | tf_op jit(solution)/shard_map/ppermute | solution.py:29
  114.2 4.6 %collective-permute-start.24 = (f32[128,128]{1,0:T(8,128)S(1)}, f32[128,128]{1,0:T(8,128)S(1)}, u32[]{:S(2)}, u32[]{:S(2)}) collective-permute-start(f32[128,128]{1,0:T(8,128)S(1)} %add.52), channel_id=1, source_target_pairs={{0,4},{4,0},{8,12},{12,8},{16,20},{20,16},{24,28},{28,24},{1,5},{5... | collective-permute-start | bytes 196616 | tf_op jit(solution)/shard_map/ppermute | solution.py:29
  118.7 6.9 %collective-permute-start.25 = (f32[256,128]{1,0:T(8,128)S(1)}, f32[256,128]{1,0:T(8,128)S(1)}, u32[]{:S(2)}, u32[]{:S(2)}) collective-permute-start(f32[256,128]{1,0:T(8,128)S(1)} %maximum_select_fusion.3), channel_id=1, source_target_pairs={{0,2},{1,3},{2,0},{3,1},{4,6},{5,7},{6,4},{7,5},{8,10},{9,11},{10,... | collective-permute-start | bytes 393224 | tf_op jit(solution)/shard_map/ppermute | solution.py:29
  123.3 4.0 %copy-start.12 = (bf16[1024,128]{1,0:T(8,128)(2,1)S(1)}, bf16[1024,128]{1,0:T(8,128)(2,1)}, u32[]{:S(2)}) copy-start(bf16[1024,128]{1,0:T(8,128)(2,1)} %param.17) | copy-start | bytes 786436
  123.3 4.9 %collective-permute-start.29 = (f32[1024,128]{1,0:T(8,128)S(1)}, f32[1024,128]{1,0:T(8,128)S(1)}, u32[]{:S(2)}, u32[]{:S(2)}) collective-permute-start(f32[1024,128]{1,0:T(8,128)S(1)} %convert_add_fusion), channel_id=1, source_target_pairs={{0,1},{1,0},{2,3},{3,2},{4,5},{5,4},{6,7},{7,6},{8,9},{9,8},{10,11... | collective-permute-start | bytes 1572872 | tf_op jit(solution)/shard_map/ppermute | solution.py:29
  125.7 1.6 %collective-permute-start.26 = (f32[512,128]{1,0:T(8,128)S(1)}, f32[512,128]{1,0:T(8,128)S(1)}, u32[]{:S(2)}, u32[]{:S(2)}) collective-permute-start(f32[512,128]{1,0:T(8,128)S(1)} %maximum_select_fusion.2), channel_id=1, source_target_pairs={{0,1},{1,0},{2,3},{3,2},{4,5},{5,4},{6,7},{7,6},{8,9},{9,8},{10,11... | collective-permute-start | bytes 786440 | tf_op jit(solution)/shard_map/ppermute | solution.py:29
  125.8 2.5 %copy-start.9 = (bf16[2048,128]{1,0:T(8,128)(2,1)S(1)}, bf16[2048,128]{1,0:T(8,128)(2,1)}, u32[]{:S(2)}) copy-start(bf16[2048,128]{1,0:T(8,128)(2,1)} %param.19) | copy-start | bytes 1572868

commit v8 on v7

--- a/solution.py
+++ b/solution.py
@@ -81,9 +81,7 @@
         ("dp", 1, lax.axis_index("dp") % 2),
     ):
         total = half_of(total, index, 2) + swap(half_of(total, 1 - index, 2), axis, distance)
-    for distance in (2, 4):
-        total = total + swap(total, "dp", distance)
-    return total
+    return total + swap(total, "dp", 2)
 
 
 LANES = 128
@@ -401,7 +399,8 @@
         )((rows_of * (owned // 2)).reshape(1), asked, grads)
 
     others = cold_sum(1 - core, incoming)
-    incoming = after(incoming, others)
+    hot_share = hot_share + swap(hot_share, "dp", 4)
+    incoming = after(incoming, others, hot_share)
     mine = cold_sum(core, incoming)
     hot_share = paired(hot_share, swap(hot_share, "dp", 1), lax.axis_index("dp") % 2)
     mine = (mine + swap(others, "rep", 1)).astype(BF)

time: 129 us -> 133 us (1.031)
  other arithmetic: 4.28 us -> 6.66 us
  Pallas kernels: 21.3 us -> 23 us
    ppermute x29, waiting for transfers between devices: 49.2 us -> 45.6 us  [swap(): return lax.ppermute(value, axis, [(i, i ^ distance) for i in range(size)])]
    all_to_all x1, waiting for transfers between devices: 0.01 us -> 3.52 us  [small_step(): lax.all_to_all(send, 'dp', split_axis=0, concat_axis=0, tiled=True)]
    all_to_all x1, starting transfers between devices: 6.29 us -> 3.55 us  [small_step(): lax.all_to_all(found, 'dp', split_axis=0, concat_axis=0, tiled=True)]
    ppermute x29, starting transfers between devices: 24 us -> 26.2 us  [swap(): return lax.ppermute(value, axis, [(i, i ^ distance) for i in range(size)])]
    pallas_call x1, Pallas kernels: 3.07 us -> 4.78 us  [small_step(): call(functools.partial(serve_body, n_data, capacity), shape((places, E),...]
    add x2, other arithmetic: 0.02 us -> 1.49 us  [the longest x1 1.48 us: small_step(): hot_share = hot_share + swap(hot_share, 'dp', 4)]
  transfers between devices with their start and end apart: 33 -> 33, of which waited for: 16 -> 17; matrix products, arithmetic and copies ran while one was open for 3% -> 5% of each run, Pallas kernels for 7% -> 8%
where the time goes in v8:
time: 133 us; the launch traced here: 134 us
  waiting for transfers between devices  53.9 us (41%)
  starting transfers between devices  44.1 us (33%)
  Pallas kernels  23 us (17%)
  other arithmetic  6.66 us (5%)
  local copies, waits for them, and re-layouts  5.2 us (4%)
    ppermute x29, waiting for transfers between devices, swap(): return lax.ppermute(value, axis, [(i, i ^ distance) for i in range(size)])  45.6 us
    ppermute x29, starting transfers between devices, swap(): return lax.ppermute(value, axis, [(i, i ^ distance) for i in range(size)])  26.2 us
    pallas_call x1, Pallas kernels, small_step(): call(cross_body, (shape((places, E), BF), shape((HOT // 2, E), F32), shap...  10.8 us
    all_to_all x1, starting transfers between devices, small_step(): lax.all_to_all(send, 'dp', split_axis=0, concat_axis=0, tiled=True)  7.29 us
    all_to_all x1, starting transfers between devices, small_step(): asked = lax.all_to_all(ask, 'dp', split_axis=0, concat_axis=0, tiled=True)  5.01 us
    pallas_call x1, Pallas kernels, small_step(): call(functools.partial(serve_body, n_data, capacity), shape((places, E),...  4.78 us
    pallas_call x2, Pallas kernels, cold_sum(): call(functools.partial(cold_sum_body, n_data, capacity), shape((owned //...  3.98 us
    all_to_all x1, starting transfers between devices, small_step(): lax.all_to_all(found, 'dp', split_axis=0, concat_axis=0, tiled=True)  3.55 us
  transfers between devices with their start and end apart: 33, of which 17 were waited for; matrix products, arithmetic and copies ran while one was open for 5% of the time, Pallas kernels for 8%

profile of v8, /device:TPU:0, one launch (start us, length us, event | category | flops | bytes accessed | tf_op | source)
XLA Modules:
  0.0 133.9 jit_solution(10531712356944998689)
XLA Ops:
  0.6 1.0 maximum_bitcast_fusion.rest_0_
  1.7 3.1 %collective-permute-start = (bf16[2,1,16,3328]{3,2,1,0:T(8,128)(2,1)S(1)}, bf16[2,1,16,3328]{3,2,1,0:T(8,128)(2,1)S(1)}, u32[]{:S(2)}, u32[]{:S(2)}) collective-permute-start(bf16[2,1,16,3328]{3,2,1,0:T(8,128)(2,1)S(1)} %maximum_bitcast_fusion.rest_0_), channel_id=1, source_target_pairs={{0,8},{4,12},{8,0},{12,4},{16,24},{20,28},{24,16},{28,20},{1,9},{5... | collective-permute-start | bytes 638984 | tf_op jit(solution)/shard_map/ppermute | solution.py:29
  4.8 2.6 %collective-permute-start.1 = (bf16[2,1,16,3328]{3,2,1,0:T(8,128)(2,1)S(1)}, bf16[2,1,16,3328]{3,2,1,0:T(8,128)(2,1)S(1)}, u32[]{:S(2)}, u32[]{:S(2)}) collective-permute-start(bf16[2,1,16,3328]{3,2,1,0:T(8,128)(2,1)S(1)} %maximum_bitcast_fusion.rest_0_), channel_id=1, source_target_pairs={{0,16},{4,20},{8,24},{12,28},{16,0},{20,4},{24,8},{28,12},{1,17},{... | collective-permute-start | bytes 638984 | tf_op jit(solution)/shard_map/ppermute | solution.py:29
  7.4 1.7 %collective-permute-start.3 = (bf16[2,1,16,3328]{3,2,1,0:T(8,128)(2,1)S(1)}, bf16[2,1,16,3328]{3,2,1,0:T(8,128)(2,1)}, u32[]{:S(2)}, u32[]{:S(2)}) collective-permute-start(bf16[2,1,16,3328]{3,2,1,0:T(8,128)(2,1)S(1)} %maximum_bitcast_fusion.rest_0_), channel_id=1, source_target_pairs={{0,2},{1,3},{2,0},{3,1},{4,6},{5,7},{6,4},{7,5},{8,10},{9,11},{10,... | collective-permute-start | bytes 638984 | tf_op jit(solution)/shard_map/ppermute | solution.py:29
  9.1 1.5 %collective-permute-start.4 = (bf16[2,1,16,3328]{3,2,1,0:T(8,128)(2,1)S(1)}, bf16[2,1,16,3328]{3,2,1,0:T(8,128)(2,1)}, u32[]{:S(2)}, u32[]{:S(2)}) collective-permute-start(bf16[2,1,16,3328]{3,2,1,0:T(8,128)(2,1)S(1)} %maximum_bitcast_fusion.rest_0_), channel_id=1, source_target_pairs={{0,4},{4,0},{8,12},{12,8},{16,20},{20,16},{24,28},{28,24},{1,5},{5... | collective-permute-start | bytes 638984 | tf_op jit(solution)/shard_map/ppermute | solution.py:29
  10.6 0.7 reduce
  11.3 0.2 reshape.35
  11.6 0.6 copy-done.4
  12.2 1.2 route.1
  13.4 0.6 copy-done.5
  14.0 5.0 %all-to-all-start = ((s32[8,4,128]{2,1,0:T(4,128)}), s32[8,4,128]{2,1,0:T(4,128)S(1)}, u32[]{:S(2)}, u32[]{:S(2)}) async-start(s32[8,4,128]{2,1,0:T(4,128)} %bitcast.5), calls=%async_computation | async-start | bytes 32768 | tf_op jit(solution)/shard_map/all_to_all | solution.py:328
  19.1 2.2 %hot_rows.1.hot_ref = bf16[1664,128]{1,0:T(8,128)(2,1)S(1)} custom-call(s32[1664]{0:T(1024)S(1)} %bitcast.34, f32[1024,128]{1,0:T(8,128)S(1)} %copy-done.1), custom_call_target="tpu_custom_call" | custom-call | flops 1 | bytes 1 | tf_op jit(solution)/shard_map/hot_rows/pallas_call | solution.py:331
  21.3 0.7 copy-done.2
  22.1 2.0 %collective-permute-start.5 = (bf16[2,1,16,3328]{3,2,1,0:T(8,128)(2,1)S(1)}, bf16[2,1,16,3328]{3,2,1,0:T(8,128)(2,1)}, u32[]{:S(2)}, u32[]{:S(2)}) collective-permute-start(bf16[2,1,16,3328]{3,2,1,0:T(8,128)(2,1)S(1)} %maximum_bitcast_fusion.rest_0_), channel_id=1, source_target_pairs={{0,6},{1,7},{2,4},{3,5},{4,2},{5,3},{6,0},{7,1},{8,14},{9,15},{10,... | collective-permute-start | bytes 638984 | tf_op jit(solution)/shard_map/ppermute | solution.py:46
  24.0 0.1 pad_maximum_fusion.rest_4_
  24.1 3.2 %all-to-all-done = s32[8,4,128]{2,1,0:T(4,128)S(1)} async-done(((s32[8,4,128]{2,1,0:T(4,128)}), s32[8,4,128]{2,1,0:T(4,128)S(1)}, u32[]{:S(2)}, u32[]{:S(2)}) %all-to-all-start) | async-done | bytes 16416 | tf_op jit(solution)/shard_map/all_to_all | solution.py:328
  27.4 1.5 %collective-permute-done.5.rest_3_ = bf16[2,1,16,3328]{3,2,1,0:T(8,128)(2,1)} collective-permute-done((bf16[2,1,16,3328]{3,2,1,0:T(8,128)(2,1)S(1)}, bf16[2,1,16,3328]{3,2,1,0:T(8,128)(2,1)}, u32[]{:S(2)}, u32[]{:S(2)}) %collective-permute-start.5) | collective-permute-done | bytes 213024 | tf_op jit(solution)/shard_map/ppermute | solution.py:46
  28.9 2.0 %collective-permute-start.7 = (bf16[2,3,16,3328]{3,2,1,0:T(8,128)(2,1)S(1)}, bf16[2,3,16,3328]{3,2,1,0:T(8,128)(2,1)}, u32[]{:S(2)}, u32[]{:S(2)}) collective-permute-start(bf16[2,3,16,3328]{3,2,1,0:T(8,128)(2,1)S(1)} %pad_maximum_fusion.rest_4_), channel_id=1, source_target_pairs={{0,4},{4,0},{8,12},{12,8},{16,20},{20,16},{24,28},{28,24},{1,5},{5... | collective-permute-start | bytes 1916936 | tf_op jit(solution)/shard_map/ppermute | solution.py:29
  31.0 0.6 collective-permute-start.6
  31.5 0.2 collective-permute-start.12
  31.8 4.8 %serve.1 = bf16[3328,128]{1,0:T(8,128)(2,1)} custom-call(s32[4096]{0:T(1024)S(1)} %bitcast.29, f32[2048,128]{1,0:T(8,128)S(1)} %copy-done), custom_call_target="tpu_custom_call" | custom-call | flops 1 | bytes 1 | tf_op jit(solution)/shard_map/serve/pallas_call | solution.py:342
  36.6 3.6 %all-to-all-start.1 = ((bf16[8,416,128]{2,1,0:T(8,128)(2,1)}), bf16[8,416,128]{2,1,0:T(8,128)(2,1)S(1)}, u32[]{:S(2)}, u32[]{:S(2)}) async-start(bf16[8,416,128]{2,1,0:T(8,128)(2,1)} %bitcast.13), calls=%async_computation.1 | async-start | bytes 1703936 | tf_op jit(solution)/shard_map/all_to_all | solution.py:350
  40.1 0.1 collective-permute-start.10
  40.2 5.8 %collective-permute-done.7.rest_6_ = bf16[2,3,16,3328]{3,2,1,0:T(8,128)(2,1)} collective-permute-done((bf16[2,3,16,3328]{3,2,1,0:T(8,128)(2,1)S(1)}, bf16[2,3,16,3328]{3,2,1,0:T(8,128)(2,1)}, u32[]{:S(2)}, u32[]{:S(2)}) %collective-permute-start.7) | collective-permute-done | bytes 639008 | tf_op jit(solution)/shard_map/ppermute | solution.py:29
  46.0 1.0 slice_bitcast_fusion.1
  47.0 0.8 collective-permute-done.6.rest_5_
  47.9 1.0 slice_bitcast_fusion
  48.9 0.6 collective-permute-start.15
  49.5 0.2 collective-permute-start.13
  49.8 0.3 collective-permute-start.14
  50.0 2.0 %collective-permute-start.17 = (bf16[3,16,3328]{2,1,0:T(8,128)(2,1)S(1)}, bf16[3,16,3328]{2,1,0:T(8,128)(2,1)}, u32[]{:S(2)}, u32[]{:S(2)}) collective-permute-start(bf16[3,16,3328]{2,1,0:T(8,128)(2,1)S(1)} %slice_bitcast_fusion), channel_id=1, source_target_pairs={{0,4},{4,0},{8,12},{12,8},{16,20},{20,16},{24,28},{28,24},{1,5},{5... | collective-permute-start | bytes 958472 | tf_op jit(solution)/shard_map/ppermute | solution.py:29
  52.0 6.9 %collective-permute-done.15.rest_14_ = bf16[3,16,3328]{2,1,0:T(8,128)(2,1)S(1)} collective-permute-done((bf16[3,16,3328]{2,1,0:T(8,128)(2,1)S(1)}, bf16[3,16,3328]{2,1,0:T(8,128)(2,1)S(1)}, u32[]{:S(2)}, u32[]{:S(2)}) %collective-permute-start.15) | collective-permute-done | bytes 319520 | tf_op jit(solution)/shard_map/ppermute | solution.py:29
  58.9 3.3 %collective-permute-done.17.rest_16_ = bf16[3,16,3328]{2,1,0:T(8,128)(2,1)} collective-permute-done((bf16[3,16,3328]{2,1,0:T(8,128)(2,1)S(1)}, bf16[3,16,3328]{2,1,0:T(8,128)(2,1)}, u32[]{:S(2)}, u32[]{:S(2)}) %collective-permute-start.17) | collective-permute-done | bytes 319520 | tf_op jit(solution)/shard_map/ppermute | solution.py:29
  62.3 1.9 %collective-permute-done.18.rest_17_ = bf16[3,16,3328]{2,1,0:T(8,128)(2,1)} collective-permute-done((bf16[3,16,3328]{2,1,0:T(8,128)(2,1)}, bf16[3,16,3328]{2,1,0:T(8,128)(2,1)}, u32[]{:S(2)}, u32[]{:S(2)}) %collective-permute-start.18) | collective-permute-done | bytes 319520 | tf_op jit(solution)/shard_map/ppermute | solution.py:29
  64.2 0.9 copy-done.6
  65.1 10.8 %cross.1 = (bf16[3328,128]{1,0:T(8,128)(2,1)}, f32[512,128]{1,0:T(8,128)}, f32[512,128]{1,0:T(8,128)}) custom-call(s32[1]{0:T(128)} %bitcast.core_ref, s32[2048]{0:T(1024)} %bitcast.36, s32[13,128]{1,0:T(8,128)} %bitcast.33, bf16[3328,128]{1,0:T(8,128)(2,1)} %bitcast.37, bf16[1664,128]{1,0:T(8,128)(2,1)} %copy-done.2, s32[1,128]{1,0:T(1,128)} %bitcast.41, ...), custom_call_target="tpu_custom_call" | custom-call | flops 1744830464 | bytes 20000000 | tf_op jit(solution)/shard_map/cross/pallas_call | solution.py:357
  75.9 7.3 %all-to-all-start.2 = ((bf16[8,416,128]{2,1,0:T(8,128)(2,1)}), bf16[8,416,128]{2,1,0:T(8,128)(2,1)S(1)}, u32[]{:S(2)}, u32[]{:S(2)}) async-start(bf16[8,416,128]{2,1,0:T(8,128)(2,1)} %bitcast.38), calls=%async_computation.2 | async-start | bytes 1703936 | tf_op jit(solution)/shard_map/all_to_all | solution.py:387
  83.2 0.1 collective-permute-start.19
  83.3 1.5 %collective-permute-done.19 = f32[512,128]{1,0:T(8,128)S(1)} collective-permute-done((f32[512,128]{1,0:T(8,128)S(1)}, f32[512,128]{1,0:T(8,128)S(1)}, u32[]{:S(2)}, u32[]{:S(2)}) %collective-permute-start.19) | collective-permute-done | bytes 262176 | tf_op jit(solution)/shard_map/ppermute | solution.py:29
  84.9 1.9 %collective-permute-start.20 = (f32[256,128]{1,0:T(8,128)S(1)}, f32[256,128]{1,0:T(8,128)S(1)}, u32[]{:S(2)}, u32[]{:S(2)}) collective-permute-start(f32[256,128]{1,0:T(8,128)S(1)} %constant_dynamic-slice_fusion.1), channel_id=1, source_target_pairs={{0,2},{1,3},{2,0},{3,1},{4,6},{5,7},{6,4},{7,5},{8,10},{9,11},{10,... | collective-permute-start | bytes 393224 | tf_op jit(solution)/shard_map/ppermute | solution.py:29
  86.8 3.8 %collective-permute-done.20 = f32[256,128]{1,0:T(8,128)S(1)} collective-permute-done((f32[256,128]{1,0:T(8,128)S(1)}, f32[256,128]{1,0:T(8,128)S(1)}, u32[]{:S(2)}, u32[]{:S(2)}) %collective-permute-start.20) | collective-permute-done | bytes 131104 | tf_op jit(solution)/shard_map/ppermute | solution.py:29
  90.7 2.0 %collective-permute-start.21 = (f32[128,128]{1,0:T(8,128)S(1)}, f32[128,128]{1,0:T(8,128)S(1)}, u32[]{:S(2)}, u32[]{:S(2)}) collective-permute-start(f32[128,128]{1,0:T(8,128)S(1)} %constant_dynamic-slice_fusion), channel_id=1, source_target_pairs={{0,4},{4,0},{8,12},{12,8},{16,20},{20,16},{24,28},{28,24},{1,5},{5... | collective-permute-start | bytes 196616 | tf_op jit(solution)/shard_map/ppermute | solution.py:29
  92.7 2.8 %collective-permute-done.21 = f32[128,128]{1,0:T(8,128)S(1)} collective-permute-done((f32[128,128]{1,0:T(8,128)S(1)}, f32[128,128]{1,0:T(8,128)S(1)}, u32[]{:S(2)}, u32[]{:S(2)}) %collective-permute-start.21) | collective-permute-done | bytes 65568 | tf_op jit(solution)/shard_map/ppermute | solution.py:29
  95.5 3.8 %collective-permute-start.22 = (f32[128,128]{1,0:T(8,128)S(1)}, f32[128,128]{1,0:T(8,128)S(1)}, u32[]{:S(2)}, u32[]{:S(2)}) collective-permute-start(f32[128,128]{1,0:T(8,128)S(1)} %dynamic-slice_add_fusion.1), channel_id=1, source_target_pairs={{0,8},{4,12},{8,0},{12,4},{16,24},{20,28},{24,16},{28,20},{1,9},{5... | collective-permute-start | bytes 196616 | tf_op jit(solution)/shard_map/ppermute | solution.py:29
  99.2 2.3 %collective-permute-done.22 = f32[128,128]{1,0:T(8,128)S(1)} collective-permute-done((f32[128,128]{1,0:T(8,128)S(1)}, f32[128,128]{1,0:T(8,128)S(1)}, u32[]{:S(2)}, u32[]{:S(2)}) %collective-permute-start.22) | collective-permute-done | bytes 65568 | tf_op jit(solution)/shard_map/ppermute | solution.py:29
  101.6 3.5 %all-to-all-done.2 = bf16[8,416,128]{2,1,0:T(8,128)(2,1)S(1)} async-done(((bf16[8,416,128]{2,1,0:T(8,128)(2,1)}), bf16[8,416,128]{2,1,0:T(8,128)(2,1)S(1)}, u32[]{:S(2)}, u32[]{:S(2)}) %all-to-all-start.2) | async-done | bytes 852000 | tf_op jit(solution)/shard_map/all_to_all | solution.py:387
  105.1 2.0 %cold_sum.2 = f32[1024,128]{1,0:T(8,128)S(1)} custom-call(s32[1]{0:T(128)} %bitcast.21.first_ref, s32[32,128]{1,0:T(8,128)S(1)} %bitcast.30, bf16[3328,128]{1,0:T(8,128)(2,1)S(1)} %bitcast.27), custom_call_target="tpu_custom_call" | custom-call | flops 1000000000 | bytes 10000000 | tf_op jit(solution)/shard_map/cold_sum/pallas_call | solution.py:392
  107.1 0.1 collective-permute-start.27
  107.2 0.9 collective-permute-start.23
  108.0 6.1 %collective-permute-done.23 = f32[128,128]{1,0:T(8,128)} collective-permute-done((f32[128,128]{1,0:T(8,128)S(1)}, f32[128,128]{1,0:T(8,128)}, u32[]{:S(2)}, u32[]{:S(2)}) %collective-permute-start.23) | collective-permute-done | bytes 65568 | tf_op jit(solution)/shard_map/ppermute | solution.py:29
  114.1 1.5 %add.52 = f32[128,128]{1,0:T(8,128)} add(f32[128,128]{1,0:T(8,128)S(1)} %add.51, f32[128,128]{1,0:T(8,128)} %collective-permute-done.23) | non-fusion elementwise | flops 16384 | bytes 196608 | tf_op jit(solution)/shard_map/add | solution.py:402
  115.5 2.0 %cold_sum.3 = f32[1024,128]{1,0:T(8,128)S(1)} custom-call(s32[1]{0:T(128)} %bitcast.20.first_ref, s32[32,128]{1,0:T(8,128)S(1)} %bitcast.31, bf16[3328,128]{1,0:T(8,128)(2,1)S(1)} %bitcast.28), custom_call_target="tpu_custom_call" | custom-call | flops 1000000000 | bytes 10000000 | tf_op jit(solution)/shard_map/cold_sum/pallas_call | solution.py:392
  117.6 1.9 %collective-permute-start.28 = (bf16[1024,128]{1,0:T(8,128)(2,1)S(1)}, bf16[1024,128]{1,0:T(8,128)(2,1)S(1)}, u32[]{:S(2)}, u32[]{:S(2)}) collective-permute-start(bf16[1024,128]{1,0:T(8,128)(2,1)S(1)} %add_convert_fusion), channel_id=1, source_target_pairs={{0,2},{1,3},{2,0},{3,1},{4,6},{5,7},{6,4},{7,5},{8,10},{9,11},{10,... | collective-permute-start | bytes 786440 | tf_op jit(solution)/shard_map/ppermute | solution.py:29
  119.5 0.3 collective-permute-start.24
  119.8 4.2 %collective-permute-done.24 = f32[128,128]{1,0:T(8,128)S(1)} collective-permute-done((f32[128,128]{1,0:T(8,128)}, f32[128,128]{1,0:T(8,128)S(1)}, u32[]{:S(2)}, u32[]{:S(2)}) %collective-permute-start.24) | collective-permute-done | bytes 65568 | tf_op jit(solution)/shard_map/ppermute | solution.py:29
  124.0 0.9 maximum_select_fusion.3
  125.0 0.2 collective-permute-start.25
  125.2 1.0 collective-permute-done.28
  126.2 0.1 collective-permute-start.29
  126.3 3.7 %collective-permute-done.25 = f32[256,128]{1,0:T(8,128)S(1)} collective-permute-done((f32[256,128]{1,0:T(8,128)S(1)}, f32[256,128]{1,0:T(8,128)S(1)}, u32[]{:S(2)}, u32[]{:S(2)}) %collective-permute-start.25) | collective-permute-done | bytes 131104 | tf_op jit(solution)/shard_map/ppermute | solution.py:29
  130.0 0.1 collective-permute-start.26
  130.1 1.5 %collective-permute-done.26 = f32[512,128]{1,0:T(8,128)S(1)} collective-permute-done((f32[512,128]{1,0:T(8,128)S(1)}, f32[512,128]{1,0:T(8,128)S(1)}, u32[]{:S(2)}, u32[]{:S(2)}) %collective-permute-start.26) | collective-permute-done | bytes 262176 | tf_op jit(solution)/shard_map/ppermute | solution.py:29
  131.6 1.0 multiply_subtract_fusion.1
  132.6 1.3 multiply_subtract_fusion
  (62 shorter events, 0.4 us)
Async XLA Ops:
  0.6 18.4 %copy-start.1 = (f32[1024,128]{1,0:T(8,128)S(1)}, f32[1024,128]{1,0:T(8,128)}, u32[]{:S(2)}) copy-start(f32[1024,128]{1,0:T(8,128)} %table_ref.2) | copy-start | bytes 1572868
  1.7 29.3 %copy-start.8 = (bf16[2,1,16,3328]{3,2,1,0:T(8,128)(2,1)}, bf16[2,1,16,3328]{3,2,1,0:T(8,128)(2,1)S(1)}, u32[]{:S(2)}) copy-start(bf16[2,1,16,3328]{3,2,1,0:T(8,128)(2,1)S(1)} %maximum_bitcast_fusion.rest_0_) | copy-start | bytes 638980
  1.7 20.4 %collective-permute-start = (bf16[2,1,16,3328]{3,2,1,0:T(8,128)(2,1)S(1)}, bf16[2,1,16,3328]{3,2,1,0:T(8,128)(2,1)S(1)}, u32[]{:S(2)}, u32[]{:S(2)}) collective-permute-start(bf16[2,1,16,3328]{3,2,1,0:T(8,128)(2,1)S(1)} %maximum_bitcast_fusion.rest_0_), channel_id=1, source_target_pairs={{0,8},{4,12},{8,0},{12,4},{16,24},{20,28},{24,16},{28,20},{1,9},{5... | collective-permute-start | bytes 638984 | tf_op jit(solution)/shard_map/ppermute | solution.py:29
  4.8 19.3 %collective-permute-start.1 = (bf16[2,1,16,3328]{3,2,1,0:T(8,128)(2,1)S(1)}, bf16[2,1,16,3328]{3,2,1,0:T(8,128)(2,1)S(1)}, u32[]{:S(2)}, u32[]{:S(2)}) collective-permute-start(bf16[2,1,16,3328]{3,2,1,0:T(8,128)(2,1)S(1)} %maximum_bitcast_fusion.rest_0_), channel_id=1, source_target_pairs={{0,16},{4,20},{8,24},{12,28},{16,0},{20,4},{24,8},{28,12},{1,17},{... | collective-permute-start | bytes 638984 | tf_op jit(solution)/shard_map/ppermute | solution.py:29
  7.4 16.7 %collective-permute-start.2 = (bf16[2,1,16,3328]{3,2,1,0:T(8,128)(2,1)S(1)}, bf16[2,1,16,3328]{3,2,1,0:T(8,128)(2,1)S(1)}, u32[]{:S(2)}, u32[]{:S(2)}) collective-permute-start(bf16[2,1,16,3328]{3,2,1,0:T(8,128)(2,1)S(1)} %maximum_bitcast_fusion.rest_0_), channel_id=1, source_target_pairs={{0,24},{4,28},{8,16},{12,20},{16,8},{20,12},{24,0},{28,4},{1,25},{... | collective-permute-start | bytes 638984 | tf_op jit(solution)/shard_map/ppermute | solution.py:29
  7.4 20.0 %collective-permute-start.3 = (bf16[2,1,16,3328]{3,2,1,0:T(8,128)(2,1)S(1)}, bf16[2,1,16,3328]{3,2,1,0:T(8,128)(2,1)}, u32[]{:S(2)}, u32[]{:S(2)}) collective-permute-start(bf16[2,1,16,3328]{3,2,1,0:T(8,128)(2,1)S(1)} %maximum_bitcast_fusion.rest_0_), channel_id=1, source_target_pairs={{0,2},{1,3},{2,0},{3,1},{4,6},{5,7},{6,4},{7,5},{8,10},{9,11},{10,... | collective-permute-start | bytes 638984 | tf_op jit(solution)/shard_map/ppermute | solution.py:29
  9.1 18.3 %collective-permute-start.4 = (bf16[2,1,16,3328]{3,2,1,0:T(8,128)(2,1)S(1)}, bf16[2,1,16,3328]{3,2,1,0:T(8,128)(2,1)}, u32[]{:S(2)}, u32[]{:S(2)}) collective-permute-start(bf16[2,1,16,3328]{3,2,1,0:T(8,128)(2,1)S(1)} %maximum_bitcast_fusion.rest_0_), channel_id=1, source_target_pairs={{0,4},{4,0},{8,12},{12,8},{16,20},{20,16},{24,28},{28,24},{1,5},{5... | collective-permute-start | bytes 638984 | tf_op jit(solution)/shard_map/ppermute | solution.py:29
  11.5 0.7 copy-start.4
  13.4 0.6 copy-start.5
  14.0 5.0 %copy-start.3 = (s32[128,13]{0,1:T(8,128)S(1)}, s32[128,13]{0,1:T(8,128)}, u32[]{:S(2)}) copy-start(s32[128,13]{0,1:T(8,128)} %param.12) | copy-start | bytes 19972
  14.0 13.4 %all-to-all-start = ((s32[8,4,128]{2,1,0:T(4,128)}), s32[8,4,128]{2,1,0:T(4,128)S(1)}, u32[]{:S(2)}, u32[]{:S(2)}) async-start(s32[8,4,128]{2,1,0:T(4,128)} %bitcast.5), calls=%async_computation | async-start | bytes 32768 | tf_op jit(solution)/shard_map/all_to_all | solution.py:328
  19.1 12.7 %copy-start = (f32[2048,128]{1,0:T(8,128)S(1)}, f32[2048,128]{1,0:T(8,128)}, u32[]{:S(2)}) copy-start(f32[2048,128]{1,0:T(8,128)} %table_ref.3) | copy-start | bytes 3145732
  21.3 0.8 copy-start.2
  22.1 6.9 %collective-permute-start.5 = (bf16[2,1,16,3328]{3,2,1,0:T(8,128)(2,1)S(1)}, bf16[2,1,16,3328]{3,2,1,0:T(8,128)(2,1)}, u32[]{:S(2)}, u32[]{:S(2)}) collective-permute-start(bf16[2,1,16,3328]{3,2,1,0:T(8,128)(2,1)S(1)} %maximum_bitcast_fusion.rest_0_), channel_id=1, source_target_pairs={{0,6},{1,7},{2,4},{3,5},{4,2},{5,3},{6,0},{7,1},{8,14},{9,15},{10,... | collective-permute-start | bytes 638984 | tf_op jit(solution)/shard_map/ppermute | solution.py:46
  24.1 12.4 %copy-start.7 = (bf16[2,3,16,3328]{3,2,1,0:T(8,128)(2,1)}, bf16[2,3,16,3328]{3,2,1,0:T(8,128)(2,1)S(1)}, u32[]{:S(2)}) copy-start(bf16[2,3,16,3328]{3,2,1,0:T(8,128)(2,1)S(1)} %pad_maximum_fusion.rest_4_) | copy-start | bytes 1916932
  28.9 17.1 %collective-permute-start.7 = (bf16[2,3,16,3328]{3,2,1,0:T(8,128)(2,1)S(1)}, bf16[2,3,16,3328]{3,2,1,0:T(8,128)(2,1)}, u32[]{:S(2)}, u32[]{:S(2)}) collective-permute-start(bf16[2,3,16,3328]{3,2,1,0:T(8,128)(2,1)S(1)} %pad_maximum_fusion.rest_4_), channel_id=1, source_target_pairs={{0,4},{4,0},{8,12},{12,8},{16,20},{20,16},{24,28},{28,24},{1,5},{5... | collective-permute-start | bytes 1916936 | tf_op jit(solution)/shard_map/ppermute | solution.py:29
  31.0 17.9 %collective-permute-start.8 = (bf16[2,1,16,3328]{3,2,1,0:T(8,128)(2,1)S(1)}, bf16[2,1,16,3328]{3,2,1,0:T(8,128)(2,1)}, u32[]{:S(2)}, u32[]{:S(2)}) collective-permute-start(bf16[2,1,16,3328]{3,2,1,0:T(8,128)(2,1)S(1)} %maximum_bitcast_fusion.rest_0_), channel_id=1, source_target_pairs={{0,1},{1,0},{2,3},{3,2},{4,5},{5,4},{6,7},{7,6},{8,9},{9,8},{10,11... | collective-permute-start | bytes 638984 | tf_op jit(solution)/shard_map/ppermute | solution.py:29
  31.0 16.9 %collective-permute-start.6 = (bf16[2,3,16,3328]{3,2,1,0:T(8,128)(2,1)S(1)}, bf16[2,3,16,3328]{3,2,1,0:T(8,128)(2,1)}, u32[]{:S(2)}, u32[]{:S(2)}) collective-permute-start(bf16[2,3,16,3328]{3,2,1,0:T(8,128)(2,1)S(1)} %pad_maximum_fusion.rest_4_), channel_id=1, source_target_pairs={{0,2},{1,3},{2,0},{3,1},{4,6},{5,7},{6,4},{7,5},{8,10},{9,11},{10,... | collective-permute-start | bytes 1916936 | tf_op jit(solution)/shard_map/ppermute | solution.py:29
  31.5 30.7 %collective-permute-start.12 = (bf16[2,3,16,3328]{3,2,1,0:T(8,128)(2,1)S(1)}, bf16[2,3,16,3328]{3,2,1,0:T(8,128)(2,1)}, u32[]{:S(2)}, u32[]{:S(2)}) collective-permute-start(bf16[2,3,16,3328]{3,2,1,0:T(8,128)(2,1)S(1)} %pad_maximum_fusion.rest_4_), channel_id=1, source_target_pairs={{0,1},{1,0},{2,3},{3,2},{4,5},{5,4},{6,7},{7,6},{8,9},{9,8},{10,11... | collective-permute-start | bytes 1916936 | tf_op jit(solution)/shard_map/ppermute | solution.py:29
  36.6 27.6 %all-to-all-start.1 = ((bf16[8,416,128]{2,1,0:T(8,128)(2,1)}), bf16[8,416,128]{2,1,0:T(8,128)(2,1)S(1)}, u32[]{:S(2)}, u32[]{:S(2)}) async-start(bf16[8,416,128]{2,1,0:T(8,128)(2,1)} %bitcast.13), calls=%async_computation.1 | async-start | bytes 1703936 | tf_op jit(solution)/shard_map/all_to_all | solution.py:350
  40.1 9.4 %collective-permute-start.10 = (bf16[2,1,16,3328]{3,2,1,0:T(8,128)(2,1)}, bf16[2,1,16,3328]{3,2,1,0:T(8,128)(2,1)S(1)}, u32[]{:S(2)}, u32[]{:S(2)}) collective-permute-start(bf16[2,1,16,3328]{3,2,1,0:T(8,128)(2,1)} %collective-permute-done.4.rest_2_), channel_id=1, source_target_pairs={{0,1},{1,0},{2,3},{3,2},{4,5},{5,4},{6,7},{7,6},{8,9},{9,8},{10,11... | collective-permute-start | bytes 638984 | tf_op jit(solution)/shard_map/ppermute | solution.py:29
  46.0 3.7 %collective-permute-start.11 = (bf16[2,1,16,3328]{3,2,1,0:T(8,128)(2,1)}, bf16[2,1,16,3328]{3,2,1,0:T(8,128)(2,1)S(1)}, u32[]{:S(2)}, u32[]{:S(2)}) collective-permute-start(bf16[2,1,16,3328]{3,2,1,0:T(8,128)(2,1)} %collective-permute-done.5.rest_3_), channel_id=1, source_target_pairs={{0,1},{1,0},{2,3},{3,2},{4,5},{5,4},{6,7},{7,6},{8,9},{9,8},{10,11... | collective-permute-start | bytes 638984 | tf_op jit(solution)/shard_map/ppermute | solution.py:29
  47.9 2.2 %collective-permute-start.9 = (bf16[2,1,16,3328]{3,2,1,0:T(8,128)(2,1)}, bf16[2,1,16,3328]{3,2,1,0:T(8,128)(2,1)S(1)}, u32[]{:S(2)}, u32[]{:S(2)}) collective-permute-start(bf16[2,1,16,3328]{3,2,1,0:T(8,128)(2,1)} %collective-permute-done.3.rest_1_), channel_id=1, source_target_pairs={{0,1},{1,0},{2,3},{3,2},{4,5},{5,4},{6,7},{7,6},{8,9},{9,8},{10,11... | collective-permute-start | bytes 638984 | tf_op jit(solution)/shard_map/ppermute | solution.py:29
  48.9 10.0 %collective-permute-start.15 = (bf16[3,16,3328]{2,1,0:T(8,128)(2,1)S(1)}, bf16[3,16,3328]{2,1,0:T(8,128)(2,1)S(1)}, u32[]{:S(2)}, u32[]{:S(2)}) collective-permute-start(bf16[3,16,3328]{2,1,0:T(8,128)(2,1)S(1)} %slice_bitcast_fusion.1), channel_id=1, source_target_pairs={{0,2},{1,3},{2,0},{3,1},{4,6},{5,7},{6,4},{7,5},{8,10},{9,11},{10,... | collective-permute-start | bytes 958472 | tf_op jit(solution)/shard_map/ppermute | solution.py:29
  49.5 12.7 %copy-start.13 = (bf16[2,1,16,3328]{3,2,1,0:T(8,128)(2,1)}, bf16[2,1,16,3328]{3,2,1,0:T(8,128)(2,1)S(1)}, u32[]{:S(2)}) copy-start(bf16[2,1,16,3328]{3,2,1,0:T(8,128)(2,1)S(1)} %collective-permute-done.10.rest_9_) | copy-start | bytes 638980
  49.5 12.7 %collective-permute-start.13 = (bf16[2,3,16,3328]{3,2,1,0:T(8,128)(2,1)}, bf16[2,3,16,3328]{3,2,1,0:T(8,128)(2,1)}, u32[]{:S(2)}, u32[]{:S(2)}) collective-permute-start(bf16[2,3,16,3328]{3,2,1,0:T(8,128)(2,1)} %collective-permute-done.6.rest_5_), channel_id=1, source_target_pairs={{0,1},{1,0},{2,3},{3,2},{4,5},{5,4},{6,7},{7,6},{8,9},{9,8},{10,11... | collective-permute-start | bytes 1916936 | tf_op jit(solution)/shard_map/ppermute | solution.py:29
  49.8 12.5 %copy-start.14 = (bf16[2,1,16,3328]{3,2,1,0:T(8,128)(2,1)}, bf16[2,1,16,3328]{3,2,1,0:T(8,128)(2,1)S(1)}, u32[]{:S(2)}) copy-start(bf16[2,1,16,3328]{3,2,1,0:T(8,128)(2,1)S(1)} %collective-permute-done.11.rest_10_) | copy-start | bytes 638980
  49.8 12.5 %collective-permute-start.14 = (bf16[2,3,16,3328]{3,2,1,0:T(8,128)(2,1)}, bf16[2,3,16,3328]{3,2,1,0:T(8,128)(2,1)}, u32[]{:S(2)}, u32[]{:S(2)}) collective-permute-start(bf16[2,3,16,3328]{3,2,1,0:T(8,128)(2,1)} %collective-permute-done.7.rest_6_), channel_id=1, source_target_pairs={{0,1},{1,0},{2,3},{3,2},{4,5},{5,4},{6,7},{7,6},{8,9},{9,8},{10,11... | collective-permute-start | bytes 1916936 | tf_op jit(solution)/shard_map/ppermute | solution.py:29
  50.0 12.2 %copy-start.15 = (bf16[2,1,16,3328]{3,2,1,0:T(8,128)(2,1)}, bf16[2,1,16,3328]{3,2,1,0:T(8,128)(2,1)S(1)}, u32[]{:S(2)}) copy-start(bf16[2,1,16,3328]{3,2,1,0:T(8,128)(2,1)S(1)} %collective-permute-done.9.rest_8_) | copy-start | bytes 638980
  50.0 12.2 %collective-permute-start.17 = (bf16[3,16,3328]{2,1,0:T(8,128)(2,1)S(1)}, bf16[3,16,3328]{2,1,0:T(8,128)(2,1)}, u32[]{:S(2)}, u32[]{:S(2)}) collective-permute-start(bf16[3,16,3328]{2,1,0:T(8,128)(2,1)S(1)} %slice_bitcast_fusion), channel_id=1, source_target_pairs={{0,4},{4,0},{8,12},{12,8},{16,20},{20,16},{24,28},{28,24},{1,5},{5... | collective-permute-start | bytes 958472 | tf_op jit(solution)/shard_map/ppermute | solution.py:29
  58.9 5.3 %copy-start.10 = (bf16[3,16,3328]{2,1,0:T(8,128)(2,1)}, bf16[3,16,3328]{2,1,0:T(8,128)(2,1)S(1)}, u32[]{:S(2)}) copy-start(bf16[3,16,3328]{2,1,0:T(8,128)(2,1)S(1)} %collective-permute-done.15.rest_14_) | copy-start | bytes 958468
  58.9 3.4 %collective-permute-start.16 = (bf16[3,16,3328]{2,1,0:T(8,128)(2,1)S(1)}, bf16[3,16,3328]{2,1,0:T(8,128)(2,1)}, u32[]{:S(2)}, u32[]{:S(2)}) collective-permute-start(bf16[3,16,3328]{2,1,0:T(8,128)(2,1)S(1)} %collective-permute-done.15.rest_14_), channel_id=1, source_target_pairs={{0,1},{1,0},{2,3},{3,2},{4,5},{5,4},{6,7},{7,6},{8,9},{9,8},{10,11... | collective-permute-start | bytes 958472 | tf_op jit(solution)/shard_map/ppermute | solution.py:29
  62.2 2.0 %collective-permute-start.18 = (bf16[3,16,3328]{2,1,0:T(8,128)(2,1)}, bf16[3,16,3328]{2,1,0:T(8,128)(2,1)}, u32[]{:S(2)}, u32[]{:S(2)}) collective-permute-start(bf16[3,16,3328]{2,1,0:T(8,128)(2,1)} %collective-permute-done.17.rest_16_), channel_id=1, source_target_pairs={{0,1},{1,0},{2,3},{3,2},{4,5},{5,4},{6,7},{7,6},{8,9},{9,8},{10,11... | collective-permute-start | bytes 958472 | tf_op jit(solution)/shard_map/ppermute | solution.py:29
  64.2 0.9 copy-start.6
  75.9 7.3 %copy-start.16 = (f32[512,128]{1,0:T(8,128)S(1)}, f32[512,128]{1,0:T(8,128)}, u32[]{:S(2)}) copy-start(f32[512,128]{1,0:T(8,128)} %get-tuple-element.18) | copy-start | bytes 786436
  75.9 8.9 %copy-start.11 = (f32[512,128]{1,0:T(8,128)S(1)}, f32[512,128]{1,0:T(8,128)}, u32[]{:S(2)}) copy-start(f32[512,128]{1,0:T(8,128)} %get-tuple-element.17) | copy-start | bytes 786436
  75.9 29.1 %all-to-all-start.2 = ((bf16[8,416,128]{2,1,0:T(8,128)(2,1)}), bf16[8,416,128]{2,1,0:T(8,128)(2,1)S(1)}, u32[]{:S(2)}, u32[]{:S(2)}) async-start(bf16[8,416,128]{2,1,0:T(8,128)(2,1)} %bitcast.38), calls=%async_computation.2 | async-start | bytes 1703936 | tf_op jit(solution)/shard_map/all_to_all | solution.py:387
  83.2 1.6 %collective-permute-start.19 = (f32[512,128]{1,0:T(8,128)S(1)}, f32[512,128]{1,0:T(8,128)S(1)}, u32[]{:S(2)}, u32[]{:S(2)}) collective-permute-start(f32[512,128]{1,0:T(8,128)S(1)} %copy-done.16), channel_id=1, source_target_pairs={{0,1},{1,0},{2,3},{3,2},{4,5},{5,4},{6,7},{7,6},{8,9},{9,8},{10,11... | collective-permute-start | bytes 786440 | tf_op jit(solution)/shard_map/ppermute | solution.py:29
  84.9 5.7 %collective-permute-start.20 = (f32[256,128]{1,0:T(8,128)S(1)}, f32[256,128]{1,0:T(8,128)S(1)}, u32[]{:S(2)}, u32[]{:S(2)}) collective-permute-start(f32[256,128]{1,0:T(8,128)S(1)} %constant_dynamic-slice_fusion.1), channel_id=1, source_target_pairs={{0,2},{1,3},{2,0},{3,1},{4,6},{5,7},{6,4},{7,5},{8,10},{9,11},{10,... | collective-permute-start | bytes 393224 | tf_op jit(solution)/shard_map/ppermute | solution.py:29
  90.7 4.8 %collective-permute-start.21 = (f32[128,128]{1,0:T(8,128)S(1)}, f32[128,128]{1,0:T(8,128)S(1)}, u32[]{:S(2)}, u32[]{:S(2)}) collective-permute-start(f32[128,128]{1,0:T(8,128)S(1)} %constant_dynamic-slice_fusion), channel_id=1, source_target_pairs={{0,4},{4,0},{8,12},{12,8},{16,20},{20,16},{24,28},{28,24},{1,5},{5... | collective-permute-start | bytes 196616 | tf_op jit(solution)/shard_map/ppermute | solution.py:29
  95.5 6.1 %collective-permute-start.22 = (f32[128,128]{1,0:T(8,128)S(1)}, f32[128,128]{1,0:T(8,128)S(1)}, u32[]{:S(2)}, u32[]{:S(2)}) collective-permute-start(f32[128,128]{1,0:T(8,128)S(1)} %dynamic-slice_add_fusion.1), channel_id=1, source_target_pairs={{0,8},{4,12},{8,0},{12,4},{16,24},{20,28},{24,16},{28,20},{1,9},{5... | collective-permute-start | bytes 196616 | tf_op jit(solution)/shard_map/ppermute | solution.py:29
  107.1 10.5 %collective-permute-start.27 = (f32[1024,128]{1,0:T(8,128)S(1)}, f32[1024,128]{1,0:T(8,128)S(1)}, u32[]{:S(2)}, u32[]{:S(2)}) collective-permute-start(f32[1024,128]{1,0:T(8,128)S(1)} %cold_sum.2), channel_id=1, source_target_pairs={{0,1},{1,0},{2,3},{3,2},{4,5},{5,4},{6,7},{7,6},{8,9},{9,8},{10,11... | collective-permute-start | bytes 1572872 | tf_op jit(solution)/shard_map/ppermute | solution.py:29
  107.2 6.9 %collective-permute-start.23 = (f32[128,128]{1,0:T(8,128)S(1)}, f32[128,128]{1,0:T(8,128)}, u32[]{:S(2)}, u32[]{:S(2)}) collective-permute-start(f32[128,128]{1,0:T(8,128)S(1)} %add.51), channel_id=1, source_target_pairs={{0,16},{4,20},{8,24},{12,28},{16,0},{20,4},{24,8},{28,12},{1,17},{... | collective-permute-start | bytes 196616 | tf_op jit(solution)/shard_map/ppermute | solution.py:29
  117.6 8.5 %collective-permute-start.28 = (bf16[1024,128]{1,0:T(8,128)(2,1)S(1)}, bf16[1024,128]{1,0:T(8,128)(2,1)S(1)}, u32[]{:S(2)}, u32[]{:S(2)}) collective-permute-start(bf16[1024,128]{1,0:T(8,128)(2,1)S(1)} %add_convert_fusion), channel_id=1, source_target_pairs={{0,2},{1,3},{2,0},{3,1},{4,6},{5,7},{6,4},{7,5},{8,10},{9,11},{10,... | collective-permute-start | bytes 786440 | tf_op jit(solution)/shard_map/ppermute | solution.py:29
  119.5 4.5 %collective-permute-start.24 = (f32[128,128]{1,0:T(8,128)}, f32[128,128]{1,0:T(8,128)S(1)}, u32[]{:S(2)}, u32[]{:S(2)}) collective-permute-start(f32[128,128]{1,0:T(8,128)} %add.52), channel_id=1, source_target_pairs={{0,4},{4,0},{8,12},{12,8},{16,20},{20,16},{24,28},{28,24},{1,5},{5... | collective-permute-start | bytes 196616 | tf_op jit(solution)/shard_map/ppermute | solution.py:29
  125.0 5.0 %collective-permute-start.25 = (f32[256,128]{1,0:T(8,128)S(1)}, f32[256,128]{1,0:T(8,128)S(1)}, u32[]{:S(2)}, u32[]{:S(2)}) collective-permute-start(f32[256,128]{1,0:T(8,128)S(1)} %maximum_select_fusion.3), channel_id=1, source_target_pairs={{0,2},{1,3},{2,0},{3,1},{4,6},{5,7},{6,4},{7,5},{8,10},{9,11},{10,... | collective-permute-start | bytes 393224 | tf_op jit(solution)/shard_map/ppermute | solution.py:29
  126.2 5.4 %copy-start.12 = (bf16[1024,128]{1,0:T(8,128)(2,1)S(1)}, bf16[1024,128]{1,0:T(8,128)(2,1)}, u32[]{:S(2)}) copy-start(bf16[1024,128]{1,0:T(8,128)(2,1)} %param.17) | copy-start | bytes 786436
  126.2 6.4 %collective-permute-start.29 = (f32[1024,128]{1,0:T(8,128)S(1)}, f32[1024,128]{1,0:T(8,128)S(1)}, u32[]{:S(2)}, u32[]{:S(2)}) collective-permute-start(f32[1024,128]{1,0:T(8,128)S(1)} %convert_add_fusion), channel_id=1, source_target_pairs={{0,1},{1,0},{2,3},{3,2},{4,5},{5,4},{6,7},{7,6},{8,9},{9,8},{10,11... | collective-permute-start | bytes 1572872 | tf_op jit(solution)/shard_map/ppermute | solution.py:29
  130.0 1.6 %collective-permute-start.26 = (f32[512,128]{1,0:T(8,128)S(1)}, f32[512,128]{1,0:T(8,128)S(1)}, u32[]{:S(2)}, u32[]{:S(2)}) collective-permute-start(f32[512,128]{1,0:T(8,128)S(1)} %maximum_select_fusion.2), channel_id=1, source_target_pairs={{0,1},{1,0},{2,3},{3,2},{4,5},{5,4},{6,7},{7,6},{8,9},{9,8},{10,11... | collective-permute-start | bytes 786440 | tf_op jit(solution)/shard_map/ppermute | solution.py:29
  130.1 2.5 %copy-start.9 = (bf16[2048,128]{1,0:T(8,128)(2,1)S(1)}, bf16[2048,128]{1,0:T(8,128)(2,1)}, u32[]{:S(2)}) copy-start(bf16[2048,128]{1,0:T(8,128)(2,1)} %param.19) | copy-start | bytes 1572868
